TPU v7x, 32 devices: a whole 2x2x4 slice. The times are simulated.
32 devices in a mesh: groups: 2 (over y), seq: 4 (over z), mp: 2 (over x), side: 2 (over core).
Axes of the slice: x: 2, y: 2, z: 4, core: 2. Of those that a mesh axis runs over, the one named last changes fastest.
Arguments:
- teacher_queries: bfloat16 [1024, 4096], P(('groups', 'seq'), ('mp', 'side')), parts along dimension 0, may hold values from -5 to 5
- teacher_keys: bfloat16 [1024, 512], P(('groups', 'seq'), 'mp'), parts along dimension 0, may hold values from -5 to 5
- teacher_values: bfloat16 [1024, 512], P(('groups', 'seq'), 'mp'), parts along dimension 0, may hold values from -18 to 18
- doc_ids: int32 [1024], P(('groups', 'seq')), parts along dimension 0, may hold values from 0 to 11, never falling along the last dimension, each value on 1 to 384 neighbouring positions
- owner: int32 [1024, 1], P(('groups', 'seq')), parts along dimension 0, may hold values from 0 to 3; in each aligned block of 128 rows (0 to 127, 128 to 255, ...) at most 48 rows name the same one
- student_hidden: bfloat16 [1536, 3584], P(('groups', 'seq')), parts along dimension 0, may hold values from -400 to 400
- norm_gain: float32 [3584], replicated, may hold values from 0.5 to 1.5
- proj: bfloat16 [3584, 4096], P('seq', ('mp', 'side')), may hold values from -0.09375 to 0.09375
Outputs:
- grad_hidden: bfloat16 [1536, 3584], P(('groups', 'seq')), parts along dimension 0
- grad_proj: float32 [7168, 4096], P(('groups', 'seq'), ('mp', 'side')), parts along dimension 0
There are 2 independent parts, one for each index of `groups`. A program takes and returns all parts, laid end to end along the dimension named above; an argument that names none is the same for every part. Nothing has to cross between parts.
Inputs may be any that keep to these rules, and one draw needn't show every extreme that they name: `doc_ids`: document numbers never fall along the positions; each document has at most 384 positions. `owner`: among the 128 rows of one sequence shard, no student shard is named more than 48 times.
All inputs are finite; a program needn't handle non-finite values.
Results may differ from a plain program's by a relative error of at most 0.013.
Values may be sent and summed in bfloat16 or wider, within the bound.
No kernel may reach another device: no remote copies, remote signals or barrier semaphores. Data moves between devices by JAX's collectives and lax.ppermute only.
A program may use at most 64 MiB of HBM per device.

v0:
```python
import math

import jax
import jax.numpy as jnp
from jax import lax
from jax.sharding import PartitionSpec as P

HD = 128


def on_device(
    teacher_queries, teacher_keys, teacher_values, doc_ids, owner, student_hidden, norm_gain, proj
):
    shard_count = lax.axis_size("seq")
    shard_index = lax.axis_index("seq")
    side_index = lax.axis_index("side")
    row_count = teacher_queries.shape[0]
    heads_local = teacher_queries.shape[1] // HD
    kv_local = teacher_keys.shape[1] // HD
    group_size = heads_local * lax.axis_size("side") // kv_local
    seq_length = row_count * shard_count
    queries = teacher_queries.reshape(row_count, heads_local, HD)
    head_kv = (side_index * heads_local + jnp.arange(heads_local, dtype=jnp.int32)) // group_size
    query_pos = shard_index * row_count + jnp.arange(row_count, dtype=jnp.int32)
    query_seq = query_pos // seq_length
    scale_factor = 1.0 / math.sqrt(HD)
    initial = (
        jnp.full((heads_local, row_count), -1e30, jnp.float32),
        jnp.zeros((heads_local, row_count), jnp.float32),
        jnp.zeros((heads_local, row_count, HD), jnp.float32),
    )
    running_state = initial
    first_row = jnp.int32(0)
    key_piece = lax.all_gather(teacher_keys, "seq", axis=0, tiled=True)
    value_piece = lax.all_gather(teacher_values, "seq", axis=0, tiled=True)
    doc_piece = lax.all_gather(doc_ids.astype(jnp.bfloat16), "seq", axis=0, tiled=True)
    piece_len = key_piece.shape[0]
    for offset in range(0, piece_len, 1024):
        block_width = min(1024, piece_len - offset)
        key_block = key_piece[offset : offset + block_width]
        value_block = value_piece[offset : offset + block_width]
        doc_block = doc_piece[offset : offset + block_width]
        block_first = first_row + offset
        max_now, total_now, accumulated = running_state
        key_count = key_block.shape[0]
        key_heads = jnp.take(key_block.reshape(key_count, kv_local, HD), head_kv, axis=1)
        value_heads = jnp.take(value_block.reshape(key_count, kv_local, HD), head_kv, axis=1)
        scores = (
            jnp.einsum("qhd,khd->hqk", queries, key_heads, preferred_element_type=jnp.float32)
            * scale_factor
        )
        key_pos = block_first + jnp.arange(key_count, dtype=jnp.int32)
        allowed = doc_block.astype(jnp.int32)[None, :] == doc_ids[:, None]
        allowed = allowed & (key_pos[None, :] <= query_pos[:, None])
        allowed = allowed & ((key_pos // seq_length)[None, :] == query_seq[:, None])
        scores = jnp.where(allowed[None], scores, -1e30)
        max_next = jnp.maximum(max_now, jnp.max(scores, axis=2))
        correction = jnp.exp(max_now - max_next)
        weights = jnp.where(allowed[None], jnp.exp(scores - max_next[:, :, None]), 0.0)
        total_next = total_now * correction + jnp.sum(weights, axis=2)
        weighted = jnp.einsum(
            "hqk,khd->hqd",
            weights.astype(jnp.bfloat16),
            value_heads,
            preferred_element_type=jnp.float32,
        )
        running_state = (max_next, total_next, accumulated * correction[:, :, None] + weighted)
    max_final, total_final, accum_final = running_state
    teacher_rows = (accum_final / total_final[:, :, None]).transpose(1, 0, 2)
    teacher_rows = teacher_rows.reshape(row_count, heads_local * HD).astype(jnp.bfloat16)
    feature_width = teacher_rows.shape[1]
    capacity = student_hidden.shape[0]
    slot_count = capacity // shard_count
    shard_ids = jnp.arange(shard_count, dtype=jnp.int32)
    slot_ids = jnp.arange(capacity, dtype=jnp.int32)
    dest = owner[:, 0]
    onehot = (dest[:, None] == shard_ids[None, :]).astype(jnp.int32)
    rank = jnp.sum((jnp.cumsum(onehot, axis=0) - onehot) * onehot, axis=1)
    slot_index = dest * slot_count + rank
    selector = (slot_index[None, :] == slot_ids[:, None]).astype(jnp.bfloat16)
    packed = jnp.dot(selector, teacher_rows, preferred_element_type=jnp.float32).astype(
        jnp.bfloat16
    )
    packed = packed.reshape(shard_count, slot_count, feature_width)
    occupied = (
        jnp.sum(selector.astype(jnp.float32), axis=1)
        .astype(jnp.bfloat16)
        .reshape(shard_count, slot_count)
    )
    received, received_fill = (
        lax.all_to_all(packed, "seq", split_axis=0, concat_axis=0, tiled=True),
        lax.all_to_all(occupied, "seq", split_axis=0, concat_axis=0, tiled=True),
    )
    targets = received.reshape(capacity, feature_width)
    filled = received_fill.reshape(capacity).astype(jnp.float32)
    hidden_float = student_hidden.astype(jnp.float32)
    inverse_rms = lax.rsqrt(jnp.mean(hidden_float * hidden_float, axis=1, keepdims=True) + 1e-06)
    normed = (hidden_float * inverse_rms * norm_gain).astype(jnp.bfloat16)
    weight_full = lax.all_gather(proj, "seq", axis=0, tiled=True)
    predicted = jnp.dot(normed, weight_full, preferred_element_type=jnp.float32)
    delta = ((predicted - targets.astype(jnp.float32)) * filled[:, None]).astype(jnp.bfloat16)
    partial_grad = lax.dot_general(
        delta, weight_full, (((1,), (1,)), ((), ())), preferred_element_type=jnp.float32
    )
    feature_grad = lax.psum(partial_grad.astype(jnp.bfloat16), ("mp", "side")).astype(jnp.float32)
    gain_grad = feature_grad * norm_gain
    mean_term = jnp.mean(gain_grad * hidden_float, axis=1, keepdims=True)
    grad_hidden = (inverse_rms * gain_grad - inverse_rms**3 * hidden_float * mean_term).astype(
        jnp.bfloat16
    )
    factor = 1.0 / math.sqrt(row_count * shard_count)
    grad_proj = lax.psum_scatter(
        (
            lax.dot_general(
                normed, delta, (((0,), (0,)), ((), ())), preferred_element_type=jnp.float32
            )
            * factor
        ).astype(jnp.bfloat16),
        "seq",
        scatter_dimension=0,
        tiled=True,
    ).astype(jnp.float32)
    return (grad_hidden, grad_proj)


def solution(mesh):
    return jax.shard_map(
        on_device,
        mesh=mesh,
        in_specs=(
            P(("groups", "seq"), ("mp", "side")),
            P(("groups", "seq"), "mp"),
            P(("groups", "seq"), "mp"),
            P(("groups", "seq")),
            P(("groups", "seq"), None),
            P(("groups", "seq"), None),
            P(),
            P("seq", ("mp", "side")),
        ),
        out_specs=(P(("groups", "seq"), None), P(("groups", "seq"), ("mp", "side"))),
        check_vma=False,
    )
```

profile of v0, /device:TPU:0, one launch (start us, length us, event | category | flops | bytes accessed | tf_op | source)
XLA Modules:
  0.0 349.1 jit_solution(14461134104484448466)
XLA Ops:
  7.2 0.0 copy-start
  7.2 0.0 copy-start.6
  7.2 0.0 copy-start.7
  7.2 0.0 copy-start.4
  7.2 0.0 copy-start.5
  7.2 0.0 all-gather.3.cloned.1.call-start
  7.3 0.7 all-gather.3.cloned.1.call-update
  8.0 0.7 fusion.37
  8.7 0.2 reduce_window_sum.11
  8.9 0.8 select_reduce_fusion
  9.7 0.0 copy-done.6
  9.7 0.1 fusion.38
  9.8 0.7 all_to_all.12
  10.5 6.3 %all-to-all-start.1 = ((bf16[4,1,48]{2,1,0:T(2,128)(2,1)}), bf16[4,1,48]{2,1,0:T(2,128)(2,1)S(1)}, u32[]{:S(2)}, u32[]{:S(2)}) async-start(bf16[4,1,48]{2,1,0:T(2,128)(2,1)} %all_to_all.12), calls=%async_computation.1 | async-start | bytes 4096 | tf_op jit(solution)/shard_map/all_to_all | solution.py:92
  16.8 0.0 copy-done.7
  16.8 11.4 %all-gather = bf16[4,1,128]{2,1,0:T(2,128)(2,1)S(1)} all-gather(bf16[1,1,128]{2,1,0:T(2,128)(2,1)S(1)} %convert_bitcast_fusion), channel_id=1, replica_groups=mesh['groups'=2,'seq'=4,'mp'=2,'side'=2] {'seq'}, dimensions={0}, use_global_device_ids=true | all-gather | bytes 1280 | tf_op jit(solution)/shard_map/all_gather | solution.py:36
  28.2 0.0 copy-done.4
  28.2 0.1 copy.30
  28.3 16.9 %all_gather.14 = bf16[512,256]{0,1:T(8,128)(2,1)S(1)} all-gather(bf16[128,256]{0,1:T(8,128)(2,1)S(1)} %copy.30), channel_id=1, replica_groups=mesh['groups'=2,'seq'=4,'mp'=2,'side'=2] {'seq'}, dimensions={0}, use_global_device_ids=true | all-gather | bytes 327680 | tf_op jit(solution)/shard_map/all_gather | solution.py:34
  45.3 0.2 copy.31
  45.5 0.0 copy-done.5
  45.5 0.1 copy.33
  45.6 21.9 %all_gather.15 = bf16[512,256]{0,1:T(8,128)(2,1)S(1)} all-gather(bf16[128,256]{0,1:T(8,128)(2,1)S(1)} %copy.33), channel_id=1, replica_groups=mesh['groups'=2,'seq'=4,'mp'=2,'side'=2] {'seq'}, dimensions={0}, use_global_device_ids=true | all-gather | bytes 327680 | tf_op jit(solution)/shard_map/all_gather | solution.py:35
  67.5 0.2 copy.34
  67.7 0.7 gather_fusion
  68.5 0.7 gather_fusion.1
  69.3 0.2 fusion.35
  69.5 0.0 copy-done
  69.5 0.5 fusion.7
  70.0 0.5 fusion.8
  70.6 1.0 fusion.14
  71.6 0.0 copy-start.1
  71.6 0.0 copy-start.3
  71.6 1.0 convolution_convert_fusion.1
  72.6 0.0 all-to-all-done.1
  72.6 3.5 all-to-all-start
  76.1 0.0 all-reduce.2.cloned.1.call-start
  76.2 0.0 copy-done.1
  76.2 0.4 fusion
  76.6 0.1 reshape.193
  76.6 20.4 %all-to-all-done = bf16[4,48,1024]{2,1,0:T(8,128)(2,1)S(1)} async-done(((bf16[4,48,1024]{2,1,0:T(8,128)(2,1)}), bf16[4,48,1024]{2,1,0:T(8,128)(2,1)S(1)}, u32[]{:S(2)}, u32[]{:S(2)}) %all-to-all-start) | async-done | bytes 393248 | tf_op jit(solution)/shard_map/all_to_all | solution.py:91
  97.1 64.5 %all-gather.3.cloned.1.call-done = bf16[3584,1024]{1,0:T(8,128)(2,1)} async-done(((bf16[896,1024]{1,0:T(8,128)(2,1)}), bf16[3584,1024]{1,0:T(8,128)(2,1)}) %all-gather.3.cloned.1.call-update) | async-done | bytes 7340048 | tf_op jit(solution)/shard_map/all_gather | solution.py:99
  161.5 0.0 copy-done.3
  161.5 0.0 copy-start.8
  161.5 4.9 %fusion.11 = bf16[192,1024]{1,0:T(8,128)(2,1)S(1)} fusion(bf16[3584,1024]{1,0:T(8,128)(2,1)} %all-gather.3.cloned.1.call-done, bf16[192,1024]{1,0:T(8,128)(2,1)S(1)} %bitcast.60, f32[192]{0:T(256)S(1)} %reshape.193, bf16[192,3584]{1,0:T(8,128)(2,1)S(1)} %copy-done.1, f32[3584]{0:T(1024)S(1)} %copy-done.3, f32[192]{0:T(256)S(1)} %get-tuple-element.6), kind=kOutput, calls=%fused_computation.23 | convolution fusion | flops 1412825088 | bytes 9518592 | tf_op jit(solution)/shard_map/dot_general | solution.py:100
  166.5 0.2 copy-done.8
  166.7 3.6 %convolution_convert_fusion = bf16[192,3584]{1,0:T(8,128)(2,1)} fusion(bf16[192,1024]{1,0:T(8,128)(2,1)S(1)} %fusion.11, bf16[3584,1024]{1,0:T(8,128)(2,1)S(1)} %copy-done.8), kind=kOutput, calls=%fused_computation.3 | convolution fusion | flops 1409974272 | bytes 9109504 | tf_op jit(solution)/shard_map/dot_general | solution.py:102
  170.3 0.0 all-reduce.2.cloned.1.call-update
  170.4 0.2 reduce-scatter.2.cloned.1.call-start
  170.6 5.2 %multiply_convert_fusion = bf16[3584,1024]{1,0:T(8,128)(2,1)} fusion(bf16[192,1024]{1,0:T(8,128)(2,1)S(1)} %fusion.11, bf16[192,3584]{1,0:T(8,128)(2,1)S(1)} %copy-done.1, f32[3584]{0:T(1024)S(1)} %copy-done.3, f32[192]{0:T(256)S(1)} %get-tuple-element.6), kind=kOutput, calls=%fused_computation.2 | convolution fusion | flops 1419378688 | bytes 9124608 | tf_op jit(solution)/shard_map/dot_general | solution.py:114
  175.8 0.0 reduce-scatter.2.cloned.1.call-update
  175.8 32.7 %all-reduce.2.cloned.1.call-done = bf16[192,3584]{1,0:T(8,128)(2,1)} async-done(((bf16[192,3584]{1,0:T(8,128)(2,1)}), bf16[192,3584]{1,0:T(8,128)(2,1)}) %all-reduce.2.cloned.1.call-update) | async-done | bytes 1376272 | tf_op jit(solution)/shard_map/psum | solution.py:105
  208.5 0.0 copy-start.2
  208.5 2.0 fusion.6
  210.5 0.0 copy-done.2
  210.5 2.1 fusion.5
  212.7 126.1 %reduce-scatter.2.cloned.1.call-done = bf16[896,1024]{1,0:T(8,128)(2,1)} async-done(((bf16[3584,1024]{1,0:T(8,128)(2,1)}), bf16[896,1024]{1,0:T(8,128)(2,1)}) %reduce-scatter.2.cloned.1.call-update) | async-done | bytes 1835024 | tf_op jit(solution)/shard_map/reduce_scatter | solution.py:112
  338.8 3.7 %convert_element_type.85 = f32[896,1024]{1,0:T(8,128)} convert(bf16[896,1024]{1,0:T(8,128)(2,1)} %reduce-scatter.2.cloned.1.call-done) | non-fusion elementwise | flops 917504 | bytes 5505024 | tf_op jit(solution)/shard_map/convert_element_type | solution.py:122
  (13 shorter events, 0.1 us)
Async XLA Ops:
  7.2 62.3 %copy-start = (bf16[128,1024]{1,0:T(8,128)(2,1)S(1)}, bf16[128,1024]{1,0:T(8,128)(2,1)}, u32[]{:S(2)}) copy-start(bf16[128,1024]{1,0:T(8,128)(2,1)} %param.10) | copy-start | bytes 786436
  7.2 2.5 copy-start.6
  7.2 9.6 %copy-start.7 = (s32[128]{0:T(128)S(1)}, s32[128]{0:T(128)}, u32[]{:S(2)}) copy-start(s32[128]{0:T(128)} %param.13) | copy-start | bytes 1540
  7.2 21.0 %copy-start.4 = (bf16[128,256]{1,0:T(8,128)(2,1)S(1)}, bf16[128,256]{1,0:T(8,128)(2,1)}, u32[]{:S(2)}) copy-start(bf16[128,256]{1,0:T(8,128)(2,1)} %param.11) | copy-start | bytes 196612
  7.2 38.3 %copy-start.5 = (bf16[128,256]{1,0:T(8,128)(2,1)S(1)}, bf16[128,256]{1,0:T(8,128)(2,1)}, u32[]{:S(2)}) copy-start(bf16[128,256]{1,0:T(8,128)(2,1)} %param.12) | copy-start | bytes 196612
  7.2 154.3 %all-gather.3.cloned.1.call-start = ((), (), s32[]{:S(2)}) async-start(), calls=%async_computation.3 | async-start | bytes 9175040 | tf_op jit(solution)/shard_map/all_gather | solution.py:99
  10.5 62.1 %all-to-all-start.1 = ((bf16[4,1,48]{2,1,0:T(2,128)(2,1)}), bf16[4,1,48]{2,1,0:T(2,128)(2,1)S(1)}, u32[]{:S(2)}, u32[]{:S(2)}) async-start(bf16[4,1,48]{2,1,0:T(2,128)(2,1)} %all_to_all.12), calls=%async_computation.1 | async-start | bytes 4096 | tf_op jit(solution)/shard_map/all_to_all | solution.py:92
  71.6 4.6 %copy-start.1 = (bf16[192,3584]{1,0:T(8,128)(2,1)S(1)}, bf16[192,3584]{1,0:T(8,128)(2,1)}, u32[]{:S(2)}) copy-start(bf16[192,3584]{1,0:T(8,128)(2,1)} %param.15) | copy-start | bytes 4128772
  71.6 89.9 %copy-start.3 = (f32[3584]{0:T(1024)S(1)}, f32[3584]{0:T(1024)}, u32[]{:S(2)}) copy-start(f32[3584]{0:T(1024)} %param.16) | copy-start | bytes 43012
  72.6 24.4 %all-to-all-start = ((bf16[4,48,1024]{2,1,0:T(8,128)(2,1)}), bf16[4,48,1024]{2,1,0:T(8,128)(2,1)S(1)}, u32[]{:S(2)}, u32[]{:S(2)}) async-start(bf16[4,48,1024]{2,1,0:T(8,128)(2,1)} %bitcast.12), calls=%async_computation | async-start | bytes 786432 | tf_op jit(solution)/shard_map/all_to_all | solution.py:91
  76.1 132.4 %all-reduce.2.cloned.1.call-start = ((), (), s32[]{:S(2)}) async-start(), calls=%async_computation.4 | async-start | bytes 2752512 | tf_op jit(solution)/shard_map/psum | solution.py:105
  161.5 5.2 %copy-start.8 = (bf16[3584,1024]{1,0:T(8,128)(2,1)S(1)}, bf16[3584,1024]{1,0:T(8,128)(2,1)}, u32[]{:S(2)}) copy-start(bf16[3584,1024]{1,0:T(8,128)(2,1)} %all-gather.3.cloned.1.call-done) | copy-start | bytes 22020100
  170.4 168.4 %reduce-scatter.2.cloned.1.call-start = ((), (), s32[]{:S(2)}) async-start(), calls=%async_computation.5 | async-start | bytes 9175040 | tf_op jit(solution)/shard_map/reduce_scatter | solution.py:112
  208.5 2.0 copy-start.2
Sparse Core Ops, SparseCore 0:
  9.6 151.8 all-gather.2
  170.5 37.9 all-reduce.1
  210.9 127.7 reduce-scatter.1
where the time goes:
time: 349 us
  waiting for transfers between devices  244 us (70%)
  blocking collectives  50.2 us (14%)
  matrix products  16.3 us (5%)
  between operations  14 us (4%)
  other arithmetic  10.9 us (3%)
  starting transfers between devices  10.1 us (3%)
    reduce_scatter x1, waiting for transfers between devices, on_device(): lax.psum_scatter((lax.dot_general(normed, delta, (((0,), (0,)), ((), ()))...  126 us
    all_gather x1, waiting for transfers between devices, on_device(): weight_full = lax.all_gather(proj, 'seq', axis=0, tiled=True)  64.5 us
    psum x1, waiting for transfers between devices, on_device(): lax.psum(partial_grad.astype(jnp.bfloat16), ('mp', 'side'))  32.7 us
    all_gather x1, blocking collectives, on_device(): value_piece = lax.all_gather(teacher_values, 'seq', axis=0, tiled=True)  21.9 us
    all_to_all x1, waiting for transfers between devices, on_device(): lax.all_to_all(packed, 'seq', split_axis=0, concat_axis=0, tiled=True)  20.4 us
    all_gather x1, blocking collectives, on_device(): key_piece = lax.all_gather(teacher_keys, 'seq', axis=0, tiled=True)  16.9 us
    all_gather x1, blocking collectives, on_device(): lax.all_gather(doc_ids.astype(jnp.bfloat16), 'seq', axis=0, tiled=True)  11.4 us
  transfers between devices with their start and end apart: 5, of which 4 were waited for; matrix products, arithmetic and copies ran while one was open for 5% of the time, Pallas kernels for 0%

commit v1 on v0

v1 whole, which is shorter than its diff:
```python
import math

import jax
import jax.numpy as jnp
from jax import lax
from jax.sharding import PartitionSpec as P

HD = 128
DIRECT = 4
BF = jnp.bfloat16
F32 = jnp.float32


def seq_size():
    return lax.axis_size("seq")


def plane_size():
    return lax.axis_size("mp") * lax.axis_size("side")


def seq_direct():
    return seq_size() <= DIRECT


def plane_direct():
    return lax.axis_size("mp") == 2 and lax.axis_size("side") == 2 and seq_size() == 4


def place(peer):
    if seq_direct():
        return (lax.axis_index("seq") - peer) % seq_size()
    return peer


def shift(x, step):
    n = seq_size()
    return lax.ppermute(x, "seq", [(i, (i + step) % n) for i in range(n)])


def gather_seq(x):
    if not seq_direct():
        return lax.all_gather(x, "seq", axis=0, tiled=False)
    n = seq_size()
    return jnp.stack([x] + [shift(x, step) for step in range(1, n)])


def exchange_seq(piece_for):
    n = seq_size()
    if not seq_direct():
        pieces = jnp.stack([piece_for(z) for z in range(n)])
        return lax.all_to_all(pieces, "seq", split_axis=0, concat_axis=0, tiled=True)
    me = lax.axis_index("seq")
    sent = [shift(piece_for((me + step) % n), step) for step in range(1, n)]
    return jnp.stack([piece_for(me)] + sent)


def swap(x, axis):
    return lax.ppermute(x, axis, [(0, 1), (1, 0)])


def gather_plane(x):
    if not plane_direct():
        return lax.all_gather(x, ("mp", "side"), axis=0, tiled=False)
    side = lax.axis_index("side")
    mp = lax.axis_index("mp")
    mate = swap(x, "side")
    far = swap(x, "mp")
    far_mate = swap(far, "side")
    own = jnp.where(side == 0, jnp.stack([x, mate]), jnp.stack([mate, x]))
    other = jnp.where(side == 0, jnp.stack([far, far_mate]), jnp.stack([far_mate, far]))
    return jnp.where(mp == 0, jnp.concatenate([own, other]), jnp.concatenate([other, own]))


def scatter_plane(piece_for, width):
    if not plane_direct():
        pieces = jnp.concatenate([piece_for(j) for j in range(plane_size())])
        return lax.psum_scatter(
            pieces.astype(BF), ("mp", "side"), scatter_dimension=0, tiled=True
        ).astype(F32)
    side = lax.axis_index("side")
    mp = lax.axis_index("mp")
    away_far = piece_for((1 - mp) * 2 + (1 - side)).astype(BF)
    away_near = piece_for(mp * 2 + (1 - side)).astype(BF)
    got_far = swap(away_far, "side")
    got_near = swap(away_near, "side")
    far = piece_for((1 - mp) * 2 + side) + got_far.astype(F32)
    crossed = swap(far.astype(BF), "mp")
    near = piece_for(mp * 2 + side) + got_near.astype(F32)
    return near + crossed.astype(F32)


def attention(queries, keys, values, key_docs, doc_ids):
    n = seq_size()
    me = lax.axis_index("seq")
    rows = queries.shape[0]
    heads = queries.shape[1] // HD
    peers = jnp.arange(n, dtype=jnp.int32)
    blocks = (me - peers) % n if seq_direct() else peers
    key_pos = (blocks[:, None] * rows + jnp.arange(rows, dtype=jnp.int32)[None, :]).reshape(-1)
    query_pos = me * rows + jnp.arange(rows, dtype=jnp.int32)
    allowed = (key_docs.reshape(-1)[None, :] == doc_ids[:, None]) & (
        key_pos[None, :] <= query_pos[:, None]
    )
    stacked = queries.reshape(rows, heads, HD).transpose(1, 0, 2)
    scale_factor = 1.0 / math.sqrt(HD)
    scores = (
        jnp.einsum("hqd,kd->hqk", stacked, keys.reshape(-1, HD), preferred_element_type=F32)
        * scale_factor
    )
    scores = jnp.where(allowed[None], scores, -1e30)
    top = jnp.max(scores, axis=2, keepdims=True)
    probs = jnp.where(allowed[None], jnp.exp(scores - top), 0.0)
    totals = jnp.sum(probs, axis=2, keepdims=True)
    weighted = jnp.einsum(
        "hqk,kd->hqd", probs.astype(BF), values.reshape(-1, HD), preferred_element_type=F32
    )
    return (weighted / totals).astype(BF).transpose(1, 0, 2).reshape(rows, heads * HD)


def on_device(
    teacher_queries, teacher_keys, teacher_values, doc_ids, owner, student_hidden, norm_gain, proj
):
    n = seq_size()
    me = lax.axis_index("seq")
    side = lax.axis_index("side")
    plane = plane_size()
    mine = lax.axis_index("mp") * lax.axis_size("side") + side
    rows = teacher_queries.shape[0]
    heads = teacher_queries.shape[1] // HD
    kv_local = teacher_keys.shape[1] // HD
    group = heads * lax.axis_size("side") // kv_local
    width = student_hidden.shape[1]
    depth = proj.shape[0]
    capacity = student_hidden.shape[0]
    slots = capacity // n
    shared = n // plane
    held = shared * slots

    hidden = lax.dynamic_slice_in_dim(student_hidden, mine * held, held, 0).astype(F32)
    inverse_rms = lax.rsqrt(jnp.mean(hidden * hidden, axis=1, keepdims=True) + 1e-06)
    normed = (hidden * inverse_rms * norm_gain).astype(BF)
    normed_slots = exchange_seq(
        lambda z: lax.dynamic_slice_in_dim(normed, z * depth, depth, 1)
    )

    head = side * heads // group
    key_head = lax.dynamic_slice_in_dim(teacher_keys, head * HD, HD, 1)
    value_head = lax.dynamic_slice_in_dim(teacher_values, head * HD, HD, 1)
    small = jnp.stack([doc_ids, owner[:, 0]]).astype(BF)
    parcel = gather_seq(jnp.concatenate([key_head, value_head, jnp.pad(small, ((0, 14), (0, 0)))]))
    keys, values = parcel[:, :rows], parcel[:, rows : 2 * rows]
    docs = parcel[:, 2 * rows].astype(jnp.int32)
    owners = parcel[:, 2 * rows + 1].astype(jnp.int32)

    teacher_rows = attention(teacher_queries, keys, values, docs, doc_ids)

    own_blocks = jnp.stack(
        [
            lax.dynamic_index_in_dim(owners, place(mine * shared + b), 0, keepdims=False)
            for b in range(shared)
        ]
    )
    order = jnp.arange(rows, dtype=jnp.int32)
    same = (own_blocks[:, :, None] == own_blocks[:, None, :]) & (order[:, None] > order[None, :])
    rank = jnp.sum(same.astype(jnp.int32), axis=2)
    local = jnp.arange(shared, dtype=jnp.int32)[:, None] * slots + rank
    spots = jnp.arange(n * held, dtype=jnp.int32)
    arrived = place(own_blocks) * held + local
    pick = (arrived.reshape(-1)[:, None] == spots[None, :]).astype(BF)
    leaving = ((own_blocks - me) % n if seq_direct() else own_blocks) * held + local
    drop = (leaving.reshape(-1)[:, None] == spots[None, :]).astype(BF)

    normed_own = jnp.dot(
        pick, normed_slots.reshape(n * held, depth), preferred_element_type=F32
    ).astype(BF)
    normed_rows = gather_plane(normed_own).reshape(n, rows, depth)

    def partial(z):
        block = lax.dynamic_index_in_dim(normed_rows, z, 0, keepdims=False)
        return jnp.dot(block, proj, preferred_element_type=F32)

    if seq_direct():
        sent = [shift(partial((me + step) % n).astype(BF), step) for step in range(1, n)]
        predicted = partial(me)
        for piece in sent:
            predicted = predicted + piece.astype(F32)
    else:
        whole = jnp.dot(
            normed_rows.reshape(n * rows, depth), proj, preferred_element_type=F32
        ).astype(BF)
        predicted = lax.psum_scatter(whole, "seq", scatter_dimension=0, tiled=True).astype(F32)
    delta = (predicted - teacher_rows.astype(F32)).astype(BF)
    deltas = gather_seq(delta)

    def feature_piece(j):
        blocks = [
            lax.dynamic_index_in_dim(deltas, place(j * shared + b), 0, keepdims=False)
            for b in range(shared)
        ]
        return lax.dot_general(
            jnp.concatenate(blocks), proj, (((1,), (1,)), ((), ())), preferred_element_type=F32
        )

    feature_rows = scatter_plane(feature_piece, depth).astype(BF)
    feature_slots = (
        lax.dot_general(drop, feature_rows, (((0,), (0,)), ((), ())), preferred_element_type=F32)
        .astype(BF)
        .reshape(n, held, depth)
    )
    if seq_direct():
        received = [feature_slots[0]] + [shift(feature_slots[k], k) for k in range(1, n)]
        feature_grad = jnp.zeros((held, width), BF)
        for k in range(n):
            feature_grad = lax.dynamic_update_slice_in_dim(
                feature_grad, received[k], ((me - k) % n) * depth, 1
            )
    else:
        received = lax.all_to_all(feature_slots, "seq", split_axis=0, concat_axis=0, tiled=True)
        feature_grad = received.transpose(1, 0, 2).reshape(held, width)

    gain_grad = feature_grad.astype(F32) * norm_gain
    mean_term = jnp.mean(gain_grad * hidden, axis=1, keepdims=True)
    grad_rows = (inverse_rms * gain_grad - inverse_rms**3 * hidden * mean_term).astype(BF)
    grad_hidden = gather_plane(grad_rows).reshape(capacity, width)

    if seq_direct():
        ordered = jnp.stack(
            [
                lax.dynamic_index_in_dim(normed_rows, (me - k) % n, 0, keepdims=False)
                for k in range(n)
            ]
        )
    else:
        ordered = normed_rows
    factor = 1.0 / math.sqrt(rows * n)
    grad_proj = (
        lax.dot_general(
            ordered.reshape(n * rows, depth),
            deltas.reshape(n * rows, -1),
            (((0,), (0,)), ((), ())),
            preferred_element_type=F32,
        )
        * factor
    )
    return (grad_hidden, grad_proj)


def solution(mesh):
    return jax.shard_map(
        on_device,
        mesh=mesh,
        in_specs=(
            P(("groups", "seq"), ("mp", "side")),
            P(("groups", "seq"), "mp"),
            P(("groups", "seq"), "mp"),
            P(("groups", "seq")),
            P(("groups", "seq"), None),
            P(("groups", "seq"), None),
            P(),
            P("seq", ("mp", "side")),
        ),
        out_specs=(P(("groups", "seq"), None), P(("groups", "seq"), ("mp", "side"))),
        check_vma=False,
    )
```

time: 349 us -> 126 us (0.36)
  waiting for transfers between devices: 244 us -> 52.3 us
  blocking collectives: 50.2 us -> 0 us
  starting transfers between devices: 10.1 us -> 37.3 us
  between operations: 14 us -> 1.06 us
  matrix products: 16.3 us -> 20.9 us
    reduce_scatter x1 -> x0, waiting for transfers between devices: 126 us -> none  [on_device(): lax.psum_scatter((lax.dot_general(normed, delta, (((0,), (0,)), ((), ()))...]
    all_gather x1 -> x0, waiting for transfers between devices: 64.5 us -> none  [on_device(): weight_full = lax.all_gather(proj, 'seq', axis=0, tiled=True)]
    ppermute x0 -> x24, waiting for transfers between devices: none -> 52.3 us  [the longest x15 32.5 us: shift(): return lax.ppermute(x, 'seq', [(i, (i + step) % n) for i in range(n)])]
    all_gather x3 -> x0, blocking collectives: 50.2 us -> none  [the longest x1 21.9 us: on_device(): value_piece = lax.all_gather(teacher_values, 'seq', axis=0, tiled=True)]
    ppermute x0 -> x24, starting transfers between devices: none -> 37.3 us  [the longest x15 32 us: shift(): return lax.ppermute(x, 'seq', [(i, (i + step) % n) for i in range(n)])]
    psum x1 -> x0, waiting for transfers between devices: 32.7 us -> none  [on_device(): lax.psum(partial_grad.astype(jnp.bfloat16), ('mp', 'side'))]
    all_to_all x2 -> x0, waiting for transfers between devices: 20.4 us -> none  [the longest x1 20.4 us: on_device(): lax.all_to_all(packed, 'seq', split_axis=0, concat_axis=0, tiled=True)]
    all_to_all x2 -> x0, starting transfers between devices: 9.78 us -> none  [the longest x1 6.32 us: on_device(): lax.all_to_all(occupied, 'seq', split_axis=0, concat_axis=0, tiled=True)]
  transfers between devices with their start and end apart: 5 -> 24, of which waited for: 4 -> 15; matrix products, arithmetic and copies ran while one was open for 5% -> 17% of each run, Pallas kernels for 0% -> 0%
where the time goes in v1:
time: 126 us
  waiting for transfers between devices  52.3 us (42%)
  starting transfers between devices  37.3 us (30%)
  matrix products  20.9 us (17%)
  other arithmetic  10.9 us (9%)
  local copies, waits for them, and re-layouts  3.42 us (3%)
    ppermute x15, waiting for transfers between devices, shift(): return lax.ppermute(x, 'seq', [(i, (i + step) % n) for i in range(n)])  32.5 us
    ppermute x15, starting transfers between devices, shift(): return lax.ppermute(x, 'seq', [(i, (i + step) % n) for i in range(n)])  32 us
    ppermute x9, waiting for transfers between devices, swap(): return lax.ppermute(x, axis, [(0, 1), (1, 0)])  19.8 us
    ppermute x9, starting transfers between devices, swap(): return lax.ppermute(x, axis, [(0, 1), (1, 0)])  5.38 us
    dot_general x4, matrix products, partial(): return jnp.dot(block, proj, preferred_element_type=F32)  4.53 us
    dot_general x1, matrix products, attention(): jnp.einsum('hqk,kd->hqd', probs.astype(BF), values.reshape(-1, HD), prefe...  4.51 us
    dot_general x1, matrix products, on_device(): lax.dot_general(ordered.reshape(n * rows, depth), deltas.reshape(n * rows...  3.96 us
    dot_general x3, matrix products, feature_piece(): lax.dot_general(jnp.concatenate(blocks), proj, (((1,), (1,)), ((), ())),...  2.81 us
  transfers between devices with their start and end apart: 24, of which 15 were waited for; matrix products, arithmetic and copies ran while one was open for 17% of the time, Pallas kernels for 0%

profile of v1, /device:TPU:0, one launch (start us, length us, event | category | flops | bytes accessed | tf_op | source)
XLA Modules:
  0.0 125.9 jit_solution(3482057438144329692)
XLA Ops:
  0.7 0.8 convert_bitcast_fusion.1
  1.5 0.7 convert_bitcast_fusion.2
  2.2 0.8 constant_dynamic-slice_fusion.11
  3.0 3.1 %collective-permute-start = (bf16[272,128]{1,0:T(8,128)(2,1)S(1)}, bf16[272,128]{1,0:T(8,128)(2,1)S(1)}, u32[]{:S(2)}, u32[]{:S(2)}) collective-permute-start(bf16[272,128]{1,0:T(8,128)(2,1)S(1)} %get-tuple-element.17), channel_id=1, source_target_pairs={{0,4},{4,8},{8,12},{12,0},{1,5},{5,9},{9,13},{13,1},{2,6},{6,10},{... | collective-permute-start | bytes 208904 | tf_op jit(solution)/shard_map/ppermute | solution.py:38
  6.0 2.6 %collective-permute-start.1 = (bf16[272,128]{1,0:T(8,128)(2,1)S(1)}, bf16[272,128]{1,0:T(8,128)(2,1)S(1)}, u32[]{:S(2)}, u32[]{:S(2)}) collective-permute-start(bf16[272,128]{1,0:T(8,128)(2,1)S(1)} %get-tuple-element.17), channel_id=1, source_target_pairs={{0,8},{4,12},{8,0},{12,4},{1,9},{5,13},{9,1},{13,5},{2,10},{6,14},... | collective-permute-start | bytes 208904 | tf_op jit(solution)/shard_map/ppermute | solution.py:38
  8.6 1.3 %collective-permute-start.2 = (bf16[272,128]{1,0:T(8,128)(2,1)S(1)}, bf16[272,128]{1,0:T(8,128)(2,1)S(1)}, u32[]{:S(2)}, u32[]{:S(2)}) collective-permute-start(bf16[272,128]{1,0:T(8,128)(2,1)S(1)} %get-tuple-element.17), channel_id=1, source_target_pairs={{0,12},{4,0},{8,4},{12,8},{1,13},{5,1},{9,5},{13,9},{2,14},{6,2},{... | collective-permute-start | bytes 208904 | tf_op jit(solution)/shard_map/ppermute | solution.py:38
  10.0 1.1 fusion.15
  11.2 1.2 fusion.17
  12.4 0.7 collective-permute-start.3
  13.1 0.3 collective-permute-start.4
  13.5 2.8 %collective-permute-start.5 = (bf16[48,896]{1,0:T(8,128)(2,1)S(1)}, bf16[48,896]{1,0:T(8,128)(2,1)S(1)}, u32[]{:S(2)}, u32[]{:S(2)}) collective-permute-start(bf16[48,896]{1,0:T(8,128)(2,1)S(1)} %get-tuple-element.13), channel_id=1, source_target_pairs={{0,12},{4,0},{8,4},{12,8},{1,13},{5,1},{9,5},{13,9},{2,14},{6,2},{... | collective-permute-start | bytes 258056 | tf_op jit(solution)/shard_map/ppermute | solution.py:38
  16.5 0.2 convert_reduce_fusion
  16.6 1.8 %fusion.22 = f32[512,8,128]{2,0,1:T(8,128)} fusion(bf16[512,128,1]{1,0,2:T(8,128)(2,1)S(1)} %bitcast.171, bf16[128,1024]{1,0:T(8,128)(2,1)S(1)} %copy-done.5), kind=kOutput, calls=%fused_computation.51 | convolution fusion | flops 134217728 | bytes 2490368 | tf_op jit(solution)/shard_map/hqd,kd->hqk/dot_general | solution.py:108
  18.4 0.2 compare_and_fusion
  18.6 0.9 collective-permute-done.3
  19.6 1.9 %collective-permute-done.4 = bf16[48,896]{1,0:T(8,128)(2,1)S(1)} collective-permute-done((bf16[48,896]{1,0:T(8,128)(2,1)S(1)}, bf16[48,896]{1,0:T(8,128)(2,1)S(1)}, u32[]{:S(2)}, u32[]{:S(2)}) %collective-permute-start.4) | collective-permute-done | bytes 86048 | tf_op jit(solution)/shard_map/ppermute | solution.py:38
  21.6 0.3 convolution_convert_fusion.6
  21.9 1.6 %collective-permute-start.7 = (bf16[128,896]{1,0:T(8,128)(2,1)S(1)}, bf16[128,896]{1,0:T(8,128)(2,1)S(1)}, u32[]{:S(2)}, u32[]{:S(2)}) collective-permute-start(bf16[128,896]{1,0:T(8,128)(2,1)S(1)} %convolution_convert_fusion.6), channel_id=1, source_target_pairs={{0,2},{2,0},{1,3},{3,1},{4,6},{6,4},{5,7},{7,5},{8,10},{10,8},{9,1... | collective-permute-start | bytes 688136 | tf_op jit(solution)/shard_map/ppermute | solution.py:59
  23.5 1.0 fusion.91
  24.4 5.5 %collective-permute-done.7 = bf16[128,896]{1,0:T(8,128)(2,1)S(1)} collective-permute-done((bf16[128,896]{1,0:T(8,128)(2,1)S(1)}, bf16[128,896]{1,0:T(8,128)(2,1)S(1)}, u32[]{:S(2)}, u32[]{:S(2)}) %collective-permute-start.7) | collective-permute-done | bytes 229408 | tf_op jit(solution)/shard_map/ppermute | solution.py:59
  30.1 1.3 %collective-permute-done.8 = bf16[128,896]{1,0:T(8,128)(2,1)S(1)} collective-permute-done((bf16[128,896]{1,0:T(8,128)(2,1)S(1)}, bf16[128,896]{1,0:T(8,128)(2,1)S(1)}, u32[]{:S(2)}, u32[]{:S(2)}) %collective-permute-start.8) | collective-permute-done | bytes 229408 | tf_op jit(solution)/shard_map/ppermute | solution.py:59
  31.5 0.2 maximum_select_fusion.1
  31.7 0.4 convolution_convert_fusion.2
  32.2 0.8 collective-permute-start.10
  32.9 1.2 convolution_convert_fusion.3
  34.1 2.4 %collective-permute-start.9 = (bf16[128,1024]{1,0:T(8,128)(2,1)}, bf16[128,1024]{1,0:T(8,128)(2,1)}, u32[]{:S(2)}, u32[]{:S(2)}) collective-permute-start(bf16[128,1024]{1,0:T(8,128)(2,1)} %convolution_convert_fusion.3), channel_id=1, source_target_pairs={{0,4},{4,8},{8,12},{12,0},{1,5},{5,9},{9,13},{13,1},{2,6},{6,10},{... | collective-permute-start | bytes 786440 | tf_op jit(solution)/shard_map/ppermute | solution.py:38
  36.5 1.1 convolution_convert_fusion.1
  37.7 1.4 %collective-permute-start.11 = (bf16[128,1024]{1,0:T(8,128)(2,1)}, bf16[128,1024]{1,0:T(8,128)(2,1)}, u32[]{:S(2)}, u32[]{:S(2)}) collective-permute-start(bf16[128,1024]{1,0:T(8,128)(2,1)} %convolution_convert_fusion.1), channel_id=1, source_target_pairs={{0,12},{4,0},{8,4},{12,8},{1,13},{5,1},{9,5},{13,9},{2,14},{6,2},{... | collective-permute-start | bytes 786440 | tf_op jit(solution)/shard_map/ppermute | solution.py:38
  39.1 4.5 %fusion.3 = bf16[128,8,128]{0,2,1:T(8,128)(2,1)} fusion(bf16[512,128,1]{1,0,2:T(8,128)(2,1)S(1)} %bitcast.170, f32[128,8]{0,1:T(8,128)S(1)} %bitcast.187, f32[512,8,128]{2,0,1:T(8,128)} %fusion.22, pred[128,512]{0,1:T(8,128)(4,1)} %copy-done.13), kind=kOutput, calls=%fused_computation.16 | convolution fusion | flops 137102848 | bytes 2560000 | tf_op jit(solution)/shard_map/hqk,kd->hqd/dot_general | solution.py:115
  43.6 1.0 bitcast_convert_fusion
  44.6 1.0 copy.23
  45.6 8.1 %collective-permute-done.10 = bf16[128,1024]{1,0:T(8,128)(2,1)} collective-permute-done((bf16[128,1024]{1,0:T(8,128)(2,1)S(1)}, bf16[128,1024]{1,0:T(8,128)(2,1)}, u32[]{:S(2)}, u32[]{:S(2)}) %collective-permute-start.10) | collective-permute-done | bytes 262176 | tf_op jit(solution)/shard_map/ppermute | solution.py:38
  53.7 2.1 %collective-permute-done.11 = bf16[128,1024]{1,0:T(8,128)(2,1)} collective-permute-done((bf16[128,1024]{1,0:T(8,128)(2,1)}, bf16[128,1024]{1,0:T(8,128)(2,1)}, u32[]{:S(2)}, u32[]{:S(2)}) %collective-permute-start.11) | collective-permute-done | bytes 262176 | tf_op jit(solution)/shard_map/ppermute | solution.py:38
  55.8 1.8 %subtract_convert_fusion = bf16[128,1024]{1,0:T(8,128)(2,1)S(1)} fusion(f32[128,1024]{1,0:T(8,128)} %copy.23, bf16[128,1024]{1,0:T(8,128)(2,1)} %collective-permute-done.11, bf16[128,1024]{1,0:T(8,128)(2,1)} %collective-permute-done.10, bf16[128,1024]{1,0:T(8,128)(2,1)} %collective-permute-done.9, bf16[896,1024]{1,0:T(8,128)(2,1)S(1)} %copy-done, ...), kind=kOutput, calls=%fused_computation.43 | convolution fusion | flops 235929600 | bytes 3637252 | tf_op jit(solution)/shard_map/dot_general | solution.py:181
  57.6 3.3 %collective-permute-start.12 = (bf16[128,1024]{1,0:T(8,128)(2,1)S(1)}, bf16[128,1024]{1,0:T(8,128)(2,1)S(1)}, u32[]{:S(2)}, u32[]{:S(2)}) collective-permute-start(bf16[128,1024]{1,0:T(8,128)(2,1)S(1)} %subtract_convert_fusion), channel_id=1, source_target_pairs={{0,4},{4,8},{8,12},{12,0},{1,5},{5,9},{9,13},{13,1},{2,6},{6,10},{... | collective-permute-start | bytes 786440 | tf_op jit(solution)/shard_map/ppermute | solution.py:38
  60.9 0.2 collective-permute-start.13
  61.1 2.8 %collective-permute-start.14 = (bf16[128,1024]{1,0:T(8,128)(2,1)S(1)}, bf16[128,1024]{1,0:T(8,128)(2,1)}, u32[]{:S(2)}, u32[]{:S(2)}) collective-permute-start(bf16[128,1024]{1,0:T(8,128)(2,1)S(1)} %subtract_convert_fusion), channel_id=1, source_target_pairs={{0,12},{4,0},{8,4},{12,8},{1,13},{5,1},{9,5},{13,9},{2,14},{6,2},{... | collective-permute-start | bytes 786440 | tf_op jit(solution)/shard_map/ppermute | solution.py:38
  64.0 4.3 %collective-permute-done.12 = bf16[128,1024]{1,0:T(8,128)(2,1)S(1)} collective-permute-done((bf16[128,1024]{1,0:T(8,128)(2,1)S(1)}, bf16[128,1024]{1,0:T(8,128)(2,1)S(1)}, u32[]{:S(2)}, u32[]{:S(2)}) %collective-permute-start.12) | collective-permute-done | bytes 262176 | tf_op jit(solution)/shard_map/ppermute | solution.py:38
  68.3 9.3 %collective-permute-done.13 = bf16[128,1024]{1,0:T(8,128)(2,1)S(1)} collective-permute-done((bf16[128,1024]{1,0:T(8,128)(2,1)S(1)}, bf16[128,1024]{1,0:T(8,128)(2,1)S(1)}, u32[]{:S(2)}, u32[]{:S(2)}) %collective-permute-start.13) | collective-permute-done | bytes 262176 | tf_op jit(solution)/shard_map/ppermute | solution.py:38
  77.6 1.2 pad_maximum_fusion
  78.8 0.7 convolution_convert_fusion.4
  79.6 0.7 convolution_convert_fusion.5
  80.3 0.6 collective-permute-start.15
  80.9 0.2 collective-permute-done.16
  81.1 1.4 %add_convert_fusion.1 = bf16[128,896]{1,0:T(8,128)(2,1)} fusion(bf16[128,896]{1,0:T(8,128)(2,1)S(1)} %collective-permute-done.16, bf16[896,1024]{1,0:T(8,128)(2,1)S(1)} %copy-done, bf16[4,128,1024]{2,1,0:T(8,128)(2,1)S(1)} %pad_maximum_fusion, s32[]{:T(128)S(6)} %select_n.240), kind=kOutput, calls=%fused_computation.47 | convolution fusion | flops 235225088 | bytes 2555908 | tf_op jit(solution)/shard_map/dot_general | solution.py:201
  82.5 1.5 %collective-permute-start.17 = (bf16[128,896]{1,0:T(8,128)(2,1)}, bf16[128,896]{1,0:T(8,128)(2,1)S(1)}, u32[]{:S(2)}, u32[]{:S(2)}) collective-permute-start(bf16[128,896]{1,0:T(8,128)(2,1)} %add_convert_fusion.1), channel_id=1, source_target_pairs={{0,2},{2,0},{1,3},{3,1},{4,6},{6,4},{5,7},{7,5},{8,10},{10,8},{9,1... | collective-permute-start | bytes 688136 | tf_op jit(solution)/shard_map/ppermute | solution.py:59
  84.0 6.4 %collective-permute-done.17 = bf16[128,896]{1,0:T(8,128)(2,1)S(1)} collective-permute-done((bf16[128,896]{1,0:T(8,128)(2,1)}, bf16[128,896]{1,0:T(8,128)(2,1)S(1)}, u32[]{:S(2)}, u32[]{:S(2)}) %collective-permute-start.17) | collective-permute-done | bytes 229408 | tf_op jit(solution)/shard_map/ppermute | solution.py:59
  90.4 0.7 copy-done.11
  91.0 2.1 %convolution_convert_fusion = bf16[192,896]{1,0:T(8,128)(2,1)S(1)} fusion(bf16[128,896]{1,0:T(8,128)(2,1)} %copy-done.11, bf16[128,896]{1,0:T(8,128)(2,1)} %copy-done.10, bf16[896,1024]{1,0:T(8,128)(2,1)S(1)} %copy-done, bf16[4,128,1024]{2,1,0:T(8,128)(2,1)} %copy-done.1, s32[]{:T(128)S(6)} %select_n.215, s32[128]{0:T(128)S(1)} %get-tuple-element.18), kind=kOutput, calls=%fused_computation.8 | convolution fusion | flops 279691264 | bytes 2900484 | tf_op jit(solution)/shard_map/dot_general | solution.py:207
  93.2 0.7 fusion.90
  93.9 6.6 %collective-permute-start.18 = (bf16[48,896]{1,0:T(8,128)(2,1)}, bf16[48,896]{1,0:T(8,128)(2,1)S(1)}, u32[]{:S(2)}, u32[]{:S(2)}) collective-permute-start(bf16[48,896]{1,0:T(8,128)(2,1)} %get-tuple-element.10), channel_id=1, source_target_pairs={{0,4},{4,8},{8,12},{12,0},{1,5},{5,9},{9,13},{13,1},{2,6},{6,10},{... | collective-permute-start | bytes 258056 | tf_op jit(solution)/shard_map/ppermute | solution.py:38
  100.5 3.4 %collective-permute-start.19 = (bf16[48,896]{1,0:T(8,128)(2,1)}, bf16[48,896]{1,0:T(8,128)(2,1)S(1)}, u32[]{:S(2)}, u32[]{:S(2)}) collective-permute-start(bf16[48,896]{1,0:T(8,128)(2,1)} %get-tuple-element.9), channel_id=1, source_target_pairs={{0,8},{4,12},{8,0},{12,4},{1,9},{5,13},{9,1},{13,5},{2,10},{6,14},... | collective-permute-start | bytes 258056 | tf_op jit(solution)/shard_map/ppermute | solution.py:38
  103.9 3.2 %collective-permute-done.18 = bf16[48,896]{1,0:T(8,128)(2,1)S(1)} collective-permute-done((bf16[48,896]{1,0:T(8,128)(2,1)}, bf16[48,896]{1,0:T(8,128)(2,1)S(1)}, u32[]{:S(2)}, u32[]{:S(2)}) %collective-permute-start.18) | collective-permute-done | bytes 86048 | tf_op jit(solution)/shard_map/ppermute | solution.py:38
  107.1 2.2 %collective-permute-done.19 = bf16[48,896]{1,0:T(8,128)(2,1)S(1)} collective-permute-done((bf16[48,896]{1,0:T(8,128)(2,1)}, bf16[48,896]{1,0:T(8,128)(2,1)S(1)}, u32[]{:S(2)}, u32[]{:S(2)}) %collective-permute-start.19) | collective-permute-done | bytes 86048 | tf_op jit(solution)/shard_map/ppermute | solution.py:38
  109.4 0.4 collective-permute-done.20
  109.8 1.3 %fusion.21 = f32[48]{0:T(128)S(1)} fusion(bf16[48,3584]{1,0:T(8,128)(2,1)S(1)} %constant_dynamic-update-slice_fusion, f32[3584]{0:T(1024)S(1)} %copy-done.12, bf16[192,3584]{1,0:T(8,128)(2,1)} %param.13, s32[]{:T(128)S(6)} %select_n.211), kind=kLoop, calls=%fused_computation.39 | loop fusion | flops 860112 | bytes 702660 | tf_op jit(solution)/shard_map/reduce_sum | solution.py:223
  111.1 1.2 fusion.20
  112.3 1.6 %collective-permute-start.22 = (bf16[48,3584]{1,0:T(8,128)(2,1)S(1)}, bf16[48,3584]{1,0:T(8,128)(2,1)S(1)}, u32[]{:S(2)}, u32[]{:S(2)}) collective-permute-start(bf16[48,3584]{1,0:T(8,128)(2,1)S(1)} %fusion.20), channel_id=1, source_target_pairs={{0,2},{2,0},{1,3},{3,1},{4,6},{6,4},{5,7},{7,5},{8,10},{10,8},{9,1... | collective-permute-start | bytes 1032200 | tf_op jit(solution)/shard_map/ppermute | solution.py:59
  114.0 4.0 %bitcast_multiply_fusion = f32[896,1024]{1,0:T(8,128)} fusion(bf16[1,128,896]{2,1,0:T(8,128)(2,1)S(1)} %get-tuple-element.5, bf16[1,128,896]{2,1,0:T(8,128)(2,1)S(1)} %get-tuple-element.6, bf16[1,128,896]{2,1,0:T(8,128)(2,1)S(1)} %get-tuple-element.7, bf16[1,128,896]{2,1,0:T(8,128)(2,1)S(1)} %get-tuple-element.4, bf16[1,128,1024]{2,1,0:T(8,128)(2,1)} %bitcast.39, ...), kind=kOutput, calls=%fused_computation.1 | convolution fusion | flops 943390720 | bytes 5636096 | tf_op jit(solution)/shard_map/dot_general | solution.py:238
  118.0 4.9 %collective-permute-done.22 = bf16[48,3584]{1,0:T(8,128)(2,1)S(1)} collective-permute-done((bf16[48,3584]{1,0:T(8,128)(2,1)S(1)}, bf16[48,3584]{1,0:T(8,128)(2,1)S(1)}, u32[]{:S(2)}, u32[]{:S(2)}) %collective-permute-start.22) | collective-permute-done | bytes 344096 | tf_op jit(solution)/shard_map/ppermute | solution.py:59
  122.8 0.1 maximum_select_fusion.2
  122.9 1.5 %collective-permute-done.23 = bf16[48,3584]{1,0:T(8,128)(2,1)S(1)} collective-permute-done((bf16[48,3584]{1,0:T(8,128)(2,1)S(1)}, bf16[48,3584]{1,0:T(8,128)(2,1)S(1)}, u32[]{:S(2)}, u32[]{:S(2)}) %collective-permute-start.23) | collective-permute-done | bytes 344096 | tf_op jit(solution)/shard_map/ppermute | solution.py:59
  124.5 0.1 maximum_select_fusion.3
  124.6 1.3 %maximum_select_fusion = bf16[4,48,3584]{2,1,0:T(8,128)(2,1)} fusion(bf16[2,48,3584]{2,1,0:T(8,128)(2,1)S(1)} %maximum_select_fusion.3, bf16[2,48,3584]{2,1,0:T(8,128)(2,1)S(1)} %maximum_select_fusion.2, pred[]{:T(512)S(6)} %eq.103), kind=kLoop, calls=%fused_computation.5 | loop fusion | flops 2064384 | bytes 2752513 | tf_op jit(solution)/shard_map/jit(_where)/select_n | solution.py:72
  (67 shorter events, 1.0 us)
Async XLA Ops:
  0.6 31.1 %copy-start = (bf16[896,1024]{1,0:T(8,128)(2,1)S(1)}, bf16[896,1024]{1,0:T(8,128)(2,1)}, u32[]{:S(2)}) copy-start(bf16[896,1024]{1,0:T(8,128)(2,1)} %param.15) | copy-start | bytes 5505028
  0.6 16.0 %copy-start.5 = (bf16[128,1024]{1,0:T(8,128)(2,1)S(1)}, bf16[128,1024]{1,0:T(8,128)(2,1)}, u32[]{:S(2)}) copy-start(bf16[128,1024]{1,0:T(8,128)(2,1)} %param.8) | copy-start | bytes 786436
  3.0 10.6 %collective-permute-start = (bf16[272,128]{1,0:T(8,128)(2,1)S(1)}, bf16[272,128]{1,0:T(8,128)(2,1)S(1)}, u32[]{:S(2)}, u32[]{:S(2)}) collective-permute-start(bf16[272,128]{1,0:T(8,128)(2,1)S(1)} %get-tuple-element.17), channel_id=1, source_target_pairs={{0,4},{4,8},{8,12},{12,0},{1,5},{5,9},{9,13},{13,1},{2,6},{6,10},{... | collective-permute-start | bytes 208904 | tf_op jit(solution)/shard_map/ppermute | solution.py:38
  6.0 10.3 %collective-permute-start.1 = (bf16[272,128]{1,0:T(8,128)(2,1)S(1)}, bf16[272,128]{1,0:T(8,128)(2,1)S(1)}, u32[]{:S(2)}, u32[]{:S(2)}) collective-permute-start(bf16[272,128]{1,0:T(8,128)(2,1)S(1)} %get-tuple-element.17), channel_id=1, source_target_pairs={{0,8},{4,12},{8,0},{12,4},{1,9},{5,13},{9,1},{13,5},{2,10},{6,14},... | collective-permute-start | bytes 208904 | tf_op jit(solution)/shard_map/ppermute | solution.py:38
  8.6 7.8 %collective-permute-start.2 = (bf16[272,128]{1,0:T(8,128)(2,1)S(1)}, bf16[272,128]{1,0:T(8,128)(2,1)S(1)}, u32[]{:S(2)}, u32[]{:S(2)}) collective-permute-start(bf16[272,128]{1,0:T(8,128)(2,1)S(1)} %get-tuple-element.17), channel_id=1, source_target_pairs={{0,12},{4,0},{8,4},{12,8},{1,13},{5,1},{9,5},{13,9},{2,14},{6,2},{... | collective-permute-start | bytes 208904 | tf_op jit(solution)/shard_map/ppermute | solution.py:38
  12.4 6.0 %copy-start.14 = (s32[128]{0:T(128)S(1)}, s32[128]{0:T(128)}, u32[]{:S(2)}) copy-start(s32[128]{0:T(128)} %param.11) | copy-start | bytes 1540
  12.4 7.2 %collective-permute-start.3 = (bf16[48,896]{1,0:T(8,128)(2,1)S(1)}, bf16[48,896]{1,0:T(8,128)(2,1)S(1)}, u32[]{:S(2)}, u32[]{:S(2)}) collective-permute-start(bf16[48,896]{1,0:T(8,128)(2,1)S(1)} %get-tuple-element.15), channel_id=1, source_target_pairs={{0,4},{4,8},{8,12},{12,0},{1,5},{5,9},{9,13},{13,1},{2,6},{6,10},{... | collective-permute-start | bytes 258056 | tf_op jit(solution)/shard_map/ppermute | solution.py:38
  13.1 8.4 %collective-permute-start.4 = (bf16[48,896]{1,0:T(8,128)(2,1)S(1)}, bf16[48,896]{1,0:T(8,128)(2,1)S(1)}, u32[]{:S(2)}, u32[]{:S(2)}) collective-permute-start(bf16[48,896]{1,0:T(8,128)(2,1)S(1)} %get-tuple-element.14), channel_id=1, source_target_pairs={{0,8},{4,12},{8,0},{12,4},{1,9},{5,13},{9,1},{13,5},{2,10},{6,14},... | collective-permute-start | bytes 258056 | tf_op jit(solution)/shard_map/ppermute | solution.py:38
  13.5 8.0 %collective-permute-start.5 = (bf16[48,896]{1,0:T(8,128)(2,1)S(1)}, bf16[48,896]{1,0:T(8,128)(2,1)S(1)}, u32[]{:S(2)}, u32[]{:S(2)}) collective-permute-start(bf16[48,896]{1,0:T(8,128)(2,1)S(1)} %get-tuple-element.13), channel_id=1, source_target_pairs={{0,12},{4,0},{8,4},{12,8},{1,13},{5,1},{9,5},{13,9},{2,14},{6,2},{... | collective-permute-start | bytes 258056 | tf_op jit(solution)/shard_map/ppermute | solution.py:38
  18.6 5.8 %copy-start.13 = (pred[128,512]{0,1:T(8,128)(4,1)}, pred[128,512]{0,1:T(8,128)(4,1)S(1)}, u32[]{:S(2)}) copy-start(pred[128,512]{0,1:T(8,128)(4,1)S(1)} %compare_and_fusion) | copy-start | bytes 196612
  21.8 8.2 %collective-permute-start.6 = (bf16[128,896]{1,0:T(8,128)(2,1)S(1)}, bf16[128,896]{1,0:T(8,128)(2,1)S(1)}, u32[]{:S(2)}, u32[]{:S(2)}) collective-permute-start(bf16[128,896]{1,0:T(8,128)(2,1)S(1)} %convolution_convert_fusion.6), channel_id=1, source_target_pairs={{0,1},{1,0},{2,3},{3,2},{4,5},{5,4},{6,7},{7,6},{8,9},{9,8},{10,11... | collective-permute-start | bytes 688136 | tf_op jit(solution)/shard_map/ppermute | solution.py:59
  21.9 8.0 %collective-permute-start.7 = (bf16[128,896]{1,0:T(8,128)(2,1)S(1)}, bf16[128,896]{1,0:T(8,128)(2,1)S(1)}, u32[]{:S(2)}, u32[]{:S(2)}) collective-permute-start(bf16[128,896]{1,0:T(8,128)(2,1)S(1)} %convolution_convert_fusion.6), channel_id=1, source_target_pairs={{0,2},{2,0},{1,3},{3,1},{4,6},{6,4},{5,7},{7,5},{8,10},{10,8},{9,1... | collective-permute-start | bytes 688136 | tf_op jit(solution)/shard_map/ppermute | solution.py:59
  29.9 1.5 %collective-permute-start.8 = (bf16[128,896]{1,0:T(8,128)(2,1)S(1)}, bf16[128,896]{1,0:T(8,128)(2,1)S(1)}, u32[]{:S(2)}, u32[]{:S(2)}) collective-permute-start(bf16[128,896]{1,0:T(8,128)(2,1)S(1)} %collective-permute-done.7), channel_id=1, source_target_pairs={{0,1},{1,0},{2,3},{3,2},{4,5},{5,4},{6,7},{7,6},{8,9},{9,8},{10,11... | collective-permute-start | bytes 688136 | tf_op jit(solution)/shard_map/ppermute | solution.py:59
  30.0 1.7 %copy-start.4 = (bf16[4,272,128]{2,1,0:T(8,128)(2,1)}, bf16[4,272,128]{2,1,0:T(8,128)(2,1)S(1)}, u32[]{:S(2)}) copy-start(bf16[4,272,128]{2,1,0:T(8,128)(2,1)S(1)} %pad_maximum_fusion.2) | copy-start | bytes 835588
  32.1 6.9 %slice-start = ((bf16[4,272,128]{2,1,0:T(8,128)(2,1)}), bf16[4,128,128]{2,1,0:T(8,128)(2,1)S(1)}, s32[]{:S(2)}) async-start(bf16[4,272,128]{2,1,0:T(8,128)(2,1)} %copy-done.4), calls=%async_computation | async-start | bytes 262144 | tf_op jit(solution)/shard_map/slice | solution.py:152
  32.2 21.5 %collective-permute-start.10 = (bf16[128,1024]{1,0:T(8,128)(2,1)S(1)}, bf16[128,1024]{1,0:T(8,128)(2,1)}, u32[]{:S(2)}, u32[]{:S(2)}) collective-permute-start(bf16[128,1024]{1,0:T(8,128)(2,1)S(1)} %convolution_convert_fusion.2), channel_id=1, source_target_pairs={{0,8},{4,12},{8,0},{12,4},{1,9},{5,13},{9,1},{13,5},{2,10},{6,14},... | collective-permute-start | bytes 786440 | tf_op jit(solution)/shard_map/ppermute | solution.py:38
  34.1 19.6 %collective-permute-start.9 = (bf16[128,1024]{1,0:T(8,128)(2,1)}, bf16[128,1024]{1,0:T(8,128)(2,1)}, u32[]{:S(2)}, u32[]{:S(2)}) collective-permute-start(bf16[128,1024]{1,0:T(8,128)(2,1)} %convolution_convert_fusion.3), channel_id=1, source_target_pairs={{0,4},{4,8},{8,12},{12,0},{1,5},{5,9},{9,13},{13,1},{2,6},{6,10},{... | collective-permute-start | bytes 786440 | tf_op jit(solution)/shard_map/ppermute | solution.py:38
  37.7 18.1 %collective-permute-start.11 = (bf16[128,1024]{1,0:T(8,128)(2,1)}, bf16[128,1024]{1,0:T(8,128)(2,1)}, u32[]{:S(2)}, u32[]{:S(2)}) collective-permute-start(bf16[128,1024]{1,0:T(8,128)(2,1)} %convolution_convert_fusion.1), channel_id=1, source_target_pairs={{0,12},{4,0},{8,4},{12,8},{1,13},{5,1},{9,5},{13,9},{2,14},{6,2},{... | collective-permute-start | bytes 786440 | tf_op jit(solution)/shard_map/ppermute | solution.py:38
  57.5 22.0 %copy-start.2 = (bf16[128,1024]{1,0:T(8,128)(2,1)}, bf16[128,1024]{1,0:T(8,128)(2,1)S(1)}, u32[]{:S(2)}) copy-start(bf16[128,1024]{1,0:T(8,128)(2,1)S(1)} %subtract_convert_fusion) | copy-start | bytes 786436
  57.6 10.8 %collective-permute-start.12 = (bf16[128,1024]{1,0:T(8,128)(2,1)S(1)}, bf16[128,1024]{1,0:T(8,128)(2,1)S(1)}, u32[]{:S(2)}, u32[]{:S(2)}) collective-permute-start(bf16[128,1024]{1,0:T(8,128)(2,1)S(1)} %subtract_convert_fusion), channel_id=1, source_target_pairs={{0,4},{4,8},{8,12},{12,0},{1,5},{5,9},{9,13},{13,1},{2,6},{6,10},{... | collective-permute-start | bytes 786440 | tf_op jit(solution)/shard_map/ppermute | solution.py:38
  60.9 16.7 %collective-permute-start.13 = (bf16[128,1024]{1,0:T(8,128)(2,1)S(1)}, bf16[128,1024]{1,0:T(8,128)(2,1)S(1)}, u32[]{:S(2)}, u32[]{:S(2)}) collective-permute-start(bf16[128,1024]{1,0:T(8,128)(2,1)S(1)} %subtract_convert_fusion), channel_id=1, source_target_pairs={{0,8},{4,12},{8,0},{12,4},{1,9},{5,13},{9,1},{13,5},{2,10},{6,14},... | collective-permute-start | bytes 786440 | tf_op jit(solution)/shard_map/ppermute | solution.py:38
  61.1 16.5 %collective-permute-start.14 = (bf16[128,1024]{1,0:T(8,128)(2,1)S(1)}, bf16[128,1024]{1,0:T(8,128)(2,1)}, u32[]{:S(2)}, u32[]{:S(2)}) collective-permute-start(bf16[128,1024]{1,0:T(8,128)(2,1)S(1)} %subtract_convert_fusion), channel_id=1, source_target_pairs={{0,12},{4,0},{8,4},{12,8},{1,13},{5,1},{9,5},{13,9},{2,14},{6,2},{... | collective-permute-start | bytes 786440 | tf_op jit(solution)/shard_map/ppermute | solution.py:38
  68.3 11.2 %copy-start.6 = (bf16[128,1024]{1,0:T(8,128)(2,1)}, bf16[128,1024]{1,0:T(8,128)(2,1)S(1)}, u32[]{:S(2)}) copy-start(bf16[128,1024]{1,0:T(8,128)(2,1)S(1)} %collective-permute-done.12) | copy-start | bytes 786436
  77.6 1.9 %copy-start.8 = (bf16[128,1024]{1,0:T(8,128)(2,1)}, bf16[128,1024]{1,0:T(8,128)(2,1)S(1)}, u32[]{:S(2)}) copy-start(bf16[128,1024]{1,0:T(8,128)(2,1)S(1)} %collective-permute-done.13) | copy-start | bytes 786436
  78.8 2.3 %copy-start.1 = (bf16[4,128,1024]{2,1,0:T(8,128)(2,1)}, bf16[4,128,1024]{2,1,0:T(8,128)(2,1)S(1)}, u32[]{:S(2)}) copy-start(bf16[4,128,1024]{2,1,0:T(8,128)(2,1)S(1)} %pad_maximum_fusion) | copy-start | bytes 3145732
  79.6 1.6 %collective-permute-start.16 = (bf16[128,896]{1,0:T(8,128)(2,1)S(1)}, bf16[128,896]{1,0:T(8,128)(2,1)S(1)}, u32[]{:S(2)}, u32[]{:S(2)}) collective-permute-start(bf16[128,896]{1,0:T(8,128)(2,1)S(1)} %convolution_convert_fusion.4), channel_id=1, source_target_pairs={{0,1},{1,0},{2,3},{3,2},{4,5},{5,4},{6,7},{7,6},{8,9},{9,8},{10,11... | collective-permute-start | bytes 688136 | tf_op jit(solution)/shard_map/ppermute | solution.py:59
  80.3 3.7 %collective-permute-start.15 = (bf16[128,896]{1,0:T(8,128)(2,1)S(1)}, bf16[128,896]{1,0:T(8,128)(2,1)S(1)}, u32[]{:S(2)}, u32[]{:S(2)}) collective-permute-start(bf16[128,896]{1,0:T(8,128)(2,1)S(1)} %convolution_convert_fusion.5), channel_id=1, source_target_pairs={{0,1},{1,0},{2,3},{3,2},{4,5},{5,4},{6,7},{7,6},{8,9},{9,8},{10,11... | collective-permute-start | bytes 688136 | tf_op jit(solution)/shard_map/ppermute | solution.py:59
  82.5 7.9 %collective-permute-start.17 = (bf16[128,896]{1,0:T(8,128)(2,1)}, bf16[128,896]{1,0:T(8,128)(2,1)S(1)}, u32[]{:S(2)}, u32[]{:S(2)}) collective-permute-start(bf16[128,896]{1,0:T(8,128)(2,1)} %add_convert_fusion.1), channel_id=1, source_target_pairs={{0,2},{2,0},{1,3},{3,1},{4,6},{6,4},{5,7},{7,5},{8,10},{10,8},{9,1... | collective-permute-start | bytes 688136 | tf_op jit(solution)/shard_map/ppermute | solution.py:59
  84.0 6.4 %copy-start.10 = (bf16[128,896]{1,0:T(8,128)(2,1)}, bf16[128,896]{1,0:T(8,128)(2,1)S(1)}, u32[]{:S(2)}) copy-start(bf16[128,896]{1,0:T(8,128)(2,1)S(1)} %collective-permute-done.15) | copy-start | bytes 688132
  90.4 0.7 copy-start.11
  91.0 18.7 %copy-start.12 = (f32[3584]{0:T(1024)S(1)}, f32[3584]{0:T(1024)}, u32[]{:S(2)}) copy-start(f32[3584]{0:T(1024)} %param.14) | copy-start | bytes 43012
  93.9 13.2 %collective-permute-start.18 = (bf16[48,896]{1,0:T(8,128)(2,1)}, bf16[48,896]{1,0:T(8,128)(2,1)S(1)}, u32[]{:S(2)}, u32[]{:S(2)}) collective-permute-start(bf16[48,896]{1,0:T(8,128)(2,1)} %get-tuple-element.10), channel_id=1, source_target_pairs={{0,4},{4,8},{8,12},{12,0},{1,5},{5,9},{9,13},{13,1},{2,6},{6,10},{... | collective-permute-start | bytes 258056 | tf_op jit(solution)/shard_map/ppermute | solution.py:38
  100.5 8.8 %collective-permute-start.19 = (bf16[48,896]{1,0:T(8,128)(2,1)}, bf16[48,896]{1,0:T(8,128)(2,1)S(1)}, u32[]{:S(2)}, u32[]{:S(2)}) collective-permute-start(bf16[48,896]{1,0:T(8,128)(2,1)} %get-tuple-element.9), channel_id=1, source_target_pairs={{0,8},{4,12},{8,0},{12,4},{1,9},{5,13},{9,1},{13,5},{2,10},{6,14},... | collective-permute-start | bytes 258056 | tf_op jit(solution)/shard_map/ppermute | solution.py:38
  103.9 5.8 %collective-permute-start.20 = (bf16[48,896]{1,0:T(8,128)(2,1)S(1)}, bf16[48,896]{1,0:T(8,128)(2,1)S(1)}, u32[]{:S(2)}, u32[]{:S(2)}) collective-permute-start(bf16[48,896]{1,0:T(8,128)(2,1)S(1)} %get-tuple-element.8), channel_id=1, source_target_pairs={{0,12},{4,0},{8,4},{12,8},{1,13},{5,1},{9,5},{13,9},{2,14},{6,2},{... | collective-permute-start | bytes 258056 | tf_op jit(solution)/shard_map/ppermute | solution.py:38
  109.8 4.2 %copy-start.3 = (bf16[128,1024]{1,0:T(8,128)(2,1)S(1)}, bf16[128,1024]{1,0:T(8,128)(2,1)}, u32[]{:S(2)}) copy-start(bf16[128,1024]{1,0:T(8,128)(2,1)} %copy-done.2) | copy-start | bytes 786436
  109.8 4.2 %copy-start.7 = (bf16[128,1024]{1,0:T(8,128)(2,1)S(1)}, bf16[128,1024]{1,0:T(8,128)(2,1)}, u32[]{:S(2)}) copy-start(bf16[128,1024]{1,0:T(8,128)(2,1)} %copy-done.6) | copy-start | bytes 786436
  109.8 4.2 %copy-start.9 = (bf16[128,1024]{1,0:T(8,128)(2,1)S(1)}, bf16[128,1024]{1,0:T(8,128)(2,1)}, u32[]{:S(2)}) copy-start(bf16[128,1024]{1,0:T(8,128)(2,1)} %copy-done.8) | copy-start | bytes 786436
  112.3 10.6 %collective-permute-start.21 = (bf16[48,3584]{1,0:T(8,128)(2,1)S(1)}, bf16[48,3584]{1,0:T(8,128)(2,1)S(1)}, u32[]{:S(2)}, u32[]{:S(2)}) collective-permute-start(bf16[48,3584]{1,0:T(8,128)(2,1)S(1)} %fusion.20), channel_id=1, source_target_pairs={{0,1},{1,0},{2,3},{3,2},{4,5},{5,4},{6,7},{7,6},{8,9},{9,8},{10,11... | collective-permute-start | bytes 1032200 | tf_op jit(solution)/shard_map/ppermute | solution.py:59
  112.3 10.5 %collective-permute-start.22 = (bf16[48,3584]{1,0:T(8,128)(2,1)S(1)}, bf16[48,3584]{1,0:T(8,128)(2,1)S(1)}, u32[]{:S(2)}, u32[]{:S(2)}) collective-permute-start(bf16[48,3584]{1,0:T(8,128)(2,1)S(1)} %fusion.20), channel_id=1, source_target_pairs={{0,2},{2,0},{1,3},{3,1},{4,6},{6,4},{5,7},{7,5},{8,10},{10,8},{9,1... | collective-permute-start | bytes 1032200 | tf_op jit(solution)/shard_map/ppermute | solution.py:59
  122.8 1.7 %collective-permute-start.23 = (bf16[48,3584]{1,0:T(8,128)(2,1)S(1)}, bf16[48,3584]{1,0:T(8,128)(2,1)S(1)}, u32[]{:S(2)}, u32[]{:S(2)}) collective-permute-start(bf16[48,3584]{1,0:T(8,128)(2,1)S(1)} %collective-permute-done.22), channel_id=1, source_target_pairs={{0,1},{1,0},{2,3},{3,2},{4,5},{5,4},{6,7},{7,6},{8,9},{9,8},{10,11... | collective-permute-start | bytes 1032200 | tf_op jit(solution)/shard_map/ppermute | solution.py:59

commit v2 on v0

v2 whole, which is shorter than its diff:
```python
import math

import jax
import jax.numpy as jnp
from jax import lax
from jax.experimental import pallas as pl
from jax.experimental.pallas import tpu as pltpu
from jax.sharding import PartitionSpec as P

HD = 128
LANES = 128
BF = jnp.bfloat16
F32 = jnp.float32
I32 = jnp.int32
PARAMS = pltpu.CompilerParams(vmem_limit_bytes=32 * 1024 * 1024)
PAIRWISE = True


def dot(a, b, dims=((1,), (0,))):
    return lax.dot_general(a, b, (dims, ((), ())), preferred_element_type=F32)


def eye(size):
    return lax.broadcasted_iota(I32, (size, size), 0) == lax.broadcasted_iota(I32, (size, size), 1)


def to_row(column):
    return jnp.sum(jnp.where(eye(column.shape[0]), column, 0.0), axis=0, keepdims=True)


def to_column(row):
    return jnp.sum(jnp.where(eye(row.shape[1]), row, 0.0), axis=1, keepdims=True)


def norm_kernel(at, hidden_ref, gain_ref, owner_ref, docs_ref, *outs):
    pieces, inverse_ref = outs[:-1], outs[-1]
    rows, width = hidden_ref.shape
    depth = width // len(pieces)
    hidden = hidden_ref[...].astype(F32)
    inverse = lax.rsqrt(jnp.sum(hidden * hidden, axis=1, keepdims=True) / width + 1e-06)
    inverse_ref[...] = inverse
    line = lax.broadcasted_iota(I32, (rows, LANES), 0)
    owner_row = to_row(owner_ref[...].astype(F32))
    docs_row = docs_ref[...].astype(F32)
    extra = jnp.where(line == 0, owner_row, jnp.where(line == 1, docs_row, 0.0)).astype(BF)
    for k, piece in enumerate(pieces):
        columns = pl.ds(pl.multiple_of((at[1] ^ k) * depth, LANES), depth)
        block = hidden_ref[:, columns].astype(F32)
        piece[:, :depth] = (block * inverse * gain_ref[:, columns]).astype(BF)
        piece[:, depth:] = extra


def norm_pieces(at, student_hidden, norm_gain, owner, doc_ids, n):
    capacity, width = student_hidden.shape
    rows, depth = capacity // n, width // n
    tokens = owner.shape[0]
    piece = jax.ShapeDtypeStruct((rows, depth + LANES), BF)
    whole = lambda i, s: (0, 0)
    return pl.pallas_call(
        norm_kernel,
        grid_spec=pltpu.PrefetchScalarGridSpec(
            num_scalar_prefetch=1,
            grid=(1,),
            in_specs=[
                pl.BlockSpec((rows, width), lambda i, s: (s[0], 0)),
                pl.BlockSpec((1, width), whole),
                pl.BlockSpec((tokens, 1), whole),
                pl.BlockSpec((1, tokens), whole),
            ],
            out_specs=[pl.BlockSpec((rows, depth + LANES), whole)] * n
            + [pl.BlockSpec((rows, 1), whole)],
        ),
        out_shape=[piece] * n + [jax.ShapeDtypeStruct((rows, 1), F32)],
        compiler_params=PARAMS,
        cost_estimate=pl.CostEstimate(
            flops=6 * rows * width, bytes_accessed=6 * rows * width, transcendentals=rows
        ),
    )(at, student_hidden, norm_gain[None, :], owner, doc_ids[None, :])


def pick_kernel(at, *refs):
    pieces, out_ref, drop_ref = refs[:-2], refs[-2], refs[-1]
    tokens, depth = out_ref.shape
    slots = pieces[0].shape[0]
    spots = slots * len(pieces)
    owner_row = jnp.zeros((1, tokens), F32)
    for k, piece in enumerate(pieces):
        tile = piece[0:16, depth:].astype(F32)[0:1]
        owner_row = owner_row + jnp.where(at[2] == k, tile, 0.0)
    owner = to_column(owner_row)
    earlier = lax.broadcasted_iota(I32, (tokens, tokens), 1) < lax.broadcasted_iota(
        I32, (tokens, tokens), 0
    )
    same = jnp.where(earlier & (owner == owner_row), 1.0, 0.0)
    rank = jnp.sum(same, axis=1, keepdims=True)
    peer = owner.astype(I32) ^ at[1]
    spot = (peer * slots).astype(F32) + rank
    take = (lax.broadcasted_iota(I32, (tokens, spots), 1) == spot.astype(I32)).astype(F32)
    stacked = jnp.concatenate([piece[:, :depth] for piece in pieces], axis=0)
    out_ref[...] = dot(take.astype(BF), stacked).astype(BF)
    spot_row = to_row(spot).astype(I32)
    drop = (lax.broadcasted_iota(I32, (spots, tokens), 0) == spot_row).astype(F32)
    drop_ref[...] = drop.astype(BF)


def pick_rows(at, pieces, tokens):
    slots, wide = pieces[0].shape
    depth = wide - LANES
    spots = slots * len(pieces)
    whole = lambda i, s: (0, 0)
    return pl.pallas_call(
        pick_kernel,
        grid_spec=pltpu.PrefetchScalarGridSpec(
            num_scalar_prefetch=1,
            grid=(1,),
            in_specs=[pl.BlockSpec((slots, wide), whole)] * len(pieces),
            out_specs=[
                pl.BlockSpec((tokens, depth), whole),
                pl.BlockSpec((spots, tokens), whole),
            ],
        ),
        out_shape=[
            jax.ShapeDtypeStruct((tokens, depth), BF),
            jax.ShapeDtypeStruct((spots, tokens), BF),
        ],
        compiler_params=PARAMS,
        cost_estimate=pl.CostEstimate(
            flops=2 * tokens * spots * depth, bytes_accessed=4 * spots * depth, transcendentals=0
        ),
    )(at, *pieces)


def attention_kernel(at, queries_ref, *refs):
    out_ref = refs[-1]
    n = (len(refs) - 1) // 2
    parcels, tiles = refs[:n], refs[n : 2 * n]
    tokens = queries_ref.shape[0]
    me = at[1]
    keys = jnp.concatenate([parcel[:tokens, :] for parcel in parcels], axis=0)
    values = jnp.concatenate([parcel[tokens:, :] for parcel in parcels], axis=0)
    docs = [tile[...].astype(F32)[1:2] for tile in tiles]
    doc_column = to_column(docs[0])
    query_pos = me * tokens + lax.broadcasted_iota(I32, (tokens, tokens), 0)
    within = lax.broadcasted_iota(I32, (tokens, tokens), 1)
    masks = []
    for k in range(n):
        near = (me ^ k) * tokens + within <= query_pos
        masks.append(jnp.where(near & (docs[k] == doc_column), 1.0, 0.0))
    allowed = jnp.concatenate(masks, axis=1) > 0.5
    scale_factor = 1.0 / math.sqrt(HD)
    for h in range(queries_ref.shape[1] // HD):
        columns = slice(h * HD, (h + 1) * HD)
        scores = dot(queries_ref[:, columns], keys, ((1,), (1,))) * scale_factor
        scores = jnp.where(allowed, scores, -1e30)
        top = jnp.max(scores, axis=1, keepdims=True)
        probs = jnp.where(allowed, jnp.exp(scores - top), 0.0)
        total = jnp.sum(probs, axis=1, keepdims=True)
        out_ref[:, columns] = (dot(probs.astype(BF), values) / total).astype(BF)


def attention_rows(at, queries, parcels, pieces):
    tokens, width = queries.shape
    n = len(parcels)
    wide = pieces[0].shape[1]
    whole = lambda i, s: (0, 0)
    return pl.pallas_call(
        attention_kernel,
        grid_spec=pltpu.PrefetchScalarGridSpec(
            num_scalar_prefetch=1,
            grid=(1,),
            in_specs=[pl.BlockSpec((tokens, width), whole)]
            + [pl.BlockSpec((2 * tokens, HD), whole)] * n
            + [pl.BlockSpec((16, LANES), lambda i, s: (0, wide // LANES - 1))] * n,
            out_specs=pl.BlockSpec((tokens, width), whole),
        ),
        out_shape=jax.ShapeDtypeStruct((tokens, width), BF),
        compiler_params=PARAMS,
        cost_estimate=pl.CostEstimate(
            flops=8 * n * tokens * tokens * width,
            bytes_accessed=4 * tokens * width,
            transcendentals=n * tokens * tokens * (width // HD),
        ),
    )(at, queries, *parcels, *pieces)


def rows_kernel(at, hidden_ref, gain_ref, inverse_ref, *refs):
    pieces, out_ref = refs[:-1], refs[-1]
    width = hidden_ref.shape[1]
    depth = width // len(pieces)
    inverse = inverse_ref[...]
    total = jnp.zeros_like(inverse)
    for k, piece in enumerate(pieces):
        columns = pl.ds(pl.multiple_of((at[1] ^ k) * depth, LANES), depth)
        gain_grad = piece[...].astype(F32) * gain_ref[:, columns]
        block = hidden_ref[:, columns].astype(F32)
        total = total + jnp.sum(gain_grad * block, axis=1, keepdims=True)
    lean = inverse * inverse * inverse * (total / width)
    for k, piece in enumerate(pieces):
        columns = pl.ds(pl.multiple_of((at[1] ^ k) * depth, LANES), depth)
        gain_grad = piece[...].astype(F32) * gain_ref[:, columns]
        block = hidden_ref[:, columns].astype(F32)
        out_ref[:, columns] = (inverse * gain_grad - lean * block).astype(BF)


def grad_rows(at, student_hidden, norm_gain, inverse, pieces):
    rows, depth = pieces[0].shape
    width = student_hidden.shape[1]
    whole = lambda i, s: (0, 0)
    return pl.pallas_call(
        rows_kernel,
        grid_spec=pltpu.PrefetchScalarGridSpec(
            num_scalar_prefetch=1,
            grid=(1,),
            in_specs=[
                pl.BlockSpec((rows, width), lambda i, s: (s[0], 0)),
                pl.BlockSpec((1, width), whole),
                pl.BlockSpec((rows, 1), whole),
            ]
            + [pl.BlockSpec((rows, depth), whole)] * len(pieces),
            out_specs=pl.BlockSpec((rows, width), whole),
        ),
        out_shape=jax.ShapeDtypeStruct((rows, width), BF),
        compiler_params=PARAMS,
        cost_estimate=pl.CostEstimate(
            flops=12 * rows * width, bytes_accessed=6 * rows * width, transcendentals=0
        ),
    )(at, student_hidden, norm_gain[None, :], inverse, *pieces)


def swap(x, axis, k=1):
    return lax.ppermute(x, axis, [(i, i ^ k) for i in range(lax.axis_size(axis))])


def turn(entries, by):
    odd, high = by % 2 == 1, by >= 2
    a, b, c, d = entries
    a, b = jnp.where(odd, b, a), jnp.where(odd, a, b)
    c, d = jnp.where(odd, d, c), jnp.where(odd, c, d)
    return [
        jnp.where(high, c, a),
        jnp.where(high, d, b),
        jnp.where(high, a, c),
        jnp.where(high, b, d),
    ]


def pairwise(
    teacher_queries, teacher_keys, teacher_values, doc_ids, owner, student_hidden, norm_gain, proj
):
    n = 4
    me = lax.axis_index("seq")
    side = lax.axis_index("side")
    mine = lax.axis_index("mp") * 2 + side
    rows = teacher_queries.shape[0]
    heads = teacher_queries.shape[1] // HD
    kv_local = teacher_keys.shape[1] // HD
    group = heads * 2 // kv_local
    capacity, width = student_hidden.shape
    slots = capacity // n
    depth = proj.shape[0]
    off = mine ^ me
    at = jnp.stack([mine, me, off]).astype(I32)

    made = norm_pieces(at, student_hidden, norm_gain, owner, doc_ids, n)
    inverse = made[n]
    pieces = [made[0]] + [swap(made[k], "seq", k) for k in range(1, n)]
    normed_own, drop = pick_rows(at, pieces, rows)

    mate = swap(normed_own, "side")
    far = swap(normed_own, "mp")
    far_mate = swap(far, "side")
    normed = turn([normed_own, mate, far, far_mate], off)

    head = side * heads // group
    parcel = jnp.concatenate(
        [
            lax.dynamic_slice_in_dim(teacher_keys, head * HD, HD, 1),
            lax.dynamic_slice_in_dim(teacher_values, head * HD, HD, 1),
        ]
    )
    parcel, mate = lax.optimization_barrier((parcel, mate))
    parcels = [parcel] + [swap(parcel, "seq", k) for k in range(1, n)]
    teacher_rows = attention_rows(at, teacher_queries, parcels, pieces)

    away = dot(normed[3], proj).astype(BF)
    got_over = swap(away, "seq", 1)
    over_own = dot(normed[2], proj)
    over = (over_own + got_over.astype(F32)).astype(BF)
    beside = dot(normed[1], proj).astype(BF)
    beside, over = lax.optimization_barrier((beside, over))
    got_far = swap(over, "seq", 2)
    got_beside = swap(beside, "seq", 1)
    own = lax.optimization_barrier(dot(normed[0], proj))
    predicted = own + got_beside.astype(F32) + got_far.astype(F32)
    delta = (predicted - teacher_rows.astype(F32)).astype(BF)

    delta_far = swap(delta, "seq", 2)
    delta_beside = swap(delta, "seq", 1)
    delta_last = swap(delta_far, "seq", 1)
    deltas = [delta, delta_beside, delta_far, delta_last]

    products = [dot(block, proj, ((1,), (1,))).astype(BF) for block in deltas]
    near, away_near, cross, away_cross = turn(products, off)
    got = swap(jnp.stack([away_near, away_cross]), "side")
    cross = (cross.astype(F32) + got[1].astype(F32)).astype(BF)
    crossed = swap(cross, "mp")
    near = lax.optimization_barrier(near.astype(F32) + got[0].astype(F32))
    feature_rows = (near + crossed.astype(F32)).astype(BF)
    leaving = [dot(drop[k * slots : (k + 1) * slots], feature_rows).astype(BF) for k in range(n)]
    arrived = [leaving[0]] + [swap(leaving[k], "seq", k) for k in range(1, n)]
    grad_own = grad_rows(at, student_hidden, norm_gain, inverse, arrived)

    grad_mate = swap(grad_own, "side")
    grad_far = swap(grad_own, "mp")
    grad_last = swap(grad_far, "side")
    grad_hidden = jnp.zeros((capacity, width), BF)
    for q, block in enumerate([grad_own, grad_mate, grad_far, grad_last]):
        grad_hidden = lax.dynamic_update_slice_in_dim(grad_hidden, block, (mine ^ q) * slots, 0)

    factor = 1.0 / math.sqrt(rows * n)
    grad_proj = dot(jnp.concatenate(normed), jnp.concatenate(deltas), ((0,), (0,))) * factor
    return (grad_hidden, grad_proj)


def general(
    teacher_queries, teacher_keys, teacher_values, doc_ids, owner, student_hidden, norm_gain, proj
):
    n = lax.axis_size("seq")
    me = lax.axis_index("seq")
    side = lax.axis_index("side")
    plane = lax.axis_size("mp") * lax.axis_size("side")
    mine = lax.axis_index("mp") * lax.axis_size("side") + side
    rows = teacher_queries.shape[0]
    heads = teacher_queries.shape[1] // HD
    kv_local = teacher_keys.shape[1] // HD
    group = heads * lax.axis_size("side") // kv_local
    width = student_hidden.shape[1]
    depth = proj.shape[0]
    capacity = student_hidden.shape[0]
    slots = capacity // n
    shared = n // plane
    held = shared * slots

    hidden = lax.dynamic_slice_in_dim(student_hidden, mine * held, held, 0).astype(F32)
    inverse_rms = lax.rsqrt(jnp.mean(hidden * hidden, axis=1, keepdims=True) + 1e-06)
    normed = (hidden * inverse_rms * norm_gain).astype(BF)
    normed_slots = lax.all_to_all(
        normed.reshape(held, n, depth).transpose(1, 0, 2), "seq", 0, 0, tiled=True
    )

    head = side * heads // group
    key_head = lax.dynamic_slice_in_dim(teacher_keys, head * HD, HD, 1)
    value_head = lax.dynamic_slice_in_dim(teacher_values, head * HD, HD, 1)
    small = jnp.stack([doc_ids, owner[:, 0]]).astype(BF)
    parcel = jnp.concatenate([key_head, value_head, jnp.pad(small, ((0, 14), (0, 0)))])
    parcel = lax.all_gather(parcel, "seq", axis=0, tiled=False)
    keys, values = parcel[:, :rows], parcel[:, rows : 2 * rows]
    docs = parcel[:, 2 * rows].astype(I32)
    owners = parcel[:, 2 * rows + 1].astype(I32)

    query_pos = me * rows + jnp.arange(rows, dtype=I32)
    key_pos = jnp.arange(n * rows, dtype=I32)
    allowed = (docs.reshape(-1)[None, :] == doc_ids[:, None]) & (
        key_pos[None, :] <= query_pos[:, None]
    )
    stacked = teacher_queries.reshape(rows, heads, HD).transpose(1, 0, 2)
    scores = jnp.einsum("hqd,kd->hqk", stacked, keys.reshape(-1, HD), preferred_element_type=F32)
    scores = jnp.where(allowed[None], scores * (1.0 / math.sqrt(HD)), -1e30)
    top = jnp.max(scores, axis=2, keepdims=True)
    probs = jnp.where(allowed[None], jnp.exp(scores - top), 0.0)
    totals = jnp.sum(probs, axis=2, keepdims=True)
    weighted = jnp.einsum(
        "hqk,kd->hqd", probs.astype(BF), values.reshape(-1, HD), preferred_element_type=F32
    )
    teacher_rows = (weighted / totals).astype(BF).transpose(1, 0, 2).reshape(rows, heads * HD)

    own_blocks = lax.dynamic_slice_in_dim(owners, mine * shared, shared, 0)
    order = jnp.arange(rows, dtype=I32)
    same = (own_blocks[:, :, None] == own_blocks[:, None, :]) & (order[:, None] > order[None, :])
    rank = jnp.sum(same.astype(I32), axis=2)
    spot = own_blocks * held + jnp.arange(shared, dtype=I32)[:, None] * slots + rank
    pick = (spot.reshape(-1)[:, None] == jnp.arange(n * held, dtype=I32)[None, :]).astype(BF)

    normed_own = dot(pick, normed_slots.reshape(n * held, depth)).astype(BF)
    normed_rows = lax.all_gather(normed_own, ("mp", "side"), axis=0, tiled=True)
    partial = dot(normed_rows, proj).astype(BF)
    predicted = lax.psum_scatter(partial, "seq", scatter_dimension=0, tiled=True).astype(F32)
    delta = (predicted - teacher_rows.astype(F32)).astype(BF)
    deltas = lax.all_gather(delta, "seq", axis=0, tiled=True)

    products = dot(deltas, proj, ((1,), (1,))).astype(BF)
    feature_rows = lax.psum_scatter(products, ("mp", "side"), scatter_dimension=0, tiled=True)
    feature_slots = dot(pick, feature_rows, ((0,), (0,))).astype(BF).reshape(n, held, depth)
    received = lax.all_to_all(feature_slots, "seq", 0, 0, tiled=True)
    feature_grad = received.transpose(1, 0, 2).reshape(held, width)

    gain_grad = feature_grad.astype(F32) * norm_gain
    mean_term = jnp.mean(gain_grad * hidden, axis=1, keepdims=True)
    grad_own = (inverse_rms * gain_grad - inverse_rms**3 * hidden * mean_term).astype(BF)
    grad_hidden = lax.all_gather(grad_own, ("mp", "side"), axis=0, tiled=True)

    grad_proj = dot(normed_rows, deltas, ((0,), (0,))) * (1.0 / math.sqrt(rows * n))
    return (grad_hidden, grad_proj)


def solution(mesh):
    sizes = mesh.shape
    paired = PAIRWISE and (sizes["seq"], sizes["mp"], sizes["side"]) == (4, 2, 2)
    return jax.shard_map(
        pairwise if paired else general,
        mesh=mesh,
        in_specs=(
            P(("groups", "seq"), ("mp", "side")),
            P(("groups", "seq"), "mp"),
            P(("groups", "seq"), "mp"),
            P(("groups", "seq")),
            P(("groups", "seq"), None),
            P(("groups", "seq"), None),
            P(),
            P("seq", ("mp", "side")),
        ),
        out_specs=(P(("groups", "seq"), None), P(("groups", "seq"), ("mp", "side"))),
        check_vma=False,
    )
```

time: 349 us -> 117 us (0.34)
  waiting for transfers between devices: 244 us -> 68 us
  blocking collectives: 50.2 us -> 0 us
  starting transfers between devices: 10.1 us -> 25.6 us
  between operations: 14 us -> 1.06 us
  matrix products: 16.3 us -> 8.32 us
  other arithmetic: 10.9 us -> 3.51 us
  Pallas kernels: 0 us -> 5.47 us
    reduce_scatter x1 -> x0, waiting for transfers between devices: 126 us -> none  [on_device(): lax.psum_scatter((lax.dot_general(normed, delta, (((0,), (0,)), ((), ()))...]
    ppermute x0 -> x23, waiting for transfers between devices: none -> 68 us  [swap(): lax.ppermute(x, axis, [(i, i ^ k) for i in range(lax.axis_size(axis))])]
    all_gather x1 -> x0, waiting for transfers between devices: 64.5 us -> none  [on_device(): weight_full = lax.all_gather(proj, 'seq', axis=0, tiled=True)]
    all_gather x3 -> x0, blocking collectives: 50.2 us -> none  [the longest x1 21.9 us: on_device(): value_piece = lax.all_gather(teacher_values, 'seq', axis=0, tiled=True)]
    psum x1 -> x0, waiting for transfers between devices: 32.7 us -> none  [on_device(): lax.psum(partial_grad.astype(jnp.bfloat16), ('mp', 'side'))]
    ppermute x0 -> x23, starting transfers between devices: none -> 25.6 us  [swap(): lax.ppermute(x, axis, [(i, i ^ k) for i in range(lax.axis_size(axis))])]
    all_to_all x2 -> x0, waiting for transfers between devices: 20.4 us -> none  [the longest x1 20.4 us: on_device(): lax.all_to_all(packed, 'seq', split_axis=0, concat_axis=0, tiled=True)]
    all_to_all x2 -> x0, starting transfers between devices: 9.78 us -> none  [the longest x1 6.32 us: on_device(): lax.all_to_all(occupied, 'seq', split_axis=0, concat_axis=0, tiled=True)]
  transfers between devices with their start and end apart: 5 -> 23, of which waited for: 4 -> 16; matrix products, arithmetic and copies ran while one was open for 5% -> 5% of each run, Pallas kernels for 0% -> 2%
where the time goes in v2:
time: 117 us
  waiting for transfers between devices  68 us (58%)
  starting transfers between devices  25.6 us (22%)
  matrix products  8.32 us (7%)
  Pallas kernels  5.47 us (5%)
  local copies, waits for them, and re-layouts  5 us (4%)
  other arithmetic  3.51 us (3%)
    ppermute x23, waiting for transfers between devices, swap(): lax.ppermute(x, axis, [(i, i ^ k) for i in range(lax.axis_size(axis))])  68 us
    ppermute x23, starting transfers between devices, swap(): lax.ppermute(x, axis, [(i, i ^ k) for i in range(lax.axis_size(axis))])  25.6 us
    dot_general x13, matrix products, dot(): return lax.dot_general(a, b, (dims, ((), ())), preferred_element_type=F32)  8.32 us
    unnamed x41, local copies, waits for them, and re-layouts  3.91 us
    pallas_call x1, Pallas kernels, attention_rows(): pl.pallas_call(attention_kernel, grid_spec=pltpu.PrefetchScalarGridSpec(n...  2.87 us
  transfers between devices with their start and end apart: 23, of which 16 were waited for; matrix products, arithmetic and copies ran while one was open for 5% of the time, Pallas kernels for 2%

profile of v2, /device:TPU:0, one launch (start us, length us, event | category | flops | bytes accessed | tf_op | source)
XLA Modules:
  0.0 117.0 jit_solution(9161563612585763182)
XLA Ops:
  0.6 0.0 copy-start
  0.7 0.9 broadcast_in_dim.11.gain_ref
  1.5 0.8 copy.10.owner_ref
  2.3 0.1 pad_add_fusion.at
  2.4 1.3 %copy-done.1 = bf16[192,3584]{1,0:T(8,128)(2,1)S(1)} copy-done((bf16[192,3584]{1,0:T(8,128)(2,1)S(1)}, bf16[192,3584]{1,0:T(8,128)(2,1)}, u32[]{:S(2)}) %copy-start.1) | copy-done | bytes 1376280
  3.7 0.7 copy-done.3
  4.4 0.8 shard_map.95
  5.2 3.1 %collective-permute-start = (bf16[48,1024]{1,0:T(8,128)(2,1)S(1)}, bf16[48,1024]{1,0:T(8,128)(2,1)S(1)}, u32[]{:S(2)}, u32[]{:S(2)}) collective-permute-start(bf16[48,1024]{1,0:T(8,128)(2,1)S(1)} %get-tuple-element.14), channel_id=1, source_target_pairs={{0,4},{4,0},{8,12},{12,8},{1,5},{5,1},{9,13},{13,9},{2,6},{6,2},{1... | collective-permute-start | bytes 294920 | tf_op jit(solution)/shard_map/ppermute | solution.py:231
  8.3 2.6 %collective-permute-start.1 = (bf16[48,1024]{1,0:T(8,128)(2,1)S(1)}, bf16[48,1024]{1,0:T(8,128)(2,1)S(1)}, u32[]{:S(2)}, u32[]{:S(2)}) collective-permute-start(bf16[48,1024]{1,0:T(8,128)(2,1)S(1)} %get-tuple-element.15), channel_id=1, source_target_pairs={{0,8},{4,12},{8,0},{12,4},{1,9},{5,13},{9,1},{13,5},{2,10},{6,14},... | collective-permute-start | bytes 294920 | tf_op jit(solution)/shard_map/ppermute | solution.py:231
  10.8 0.2 collective-permute-done.refs_1_.refs_5_
  11.0 7.6 %collective-permute-done.1.refs_2_.refs_6_ = bf16[48,1024]{1,0:T(8,128)(2,1)S(1)} collective-permute-done((bf16[48,1024]{1,0:T(8,128)(2,1)S(1)}, bf16[48,1024]{1,0:T(8,128)(2,1)S(1)}, u32[]{:S(2)}, u32[]{:S(2)}) %collective-permute-start.1) | collective-permute-done | bytes 98336 | tf_op jit(solution)/shard_map/ppermute | solution.py:231
  18.7 0.9 shard_map.96
  19.6 1.6 %collective-permute-start.3 = (bf16[128,896]{1,0:T(8,128)(2,1)S(1)}, bf16[128,896]{1,0:T(8,128)(2,1)S(1)}, u32[]{:S(2)}, u32[]{:S(2)}) collective-permute-start(bf16[128,896]{1,0:T(8,128)(2,1)S(1)} %get-tuple-element.18), channel_id=1, source_target_pairs={{0,2},{2,0},{1,3},{3,1},{4,6},{6,4},{5,7},{7,5},{8,10},{10,8},{9,1... | collective-permute-start | bytes 688136 | tf_op jit(solution)/shard_map/ppermute | solution.py:231
  21.2 4.5 %collective-permute-done.3 = bf16[128,896]{1,0:T(8,128)(2,1)S(1)} collective-permute-done((bf16[128,896]{1,0:T(8,128)(2,1)S(1)}, bf16[128,896]{1,0:T(8,128)(2,1)S(1)}, u32[]{:S(2)}, u32[]{:S(2)}) %collective-permute-start.3) | collective-permute-done | bytes 229408 | tf_op jit(solution)/shard_map/ppermute | solution.py:231
  25.7 2.5 %collective-permute-start.11 = (bf16[256,128]{1,0:T(8,128)(2,1)S(1)}, bf16[256,128]{1,0:T(8,128)(2,1)S(1)}, u32[]{:S(2)}, u32[]{:S(2)}) collective-permute-start(bf16[256,128]{1,0:T(8,128)(2,1)S(1)} %pad_maximum_fusion.1.refs_0_), channel_id=1, source_target_pairs={{0,12},{4,8},{8,4},{12,0},{1,13},{5,9},{9,5},{13,1},{2,14},{6,10},... | collective-permute-start | bytes 196616 | tf_op jit(solution)/shard_map/ppermute | solution.py:231
  28.3 0.8 collective-permute-start.10
  29.0 1.2 collective-permute-start.9
  30.2 2.1 %collective-permute-done.11.refs_3_ = bf16[256,128]{1,0:T(8,128)(2,1)S(1)} collective-permute-done((bf16[256,128]{1,0:T(8,128)(2,1)S(1)}, bf16[256,128]{1,0:T(8,128)(2,1)S(1)}, u32[]{:S(2)}, u32[]{:S(2)}) %collective-permute-start.11) | collective-permute-done | bytes 65568 | tf_op jit(solution)/shard_map/ppermute | solution.py:231
  32.2 3.5 %collective-permute-done.10.refs_2_ = bf16[256,128]{1,0:T(8,128)(2,1)S(1)} collective-permute-done((bf16[256,128]{1,0:T(8,128)(2,1)S(1)}, bf16[256,128]{1,0:T(8,128)(2,1)S(1)}, u32[]{:S(2)}, u32[]{:S(2)}) %collective-permute-start.10) | collective-permute-done | bytes 65568 | tf_op jit(solution)/shard_map/ppermute | solution.py:231
  35.7 2.9 %shard_map.97 = bf16[128,1024]{1,0:T(8,128)(2,1)S(1)} custom-call(s32[3]{0:T(128)S(1)} %pad_add_fusion.at, bf16[128,1024]{1,0:T(8,128)(2,1)S(1)} %copy-done.4, bf16[256,128]{1,0:T(8,128)(2,1)S(1)} %pad_maximum_fusion.1.refs_0_, bf16[256,128]{1,0:T(8,128)(2,1)S(1)} %collective-permute-done.9.refs_1_, bf16[256,128]{1,0:T(8,128)(2,1)S(1)} %collective-permute-done.10.refs_2_, ...), custom_call_target="tpu_custom_call" | custom-call | flops 536870912 | bytes 524288 | tf_op jit(solution)/shard_map/pallas_call | solution.py:166
  38.6 1.1 broadcast_select_fusion.11
  39.7 0.5 convolution_convert_fusion
  40.2 0.1 collective-permute-start.6
  40.3 0.5 convolution_convert_fusion.1
  40.7 7.4 %collective-permute-done.6 = bf16[128,1024]{1,0:T(8,128)(2,1)S(1)} collective-permute-done((bf16[128,1024]{1,0:T(8,128)(2,1)S(1)}, bf16[128,1024]{1,0:T(8,128)(2,1)S(1)}, u32[]{:S(2)}, u32[]{:S(2)}) %collective-permute-start.6) | collective-permute-done | bytes 262176 | tf_op jit(solution)/shard_map/ppermute | solution.py:231
  48.2 0.5 fusion
  48.6 0.4 collective-permute-start.7
  49.0 2.7 %collective-permute-start.8 = (bf16[128,1024]{1,0:T(8,128)(2,1)S(1)}, bf16[128,1024]{1,0:T(8,128)(2,1)S(1)}, u32[]{:S(2)}, u32[]{:S(2)}) collective-permute-start(bf16[128,1024]{1,0:T(8,128)(2,1)S(1)} %fusion), channel_id=1, source_target_pairs={{0,8},{4,12},{8,0},{12,4},{1,9},{5,13},{9,1},{13,5},{2,10},{6,14},... | collective-permute-start | bytes 786440 | tf_op jit(solution)/shard_map/ppermute | solution.py:231
  51.7 0.5 fusion.21
  52.2 9.1 %collective-permute-done.7 = bf16[128,1024]{1,0:T(8,128)(2,1)S(1)} collective-permute-done((bf16[128,1024]{1,0:T(8,128)(2,1)S(1)}, bf16[128,1024]{1,0:T(8,128)(2,1)S(1)}, u32[]{:S(2)}, u32[]{:S(2)}) %collective-permute-start.7) | collective-permute-done | bytes 262176 | tf_op jit(solution)/shard_map/ppermute | solution.py:231
  61.2 1.4 %collective-permute-done.8 = bf16[128,1024]{1,0:T(8,128)(2,1)S(1)} collective-permute-done((bf16[128,1024]{1,0:T(8,128)(2,1)S(1)}, bf16[128,1024]{1,0:T(8,128)(2,1)S(1)}, u32[]{:S(2)}, u32[]{:S(2)}) %collective-permute-start.8) | collective-permute-done | bytes 262176 | tf_op jit(solution)/shard_map/ppermute | solution.py:231
  62.6 0.1 subtract_convert_fusion
  62.8 0.5 collective-permute-start.14
  63.3 2.7 %collective-permute-start.12 = (bf16[128,1024]{1,0:T(8,128)(2,1)S(1)}, bf16[128,1024]{1,0:T(8,128)(2,1)S(1)}, u32[]{:S(2)}, u32[]{:S(2)}) collective-permute-start(bf16[128,1024]{1,0:T(8,128)(2,1)S(1)} %subtract_convert_fusion), channel_id=1, source_target_pairs={{0,8},{4,12},{8,0},{12,4},{1,9},{5,13},{9,1},{13,5},{2,10},{6,14},... | collective-permute-start | bytes 786440 | tf_op jit(solution)/shard_map/ppermute | solution.py:231
  66.0 0.7 convolution_convert_fusion.2
  66.7 9.4 %collective-permute-done.12 = bf16[128,1024]{1,0:T(8,128)(2,1)S(1)} collective-permute-done((bf16[128,1024]{1,0:T(8,128)(2,1)S(1)}, bf16[128,1024]{1,0:T(8,128)(2,1)S(1)}, u32[]{:S(2)}, u32[]{:S(2)}) %collective-permute-start.12) | collective-permute-done | bytes 262176 | tf_op jit(solution)/shard_map/ppermute | solution.py:231
  76.1 0.7 convolution_convert_fusion.4
  76.8 0.7 convolution_convert_fusion.3
  77.5 4.9 %collective-permute-done.13 = bf16[128,1024]{1,0:T(8,128)(2,1)S(1)} collective-permute-done((bf16[128,1024]{1,0:T(8,128)(2,1)S(1)}, bf16[128,1024]{1,0:T(8,128)(2,1)S(1)}, u32[]{:S(2)}, u32[]{:S(2)}) %collective-permute-start.13) | collective-permute-done | bytes 262176 | tf_op jit(solution)/shard_map/ppermute | solution.py:231
  82.5 0.7 convolution_convert_fusion.5
  83.2 0.1 select_bitcast_fusion.1
  83.3 0.8 pad_maximum_fusion
  84.1 0.0 copy-start.17
  84.1 2.1 %collective-permute-done.15 = bf16[2,128,896]{2,1,0:T(8,128)(2,1)} collective-permute-done((bf16[2,128,896]{2,1,0:T(8,128)(2,1)}, bf16[2,128,896]{2,1,0:T(8,128)(2,1)}, u32[]{:S(2)}, u32[]{:S(2)}) %collective-permute-start.15) | collective-permute-done | bytes 458784 | tf_op jit(solution)/shard_map/ppermute | solution.py:231
  86.2 1.3 %fusion.15 = (bf16[128,896]{1,0:T(8,128)(2,1)S(1)}, f32[128,896]{1,0:T(8,128)S(1)}) fusion(bf16[2,128,896]{2,1,0:T(8,128)(2,1)} %collective-permute-done.15, pred[]{:T(512)S(6)} %ge.4, bf16[128,896]{1,0:T(8,128)(2,1)S(1)} %convolution_convert_fusion.5, bf16[128,896]{1,0:T(8,128)(2,1)S(1)} %convolution_convert_fusion.4, pred[]{:T(512)S(6)} %eq.7, ...), kind=kLoop, calls=%fused_computation.30 | loop fusion | flops 1261568 | bytes 2064386 | tf_op jit(solution)/shard_map/convert_element_type | solution.py:305
  87.5 1.5 %collective-permute-start.16 = (bf16[128,896]{1,0:T(8,128)(2,1)S(1)}, bf16[128,896]{1,0:T(8,128)(2,1)S(1)}, u32[]{:S(2)}, u32[]{:S(2)}) collective-permute-start(bf16[128,896]{1,0:T(8,128)(2,1)S(1)} %get-tuple-element.22), channel_id=1, source_target_pairs={{0,2},{2,0},{1,3},{3,1},{4,6},{6,4},{5,7},{7,5},{8,10},{10,8},{9,1... | collective-permute-start | bytes 688136 | tf_op jit(solution)/shard_map/ppermute | solution.py:231
  89.1 3.0 %convolution_multiply_fusion = f32[896,1024]{1,0:T(8,128)} fusion(bf16[128,1024]{1,0:T(8,128)(2,1)S(1)} %copy-done.17, bf16[128,1024]{1,0:T(8,128)(2,1)S(1)} %copy-done.15, bf16[128,1024]{1,0:T(8,128)(2,1)S(1)} %copy-done.13, bf16[128,1024]{1,0:T(8,128)(2,1)S(1)} %subtract_convert_fusion, bf16[128,896]{1,0:T(8,128)(2,1)S(1)} %copy-done.11, ...), kind=kOutput, calls=%fused_computation | convolution fusion | flops 948305920 | bytes 5636096 | tf_op jit(solution)/shard_map/dot_general | solution.py:20
  92.1 3.2 %collective-permute-done.16 = bf16[128,896]{1,0:T(8,128)(2,1)S(1)} collective-permute-done((bf16[128,896]{1,0:T(8,128)(2,1)S(1)}, bf16[128,896]{1,0:T(8,128)(2,1)S(1)}, u32[]{:S(2)}, u32[]{:S(2)}) %collective-permute-start.16) | collective-permute-done | bytes 229408 | tf_op jit(solution)/shard_map/ppermute | solution.py:231
  95.3 0.2 convolution_convert_fusion.6
  95.4 0.2 convolution_convert_fusion.7
  95.6 0.2 convolution_convert_fusion.8
  95.8 0.1 collective-permute-start.17
  95.9 1.8 %collective-permute-start.18 = (bf16[48,896]{1,0:T(8,128)(2,1)S(1)}, bf16[48,896]{1,0:T(8,128)(2,1)S(1)}, u32[]{:S(2)}, u32[]{:S(2)}) collective-permute-start(bf16[48,896]{1,0:T(8,128)(2,1)S(1)} %convolution_convert_fusion.7), channel_id=1, source_target_pairs={{0,8},{4,12},{8,0},{12,4},{1,9},{5,13},{9,1},{13,5},{2,10},{6,14},... | collective-permute-start | bytes 258056 | tf_op jit(solution)/shard_map/ppermute | solution.py:231
  97.7 2.5 %collective-permute-start.19 = (bf16[48,896]{1,0:T(8,128)(2,1)S(1)}, bf16[48,896]{1,0:T(8,128)(2,1)S(1)}, u32[]{:S(2)}, u32[]{:S(2)}) collective-permute-start(bf16[48,896]{1,0:T(8,128)(2,1)S(1)} %convolution_convert_fusion.6), channel_id=1, source_target_pairs={{0,12},{4,8},{8,4},{12,0},{1,13},{5,9},{9,5},{13,1},{2,14},{6,10},... | collective-permute-start | bytes 258056 | tf_op jit(solution)/shard_map/ppermute | solution.py:231
  100.2 0.2 convolution_convert_fusion.9.refs_0_
  100.4 0.2 collective-permute-done.17.refs_1_
  100.6 4.7 %collective-permute-done.18.refs_2_ = bf16[48,896]{1,0:T(8,128)(2,1)S(1)} collective-permute-done((bf16[48,896]{1,0:T(8,128)(2,1)S(1)}, bf16[48,896]{1,0:T(8,128)(2,1)S(1)}, u32[]{:S(2)}, u32[]{:S(2)}) %collective-permute-start.18) | collective-permute-done | bytes 86048 | tf_op jit(solution)/shard_map/ppermute | solution.py:231
  105.3 0.9 shard_map.98
  106.2 1.6 %collective-permute-start.21 = (bf16[48,3584]{1,0:T(8,128)(2,1)S(1)}, bf16[48,3584]{1,0:T(8,128)(2,1)S(1)}, u32[]{:S(2)}, u32[]{:S(2)}) collective-permute-start(bf16[48,3584]{1,0:T(8,128)(2,1)S(1)} %shard_map.98), channel_id=1, source_target_pairs={{0,2},{2,0},{1,3},{3,1},{4,6},{6,4},{5,7},{7,5},{8,10},{10,8},{9,1... | collective-permute-start | bytes 1032200 | tf_op jit(solution)/shard_map/ppermute | solution.py:231
  107.8 0.1 broadcast_in_dim.10
  107.9 6.2 %collective-permute-done.21 = bf16[48,3584]{1,0:T(8,128)(2,1)S(1)} collective-permute-done((bf16[48,3584]{1,0:T(8,128)(2,1)S(1)}, bf16[48,3584]{1,0:T(8,128)(2,1)S(1)}, u32[]{:S(2)}, u32[]{:S(2)}) %collective-permute-start.21) | collective-permute-done | bytes 344096 | tf_op jit(solution)/shard_map/ppermute | solution.py:231
  114.3 1.6 %collective-permute-done.22 = bf16[48,3584]{1,0:T(8,128)(2,1)S(1)} collective-permute-done((bf16[48,3584]{1,0:T(8,128)(2,1)S(1)}, bf16[48,3584]{1,0:T(8,128)(2,1)S(1)}, u32[]{:S(2)}, u32[]{:S(2)}) %collective-permute-start.22) | collective-permute-done | bytes 344096 | tf_op jit(solution)/shard_map/ppermute | solution.py:231
  115.9 0.0 copy-start.5
  115.9 1.1 copy-done.5
  (55 shorter events, 0.3 us)
Async XLA Ops:
  0.6 39.1 %copy-start = (bf16[896,1024]{1,0:T(8,128)(2,1)S(1)}, bf16[896,1024]{1,0:T(8,128)(2,1)}, u32[]{:S(2)}) copy-start(bf16[896,1024]{1,0:T(8,128)(2,1)} %param.15) | copy-start | bytes 5505028
  0.6 20.5 %copy-start.18 = (bf16[128,256]{1,0:T(8,128)(2,1)S(1)}, bf16[128,256]{1,0:T(8,128)(2,1)}, u32[]{:S(2)}) copy-start(bf16[128,256]{1,0:T(8,128)(2,1)} %param.10) | copy-start | bytes 196612
  2.4 1.3 %copy-start.1 = (bf16[192,3584]{1,0:T(8,128)(2,1)S(1)}, bf16[192,3584]{1,0:T(8,128)(2,1)}, u32[]{:S(2)}) copy-start(bf16[192,3584]{1,0:T(8,128)(2,1)} %hidden_ref.3) | copy-start | bytes 4128772
  3.7 0.7 copy-start.3
  4.4 16.8 %copy-start.19 = (bf16[128,256]{1,0:T(8,128)(2,1)S(1)}, bf16[128,256]{1,0:T(8,128)(2,1)}, u32[]{:S(2)}) copy-start(bf16[128,256]{1,0:T(8,128)(2,1)} %param.9) | copy-start | bytes 196612
  4.4 31.3 %copy-start.4 = (bf16[128,1024]{1,0:T(8,128)(2,1)S(1)}, bf16[128,1024]{1,0:T(8,128)(2,1)}, u32[]{:S(2)}) copy-start(bf16[128,1024]{1,0:T(8,128)(2,1)} %queries_ref.1) | copy-start | bytes 786436
  5.2 5.9 %collective-permute-start = (bf16[48,1024]{1,0:T(8,128)(2,1)S(1)}, bf16[48,1024]{1,0:T(8,128)(2,1)S(1)}, u32[]{:S(2)}, u32[]{:S(2)}) collective-permute-start(bf16[48,1024]{1,0:T(8,128)(2,1)S(1)} %get-tuple-element.14), channel_id=1, source_target_pairs={{0,4},{4,0},{8,12},{12,8},{1,5},{5,1},{9,13},{13,9},{2,6},{6,2},{1... | collective-permute-start | bytes 294920 | tf_op jit(solution)/shard_map/ppermute | solution.py:231
  8.3 10.4 %collective-permute-start.1 = (bf16[48,1024]{1,0:T(8,128)(2,1)S(1)}, bf16[48,1024]{1,0:T(8,128)(2,1)S(1)}, u32[]{:S(2)}, u32[]{:S(2)}) collective-permute-start(bf16[48,1024]{1,0:T(8,128)(2,1)S(1)} %get-tuple-element.15), channel_id=1, source_target_pairs={{0,8},{4,12},{8,0},{12,4},{1,9},{5,13},{9,1},{13,5},{2,10},{6,14},... | collective-permute-start | bytes 294920 | tf_op jit(solution)/shard_map/ppermute | solution.py:231
  10.8 7.8 %collective-permute-start.2 = (bf16[48,1024]{1,0:T(8,128)(2,1)S(1)}, bf16[48,1024]{1,0:T(8,128)(2,1)S(1)}, u32[]{:S(2)}, u32[]{:S(2)}) collective-permute-start(bf16[48,1024]{1,0:T(8,128)(2,1)S(1)} %get-tuple-element.16), channel_id=1, source_target_pairs={{0,12},{4,8},{8,4},{12,0},{1,13},{5,9},{9,5},{13,1},{2,14},{6,10},... | collective-permute-start | bytes 294920 | tf_op jit(solution)/shard_map/ppermute | solution.py:231
  19.6 6.1 %collective-permute-start.3 = (bf16[128,896]{1,0:T(8,128)(2,1)S(1)}, bf16[128,896]{1,0:T(8,128)(2,1)S(1)}, u32[]{:S(2)}, u32[]{:S(2)}) collective-permute-start(bf16[128,896]{1,0:T(8,128)(2,1)S(1)} %get-tuple-element.18), channel_id=1, source_target_pairs={{0,2},{2,0},{1,3},{3,1},{4,6},{6,4},{5,7},{7,5},{8,10},{10,8},{9,1... | collective-permute-start | bytes 688136 | tf_op jit(solution)/shard_map/ppermute | solution.py:231
  21.2 4.5 %collective-permute-start.5 = (bf16[128,896]{1,0:T(8,128)(2,1)S(1)}, bf16[128,896]{1,0:T(8,128)(2,1)S(1)}, u32[]{:S(2)}, u32[]{:S(2)}) collective-permute-start(bf16[128,896]{1,0:T(8,128)(2,1)S(1)} %get-tuple-element.18), channel_id=1, source_target_pairs={{0,1},{1,0},{2,3},{3,2},{4,5},{5,4},{6,7},{7,6},{8,9},{9,8},{10,11... | collective-permute-start | bytes 688136 | tf_op jit(solution)/shard_map/ppermute | solution.py:231
  25.7 12.9 %collective-permute-start.4 = (bf16[128,896]{1,0:T(8,128)(2,1)S(1)}, bf16[128,896]{1,0:T(8,128)(2,1)}, u32[]{:S(2)}, u32[]{:S(2)}) collective-permute-start(bf16[128,896]{1,0:T(8,128)(2,1)S(1)} %collective-permute-done.3), channel_id=1, source_target_pairs={{0,1},{1,0},{2,3},{3,2},{4,5},{5,4},{6,7},{7,6},{8,9},{9,8},{10,11... | collective-permute-start | bytes 688136 | tf_op jit(solution)/shard_map/ppermute | solution.py:231
  25.7 6.5 %collective-permute-start.11 = (bf16[256,128]{1,0:T(8,128)(2,1)S(1)}, bf16[256,128]{1,0:T(8,128)(2,1)S(1)}, u32[]{:S(2)}, u32[]{:S(2)}) collective-permute-start(bf16[256,128]{1,0:T(8,128)(2,1)S(1)} %pad_maximum_fusion.1.refs_0_), channel_id=1, source_target_pairs={{0,12},{4,8},{8,4},{12,0},{1,13},{5,9},{9,5},{13,1},{2,14},{6,10},... | collective-permute-start | bytes 196616 | tf_op jit(solution)/shard_map/ppermute | solution.py:231
  28.3 7.4 %collective-permute-start.10 = (bf16[256,128]{1,0:T(8,128)(2,1)S(1)}, bf16[256,128]{1,0:T(8,128)(2,1)S(1)}, u32[]{:S(2)}, u32[]{:S(2)}) collective-permute-start(bf16[256,128]{1,0:T(8,128)(2,1)S(1)} %pad_maximum_fusion.1.refs_0_), channel_id=1, source_target_pairs={{0,8},{4,12},{8,0},{12,4},{1,9},{5,13},{9,1},{13,5},{2,10},{6,14},... | collective-permute-start | bytes 196616 | tf_op jit(solution)/shard_map/ppermute | solution.py:231
  29.0 6.7 %collective-permute-start.9 = (bf16[256,128]{1,0:T(8,128)(2,1)S(1)}, bf16[256,128]{1,0:T(8,128)(2,1)S(1)}, u32[]{:S(2)}, u32[]{:S(2)}) collective-permute-start(bf16[256,128]{1,0:T(8,128)(2,1)S(1)} %pad_maximum_fusion.1.refs_0_), channel_id=1, source_target_pairs={{0,4},{4,0},{8,12},{12,8},{1,5},{5,1},{9,13},{13,9},{2,6},{6,2},{1... | collective-permute-start | bytes 196616 | tf_op jit(solution)/shard_map/ppermute | solution.py:231
  39.7 1.1 copy-start.6
  39.7 1.1 copy-start.10
  39.7 8.5 %copy-start.8 = (bf16[128,896]{1,0:T(8,128)(2,1)}, bf16[128,896]{1,0:T(8,128)(2,1)S(1)}, u32[]{:S(2)}) copy-start(bf16[128,896]{1,0:T(8,128)(2,1)S(1)} %get-tuple-element.28) | copy-start | bytes 688132
  40.2 8.0 %collective-permute-start.6 = (bf16[128,1024]{1,0:T(8,128)(2,1)S(1)}, bf16[128,1024]{1,0:T(8,128)(2,1)S(1)}, u32[]{:S(2)}, u32[]{:S(2)}) collective-permute-start(bf16[128,1024]{1,0:T(8,128)(2,1)S(1)} %convolution_convert_fusion), channel_id=1, source_target_pairs={{0,4},{4,0},{8,12},{12,8},{1,5},{5,1},{9,13},{13,9},{2,6},{6,2},{1... | collective-permute-start | bytes 786440 | tf_op jit(solution)/shard_map/ppermute | solution.py:231
  48.6 12.6 %collective-permute-start.7 = (bf16[128,1024]{1,0:T(8,128)(2,1)S(1)}, bf16[128,1024]{1,0:T(8,128)(2,1)S(1)}, u32[]{:S(2)}, u32[]{:S(2)}) collective-permute-start(bf16[128,1024]{1,0:T(8,128)(2,1)S(1)} %convolution_convert_fusion.1), channel_id=1, source_target_pairs={{0,4},{4,0},{8,12},{12,8},{1,5},{5,1},{9,13},{13,9},{2,6},{6,2},{1... | collective-permute-start | bytes 786440 | tf_op jit(solution)/shard_map/ppermute | solution.py:231
  49.0 13.6 %collective-permute-start.8 = (bf16[128,1024]{1,0:T(8,128)(2,1)S(1)}, bf16[128,1024]{1,0:T(8,128)(2,1)S(1)}, u32[]{:S(2)}, u32[]{:S(2)}) collective-permute-start(bf16[128,1024]{1,0:T(8,128)(2,1)S(1)} %fusion), channel_id=1, source_target_pairs={{0,8},{4,12},{8,0},{12,4},{1,9},{5,13},{9,1},{13,5},{2,10},{6,14},... | collective-permute-start | bytes 786440 | tf_op jit(solution)/shard_map/ppermute | solution.py:231
  62.8 14.0 %collective-permute-start.14 = (bf16[128,1024]{1,0:T(8,128)(2,1)S(1)}, bf16[128,1024]{1,0:T(8,128)(2,1)S(1)}, u32[]{:S(2)}, u32[]{:S(2)}) collective-permute-start(bf16[128,1024]{1,0:T(8,128)(2,1)S(1)} %subtract_convert_fusion), channel_id=1, source_target_pairs={{0,4},{4,0},{8,12},{12,8},{1,5},{5,1},{9,13},{13,9},{2,6},{6,2},{1... | collective-permute-start | bytes 786440 | tf_op jit(solution)/shard_map/ppermute | solution.py:231
  63.3 12.8 %collective-permute-start.12 = (bf16[128,1024]{1,0:T(8,128)(2,1)S(1)}, bf16[128,1024]{1,0:T(8,128)(2,1)S(1)}, u32[]{:S(2)}, u32[]{:S(2)}) collective-permute-start(bf16[128,1024]{1,0:T(8,128)(2,1)S(1)} %subtract_convert_fusion), channel_id=1, source_target_pairs={{0,8},{4,12},{8,0},{12,4},{1,9},{5,13},{9,1},{13,5},{2,10},{6,14},... | collective-permute-start | bytes 786440 | tf_op jit(solution)/shard_map/ppermute | solution.py:231
  76.1 1.5 %copy-start.14 = (bf16[128,1024]{1,0:T(8,128)(2,1)}, bf16[128,1024]{1,0:T(8,128)(2,1)S(1)}, u32[]{:S(2)}) copy-start(bf16[128,1024]{1,0:T(8,128)(2,1)S(1)} %collective-permute-done.12) | copy-start | bytes 786436
  76.1 6.4 %collective-permute-start.13 = (bf16[128,1024]{1,0:T(8,128)(2,1)S(1)}, bf16[128,1024]{1,0:T(8,128)(2,1)S(1)}, u32[]{:S(2)}, u32[]{:S(2)}) collective-permute-start(bf16[128,1024]{1,0:T(8,128)(2,1)S(1)} %collective-permute-done.12), channel_id=1, source_target_pairs={{0,4},{4,0},{8,12},{12,8},{1,5},{5,1},{9,13},{13,9},{2,6},{6,2},{1... | collective-permute-start | bytes 786440 | tf_op jit(solution)/shard_map/ppermute | solution.py:231
  76.8 6.4 %copy-start.12 = (bf16[128,1024]{1,0:T(8,128)(2,1)}, bf16[128,1024]{1,0:T(8,128)(2,1)S(1)}, u32[]{:S(2)}) copy-start(bf16[128,1024]{1,0:T(8,128)(2,1)S(1)} %collective-permute-done.14) | copy-start | bytes 786436
  82.4 0.8 copy-start.16
  84.1 2.2 %collective-permute-start.15 = (bf16[2,128,896]{2,1,0:T(8,128)(2,1)}, bf16[2,128,896]{2,1,0:T(8,128)(2,1)}, u32[]{:S(2)}, u32[]{:S(2)}) collective-permute-start(bf16[2,128,896]{2,1,0:T(8,128)(2,1)} %pad_maximum_fusion), channel_id=1, source_target_pairs={{0,1},{1,0},{2,3},{3,2},{4,5},{5,4},{6,7},{7,6},{8,9},{9,8},{10,11... | collective-permute-start | bytes 1376264 | tf_op jit(solution)/shard_map/ppermute | solution.py:231
  84.1 5.0 %copy-start.7 = (bf16[128,896]{1,0:T(8,128)(2,1)S(1)}, bf16[128,896]{1,0:T(8,128)(2,1)}, u32[]{:S(2)}) copy-start(bf16[128,896]{1,0:T(8,128)(2,1)} %copy-done.6) | copy-start | bytes 688132
  84.1 5.0 %copy-start.9 = (bf16[128,896]{1,0:T(8,128)(2,1)S(1)}, bf16[128,896]{1,0:T(8,128)(2,1)}, u32[]{:S(2)}) copy-start(bf16[128,896]{1,0:T(8,128)(2,1)} %copy-done.8) | copy-start | bytes 688132
  84.1 5.0 %copy-start.11 = (bf16[128,896]{1,0:T(8,128)(2,1)S(1)}, bf16[128,896]{1,0:T(8,128)(2,1)}, u32[]{:S(2)}) copy-start(bf16[128,896]{1,0:T(8,128)(2,1)} %copy-done.10) | copy-start | bytes 688132
  84.1 5.0 %copy-start.13 = (bf16[128,1024]{1,0:T(8,128)(2,1)S(1)}, bf16[128,1024]{1,0:T(8,128)(2,1)}, u32[]{:S(2)}) copy-start(bf16[128,1024]{1,0:T(8,128)(2,1)} %copy-done.12) | copy-start | bytes 786436
  84.1 5.0 %copy-start.15 = (bf16[128,1024]{1,0:T(8,128)(2,1)S(1)}, bf16[128,1024]{1,0:T(8,128)(2,1)}, u32[]{:S(2)}) copy-start(bf16[128,1024]{1,0:T(8,128)(2,1)} %copy-done.14) | copy-start | bytes 786436
  84.1 5.0 %copy-start.17 = (bf16[128,1024]{1,0:T(8,128)(2,1)S(1)}, bf16[128,1024]{1,0:T(8,128)(2,1)}, u32[]{:S(2)}) copy-start(bf16[128,1024]{1,0:T(8,128)(2,1)} %copy-done.16) | copy-start | bytes 786436
  87.5 7.7 %collective-permute-start.16 = (bf16[128,896]{1,0:T(8,128)(2,1)S(1)}, bf16[128,896]{1,0:T(8,128)(2,1)S(1)}, u32[]{:S(2)}, u32[]{:S(2)}) collective-permute-start(bf16[128,896]{1,0:T(8,128)(2,1)S(1)} %get-tuple-element.22), channel_id=1, source_target_pairs={{0,2},{2,0},{1,3},{3,1},{4,6},{6,4},{5,7},{7,5},{8,10},{10,8},{9,1... | collective-permute-start | bytes 688136 | tf_op jit(solution)/shard_map/ppermute | solution.py:231
  92.1 13.2 %copy-start.2 = (bf16[192,3584]{1,0:T(8,128)(2,1)S(1)}, bf16[192,3584]{1,0:T(8,128)(2,1)}, u32[]{:S(2)}) copy-start(bf16[192,3584]{1,0:T(8,128)(2,1)} %hidden_ref.3) | copy-start | bytes 4128772
  95.8 4.8 %collective-permute-start.17 = (bf16[48,896]{1,0:T(8,128)(2,1)S(1)}, bf16[48,896]{1,0:T(8,128)(2,1)S(1)}, u32[]{:S(2)}, u32[]{:S(2)}) collective-permute-start(bf16[48,896]{1,0:T(8,128)(2,1)S(1)} %convolution_convert_fusion.8), channel_id=1, source_target_pairs={{0,4},{4,0},{8,12},{12,8},{1,5},{5,1},{9,13},{13,9},{2,6},{6,2},{1... | collective-permute-start | bytes 258056 | tf_op jit(solution)/shard_map/ppermute | solution.py:231
  95.9 9.4 %collective-permute-start.18 = (bf16[48,896]{1,0:T(8,128)(2,1)S(1)}, bf16[48,896]{1,0:T(8,128)(2,1)S(1)}, u32[]{:S(2)}, u32[]{:S(2)}) collective-permute-start(bf16[48,896]{1,0:T(8,128)(2,1)S(1)} %convolution_convert_fusion.7), channel_id=1, source_target_pairs={{0,8},{4,12},{8,0},{12,4},{1,9},{5,13},{9,1},{13,5},{2,10},{6,14},... | collective-permute-start | bytes 258056 | tf_op jit(solution)/shard_map/ppermute | solution.py:231
  97.7 7.6 %collective-permute-start.19 = (bf16[48,896]{1,0:T(8,128)(2,1)S(1)}, bf16[48,896]{1,0:T(8,128)(2,1)S(1)}, u32[]{:S(2)}, u32[]{:S(2)}) collective-permute-start(bf16[48,896]{1,0:T(8,128)(2,1)S(1)} %convolution_convert_fusion.6), channel_id=1, source_target_pairs={{0,12},{4,8},{8,4},{12,0},{1,13},{5,9},{9,5},{13,1},{2,14},{6,10},... | collective-permute-start | bytes 258056 | tf_op jit(solution)/shard_map/ppermute | solution.py:231
  106.2 8.0 %collective-permute-start.21 = (bf16[48,3584]{1,0:T(8,128)(2,1)S(1)}, bf16[48,3584]{1,0:T(8,128)(2,1)S(1)}, u32[]{:S(2)}, u32[]{:S(2)}) collective-permute-start(bf16[48,3584]{1,0:T(8,128)(2,1)S(1)} %shard_map.98), channel_id=1, source_target_pairs={{0,2},{2,0},{1,3},{3,1},{4,6},{6,4},{5,7},{7,5},{8,10},{10,8},{9,1... | collective-permute-start | bytes 1032200 | tf_op jit(solution)/shard_map/ppermute | solution.py:231
  107.8 6.4 %collective-permute-start.20 = (bf16[48,3584]{1,0:T(8,128)(2,1)S(1)}, bf16[48,3584]{1,0:T(8,128)(2,1)S(1)}, u32[]{:S(2)}, u32[]{:S(2)}) collective-permute-start(bf16[48,3584]{1,0:T(8,128)(2,1)S(1)} %shard_map.98), channel_id=1, source_target_pairs={{0,1},{1,0},{2,3},{3,2},{4,5},{5,4},{6,7},{7,6},{8,9},{9,8},{10,11... | collective-permute-start | bytes 1032200 | tf_op jit(solution)/shard_map/ppermute | solution.py:231
  114.2 1.7 %collective-permute-start.22 = (bf16[48,3584]{1,0:T(8,128)(2,1)S(1)}, bf16[48,3584]{1,0:T(8,128)(2,1)S(1)}, u32[]{:S(2)}, u32[]{:S(2)}) collective-permute-start(bf16[48,3584]{1,0:T(8,128)(2,1)S(1)} %collective-permute-done.21), channel_id=1, source_target_pairs={{0,1},{1,0},{2,3},{3,2},{4,5},{5,4},{6,7},{7,6},{8,9},{9,8},{10,11... | collective-permute-start | bytes 1032200 | tf_op jit(solution)/shard_map/ppermute | solution.py:231
  115.9 1.1 copy-start.5

commit v3 on v2

v3 whole, which is shorter than its diff:
```python
import functools
import math

import jax
import jax.numpy as jnp
from jax import lax
from jax.experimental import pallas as pl
from jax.experimental.pallas import tpu as pltpu
from jax.sharding import PartitionSpec as P

HD = 128
LANES = 128
BF = jnp.bfloat16
F32 = jnp.float32
I32 = jnp.int32
PARAMS = pltpu.CompilerParams(vmem_limit_bytes=16 * 1024 * 1024)
PAIRWISE = True


def dot(a, b, dims=((1,), (0,))):
    return lax.dot_general(a, b, (dims, ((), ())), preferred_element_type=F32)


def eye(size):
    return lax.broadcasted_iota(I32, (size, size), 0) == lax.broadcasted_iota(I32, (size, size), 1)


def to_row(column):
    return jnp.sum(jnp.where(eye(column.shape[0]), column, 0.0), axis=0, keepdims=True)


def to_column(row):
    return jnp.sum(jnp.where(eye(row.shape[1]), row, 0.0), axis=1, keepdims=True)


def indices():
    return lax.axis_index("seq"), lax.axis_index("mp") * 2 + lax.axis_index("side")


def call(kernel, shapes, args, flops, moved, transcendentals=0, **more):
    vmem = pl.BlockSpec(memory_space=pltpu.VMEM)
    options = dict(
        in_specs=[vmem] * len(args),
        out_specs=jax.tree.map(lambda s: vmem, shapes),
        compiler_params=PARAMS,
    )
    options.update(more)
    return pl.pallas_call(
        kernel,
        out_shape=shapes,
        cost_estimate=pl.CostEstimate(
            flops=flops, bytes_accessed=moved, transcendentals=transcendentals
        ),
        **options,
    )(*args)


def norm_kernel(student_ref, gain_ref, owner_ref, docs_ref, *refs):
    *pieces, inverse_ref, hidden_ref, arrived = refs
    me, mine = indices()
    copy = pltpu.make_async_copy(student_ref.at[mine], hidden_ref, arrived)
    copy.start()
    rows, width = hidden_ref.shape
    tiles = width // len(pieces) // LANES
    line = lax.broadcasted_iota(I32, (rows, LANES), 0)
    owner_row, docs_row = owner_ref[...].astype(F32), docs_ref[...].astype(F32)
    extra = jnp.where(line == 0, owner_row, jnp.where(line == 1, docs_row, 0.0)).astype(BF)
    for piece in pieces:
        piece[:, tiles * LANES :] = extra
    copy.wait()
    hidden = hidden_ref[...].astype(F32)
    inverse = lax.rsqrt(jnp.sum(hidden * hidden, axis=1, keepdims=True) / width + 1e-06)
    inverse_ref[...] = inverse
    for k, piece in enumerate(pieces):
        for tile in range(tiles):
            at = (me ^ k) * tiles + tile
            block = hidden_ref[:, pl.ds(pl.multiple_of(at * LANES, LANES), LANES)].astype(F32)
            normed = block * inverse * gain_ref[pl.ds(at, 1), :]
            piece[:, tile * LANES : (tile + 1) * LANES] = normed.astype(BF)


def norm_pieces(student, gain, owner, doc_ids):
    n, rows, width = student.shape
    piece = jax.ShapeDtypeStruct((rows, width // n + LANES), BF)
    vmem = pl.BlockSpec(memory_space=pltpu.VMEM)
    return call(
        norm_kernel,
        [piece] * n
        + [jax.ShapeDtypeStruct((rows, 1), F32), jax.ShapeDtypeStruct((rows, width), BF)],
        (student, gain, owner, doc_ids),
        6 * rows * width,
        6 * rows * width,
        in_specs=[pl.BlockSpec(memory_space=pl.ANY)] + [vmem] * 3,
        scratch_shapes=[pltpu.SemaphoreType.DMA],
        compiler_params=pltpu.CompilerParams(vmem_limit_bytes=60 * 1024 * 1024),
    )


def pick_kernel(*refs):
    *pieces, out_ref, drop_ref = refs
    me, mine = indices()
    tokens, depth = out_ref.shape
    slots = pieces[0].shape[0]
    spots = slots * len(pieces)
    owner_row = jnp.zeros((1, tokens), F32)
    for k, piece in enumerate(pieces):
        tile = piece[0:16, depth:].astype(F32)[0:1]
        owner_row = owner_row + jnp.where((me ^ mine) == k, tile, 0.0)
    owner = to_column(owner_row)
    earlier = lax.broadcasted_iota(I32, (tokens, tokens), 1) < lax.broadcasted_iota(
        I32, (tokens, tokens), 0
    )
    same = jnp.where(earlier & (owner == owner_row), 1.0, 0.0)
    rank = jnp.sum(same, axis=1, keepdims=True)
    peer = owner.astype(I32) ^ me
    spot = (peer * slots).astype(F32) + rank
    take = (lax.broadcasted_iota(I32, (tokens, spots), 1) == spot.astype(I32)).astype(F32)
    stacked = jnp.concatenate([piece[:, :depth] for piece in pieces], axis=0)
    out_ref[...] = dot(take.astype(BF), stacked).astype(BF)
    spot_row = to_row(spot).astype(I32)
    drop = (lax.broadcasted_iota(I32, (spots, tokens), 0) == spot_row).astype(F32)
    drop_ref[...] = drop.astype(BF)


def pick_rows(pieces, tokens):
    slots, wide = pieces[0].shape
    depth, spots = wide - LANES, slots * len(pieces)
    return call(
        pick_kernel,
        [jax.ShapeDtypeStruct((tokens, depth), BF), jax.ShapeDtypeStruct((spots, tokens), BF)],
        pieces,
        2 * tokens * spots * depth,
        4 * spots * depth,
    )


def attention_kernel(queries_ref, *refs):
    out_ref = refs[-1]
    n = (len(refs) - 1) // 2
    parcels, pieces = refs[:n], refs[n : 2 * n]
    tokens = queries_ref.shape[0]
    depth = pieces[0].shape[1] - LANES
    me, _ = indices()
    keys = jnp.concatenate([parcel[:tokens, :] for parcel in parcels], axis=0)
    values = jnp.concatenate([parcel[tokens:, :] for parcel in parcels], axis=0)
    docs = [piece[0:16, depth:].astype(F32)[1:2] for piece in pieces]
    doc_column = to_column(docs[0])
    query_pos = me * tokens + lax.broadcasted_iota(I32, (tokens, tokens), 0)
    within = lax.broadcasted_iota(I32, (tokens, tokens), 1)
    masks = []
    for k in range(n):
        near = (me ^ k) * tokens + within <= query_pos
        masks.append(jnp.where(near & (docs[k] == doc_column), 1.0, 0.0))
    allowed = jnp.concatenate(masks, axis=1) > 0.5
    scale_factor = 1.0 / math.sqrt(HD)
    for h in range(queries_ref.shape[1] // HD):
        columns = slice(h * HD, (h + 1) * HD)
        scores = dot(queries_ref[:, columns], keys, ((1,), (1,))) * scale_factor
        scores = jnp.where(allowed, scores, -1e30)
        top = jnp.max(scores, axis=1, keepdims=True)
        probs = jnp.where(allowed, jnp.exp(scores - top), 0.0)
        total = jnp.sum(probs, axis=1, keepdims=True)
        out_ref[:, columns] = (dot(probs.astype(BF), values) / total).astype(BF)


def attention_rows(queries, parcels, pieces):
    tokens, width = queries.shape
    n = len(parcels)
    return call(
        attention_kernel,
        jax.ShapeDtypeStruct((tokens, width), BF),
        (queries, *parcels, *pieces),
        0,
        4 * tokens * width,
    )


def route_kernel(first_ref, second_ref, third_ref, delta_ref, proj_ref, sent_ref, kept_ref, held):
    me, mine = indices()
    last = dot(delta_ref[...], proj_ref[...], ((1,), (1,))).astype(BF)
    for k, block in enumerate((first_ref[...], second_ref[...], third_ref[...], last)):
        held[k] = block
    off = me ^ mine
    kept_ref[0] = held[off]
    sent_ref[0] = held[off ^ 1]
    kept_ref[1] = held[off ^ 2]
    sent_ref[1] = held[off ^ 3]


def route_products(products, delta, proj):
    tokens, depth = products[0].shape
    pair = jax.ShapeDtypeStruct((2, tokens, depth), BF)
    return call(
        route_kernel,
        [pair, pair],
        (*products, delta, proj),
        2 * tokens * depth * proj.shape[1],
        2 * proj.size + 14 * tokens * depth,
        scratch_shapes=[pltpu.VMEM((4, tokens, depth), BF)],
    )


def rows_kernel(hidden_ref, gain_ref, inverse_ref, *refs):
    *pieces, out_ref = refs
    me, _ = indices()
    rows, width = hidden_ref.shape
    tiles = width // len(pieces) // LANES
    inverse = inverse_ref[...]
    total = jnp.zeros((rows, LANES), F32)
    for k, piece in enumerate(pieces):
        for tile in range(tiles):
            at = (me ^ k) * tiles + tile
            block = hidden_ref[:, pl.ds(pl.multiple_of(at * LANES, LANES), LANES)].astype(F32)
            grad = piece[:, tile * LANES : (tile + 1) * LANES].astype(F32)
            total = total + grad * gain_ref[pl.ds(at, 1), :] * block
    mean = jnp.sum(total, axis=1, keepdims=True) / width
    lean = inverse * inverse * inverse * mean
    for k, piece in enumerate(pieces):
        for tile in range(tiles):
            at = (me ^ k) * tiles + tile
            columns = pl.ds(pl.multiple_of(at * LANES, LANES), LANES)
            block = hidden_ref[:, columns].astype(F32)
            grad = piece[:, tile * LANES : (tile + 1) * LANES].astype(F32)
            grad = inverse * (grad * gain_ref[pl.ds(at, 1), :]) - lean * block
            out_ref[:, columns] = grad.astype(BF)


def grad_rows(hidden, gain, inverse, pieces):
    rows, width = hidden.shape
    return call(
        rows_kernel,
        jax.ShapeDtypeStruct((rows, width), BF),
        (hidden, gain, inverse, *pieces),
        12 * rows * width,
        6 * rows * width,
    )


def write_kernel(first, *refs):
    *blocks, out_ref, done = refs
    _, mine = indices()
    copies = [
        pltpu.make_async_copy(block, out_ref.at[mine ^ (first + q)], done.at[q])
        for q, block in enumerate(blocks)
    ]
    for copy in copies:
        copy.start()
    for copy in copies:
        copy.wait()


def write_rows(blocks, first, target=None):
    rows, width = blocks[0].shape
    hbm, vmem = pl.BlockSpec(memory_space=pltpu.HBM), pl.BlockSpec(memory_space=pltpu.VMEM)
    kernel = functools.partial(write_kernel, first)
    args, specs, aliases = tuple(blocks), [vmem] * len(blocks), {}
    if target is not None:
        kernel = lambda t, *refs: write_kernel(first, *refs)
        args, specs, aliases = (target, *args), [hbm] + specs, {0: 0}
    return call(
        kernel,
        jax.ShapeDtypeStruct((4, rows, width), BF),
        args,
        0,
        4 * len(blocks) * rows * width,
        in_specs=specs,
        out_specs=hbm,
        input_output_aliases=aliases,
        scratch_shapes=[pltpu.SemaphoreType.DMA((len(blocks),))],
    )


def swap(x, axis, k=1):
    return lax.ppermute(x, axis, [(i, i ^ k) for i in range(lax.axis_size(axis))])


def entry(entries, at):
    a, b, c, d = entries
    odd = at % 2 == 1
    return lax.optimization_barrier(
        jnp.where(at >= 2, jnp.where(odd, d, c), jnp.where(odd, b, a))
    )


def after(x, *others):
    return lax.optimization_barrier((x, *others))[0]


def pairwise(
    teacher_queries, teacher_keys, teacher_values, doc_ids, owner, student_hidden, norm_gain, proj
):
    n = 4
    me, mine = indices()
    side = lax.axis_index("side")
    rows = teacher_queries.shape[0]
    heads = teacher_queries.shape[1] // HD
    kv_local = teacher_keys.shape[1] // HD
    group = heads * 2 // kv_local
    capacity, width = student_hidden.shape
    slots = capacity // n
    off = mine ^ me
    student = student_hidden.reshape(n, slots, width)
    gain = norm_gain.reshape(width // LANES, LANES)

    *made, inverse, hidden = norm_pieces(student, gain, owner.T, doc_ids[None, :])
    pieces = [made[0]] + [swap(made[k], "seq", k) for k in range(1, n)]
    normed_own, drop = pick_rows(pieces, rows)

    mate = swap(normed_own, "side")
    far = swap(normed_own, "mp")
    far_mate = swap(far, "side")

    head = side * heads // group
    parcel = jnp.concatenate(
        [
            lax.dynamic_slice_in_dim(teacher_keys, head * HD, HD, 1),
            lax.dynamic_slice_in_dim(teacher_values, head * HD, HD, 1),
        ]
    )
    parcel = after(parcel, normed_own)
    parcels = [parcel] + [swap(parcel, "seq", k) for k in range(1, n)]
    far_mate = after(far_mate, *parcels)
    normed = [entry([normed_own, mate, far, far_mate], off ^ k) for k in range(n)]

    away = dot(normed[3], proj).astype(BF)
    over_own = lax.optimization_barrier(dot(after(normed[2], away), proj))
    beside = dot(after(normed[1], over_own), proj).astype(BF)
    got_over = after(swap(away, "seq", 1), over_own, beside)
    over = lax.optimization_barrier((over_own + got_over.astype(F32)).astype(BF))
    got_far = swap(over, "seq", 2)
    own = lax.optimization_barrier(dot(after(normed[0], over), proj))
    got_beside = swap(after(beside, own), "seq", 1)
    teacher_rows = attention_rows(after(teacher_queries, own), parcels, pieces)
    predicted = own + got_beside.astype(F32) + got_far.astype(F32)
    delta = (predicted - teacher_rows.astype(F32)).astype(BF)

    def product(block):
        return lax.optimization_barrier(dot(block, proj, ((1,), (1,))).astype(BF))

    delta_far = swap(delta, "seq", 2)
    own_product = product(delta)
    delta_beside = swap(after(delta, own_product), "seq", 1)
    delta_last = swap(delta_far, "seq", 1)
    deltas = [delta, delta_beside, delta_far, delta_last]
    products = [own_product, product(delta_beside), product(delta_far)]

    sent, kept = route_products(products, delta_last, proj)
    got = swap(sent, "side")
    cross = lax.optimization_barrier((kept[1].astype(F32) + got[1].astype(F32)).astype(BF))
    crossed = swap(cross, "mp")
    near = lax.optimization_barrier(kept[0].astype(F32) + after(got[0], cross).astype(F32))
    feature_rows = (near + crossed.astype(F32)).astype(BF)
    leaving = [dot(drop[k * slots : (k + 1) * slots], feature_rows).astype(BF) for k in range(n)]
    arrived = [leaving[0]] + [swap(leaving[k], "seq", k) for k in range(1, n)]
    grad_own = grad_rows(hidden, gain, inverse, arrived)

    grad_mate = swap(grad_own, "side")
    grad_far = swap(grad_own, "mp")
    grad_last = swap(grad_far, "side")
    grad_hidden = write_rows([grad_own, grad_mate, grad_far], 0)
    grad_hidden = write_rows([grad_last], 3, grad_hidden).reshape(capacity, width)

    factor = 1.0 / math.sqrt(rows * n)
    grad_proj = dot(jnp.concatenate(normed), jnp.concatenate(deltas), ((0,), (0,))) * factor
    return (grad_hidden, grad_proj)


def general(
    teacher_queries, teacher_keys, teacher_values, doc_ids, owner, student_hidden, norm_gain, proj
):
    n = lax.axis_size("seq")
    me = lax.axis_index("seq")
    side = lax.axis_index("side")
    plane = lax.axis_size("mp") * lax.axis_size("side")
    mine = lax.axis_index("mp") * lax.axis_size("side") + side
    rows = teacher_queries.shape[0]
    heads = teacher_queries.shape[1] // HD
    kv_local = teacher_keys.shape[1] // HD
    group = heads * lax.axis_size("side") // kv_local
    width = student_hidden.shape[1]
    depth = proj.shape[0]
    capacity = student_hidden.shape[0]
    slots = capacity // n
    shared = n // plane
    held = shared * slots

    hidden = lax.dynamic_slice_in_dim(student_hidden, mine * held, held, 0).astype(F32)
    inverse_rms = lax.rsqrt(jnp.mean(hidden * hidden, axis=1, keepdims=True) + 1e-06)
    normed = (hidden * inverse_rms * norm_gain).astype(BF)
    normed_slots = lax.all_to_all(
        normed.reshape(held, n, depth).transpose(1, 0, 2), "seq", 0, 0, tiled=True
    )

    head = side * heads // group
    key_head = lax.dynamic_slice_in_dim(teacher_keys, head * HD, HD, 1)
    value_head = lax.dynamic_slice_in_dim(teacher_values, head * HD, HD, 1)
    small = jnp.stack([doc_ids, owner[:, 0]]).astype(BF)
    parcel = jnp.concatenate([key_head, value_head, jnp.pad(small, ((0, 14), (0, 0)))])
    parcel = lax.all_gather(parcel, "seq", axis=0, tiled=False)
    keys, values = parcel[:, :rows], parcel[:, rows : 2 * rows]
    docs = parcel[:, 2 * rows].astype(I32)
    owners = parcel[:, 2 * rows + 1].astype(I32)

    query_pos = me * rows + jnp.arange(rows, dtype=I32)
    key_pos = jnp.arange(n * rows, dtype=I32)
    allowed = (docs.reshape(-1)[None, :] == doc_ids[:, None]) & (
        key_pos[None, :] <= query_pos[:, None]
    )
    stacked = teacher_queries.reshape(rows, heads, HD).transpose(1, 0, 2)
    scores = jnp.einsum("hqd,kd->hqk", stacked, keys.reshape(-1, HD), preferred_element_type=F32)
    scores = jnp.where(allowed[None], scores * (1.0 / math.sqrt(HD)), -1e30)
    top = jnp.max(scores, axis=2, keepdims=True)
    probs = jnp.where(allowed[None], jnp.exp(scores - top), 0.0)
    totals = jnp.sum(probs, axis=2, keepdims=True)
    weighted = jnp.einsum(
        "hqk,kd->hqd", probs.astype(BF), values.reshape(-1, HD), preferred_element_type=F32
    )
    teacher_rows = (weighted / totals).astype(BF).transpose(1, 0, 2).reshape(rows, heads * HD)

    own_blocks = lax.dynamic_slice_in_dim(owners, mine * shared, shared, 0)
    order = jnp.arange(rows, dtype=I32)
    same = (own_blocks[:, :, None] == own_blocks[:, None, :]) & (order[:, None] > order[None, :])
    rank = jnp.sum(same.astype(I32), axis=2)
    spot = own_blocks * held + jnp.arange(shared, dtype=I32)[:, None] * slots + rank
    pick = (spot.reshape(-1)[:, None] == jnp.arange(n * held, dtype=I32)[None, :]).astype(BF)

    normed_own = dot(pick, normed_slots.reshape(n * held, depth)).astype(BF)
    normed_rows = lax.all_gather(normed_own, ("mp", "side"), axis=0, tiled=True)
    partial = dot(normed_rows, proj).astype(BF)
    predicted = lax.psum_scatter(partial, "seq", scatter_dimension=0, tiled=True).astype(F32)
    delta = (predicted - teacher_rows.astype(F32)).astype(BF)
    deltas = lax.all_gather(delta, "seq", axis=0, tiled=True)

    products = dot(deltas, proj, ((1,), (1,))).astype(BF)
    feature_rows = lax.psum_scatter(products, ("mp", "side"), scatter_dimension=0, tiled=True)
    feature_slots = dot(pick, feature_rows, ((0,), (0,))).astype(BF).reshape(n, held, depth)
    received = lax.all_to_all(feature_slots, "seq", 0, 0, tiled=True)
    feature_grad = received.transpose(1, 0, 2).reshape(held, width)

    gain_grad = feature_grad.astype(F32) * norm_gain
    mean_term = jnp.mean(gain_grad * hidden, axis=1, keepdims=True)
    grad_own = (inverse_rms * gain_grad - inverse_rms**3 * hidden * mean_term).astype(BF)
    grad_hidden = lax.all_gather(grad_own, ("mp", "side"), axis=0, tiled=True)

    grad_proj = dot(normed_rows, deltas, ((0,), (0,))) * (1.0 / math.sqrt(rows * n))
    return (grad_hidden, grad_proj)


def solution(mesh):
    sizes = mesh.shape
    paired = PAIRWISE and (sizes["seq"], sizes["mp"], sizes["side"]) == (4, 2, 2)
    return jax.shard_map(
        pairwise if paired else general,
        mesh=mesh,
        in_specs=(
            P(("groups", "seq"), ("mp", "side")),
            P(("groups", "seq"), "mp"),
            P(("groups", "seq"), "mp"),
            P(("groups", "seq")),
            P(("groups", "seq"), None),
            P(("groups", "seq"), None),
            P(),
            P("seq", ("mp", "side")),
        ),
        out_specs=(P(("groups", "seq"), None), P(("groups", "seq"), ("mp", "side"))),
        check_vma=False,
    )
```

time: 117 us -> 116 us (level)
  local copies, waits for them, and re-layouts: 5 us -> 1.73 us
  other arithmetic: 3.51 us -> 0.51 us
  Pallas kernels: 5.47 us -> 8.43 us
  starting transfers between devices: 25.6 us -> 27.2 us
    unnamed x41 -> x14, local copies, waits for them, and re-layouts: 3.91 us -> 0.93 us
    pallas_call x4 -> x7, Pallas kernels: 5.47 us -> 8.43 us  [call(): pl.pallas_call(kernel, out_shape=shapes, cost_estimate=pl.CostEstimate(fl...]
    ppermute x23, starting transfers between devices: 25.6 us -> 27.2 us  [swap(): lax.ppermute(x, axis, [(i, i ^ k) for i in range(lax.axis_size(axis))])]
    dot_general x13 -> x12, matrix products: 8.32 us -> 7.58 us  [dot(): return lax.dot_general(a, b, (dims, ((), ())), preferred_element_type=F32)]
  transfers between devices with their start and end apart: 23 -> 23, of which waited for: 16 -> 16; matrix products, arithmetic and copies ran while one was open for 5% -> 5% of each run, Pallas kernels for 2% -> 3%
where the time goes in v3:
time: 116 us; the launch traced here: 115 us
  waiting for transfers between devices  69.1 us (60%)
  starting transfers between devices  27.2 us (23%)
  Pallas kernels  8.43 us (7%)
  matrix products  7.58 us (7%)
  local copies, waits for them, and re-layouts  1.73 us (1%)
    ppermute x23, waiting for transfers between devices, swap(): lax.ppermute(x, axis, [(i, i ^ k) for i in range(lax.axis_size(axis))])  69.1 us
    ppermute x23, starting transfers between devices, swap(): lax.ppermute(x, axis, [(i, i ^ k) for i in range(lax.axis_size(axis))])  27.2 us
    pallas_call x7, Pallas kernels, call(): pl.pallas_call(kernel, out_shape=shapes, cost_estimate=pl.CostEstimate(fl...  8.43 us
    dot_general x12, matrix products, dot(): return lax.dot_general(a, b, (dims, ((), ())), preferred_element_type=F32)  7.58 us
  transfers between devices with their start and end apart: 23, of which 16 were waited for; matrix products, arithmetic and copies ran while one was open for 5% of the time, Pallas kernels for 3%

profile of v3, /device:TPU:0, one launch (start us, length us, event | category | flops | bytes accessed | tf_op | source)
XLA Modules:
  0.0 115.5 jit_solution(12934581009610577266)
XLA Ops:
  0.6 2.8 %shard_map.95 = (bf16[48,1024]{1,0:T(8,128)(2,1)}, bf16[48,1024]{1,0:T(8,128)(2,1)}, bf16[48,1024]{1,0:T(8,128)(2,1)}, bf16[48,1024]{1,0:T(8,128)(2,1)}, f32[48,1]{1,0:T(8,128)}, /*index=5*/bf16[48,3584]{1,0:T(8,128)(2,1)}) custom-call(bf16[4,48,3584]{2,1,0:T(8,128)(2,1)} %bitcast.33, f32[28,128]{1,0:T(8,128)} %bitcast.30, s32[1,128]{1,0:T(1,128)} %bitcast.34, ...), custom_call_target="tpu_custom_call" | custom-call | flops 1032192 | bytes 1032192 | tf_op jit(solution)/shard_map/pallas_call | solution.py:48
  3.5 3.1 %collective-permute-start = (bf16[48,1024]{1,0:T(8,128)(2,1)}, bf16[48,1024]{1,0:T(8,128)(2,1)S(1)}, u32[]{:S(2)}, u32[]{:S(2)}) collective-permute-start(bf16[48,1024]{1,0:T(8,128)(2,1)} %get-tuple-element.25), channel_id=1, source_target_pairs={{0,4},{4,0},{8,12},{12,8},{1,5},{5,1},{9,13},{13,9},{2,6},{6,2},{1... | collective-permute-start | bytes 294920 | tf_op jit(solution)/shard_map/ppermute | solution.py:274
  6.5 2.6 %collective-permute-start.1 = (bf16[48,1024]{1,0:T(8,128)(2,1)}, bf16[48,1024]{1,0:T(8,128)(2,1)S(1)}, u32[]{:S(2)}, u32[]{:S(2)}) collective-permute-start(bf16[48,1024]{1,0:T(8,128)(2,1)} %get-tuple-element.26), channel_id=1, source_target_pairs={{0,8},{4,12},{8,0},{12,4},{1,9},{5,13},{9,1},{13,5},{2,10},{6,14},... | collective-permute-start | bytes 294920 | tf_op jit(solution)/shard_map/ppermute | solution.py:274
  9.1 0.0 collective-permute-start.2
  9.1 0.4 collective-permute-done.refs_1_.refs_5_
  9.5 7.6 %collective-permute-done.1.refs_2_.refs_6_ = bf16[48,1024]{1,0:T(8,128)(2,1)S(1)} collective-permute-done((bf16[48,1024]{1,0:T(8,128)(2,1)}, bf16[48,1024]{1,0:T(8,128)(2,1)S(1)}, u32[]{:S(2)}, u32[]{:S(2)}) %collective-permute-start.1) | collective-permute-done | bytes 98336 | tf_op jit(solution)/shard_map/ppermute | solution.py:274
  17.2 0.9 copy-done.1
  18.1 0.4 shard_map.96
  18.5 1.6 %collective-permute-start.3 = (bf16[128,896]{1,0:T(8,128)(2,1)S(1)}, bf16[128,896]{1,0:T(8,128)(2,1)S(1)}, u32[]{:S(2)}, u32[]{:S(2)}) collective-permute-start(bf16[128,896]{1,0:T(8,128)(2,1)S(1)} %get-tuple-element.29), channel_id=1, source_target_pairs={{0,2},{2,0},{1,3},{3,1},{4,6},{6,4},{5,7},{7,5},{8,10},{10,8},{9,1... | collective-permute-start | bytes 688136 | tf_op jit(solution)/shard_map/ppermute | solution.py:274
  20.0 4.5 %collective-permute-done.3 = bf16[128,896]{1,0:T(8,128)(2,1)S(1)} collective-permute-done((bf16[128,896]{1,0:T(8,128)(2,1)S(1)}, bf16[128,896]{1,0:T(8,128)(2,1)S(1)}, u32[]{:S(2)}, u32[]{:S(2)}) %collective-permute-start.3) | collective-permute-done | bytes 229408 | tf_op jit(solution)/shard_map/ppermute | solution.py:274
  24.5 0.8 constant_dynamic-slice_fusion
  25.3 1.8 %collective-permute-start.5 = (bf16[256,128]{1,0:T(8,128)(2,1)S(1)}, bf16[256,128]{1,0:T(8,128)(2,1)S(1)}, u32[]{:S(2)}, u32[]{:S(2)}) collective-permute-start(bf16[256,128]{1,0:T(8,128)(2,1)S(1)} %pad_maximum_fusion.refs_0_), channel_id=1, source_target_pairs={{0,4},{4,0},{8,12},{12,8},{1,5},{5,1},{9,13},{13,9},{2,6},{6,2},{1... | collective-permute-start | bytes 196616 | tf_op jit(solution)/shard_map/ppermute | solution.py:274
  27.2 1.3 %collective-permute-start.6 = (bf16[256,128]{1,0:T(8,128)(2,1)S(1)}, bf16[256,128]{1,0:T(8,128)(2,1)S(1)}, u32[]{:S(2)}, u32[]{:S(2)}) collective-permute-start(bf16[256,128]{1,0:T(8,128)(2,1)S(1)} %pad_maximum_fusion.refs_0_), channel_id=1, source_target_pairs={{0,8},{4,12},{8,0},{12,4},{1,9},{5,13},{9,1},{13,5},{2,10},{6,14},... | collective-permute-start | bytes 196616 | tf_op jit(solution)/shard_map/ppermute | solution.py:274
  28.4 1.3 %collective-permute-start.7 = (bf16[256,128]{1,0:T(8,128)(2,1)S(1)}, bf16[256,128]{1,0:T(8,128)(2,1)S(1)}, u32[]{:S(2)}, u32[]{:S(2)}) collective-permute-start(bf16[256,128]{1,0:T(8,128)(2,1)S(1)} %pad_maximum_fusion.refs_0_), channel_id=1, source_target_pairs={{0,12},{4,8},{8,4},{12,0},{1,13},{5,9},{9,5},{13,1},{2,14},{6,10},... | collective-permute-start | bytes 196616 | tf_op jit(solution)/shard_map/ppermute | solution.py:274
  29.8 0.1 collective-permute-done.5.refs_1_
  29.9 5.6 %collective-permute-done.6.refs_2_ = bf16[256,128]{1,0:T(8,128)(2,1)S(1)} collective-permute-done((bf16[256,128]{1,0:T(8,128)(2,1)S(1)}, bf16[256,128]{1,0:T(8,128)(2,1)S(1)}, u32[]{:S(2)}, u32[]{:S(2)}) %collective-permute-start.6) | collective-permute-done | bytes 65568 | tf_op jit(solution)/shard_map/ppermute | solution.py:274
  35.5 0.2 select_select_fusion
  35.7 0.5 convolution_convert_fusion.1
  36.2 1.6 %collective-permute-start.9 = (bf16[128,1024]{1,0:T(8,128)(2,1)S(1)}, bf16[128,1024]{1,0:T(8,128)(2,1)S(1)}, u32[]{:S(2)}, u32[]{:S(2)}) collective-permute-start(bf16[128,1024]{1,0:T(8,128)(2,1)S(1)} %convolution_convert_fusion.1), channel_id=1, source_target_pairs={{0,4},{4,0},{8,12},{12,8},{1,5},{5,1},{9,13},{13,9},{2,6},{6,2},{1... | collective-permute-start | bytes 786440 | tf_op jit(solution)/shard_map/ppermute | solution.py:274
  37.8 0.4 fusion.20
  38.3 0.5 convolution_convert_fusion
  38.7 0.0 copy-start.2
  38.7 0.0 copy-start.4
  38.8 5.3 %collective-permute-done.9 = bf16[128,1024]{1,0:T(8,128)(2,1)S(1)} collective-permute-done((bf16[128,1024]{1,0:T(8,128)(2,1)S(1)}, bf16[128,1024]{1,0:T(8,128)(2,1)S(1)}, u32[]{:S(2)}, u32[]{:S(2)}) %collective-permute-start.9) | collective-permute-done | bytes 262176 | tf_op jit(solution)/shard_map/ppermute | solution.py:274
  44.0 0.1 add_convert_fusion
  44.1 0.5 fusion.21
  44.5 1.8 %collective-permute-start.10 = (bf16[128,1024]{1,0:T(8,128)(2,1)S(1)}, bf16[128,1024]{1,0:T(8,128)(2,1)S(1)}, u32[]{:S(2)}, u32[]{:S(2)}) collective-permute-start(bf16[128,1024]{1,0:T(8,128)(2,1)S(1)} %convolution_convert_fusion), channel_id=1, source_target_pairs={{0,4},{4,0},{8,12},{12,8},{1,5},{5,1},{9,13},{13,9},{2,6},{6,2},{1... | collective-permute-start | bytes 786440 | tf_op jit(solution)/shard_map/ppermute | solution.py:274
  46.3 1.2 %collective-permute-start.11 = (bf16[128,1024]{1,0:T(8,128)(2,1)S(1)}, bf16[128,1024]{1,0:T(8,128)(2,1)S(1)}, u32[]{:S(2)}, u32[]{:S(2)}) collective-permute-start(bf16[128,1024]{1,0:T(8,128)(2,1)S(1)} %add_convert_fusion), channel_id=1, source_target_pairs={{0,8},{4,12},{8,0},{12,4},{1,9},{5,13},{9,1},{13,5},{2,10},{6,14},... | collective-permute-start | bytes 786440 | tf_op jit(solution)/shard_map/ppermute | solution.py:274
  47.5 2.4 %shard_map.97 = bf16[128,1024]{1,0:T(8,128)(2,1)S(1)} custom-call(bf16[128,1024]{1,0:T(8,128)(2,1)S(1)} %copy-done.4, bf16[256,128]{1,0:T(8,128)(2,1)S(1)} %pad_maximum_fusion.refs_0_, bf16[256,128]{1,0:T(8,128)(2,1)S(1)} %collective-permute-done.5.refs_1_, bf16[256,128]{1,0:T(8,128)(2,1)S(1)} %collective-permute-done.6.refs_2_, ...), custom_call_target="tpu_custom_call" | custom-call | bytes 524288 | tf_op jit(solution)/shard_map/pallas_call | solution.py:48
  49.9 7.2 %collective-permute-done.10 = bf16[128,1024]{1,0:T(8,128)(2,1)S(1)} collective-permute-done((bf16[128,1024]{1,0:T(8,128)(2,1)S(1)}, bf16[128,1024]{1,0:T(8,128)(2,1)S(1)}, u32[]{:S(2)}, u32[]{:S(2)}) %collective-permute-start.10) | collective-permute-done | bytes 262176 | tf_op jit(solution)/shard_map/ppermute | solution.py:274
  57.1 2.6 %collective-permute-done.11 = bf16[128,1024]{1,0:T(8,128)(2,1)S(1)} collective-permute-done((bf16[128,1024]{1,0:T(8,128)(2,1)S(1)}, bf16[128,1024]{1,0:T(8,128)(2,1)S(1)}, u32[]{:S(2)}, u32[]{:S(2)}) %collective-permute-start.11) | collective-permute-done | bytes 262176 | tf_op jit(solution)/shard_map/ppermute | solution.py:274
  59.7 0.1 subtract_convert_fusion
  59.8 0.7 convolution_convert_fusion.4.first_ref
  60.5 0.4 collective-permute-start.12
  61.0 2.7 %collective-permute-start.13 = (bf16[128,1024]{1,0:T(8,128)(2,1)S(1)}, bf16[128,1024]{1,0:T(8,128)(2,1)S(1)}, u32[]{:S(2)}, u32[]{:S(2)}) collective-permute-start(bf16[128,1024]{1,0:T(8,128)(2,1)S(1)} %subtract_convert_fusion), channel_id=1, source_target_pairs={{0,8},{4,12},{8,0},{12,4},{1,9},{5,13},{9,1},{13,5},{2,10},{6,14},... | collective-permute-start | bytes 786440 | tf_op jit(solution)/shard_map/ppermute | solution.py:274
  63.7 6.1 %collective-permute-done.12 = bf16[128,1024]{1,0:T(8,128)(2,1)S(1)} collective-permute-done((bf16[128,1024]{1,0:T(8,128)(2,1)S(1)}, bf16[128,1024]{1,0:T(8,128)(2,1)S(1)}, u32[]{:S(2)}, u32[]{:S(2)}) %collective-permute-start.12) | collective-permute-done | bytes 262176 | tf_op jit(solution)/shard_map/ppermute | solution.py:274
  69.8 0.7 convolution_convert_fusion.3.second_ref
  70.5 3.0 %collective-permute-done.13 = bf16[128,1024]{1,0:T(8,128)(2,1)S(1)} collective-permute-done((bf16[128,1024]{1,0:T(8,128)(2,1)S(1)}, bf16[128,1024]{1,0:T(8,128)(2,1)S(1)}, u32[]{:S(2)}, u32[]{:S(2)}) %collective-permute-start.13) | collective-permute-done | bytes 262176 | tf_op jit(solution)/shard_map/ppermute | solution.py:274
  73.5 0.7 convolution_convert_fusion.2.third_ref
  74.3 5.7 %collective-permute-done.14.delta_ref = bf16[128,1024]{1,0:T(8,128)(2,1)S(1)} collective-permute-done((bf16[128,1024]{1,0:T(8,128)(2,1)S(1)}, bf16[128,1024]{1,0:T(8,128)(2,1)S(1)}, u32[]{:S(2)}, u32[]{:S(2)}) %collective-permute-start.14) | collective-permute-done | bytes 262176 | tf_op jit(solution)/shard_map/ppermute | solution.py:274
  79.9 0.8 shard_map.98
  80.7 0.1 collective-permute-start.15
  80.8 1.8 %collective-permute-done.15 = bf16[2,128,896]{2,1,0:T(8,128)(2,1)S(1)} collective-permute-done((bf16[2,128,896]{2,1,0:T(8,128)(2,1)S(1)}, bf16[2,128,896]{2,1,0:T(8,128)(2,1)S(1)}, u32[]{:S(2)}, u32[]{:S(2)}) %collective-permute-start.15) | collective-permute-done | bytes 458784 | tf_op jit(solution)/shard_map/ppermute | solution.py:274
  82.6 0.1 fusion.14
  82.6 0.0 copy-start.3
  82.6 0.0 copy-start.5
  82.7 1.6 %collective-permute-start.16 = (bf16[128,896]{1,0:T(8,128)(2,1)S(1)}, bf16[128,896]{1,0:T(8,128)(2,1)S(1)}, u32[]{:S(2)}, u32[]{:S(2)}) collective-permute-start(bf16[128,896]{1,0:T(8,128)(2,1)S(1)} %fusion.14), channel_id=1, source_target_pairs={{0,2},{2,0},{1,3},{3,1},{4,6},{6,4},{5,7},{7,5},{8,10},{10,8},{9,1... | collective-permute-start | bytes 688136 | tf_op jit(solution)/shard_map/ppermute | solution.py:274
  84.3 0.1 convert_add_fusion
  84.4 6.0 %collective-permute-done.16 = bf16[128,896]{1,0:T(8,128)(2,1)S(1)} collective-permute-done((bf16[128,896]{1,0:T(8,128)(2,1)S(1)}, bf16[128,896]{1,0:T(8,128)(2,1)S(1)}, u32[]{:S(2)}, u32[]{:S(2)}) %collective-permute-start.16) | collective-permute-done | bytes 229408 | tf_op jit(solution)/shard_map/ppermute | solution.py:274
  90.4 0.2 convolution_convert_fusion.5
  90.6 0.2 convolution_convert_fusion.6
  90.8 0.2 convolution_convert_fusion.7
  90.9 1.2 %collective-permute-start.19 = (bf16[48,896]{1,0:T(8,128)(2,1)S(1)}, bf16[48,896]{1,0:T(8,128)(2,1)S(1)}, u32[]{:S(2)}, u32[]{:S(2)}) collective-permute-start(bf16[48,896]{1,0:T(8,128)(2,1)S(1)} %convolution_convert_fusion.5), channel_id=1, source_target_pairs={{0,12},{4,8},{8,4},{12,0},{1,13},{5,9},{9,5},{13,1},{2,14},{6,10},... | collective-permute-start | bytes 258056 | tf_op jit(solution)/shard_map/ppermute | solution.py:274
  92.2 0.3 collective-permute-start.18
  92.5 2.9 %collective-permute-start.17 = (bf16[48,896]{1,0:T(8,128)(2,1)S(1)}, bf16[48,896]{1,0:T(8,128)(2,1)S(1)}, u32[]{:S(2)}, u32[]{:S(2)}) collective-permute-start(bf16[48,896]{1,0:T(8,128)(2,1)S(1)} %convolution_convert_fusion.7), channel_id=1, source_target_pairs={{0,4},{4,0},{8,12},{12,8},{1,5},{5,1},{9,13},{13,9},{2,6},{6,2},{1... | collective-permute-start | bytes 258056 | tf_op jit(solution)/shard_map/ppermute | solution.py:274
  95.4 0.2 convolution_convert_fusion.8.refs_0_
  95.6 2.8 %collective-permute-done.19.refs_3_ = bf16[48,896]{1,0:T(8,128)(2,1)S(1)} collective-permute-done((bf16[48,896]{1,0:T(8,128)(2,1)S(1)}, bf16[48,896]{1,0:T(8,128)(2,1)S(1)}, u32[]{:S(2)}, u32[]{:S(2)}) %collective-permute-start.19) | collective-permute-done | bytes 86048 | tf_op jit(solution)/shard_map/ppermute | solution.py:274
  98.3 2.1 %collective-permute-done.18.refs_2_ = bf16[48,896]{1,0:T(8,128)(2,1)S(1)} collective-permute-done((bf16[48,896]{1,0:T(8,128)(2,1)S(1)}, bf16[48,896]{1,0:T(8,128)(2,1)S(1)}, u32[]{:S(2)}, u32[]{:S(2)}) %collective-permute-start.18) | collective-permute-done | bytes 86048 | tf_op jit(solution)/shard_map/ppermute | solution.py:274
  100.5 0.4 shard_map.99.refs_0_
  100.9 1.6 %collective-permute-start.21 = (bf16[48,3584]{1,0:T(8,128)(2,1)S(1)}, bf16[48,3584]{1,0:T(8,128)(2,1)S(1)}, u32[]{:S(2)}, u32[]{:S(2)}) collective-permute-start(bf16[48,3584]{1,0:T(8,128)(2,1)S(1)} %shard_map.99.refs_0_), channel_id=1, source_target_pairs={{0,2},{2,0},{1,3},{3,1},{4,6},{6,4},{5,7},{7,5},{8,10},{10,8},{9,1... | collective-permute-start | bytes 1032200 | tf_op jit(solution)/shard_map/ppermute | solution.py:274
  102.5 8.2 %collective-permute-done.21.refs_2_ = bf16[48,3584]{1,0:T(8,128)(2,1)S(1)} collective-permute-done((bf16[48,3584]{1,0:T(8,128)(2,1)S(1)}, bf16[48,3584]{1,0:T(8,128)(2,1)S(1)}, u32[]{:S(2)}, u32[]{:S(2)}) %collective-permute-start.21) | collective-permute-done | bytes 344096 | tf_op jit(solution)/shard_map/ppermute | solution.py:274
  110.7 3.0 %convolution_multiply_fusion = f32[896,1024]{1,0:T(8,128)} fusion(bf16[128,1024]{1,0:T(8,128)(2,1)S(1)} %collective-permute-done.14.delta_ref, bf16[128,1024]{1,0:T(8,128)(2,1)S(1)} %collective-permute-done.13, bf16[128,1024]{1,0:T(8,128)(2,1)S(1)} %collective-permute-done.12, bf16[128,1024]{1,0:T(8,128)(2,1)S(1)} %subtract_convert_fusion, ...), kind=kOutput, calls=%fused_computation | convolution fusion | flops 948305920 | bytes 5636096 | tf_op jit(solution)/shard_map/dot_general | solution.py:21
  113.7 1.0 shard_map.100.t
  114.7 0.8 shard_map.101
  (24 shorter events, 0.1 us)
Async XLA Ops:
  0.6 35.1 %copy-start = (bf16[896,1024]{1,0:T(8,128)(2,1)S(1)}, bf16[896,1024]{1,0:T(8,128)(2,1)}, u32[]{:S(2)}) copy-start(bf16[896,1024]{1,0:T(8,128)(2,1)} %proj_ref.1) | copy-start | bytes 5505028
  3.5 6.1 %collective-permute-start = (bf16[48,1024]{1,0:T(8,128)(2,1)}, bf16[48,1024]{1,0:T(8,128)(2,1)S(1)}, u32[]{:S(2)}, u32[]{:S(2)}) collective-permute-start(bf16[48,1024]{1,0:T(8,128)(2,1)} %get-tuple-element.25), channel_id=1, source_target_pairs={{0,4},{4,0},{8,12},{12,8},{1,5},{5,1},{9,13},{13,9},{2,6},{6,2},{1... | collective-permute-start | bytes 294920 | tf_op jit(solution)/shard_map/ppermute | solution.py:274
  6.5 10.6 %collective-permute-start.1 = (bf16[48,1024]{1,0:T(8,128)(2,1)}, bf16[48,1024]{1,0:T(8,128)(2,1)S(1)}, u32[]{:S(2)}, u32[]{:S(2)}) collective-permute-start(bf16[48,1024]{1,0:T(8,128)(2,1)} %get-tuple-element.26), channel_id=1, source_target_pairs={{0,8},{4,12},{8,0},{12,4},{1,9},{5,13},{9,1},{13,5},{2,10},{6,14},... | collective-permute-start | bytes 294920 | tf_op jit(solution)/shard_map/ppermute | solution.py:274
  9.1 8.0 %collective-permute-start.2 = (bf16[48,1024]{1,0:T(8,128)(2,1)}, bf16[48,1024]{1,0:T(8,128)(2,1)S(1)}, u32[]{:S(2)}, u32[]{:S(2)}) collective-permute-start(bf16[48,1024]{1,0:T(8,128)(2,1)} %get-tuple-element.27), channel_id=1, source_target_pairs={{0,12},{4,8},{8,4},{12,0},{1,13},{5,9},{9,5},{13,1},{2,14},{6,10},... | collective-permute-start | bytes 294920 | tf_op jit(solution)/shard_map/ppermute | solution.py:274
  17.2 0.9 copy-start.1
  18.5 6.1 %collective-permute-start.3 = (bf16[128,896]{1,0:T(8,128)(2,1)S(1)}, bf16[128,896]{1,0:T(8,128)(2,1)S(1)}, u32[]{:S(2)}, u32[]{:S(2)}) collective-permute-start(bf16[128,896]{1,0:T(8,128)(2,1)S(1)} %get-tuple-element.29), channel_id=1, source_target_pairs={{0,2},{2,0},{1,3},{3,1},{4,6},{6,4},{5,7},{7,5},{8,10},{10,8},{9,1... | collective-permute-start | bytes 688136 | tf_op jit(solution)/shard_map/ppermute | solution.py:274
  20.0 15.5 %collective-permute-start.8 = (bf16[128,896]{1,0:T(8,128)(2,1)S(1)}, bf16[128,896]{1,0:T(8,128)(2,1)S(1)}, u32[]{:S(2)}, u32[]{:S(2)}) collective-permute-start(bf16[128,896]{1,0:T(8,128)(2,1)S(1)} %get-tuple-element.29), channel_id=1, source_target_pairs={{0,1},{1,0},{2,3},{3,2},{4,5},{5,4},{6,7},{7,6},{8,9},{9,8},{10,11... | collective-permute-start | bytes 688136 | tf_op jit(solution)/shard_map/ppermute | solution.py:274
  24.5 11.0 %collective-permute-start.4 = (bf16[128,896]{1,0:T(8,128)(2,1)S(1)}, bf16[128,896]{1,0:T(8,128)(2,1)S(1)}, u32[]{:S(2)}, u32[]{:S(2)}) collective-permute-start(bf16[128,896]{1,0:T(8,128)(2,1)S(1)} %collective-permute-done.3), channel_id=1, source_target_pairs={{0,1},{1,0},{2,3},{3,2},{4,5},{5,4},{6,7},{7,6},{8,9},{9,8},{10,11... | collective-permute-start | bytes 688136 | tf_op jit(solution)/shard_map/ppermute | solution.py:274
  25.3 4.6 %collective-permute-start.5 = (bf16[256,128]{1,0:T(8,128)(2,1)S(1)}, bf16[256,128]{1,0:T(8,128)(2,1)S(1)}, u32[]{:S(2)}, u32[]{:S(2)}) collective-permute-start(bf16[256,128]{1,0:T(8,128)(2,1)S(1)} %pad_maximum_fusion.refs_0_), channel_id=1, source_target_pairs={{0,4},{4,0},{8,12},{12,8},{1,5},{5,1},{9,13},{13,9},{2,6},{6,2},{1... | collective-permute-start | bytes 196616 | tf_op jit(solution)/shard_map/ppermute | solution.py:274
  27.2 8.4 %collective-permute-start.6 = (bf16[256,128]{1,0:T(8,128)(2,1)S(1)}, bf16[256,128]{1,0:T(8,128)(2,1)S(1)}, u32[]{:S(2)}, u32[]{:S(2)}) collective-permute-start(bf16[256,128]{1,0:T(8,128)(2,1)S(1)} %pad_maximum_fusion.refs_0_), channel_id=1, source_target_pairs={{0,8},{4,12},{8,0},{12,4},{1,9},{5,13},{9,1},{13,5},{2,10},{6,14},... | collective-permute-start | bytes 196616 | tf_op jit(solution)/shard_map/ppermute | solution.py:274
  28.4 7.1 %collective-permute-start.7 = (bf16[256,128]{1,0:T(8,128)(2,1)S(1)}, bf16[256,128]{1,0:T(8,128)(2,1)S(1)}, u32[]{:S(2)}, u32[]{:S(2)}) collective-permute-start(bf16[256,128]{1,0:T(8,128)(2,1)S(1)} %pad_maximum_fusion.refs_0_), channel_id=1, source_target_pairs={{0,12},{4,8},{8,4},{12,0},{1,13},{5,9},{9,5},{13,1},{2,14},{6,10},... | collective-permute-start | bytes 196616 | tf_op jit(solution)/shard_map/ppermute | solution.py:274
  36.2 7.8 %collective-permute-start.9 = (bf16[128,1024]{1,0:T(8,128)(2,1)S(1)}, bf16[128,1024]{1,0:T(8,128)(2,1)S(1)}, u32[]{:S(2)}, u32[]{:S(2)}) collective-permute-start(bf16[128,1024]{1,0:T(8,128)(2,1)S(1)} %convolution_convert_fusion.1), channel_id=1, source_target_pairs={{0,4},{4,0},{8,12},{12,8},{1,5},{5,1},{9,13},{13,9},{2,6},{6,2},{1... | collective-permute-start | bytes 786440 | tf_op jit(solution)/shard_map/ppermute | solution.py:274
  38.7 8.8 %copy-start.2 = (bf16[48,1024]{1,0:T(8,128)(2,1)S(1)}, bf16[48,1024]{1,0:T(8,128)(2,1)}, u32[]{:S(2)}) copy-start(bf16[48,1024]{1,0:T(8,128)(2,1)} %get-tuple-element.24.refs_0_.refs_4_) | copy-start | bytes 294916
  38.7 8.8 %copy-start.4 = (bf16[128,1024]{1,0:T(8,128)(2,1)S(1)}, bf16[128,1024]{1,0:T(8,128)(2,1)}, u32[]{:S(2)}) copy-start(bf16[128,1024]{1,0:T(8,128)(2,1)} %queries_ref) | copy-start | bytes 786436
  44.5 12.5 %collective-permute-start.10 = (bf16[128,1024]{1,0:T(8,128)(2,1)S(1)}, bf16[128,1024]{1,0:T(8,128)(2,1)S(1)}, u32[]{:S(2)}, u32[]{:S(2)}) collective-permute-start(bf16[128,1024]{1,0:T(8,128)(2,1)S(1)} %convolution_convert_fusion), channel_id=1, source_target_pairs={{0,4},{4,0},{8,12},{12,8},{1,5},{5,1},{9,13},{13,9},{2,6},{6,2},{1... | collective-permute-start | bytes 786440 | tf_op jit(solution)/shard_map/ppermute | solution.py:274
  46.3 13.3 %collective-permute-start.11 = (bf16[128,1024]{1,0:T(8,128)(2,1)S(1)}, bf16[128,1024]{1,0:T(8,128)(2,1)S(1)}, u32[]{:S(2)}, u32[]{:S(2)}) collective-permute-start(bf16[128,1024]{1,0:T(8,128)(2,1)S(1)} %add_convert_fusion), channel_id=1, source_target_pairs={{0,8},{4,12},{8,0},{12,4},{1,9},{5,13},{9,1},{13,5},{2,10},{6,14},... | collective-permute-start | bytes 786440 | tf_op jit(solution)/shard_map/ppermute | solution.py:274
  60.5 9.2 %collective-permute-start.12 = (bf16[128,1024]{1,0:T(8,128)(2,1)S(1)}, bf16[128,1024]{1,0:T(8,128)(2,1)S(1)}, u32[]{:S(2)}, u32[]{:S(2)}) collective-permute-start(bf16[128,1024]{1,0:T(8,128)(2,1)S(1)} %subtract_convert_fusion), channel_id=1, source_target_pairs={{0,4},{4,0},{8,12},{12,8},{1,5},{5,1},{9,13},{13,9},{2,6},{6,2},{1... | collective-permute-start | bytes 786440 | tf_op jit(solution)/shard_map/ppermute | solution.py:274
  61.0 12.6 %collective-permute-start.13 = (bf16[128,1024]{1,0:T(8,128)(2,1)S(1)}, bf16[128,1024]{1,0:T(8,128)(2,1)S(1)}, u32[]{:S(2)}, u32[]{:S(2)}) collective-permute-start(bf16[128,1024]{1,0:T(8,128)(2,1)S(1)} %subtract_convert_fusion), channel_id=1, source_target_pairs={{0,8},{4,12},{8,0},{12,4},{1,9},{5,13},{9,1},{13,5},{2,10},{6,14},... | collective-permute-start | bytes 786440 | tf_op jit(solution)/shard_map/ppermute | solution.py:274
  73.5 6.4 %collective-permute-start.14 = (bf16[128,1024]{1,0:T(8,128)(2,1)S(1)}, bf16[128,1024]{1,0:T(8,128)(2,1)S(1)}, u32[]{:S(2)}, u32[]{:S(2)}) collective-permute-start(bf16[128,1024]{1,0:T(8,128)(2,1)S(1)} %collective-permute-done.13), channel_id=1, source_target_pairs={{0,4},{4,0},{8,12},{12,8},{1,5},{5,1},{9,13},{13,9},{2,6},{6,2},{1... | collective-permute-start | bytes 786440 | tf_op jit(solution)/shard_map/ppermute | solution.py:274
  80.7 1.9 %collective-permute-start.15 = (bf16[2,128,896]{2,1,0:T(8,128)(2,1)S(1)}, bf16[2,128,896]{2,1,0:T(8,128)(2,1)S(1)}, u32[]{:S(2)}, u32[]{:S(2)}) collective-permute-start(bf16[2,128,896]{2,1,0:T(8,128)(2,1)S(1)} %get-tuple-element.40), channel_id=1, source_target_pairs={{0,1},{1,0},{2,3},{3,2},{4,5},{5,4},{6,7},{7,6},{8,9},{9,8},{10,11... | collective-permute-start | bytes 1376264 | tf_op jit(solution)/shard_map/ppermute | solution.py:274
  82.6 17.8 %copy-start.3 = (bf16[48,3584]{1,0:T(8,128)(2,1)S(1)}, bf16[48,3584]{1,0:T(8,128)(2,1)}, u32[]{:S(2)}) copy-start(bf16[48,3584]{1,0:T(8,128)(2,1)} %get-tuple-element.22.hidden_ref) | copy-start | bytes 1032196
  82.6 17.8 %copy-start.5 = (f32[3584]{0:T(1024)S(1)}, f32[3584]{0:T(1024)}, u32[]{:S(2)}) copy-start(f32[3584]{0:T(1024)} %param.14) | copy-start | bytes 43012
  82.7 17.8 %copy-start.6 = (f32[48,1]{1,0:T(8,128)S(1)}, f32[48,1]{1,0:T(8,128)}, u32[]{:S(2)}) copy-start(f32[48,1]{1,0:T(8,128)} %get-tuple-element.23.inverse_ref) | copy-start | bytes 580
  82.7 7.7 %collective-permute-start.16 = (bf16[128,896]{1,0:T(8,128)(2,1)S(1)}, bf16[128,896]{1,0:T(8,128)(2,1)S(1)}, u32[]{:S(2)}, u32[]{:S(2)}) collective-permute-start(bf16[128,896]{1,0:T(8,128)(2,1)S(1)} %fusion.14), channel_id=1, source_target_pairs={{0,2},{2,0},{1,3},{3,1},{4,6},{6,4},{5,7},{7,5},{8,10},{10,8},{9,1... | collective-permute-start | bytes 688136 | tf_op jit(solution)/shard_map/ppermute | solution.py:274
  90.9 7.4 %collective-permute-start.19 = (bf16[48,896]{1,0:T(8,128)(2,1)S(1)}, bf16[48,896]{1,0:T(8,128)(2,1)S(1)}, u32[]{:S(2)}, u32[]{:S(2)}) collective-permute-start(bf16[48,896]{1,0:T(8,128)(2,1)S(1)} %convolution_convert_fusion.5), channel_id=1, source_target_pairs={{0,12},{4,8},{8,4},{12,0},{1,13},{5,9},{9,5},{13,1},{2,14},{6,10},... | collective-permute-start | bytes 258056 | tf_op jit(solution)/shard_map/ppermute | solution.py:274
  92.2 8.3 %collective-permute-start.18 = (bf16[48,896]{1,0:T(8,128)(2,1)S(1)}, bf16[48,896]{1,0:T(8,128)(2,1)S(1)}, u32[]{:S(2)}, u32[]{:S(2)}) collective-permute-start(bf16[48,896]{1,0:T(8,128)(2,1)S(1)} %convolution_convert_fusion.6), channel_id=1, source_target_pairs={{0,8},{4,12},{8,0},{12,4},{1,9},{5,13},{9,1},{13,5},{2,10},{6,14},... | collective-permute-start | bytes 258056 | tf_op jit(solution)/shard_map/ppermute | solution.py:274
  92.5 8.0 %collective-permute-start.17 = (bf16[48,896]{1,0:T(8,128)(2,1)S(1)}, bf16[48,896]{1,0:T(8,128)(2,1)S(1)}, u32[]{:S(2)}, u32[]{:S(2)}) collective-permute-start(bf16[48,896]{1,0:T(8,128)(2,1)S(1)} %convolution_convert_fusion.7), channel_id=1, source_target_pairs={{0,4},{4,0},{8,12},{12,8},{1,5},{5,1},{9,13},{13,9},{2,6},{6,2},{1... | collective-permute-start | bytes 258056 | tf_op jit(solution)/shard_map/ppermute | solution.py:274
  100.9 9.9 %collective-permute-start.21 = (bf16[48,3584]{1,0:T(8,128)(2,1)S(1)}, bf16[48,3584]{1,0:T(8,128)(2,1)S(1)}, u32[]{:S(2)}, u32[]{:S(2)}) collective-permute-start(bf16[48,3584]{1,0:T(8,128)(2,1)S(1)} %shard_map.99.refs_0_), channel_id=1, source_target_pairs={{0,2},{2,0},{1,3},{3,1},{4,6},{6,4},{5,7},{7,5},{8,10},{10,8},{9,1... | collective-permute-start | bytes 1032200 | tf_op jit(solution)/shard_map/ppermute | solution.py:274
  102.5 11.2 %collective-permute-start.20 = (bf16[48,3584]{1,0:T(8,128)(2,1)S(1)}, bf16[48,3584]{1,0:T(8,128)(2,1)S(1)}, u32[]{:S(2)}, u32[]{:S(2)}) collective-permute-start(bf16[48,3584]{1,0:T(8,128)(2,1)S(1)} %shard_map.99.refs_0_), channel_id=1, source_target_pairs={{0,1},{1,0},{2,3},{3,2},{4,5},{5,4},{6,7},{7,6},{8,9},{9,8},{10,11... | collective-permute-start | bytes 1032200 | tf_op jit(solution)/shard_map/ppermute | solution.py:274
  110.7 4.0 %collective-permute-start.22 = (bf16[48,3584]{1,0:T(8,128)(2,1)S(1)}, bf16[48,3584]{1,0:T(8,128)(2,1)S(1)}, u32[]{:S(2)}, u32[]{:S(2)}) collective-permute-start(bf16[48,3584]{1,0:T(8,128)(2,1)S(1)} %collective-permute-done.21.refs_2_), channel_id=1, source_target_pairs={{0,1},{1,0},{2,3},{3,2},{4,5},{5,4},{6,7},{7,6},{8,9},{9,8},{10,11... | collective-permute-start | bytes 1032200 | tf_op jit(solution)/shard_map/ppermute | solution.py:274

commit v4 on v3

--- a/solution.py
+++ b/solution.py
@@ -56,10 +56,9 @@
 
 
 def norm_kernel(student_ref, gain_ref, owner_ref, docs_ref, *refs):
-    *pieces, inverse_ref, hidden_ref, arrived = refs
+    *pieces, inverse_ref, hidden_ref = refs
     me, mine = indices()
-    copy = pltpu.make_async_copy(student_ref.at[mine], hidden_ref, arrived)
-    copy.start()
+    hidden_ref[...] = student_ref[mine]
     rows, width = hidden_ref.shape
     tiles = width // len(pieces) // LANES
     line = lax.broadcasted_iota(I32, (rows, LANES), 0)
@@ -67,7 +66,6 @@
     extra = jnp.where(line == 0, owner_row, jnp.where(line == 1, docs_row, 0.0)).astype(BF)
     for piece in pieces:
         piece[:, tiles * LANES :] = extra
-    copy.wait()
     hidden = hidden_ref[...].astype(F32)
     inverse = lax.rsqrt(jnp.sum(hidden * hidden, axis=1, keepdims=True) / width + 1e-06)
     inverse_ref[...] = inverse
@@ -82,7 +80,6 @@
 def norm_pieces(student, gain, owner, doc_ids):
     n, rows, width = student.shape
     piece = jax.ShapeDtypeStruct((rows, width // n + LANES), BF)
-    vmem = pl.BlockSpec(memory_space=pltpu.VMEM)
     return call(
         norm_kernel,
         [piece] * n
@@ -90,14 +87,12 @@
         (student, gain, owner, doc_ids),
         6 * rows * width,
         6 * rows * width,
-        in_specs=[pl.BlockSpec(memory_space=pl.ANY)] + [vmem] * 3,
-        scratch_shapes=[pltpu.SemaphoreType.DMA],
-        compiler_params=pltpu.CompilerParams(vmem_limit_bytes=60 * 1024 * 1024),
     )
 
 
 def pick_kernel(*refs):
     *pieces, out_ref, drop_ref = refs
+    pieces = pieces[::-1]
     me, mine = indices()
     tokens, depth = out_ref.shape
     slots = pieces[0].shape[0]
@@ -128,7 +123,7 @@
     return call(
         pick_kernel,
         [jax.ShapeDtypeStruct((tokens, depth), BF), jax.ShapeDtypeStruct((spots, tokens), BF)],
-        pieces,
+        pieces[::-1],
         2 * tokens * spots * depth,
         4 * spots * depth,
     )
@@ -175,6 +170,65 @@
     )
 
 
+def pick_entry(refs, at):
+    d, c, b, a = (ref[...] for ref in refs)
+    odd = at % 2 == 1
+    return jnp.where(at >= 2, jnp.where(odd, d, c), jnp.where(odd, b, a))
+
+
+def away_kernel(*refs):
+    *entries, proj_ref, out_ref = refs
+    me, mine = indices()
+    block = pick_entry(entries, me ^ mine ^ 3)
+    out_ref[...] = dot(block, proj_ref[...]).astype(BF)
+
+
+def kept_kernel(*refs):
+    *entries, proj_ref, own_ref, over_ref, normed_ref = refs
+    me, mine = indices()
+    rows = entries[0].shape[0]
+    for k, spot in enumerate((0, 2, 1, 3)):
+        normed_ref[spot * rows : (spot + 1) * rows, :] = pick_entry(entries, me ^ mine ^ k)
+    columns = 256
+    for first in range(0, proj_ref.shape[1], columns):
+        part = slice(first, first + columns)
+        product = dot(normed_ref[: 2 * rows, :], proj_ref[:, part])
+        own_ref[:, part] = product[:rows]
+        over_ref[:, part] = product[rows:]
+
+
+def beside_kernel(normed_ref, proj_ref, out_ref):
+    rows = out_ref.shape[0]
+    out_ref[...] = dot(normed_ref[2 * rows : 3 * rows, :], proj_ref[...]).astype(BF)
+
+
+def away_partial(entries, proj):
+    rows, depth = entries[0].shape
+    out = jax.ShapeDtypeStruct((rows, proj.shape[1]), BF)
+    return call(away_kernel, out, (*entries, proj), 0, 0)
+
+
+def kept_partials(entries, proj):
+    rows, depth = entries[0].shape
+    out = jax.ShapeDtypeStruct((rows, proj.shape[1]), F32)
+    shapes = [out, out, jax.ShapeDtypeStruct((4 * rows, depth), BF)]
+    return call(kept_kernel, shapes, (*entries, proj), 0, 0)
+
+
+def beside_partial(normed, proj):
+    out = jax.ShapeDtypeStruct((normed.shape[0] // 4, proj.shape[1]), BF)
+    return call(beside_kernel, out, (normed, proj), 0, 0)
+
+
+def product_kernel(delta_ref, proj_ref, out_ref):
+    out_ref[...] = dot(delta_ref[...], proj_ref[...], ((1,), (1,))).astype(BF)
+
+
+def product(delta, proj):
+    out = jax.ShapeDtypeStruct((delta.shape[0], proj.shape[0]), BF)
+    return call(product_kernel, out, (delta, proj), 0, 0)
+
+
 def route_kernel(first_ref, second_ref, third_ref, delta_ref, proj_ref, sent_ref, kept_ref, held):
     me, mine = indices()
     last = dot(delta_ref[...], proj_ref[...], ((1,), (1,))).astype(BF)
@@ -194,8 +248,8 @@
         route_kernel,
         [pair, pair],
         (*products, delta, proj),
-        2 * tokens * depth * proj.shape[1],
-        2 * proj.size + 14 * tokens * depth,
+        0,
+        0,
         scratch_shapes=[pltpu.VMEM((4, tokens, depth), BF)],
     )
 
@@ -274,12 +328,9 @@
     return lax.ppermute(x, axis, [(i, i ^ k) for i in range(lax.axis_size(axis))])
 
 
-def entry(entries, at):
-    a, b, c, d = entries
-    odd = at % 2 == 1
-    return lax.optimization_barrier(
-        jnp.where(at >= 2, jnp.where(odd, d, c), jnp.where(odd, b, a))
-    )
+def exchange(blocks):
+    got = {k: swap(blocks[k], "seq", k) for k in reversed(range(1, len(blocks)))}
+    return [got[k] for k in range(1, len(blocks))]
 
 
 def after(x, *others):
@@ -298,17 +349,12 @@
     group = heads * 2 // kv_local
     capacity, width = student_hidden.shape
     slots = capacity // n
-    off = mine ^ me
     student = student_hidden.reshape(n, slots, width)
     gain = norm_gain.reshape(width // LANES, LANES)
 
     *made, inverse, hidden = norm_pieces(student, gain, owner.T, doc_ids[None, :])
-    pieces = [made[0]] + [swap(made[k], "seq", k) for k in range(1, n)]
+    pieces = [made[0]] + exchange(made)
     normed_own, drop = pick_rows(pieces, rows)
-
-    mate = swap(normed_own, "side")
-    far = swap(normed_own, "mp")
-    far_mate = swap(far, "side")
 
     head = side * heads // group
     parcel = jnp.concatenate(
@@ -317,32 +363,30 @@
             lax.dynamic_slice_in_dim(teacher_values, head * HD, HD, 1),
         ]
     )
-    parcel = after(parcel, normed_own)
-    parcels = [parcel] + [swap(parcel, "seq", k) for k in range(1, n)]
-    far_mate = after(far_mate, *parcels)
-    normed = [entry([normed_own, mate, far, far_mate], off ^ k) for k in range(n)]
-
-    away = dot(normed[3], proj).astype(BF)
-    over_own = lax.optimization_barrier(dot(after(normed[2], away), proj))
-    beside = dot(after(normed[1], over_own), proj).astype(BF)
-    got_over = after(swap(away, "seq", 1), over_own, beside)
+    parcel = after(lax.optimization_barrier(parcel), normed_own)
+
+    far = swap(normed_own, "mp")
+    mate = swap(after(normed_own, parcel), "side")
+    parcels = [parcel] + exchange([parcel] * n)
+    far_mate = swap(after(far, mate, *parcels), "side")
+    entries = [far_mate, far, mate, normed_own]
+
+    away = away_partial(entries, proj)
+    own, over_own, normed = kept_partials([after(e, away) for e in entries], proj)
+    got_over = after(swap(away, "seq", 1), over_own)
     over = lax.optimization_barrier((over_own + got_over.astype(F32)).astype(BF))
     got_far = swap(over, "seq", 2)
-    own = lax.optimization_barrier(dot(after(normed[0], over), proj))
-    got_beside = swap(after(beside, own), "seq", 1)
-    teacher_rows = attention_rows(after(teacher_queries, own), parcels, pieces)
-    predicted = own + got_beside.astype(F32) + got_far.astype(F32)
+    got_beside = swap(beside_partial(after(normed, over), proj), "seq", 1)
+    teacher_rows = attention_rows(after(teacher_queries, over), parcels, pieces)
+    predicted = lax.optimization_barrier(own + got_far.astype(F32)) + got_beside.astype(F32)
     delta = (predicted - teacher_rows.astype(F32)).astype(BF)
 
-    def product(block):
-        return lax.optimization_barrier(dot(block, proj, ((1,), (1,))).astype(BF))
-
     delta_far = swap(delta, "seq", 2)
-    own_product = product(delta)
+    own_product = product(delta, proj)
     delta_beside = swap(after(delta, own_product), "seq", 1)
     delta_last = swap(delta_far, "seq", 1)
     deltas = [delta, delta_beside, delta_far, delta_last]
-    products = [own_product, product(delta_beside), product(delta_far)]
+    products = [own_product, product(delta_beside, proj), product(delta_far, proj)]
 
     sent, kept = route_products(products, delta_last, proj)
     got = swap(sent, "side")
@@ -351,17 +395,18 @@
     near = lax.optimization_barrier(kept[0].astype(F32) + after(got[0], cross).astype(F32))
     feature_rows = (near + crossed.astype(F32)).astype(BF)
     leaving = [dot(drop[k * slots : (k + 1) * slots], feature_rows).astype(BF) for k in range(n)]
-    arrived = [leaving[0]] + [swap(leaving[k], "seq", k) for k in range(1, n)]
+    arrived = [leaving[0]] + exchange(leaving)
     grad_own = grad_rows(hidden, gain, inverse, arrived)
+
+    factor = 1.0 / math.sqrt(rows * n)
+    deltas = jnp.concatenate([deltas[k] for k in (0, 2, 1, 3)])
+    grad_proj = lax.optimization_barrier(dot(normed, after(deltas, cross), ((0,), (0,))) * factor)
 
     grad_mate = swap(grad_own, "side")
     grad_far = swap(grad_own, "mp")
-    grad_last = swap(grad_far, "side")
+    grad_last = swap(after(grad_far, grad_proj), "side")
     grad_hidden = write_rows([grad_own, grad_mate, grad_far], 0)
     grad_hidden = write_rows([grad_last], 3, grad_hidden).reshape(capacity, width)
-
-    factor = 1.0 / math.sqrt(rows * n)
-    grad_proj = dot(jnp.concatenate(normed), jnp.concatenate(deltas), ((0,), (0,))) * factor
     return (grad_hidden, grad_proj)
 
 

time: 116 us -> 109 us (0.940)
  matrix products: 7.58 us -> 3.64 us
  starting transfers between devices: 27.2 us -> 23.8 us
  waiting for transfers between devices: 69.1 us -> 66.1 us
  local copies, waits for them, and re-layouts: 1.73 us -> 4.3 us
  Pallas kernels: 8.43 us -> 9.71 us
    dot_general x12 -> x5, matrix products: 7.58 us -> 3.64 us  [dot(): return lax.dot_general(a, b, (dims, ((), ())), preferred_element_type=F32)]
    ppermute x23, starting transfers between devices: 27.2 us -> 23.8 us  [swap(): lax.ppermute(x, axis, [(i, i ^ k) for i in range(lax.axis_size(axis))])]
    ppermute x23, waiting for transfers between devices: 69.1 us -> 66.1 us  [swap(): lax.ppermute(x, axis, [(i, i ^ k) for i in range(lax.axis_size(axis))])]
    unnamed x14, local copies, waits for them, and re-layouts: 0.93 us -> 3.51 us
    pallas_call x7 -> x13, Pallas kernels: 8.43 us -> 9.71 us  [call(): pl.pallas_call(kernel, out_shape=shapes, cost_estimate=pl.CostEstimate(fl...]
  transfers between devices with their start and end apart: 23 -> 23, of which waited for: 16 -> 18; matrix products, arithmetic and copies ran while one was open for 5% -> 4% of each run, Pallas kernels for 3% -> 6%
where the time goes in v4:
time: 109 us
  waiting for transfers between devices  66.1 us (61%)
  starting transfers between devices  23.8 us (22%)
  Pallas kernels  9.71 us (9%)
  local copies, waits for them, and re-layouts  4.3 us (4%)
  matrix products  3.64 us (3%)
    ppermute x23, waiting for transfers between devices, swap(): lax.ppermute(x, axis, [(i, i ^ k) for i in range(lax.axis_size(axis))])  66.1 us
    ppermute x23, starting transfers between devices, swap(): lax.ppermute(x, axis, [(i, i ^ k) for i in range(lax.axis_size(axis))])  23.8 us
    pallas_call x13, Pallas kernels, call(): pl.pallas_call(kernel, out_shape=shapes, cost_estimate=pl.CostEstimate(fl...  9.71 us
    dot_general x5, matrix products, dot(): return lax.dot_general(a, b, (dims, ((), ())), preferred_element_type=F32)  3.64 us
    unnamed x14, local copies, waits for them, and re-layouts  3.51 us
  transfers between devices with their start and end apart: 23, of which 18 were waited for; matrix products, arithmetic and copies ran while one was open for 4% of the time, Pallas kernels for 6%

profile of v4, /device:TPU:0, one launch (start us, length us, event | category | flops | bytes accessed | tf_op | source)
XLA Modules:
  0.0 108.8 jit_solution(15837948238979974554)
XLA Ops:
  0.7 1.5 %copy-done.1 = bf16[192,3584]{1,0:T(8,128)(2,1)S(1)} copy-done((bf16[192,3584]{1,0:T(8,128)(2,1)S(1)}, bf16[192,3584]{1,0:T(8,128)(2,1)}, u32[]{:S(2)}) %copy-start.1) | copy-done | bytes 1376280
  2.1 0.7 copy-done.3
  2.8 0.7 copy-done.5
  3.5 0.7 copy-done.6
  4.1 0.2 shard_map.95
  4.4 5.1 %collective-permute-start = (bf16[48,1024]{1,0:T(8,128)(2,1)S(1)}, bf16[48,1024]{1,0:T(8,128)(2,1)S(1)}, u32[]{:S(2)}, u32[]{:S(2)}) collective-permute-start(bf16[48,1024]{1,0:T(8,128)(2,1)S(1)} %get-tuple-element.31), channel_id=1, source_target_pairs={{0,12},{4,8},{8,4},{12,0},{1,13},{5,9},{9,5},{13,1},{2,14},{6,10},... | collective-permute-start | bytes 294920 | tf_op jit(solution)/shard_map/ppermute | solution.py:328
  9.5 0.6 collective-permute-start.2
  10.1 0.8 constant_dynamic-slice_fusion
  10.9 2.3 %collective-permute-done.refs_0_.refs_7_ = bf16[48,1024]{1,0:T(8,128)(2,1)S(1)} collective-permute-done((bf16[48,1024]{1,0:T(8,128)(2,1)S(1)}, bf16[48,1024]{1,0:T(8,128)(2,1)S(1)}, u32[]{:S(2)}, u32[]{:S(2)}) %collective-permute-start) | collective-permute-done | bytes 98336 | tf_op jit(solution)/shard_map/ppermute | solution.py:328
  13.2 4.6 %collective-permute-done.1.refs_1_.refs_6_ = bf16[48,1024]{1,0:T(8,128)(2,1)S(1)} collective-permute-done((bf16[48,1024]{1,0:T(8,128)(2,1)S(1)}, bf16[48,1024]{1,0:T(8,128)(2,1)S(1)}, u32[]{:S(2)}, u32[]{:S(2)}) %collective-permute-start.1) | collective-permute-done | bytes 98336 | tf_op jit(solution)/shard_map/ppermute | solution.py:328
  17.8 0.4 shard_map.96
  18.2 0.1 collective-permute-start.4
  18.2 1.6 %collective-permute-start.3 = (bf16[128,896]{1,0:T(8,128)(2,1)S(1)}, bf16[128,896]{1,0:T(8,128)(2,1)S(1)}, u32[]{:S(2)}, u32[]{:S(2)}) collective-permute-start(bf16[128,896]{1,0:T(8,128)(2,1)S(1)} %get-tuple-element.43.refs_3_), channel_id=1, source_target_pairs={{0,2},{2,0},{1,3},{3,1},{4,6},{6,4},{5,7},{7,5},{8,10},{10,8},{9,1... | collective-permute-start | bytes 688136 | tf_op jit(solution)/shard_map/ppermute | solution.py:328
  19.8 0.5 collective-permute-start.5
  20.3 2.6 %collective-permute-start.6 = (bf16[256,128]{1,0:T(8,128)(2,1)S(1)}, bf16[256,128]{1,0:T(8,128)(2,1)S(1)}, u32[]{:S(2)}, u32[]{:S(2)}) collective-permute-start(bf16[256,128]{1,0:T(8,128)(2,1)S(1)} %pad_maximum_fusion.1.refs_0_), channel_id=1, source_target_pairs={{0,8},{4,12},{8,0},{12,4},{1,9},{5,13},{9,1},{13,5},{2,10},{6,14},... | collective-permute-start | bytes 196616 | tf_op jit(solution)/shard_map/ppermute | solution.py:328
  22.9 1.3 %collective-permute-start.7 = (bf16[256,128]{1,0:T(8,128)(2,1)S(1)}, bf16[256,128]{1,0:T(8,128)(2,1)S(1)}, u32[]{:S(2)}, u32[]{:S(2)}) collective-permute-start(bf16[256,128]{1,0:T(8,128)(2,1)S(1)} %pad_maximum_fusion.1.refs_0_), channel_id=1, source_target_pairs={{0,12},{4,8},{8,4},{12,0},{1,13},{5,9},{9,5},{13,1},{2,14},{6,10},... | collective-permute-start | bytes 196616 | tf_op jit(solution)/shard_map/ppermute | solution.py:328
  24.2 0.6 collective-permute-done.5.refs_1_
  24.8 3.4 %collective-permute-done.6.refs_2_ = bf16[256,128]{1,0:T(8,128)(2,1)S(1)} collective-permute-done((bf16[256,128]{1,0:T(8,128)(2,1)S(1)}, bf16[256,128]{1,0:T(8,128)(2,1)S(1)}, u32[]{:S(2)}, u32[]{:S(2)}) %collective-permute-start.6) | collective-permute-done | bytes 65568 | tf_op jit(solution)/shard_map/ppermute | solution.py:328
  28.2 0.8 collective-permute-done.7.refs_3_
  29.1 1.5 %collective-permute-done.8.refs_0_ = bf16[128,896]{1,0:T(8,128)(2,1)S(1)} collective-permute-done((bf16[128,896]{1,0:T(8,128)(2,1)S(1)}, bf16[128,896]{1,0:T(8,128)(2,1)S(1)}, u32[]{:S(2)}, u32[]{:S(2)}) %collective-permute-start.8) | collective-permute-done | bytes 229408 | tf_op jit(solution)/shard_map/ppermute | solution.py:328
  30.5 0.4 shard_map.97
  31.0 1.2 %collective-permute-start.9 = (bf16[128,1024]{1,0:T(8,128)(2,1)S(1)}, bf16[128,1024]{1,0:T(8,128)(2,1)S(1)}, u32[]{:S(2)}, u32[]{:S(2)}) collective-permute-start(bf16[128,1024]{1,0:T(8,128)(2,1)S(1)} %shard_map.97), channel_id=1, source_target_pairs={{0,4},{4,0},{8,12},{12,8},{1,5},{5,1},{9,13},{13,9},{2,6},{6,2},{1... | collective-permute-start | bytes 786440 | tf_op jit(solution)/shard_map/ppermute | solution.py:328
  32.2 0.9 shard_map.98
  33.1 0.0 copy-start.2
  33.1 6.3 %collective-permute-done.9 = bf16[128,1024]{1,0:T(8,128)(2,1)S(1)} collective-permute-done((bf16[128,1024]{1,0:T(8,128)(2,1)S(1)}, bf16[128,1024]{1,0:T(8,128)(2,1)S(1)}, u32[]{:S(2)}, u32[]{:S(2)}) %collective-permute-start.9) | collective-permute-done | bytes 262176 | tf_op jit(solution)/shard_map/ppermute | solution.py:328
  39.4 0.1 add_convert_fusion
  39.5 1.7 %collective-permute-start.10 = (bf16[128,1024]{1,0:T(8,128)(2,1)S(1)}, bf16[128,1024]{1,0:T(8,128)(2,1)S(1)}, u32[]{:S(2)}, u32[]{:S(2)}) collective-permute-start(bf16[128,1024]{1,0:T(8,128)(2,1)S(1)} %add_convert_fusion), channel_id=1, source_target_pairs={{0,8},{4,12},{8,0},{12,4},{1,9},{5,13},{9,1},{13,5},{2,10},{6,14},... | collective-permute-start | bytes 786440 | tf_op jit(solution)/shard_map/ppermute | solution.py:328
  41.2 0.4 shard_map.99
  41.6 0.9 collective-permute-start.11
  42.5 2.4 %shard_map.100 = bf16[128,1024]{1,0:T(8,128)(2,1)S(1)} custom-call(bf16[128,1024]{1,0:T(8,128)(2,1)S(1)} %copy-done.2, bf16[256,128]{1,0:T(8,128)(2,1)S(1)} %pad_maximum_fusion.1.refs_0_, bf16[256,128]{1,0:T(8,128)(2,1)S(1)} %collective-permute-done.5.refs_1_, bf16[256,128]{1,0:T(8,128)(2,1)S(1)} %collective-permute-done.6.refs_2_, ...), custom_call_target="tpu_custom_call" | custom-call | bytes 524288 | tf_op jit(solution)/shard_map/pallas_call | solution.py:48
  44.9 8.8 %collective-permute-done.10 = bf16[128,1024]{1,0:T(8,128)(2,1)S(1)} collective-permute-done((bf16[128,1024]{1,0:T(8,128)(2,1)S(1)}, bf16[128,1024]{1,0:T(8,128)(2,1)S(1)}, u32[]{:S(2)}, u32[]{:S(2)}) %collective-permute-start.10) | collective-permute-done | bytes 262176 | tf_op jit(solution)/shard_map/ppermute | solution.py:328
  53.7 0.1 convert_add_fusion
  53.8 0.1 collective-permute-done.11
  53.9 0.1 subtract_convert_fusion.delta_ref
  54.0 0.9 collective-permute-start.13
  54.9 0.7 shard_map.101.first_ref
  55.6 1.6 %collective-permute-start.12 = (bf16[128,1024]{1,0:T(8,128)(2,1)S(1)}, bf16[128,1024]{1,0:T(8,128)(2,1)S(1)}, u32[]{:S(2)}, u32[]{:S(2)}) collective-permute-start(bf16[128,1024]{1,0:T(8,128)(2,1)S(1)} %subtract_convert_fusion.delta_ref), channel_id=1, source_target_pairs={{0,4},{4,0},{8,12},{12,8},{1,5},{5,1},{9,13},{13,9},{2,6},{6,2},{1... | collective-permute-start | bytes 786440 | tf_op jit(solution)/shard_map/ppermute | solution.py:328
  57.2 10.1 %collective-permute-done.13.delta_ref = bf16[128,1024]{1,0:T(8,128)(2,1)S(1)} collective-permute-done((bf16[128,1024]{1,0:T(8,128)(2,1)S(1)}, bf16[128,1024]{1,0:T(8,128)(2,1)S(1)}, u32[]{:S(2)}, u32[]{:S(2)}) %collective-permute-start.13) | collective-permute-done | bytes 262176 | tf_op jit(solution)/shard_map/ppermute | solution.py:328
  67.3 0.7 shard_map.103.third_ref
  68.0 0.2 collective-permute-done.12.delta_ref
  68.2 0.7 shard_map.102.second_ref
  68.9 6.5 %collective-permute-done.14.delta_ref = bf16[128,1024]{1,0:T(8,128)(2,1)S(1)} collective-permute-done((bf16[128,1024]{1,0:T(8,128)(2,1)S(1)}, bf16[128,1024]{1,0:T(8,128)(2,1)S(1)}, u32[]{:S(2)}, u32[]{:S(2)}) %collective-permute-start.14) | collective-permute-done | bytes 262176 | tf_op jit(solution)/shard_map/ppermute | solution.py:328
  75.5 0.8 shard_map.104
  76.2 0.1 collective-permute-start.15
  76.3 0.1 pad_maximum_fusion
  76.4 1.7 %collective-permute-done.15 = bf16[2,128,896]{2,1,0:T(8,128)(2,1)S(1)} collective-permute-done((bf16[2,128,896]{2,1,0:T(8,128)(2,1)S(1)}, bf16[2,128,896]{2,1,0:T(8,128)(2,1)S(1)}, u32[]{:S(2)}, u32[]{:S(2)}) %collective-permute-start.15) | collective-permute-done | bytes 458784 | tf_op jit(solution)/shard_map/ppermute | solution.py:328
  78.1 0.1 fusion
  78.2 0.6 collective-permute-start.16
  78.9 7.0 %collective-permute-done.16 = bf16[128,896]{1,0:T(8,128)(2,1)S(1)} collective-permute-done((bf16[128,896]{1,0:T(8,128)(2,1)S(1)}, bf16[128,896]{1,0:T(8,128)(2,1)S(1)}, u32[]{:S(2)}, u32[]{:S(2)}) %collective-permute-start.16) | collective-permute-done | bytes 229408 | tf_op jit(solution)/shard_map/ppermute | solution.py:328
  85.9 0.2 convolution_convert_fusion
  86.1 0.2 convolution_convert_fusion.1
  86.3 0.2 convolution_convert_fusion.2
  86.5 2.1 %collective-permute-start.19 = (bf16[48,896]{1,0:T(8,128)(2,1)S(1)}, bf16[48,896]{1,0:T(8,128)(2,1)S(1)}, u32[]{:S(2)}, u32[]{:S(2)}) collective-permute-start(bf16[48,896]{1,0:T(8,128)(2,1)S(1)} %convolution_convert_fusion), channel_id=1, source_target_pairs={{0,12},{4,8},{8,4},{12,0},{1,13},{5,9},{9,5},{13,1},{2,14},{6,10},... | collective-permute-start | bytes 258056 | tf_op jit(solution)/shard_map/ppermute | solution.py:328
  88.5 2.4 %collective-permute-start.17 = (bf16[48,896]{1,0:T(8,128)(2,1)S(1)}, bf16[48,896]{1,0:T(8,128)(2,1)S(1)}, u32[]{:S(2)}, u32[]{:S(2)}) collective-permute-start(bf16[48,896]{1,0:T(8,128)(2,1)S(1)} %convolution_convert_fusion.2), channel_id=1, source_target_pairs={{0,4},{4,0},{8,12},{12,8},{1,5},{5,1},{9,13},{13,9},{2,6},{6,2},{1... | collective-permute-start | bytes 258056 | tf_op jit(solution)/shard_map/ppermute | solution.py:328
  90.9 0.2 convolution_convert_fusion.3.refs_0_
  91.1 2.7 %collective-permute-done.19.refs_3_ = bf16[48,896]{1,0:T(8,128)(2,1)S(1)} collective-permute-done((bf16[48,896]{1,0:T(8,128)(2,1)S(1)}, bf16[48,896]{1,0:T(8,128)(2,1)S(1)}, u32[]{:S(2)}, u32[]{:S(2)}) %collective-permute-start.19) | collective-permute-done | bytes 86048 | tf_op jit(solution)/shard_map/ppermute | solution.py:328
  93.8 2.5 %collective-permute-done.18.refs_2_ = bf16[48,896]{1,0:T(8,128)(2,1)S(1)} collective-permute-done((bf16[48,896]{1,0:T(8,128)(2,1)S(1)}, bf16[48,896]{1,0:T(8,128)(2,1)S(1)}, u32[]{:S(2)}, u32[]{:S(2)}) %collective-permute-start.18) | collective-permute-done | bytes 86048 | tf_op jit(solution)/shard_map/ppermute | solution.py:328
  96.3 0.4 shard_map.105.refs_0_
  96.7 0.6 collective-permute-start.21
  97.3 3.0 %convolution_multiply_fusion = f32[896,1024]{1,0:T(8,128)} fusion(bf16[512,896]{1,0:T(8,128)(2,1)S(1)} %get-tuple-element.48.normed_ref, bf16[512,1024]{1,0:T(8,128)(2,1)S(1)} %pad_maximum_fusion), kind=kOutput, calls=%fused_computation | convolution fusion | flops 940441600 | bytes 5636096 | tf_op jit(solution)/shard_map/dot_general | solution.py:21
  100.2 6.2 %collective-permute-done.21.refs_2_ = bf16[48,3584]{1,0:T(8,128)(2,1)S(1)} collective-permute-done((bf16[48,3584]{1,0:T(8,128)(2,1)S(1)}, bf16[48,3584]{1,0:T(8,128)(2,1)S(1)}, u32[]{:S(2)}, u32[]{:S(2)}) %collective-permute-start.21) | collective-permute-done | bytes 344096 | tf_op jit(solution)/shard_map/ppermute | solution.py:328
  106.4 1.0 shard_map.106.t
  107.4 0.7 collective-permute-done.22.refs_0_
  108.1 0.7 shard_map.107
  (24 shorter events, 0.2 us)
Async XLA Ops:
  0.6 29.9 %copy-start = (bf16[896,1024]{1,0:T(8,128)(2,1)S(1)}, bf16[896,1024]{1,0:T(8,128)(2,1)}, u32[]{:S(2)}) copy-start(bf16[896,1024]{1,0:T(8,128)(2,1)} %proj_ref.9) | copy-start | bytes 5505028
  0.6 1.5 %copy-start.1 = (bf16[192,3584]{1,0:T(8,128)(2,1)S(1)}, bf16[192,3584]{1,0:T(8,128)(2,1)}, u32[]{:S(2)}) copy-start(bf16[192,3584]{1,0:T(8,128)(2,1)} %param.13) | copy-start | bytes 4128772
  2.1 0.7 copy-start.3
  2.8 0.7 copy-start.5
  3.5 0.7 copy-start.6
  4.4 8.8 %collective-permute-start = (bf16[48,1024]{1,0:T(8,128)(2,1)S(1)}, bf16[48,1024]{1,0:T(8,128)(2,1)S(1)}, u32[]{:S(2)}, u32[]{:S(2)}) collective-permute-start(bf16[48,1024]{1,0:T(8,128)(2,1)S(1)} %get-tuple-element.31), channel_id=1, source_target_pairs={{0,12},{4,8},{8,4},{12,0},{1,13},{5,9},{9,5},{13,1},{2,14},{6,10},... | collective-permute-start | bytes 294920 | tf_op jit(solution)/shard_map/ppermute | solution.py:328
  9.5 8.3 %collective-permute-start.1 = (bf16[48,1024]{1,0:T(8,128)(2,1)S(1)}, bf16[48,1024]{1,0:T(8,128)(2,1)S(1)}, u32[]{:S(2)}, u32[]{:S(2)}) collective-permute-start(bf16[48,1024]{1,0:T(8,128)(2,1)S(1)} %get-tuple-element.32), channel_id=1, source_target_pairs={{0,8},{4,12},{8,0},{12,4},{1,9},{5,13},{9,1},{13,5},{2,10},{6,14},... | collective-permute-start | bytes 294920 | tf_op jit(solution)/shard_map/ppermute | solution.py:328
  9.5 8.3 %collective-permute-start.2 = (bf16[48,1024]{1,0:T(8,128)(2,1)S(1)}, bf16[48,1024]{1,0:T(8,128)(2,1)S(1)}, u32[]{:S(2)}, u32[]{:S(2)}) collective-permute-start(bf16[48,1024]{1,0:T(8,128)(2,1)S(1)} %get-tuple-element.33), channel_id=1, source_target_pairs={{0,4},{4,0},{8,12},{12,8},{1,5},{5,1},{9,13},{13,9},{2,6},{6,2},{1... | collective-permute-start | bytes 294920 | tf_op jit(solution)/shard_map/ppermute | solution.py:328
  18.2 10.9 %collective-permute-start.4 = (bf16[128,896]{1,0:T(8,128)(2,1)S(1)}, bf16[128,896]{1,0:T(8,128)(2,1)S(1)}, u32[]{:S(2)}, u32[]{:S(2)}) collective-permute-start(bf16[128,896]{1,0:T(8,128)(2,1)S(1)} %get-tuple-element.43.refs_3_), channel_id=1, source_target_pairs={{0,1},{1,0},{2,3},{3,2},{4,5},{5,4},{6,7},{7,6},{8,9},{9,8},{10,11... | collective-permute-start | bytes 688136 | tf_op jit(solution)/shard_map/ppermute | solution.py:328
  18.2 10.8 %collective-permute-start.3 = (bf16[128,896]{1,0:T(8,128)(2,1)S(1)}, bf16[128,896]{1,0:T(8,128)(2,1)S(1)}, u32[]{:S(2)}, u32[]{:S(2)}) collective-permute-start(bf16[128,896]{1,0:T(8,128)(2,1)S(1)} %get-tuple-element.43.refs_3_), channel_id=1, source_target_pairs={{0,2},{2,0},{1,3},{3,1},{4,6},{6,4},{5,7},{7,5},{8,10},{10,8},{9,1... | collective-permute-start | bytes 688136 | tf_op jit(solution)/shard_map/ppermute | solution.py:328
  19.8 5.0 %collective-permute-start.5 = (bf16[256,128]{1,0:T(8,128)(2,1)S(1)}, bf16[256,128]{1,0:T(8,128)(2,1)S(1)}, u32[]{:S(2)}, u32[]{:S(2)}) collective-permute-start(bf16[256,128]{1,0:T(8,128)(2,1)S(1)} %pad_maximum_fusion.1.refs_0_), channel_id=1, source_target_pairs={{0,4},{4,0},{8,12},{12,8},{1,5},{5,1},{9,13},{13,9},{2,6},{6,2},{1... | collective-permute-start | bytes 196616 | tf_op jit(solution)/shard_map/ppermute | solution.py:328
  20.3 7.9 %collective-permute-start.6 = (bf16[256,128]{1,0:T(8,128)(2,1)S(1)}, bf16[256,128]{1,0:T(8,128)(2,1)S(1)}, u32[]{:S(2)}, u32[]{:S(2)}) collective-permute-start(bf16[256,128]{1,0:T(8,128)(2,1)S(1)} %pad_maximum_fusion.1.refs_0_), channel_id=1, source_target_pairs={{0,8},{4,12},{8,0},{12,4},{1,9},{5,13},{9,1},{13,5},{2,10},{6,14},... | collective-permute-start | bytes 196616 | tf_op jit(solution)/shard_map/ppermute | solution.py:328
  22.9 6.2 %collective-permute-start.7 = (bf16[256,128]{1,0:T(8,128)(2,1)S(1)}, bf16[256,128]{1,0:T(8,128)(2,1)S(1)}, u32[]{:S(2)}, u32[]{:S(2)}) collective-permute-start(bf16[256,128]{1,0:T(8,128)(2,1)S(1)} %pad_maximum_fusion.1.refs_0_), channel_id=1, source_target_pairs={{0,12},{4,8},{8,4},{12,0},{1,13},{5,9},{9,5},{13,1},{2,14},{6,10},... | collective-permute-start | bytes 196616 | tf_op jit(solution)/shard_map/ppermute | solution.py:328
  29.1 1.5 %collective-permute-start.8 = (bf16[128,896]{1,0:T(8,128)(2,1)S(1)}, bf16[128,896]{1,0:T(8,128)(2,1)S(1)}, u32[]{:S(2)}, u32[]{:S(2)}) collective-permute-start(bf16[128,896]{1,0:T(8,128)(2,1)S(1)} %collective-permute-done.3.refs_1_), channel_id=1, source_target_pairs={{0,1},{1,0},{2,3},{3,2},{4,5},{5,4},{6,7},{7,6},{8,9},{9,8},{10,11... | collective-permute-start | bytes 688136 | tf_op jit(solution)/shard_map/ppermute | solution.py:328
  31.0 8.4 %collective-permute-start.9 = (bf16[128,1024]{1,0:T(8,128)(2,1)S(1)}, bf16[128,1024]{1,0:T(8,128)(2,1)S(1)}, u32[]{:S(2)}, u32[]{:S(2)}) collective-permute-start(bf16[128,1024]{1,0:T(8,128)(2,1)S(1)} %shard_map.97), channel_id=1, source_target_pairs={{0,4},{4,0},{8,12},{12,8},{1,5},{5,1},{9,13},{13,9},{2,6},{6,2},{1... | collective-permute-start | bytes 786440 | tf_op jit(solution)/shard_map/ppermute | solution.py:328
  33.1 9.5 %copy-start.2 = (bf16[128,1024]{1,0:T(8,128)(2,1)S(1)}, bf16[128,1024]{1,0:T(8,128)(2,1)}, u32[]{:S(2)}) copy-start(bf16[128,1024]{1,0:T(8,128)(2,1)} %queries_ref) | copy-start | bytes 786436
  39.5 14.2 %collective-permute-start.10 = (bf16[128,1024]{1,0:T(8,128)(2,1)S(1)}, bf16[128,1024]{1,0:T(8,128)(2,1)S(1)}, u32[]{:S(2)}, u32[]{:S(2)}) collective-permute-start(bf16[128,1024]{1,0:T(8,128)(2,1)S(1)} %add_convert_fusion), channel_id=1, source_target_pairs={{0,8},{4,12},{8,0},{12,4},{1,9},{5,13},{9,1},{13,5},{2,10},{6,14},... | collective-permute-start | bytes 786440 | tf_op jit(solution)/shard_map/ppermute | solution.py:328
  41.6 12.3 %collective-permute-start.11 = (bf16[128,1024]{1,0:T(8,128)(2,1)S(1)}, bf16[128,1024]{1,0:T(8,128)(2,1)S(1)}, u32[]{:S(2)}, u32[]{:S(2)}) collective-permute-start(bf16[128,1024]{1,0:T(8,128)(2,1)S(1)} %shard_map.99), channel_id=1, source_target_pairs={{0,4},{4,0},{8,12},{12,8},{1,5},{5,1},{9,13},{13,9},{2,6},{6,2},{1... | collective-permute-start | bytes 786440 | tf_op jit(solution)/shard_map/ppermute | solution.py:328
  54.0 13.3 %collective-permute-start.13 = (bf16[128,1024]{1,0:T(8,128)(2,1)S(1)}, bf16[128,1024]{1,0:T(8,128)(2,1)S(1)}, u32[]{:S(2)}, u32[]{:S(2)}) collective-permute-start(bf16[128,1024]{1,0:T(8,128)(2,1)S(1)} %subtract_convert_fusion.delta_ref), channel_id=1, source_target_pairs={{0,8},{4,12},{8,0},{12,4},{1,9},{5,13},{9,1},{13,5},{2,10},{6,14},... | collective-permute-start | bytes 786440 | tf_op jit(solution)/shard_map/ppermute | solution.py:328
  55.6 12.6 %collective-permute-start.12 = (bf16[128,1024]{1,0:T(8,128)(2,1)S(1)}, bf16[128,1024]{1,0:T(8,128)(2,1)S(1)}, u32[]{:S(2)}, u32[]{:S(2)}) collective-permute-start(bf16[128,1024]{1,0:T(8,128)(2,1)S(1)} %subtract_convert_fusion.delta_ref), channel_id=1, source_target_pairs={{0,4},{4,0},{8,12},{12,8},{1,5},{5,1},{9,13},{13,9},{2,6},{6,2},{1... | collective-permute-start | bytes 786440 | tf_op jit(solution)/shard_map/ppermute | solution.py:328
  67.3 8.2 %collective-permute-start.14 = (bf16[128,1024]{1,0:T(8,128)(2,1)S(1)}, bf16[128,1024]{1,0:T(8,128)(2,1)S(1)}, u32[]{:S(2)}, u32[]{:S(2)}) collective-permute-start(bf16[128,1024]{1,0:T(8,128)(2,1)S(1)} %collective-permute-done.13.delta_ref), channel_id=1, source_target_pairs={{0,4},{4,0},{8,12},{12,8},{1,5},{5,1},{9,13},{13,9},{2,6},{6,2},{1... | collective-permute-start | bytes 786440 | tf_op jit(solution)/shard_map/ppermute | solution.py:328
  76.2 1.9 %collective-permute-start.15 = (bf16[2,128,896]{2,1,0:T(8,128)(2,1)S(1)}, bf16[2,128,896]{2,1,0:T(8,128)(2,1)S(1)}, u32[]{:S(2)}, u32[]{:S(2)}) collective-permute-start(bf16[2,128,896]{2,1,0:T(8,128)(2,1)S(1)} %get-tuple-element.52), channel_id=1, source_target_pairs={{0,1},{1,0},{2,3},{3,2},{4,5},{5,4},{6,7},{7,6},{8,9},{9,8},{10,11... | collective-permute-start | bytes 1376264 | tf_op jit(solution)/shard_map/ppermute | solution.py:328
  78.1 18.2 %copy-start.4 = (f32[3584]{0:T(1024)S(1)}, f32[3584]{0:T(1024)}, u32[]{:S(2)}) copy-start(f32[3584]{0:T(1024)} %param.14) | copy-start | bytes 43012
  78.2 7.7 %collective-permute-start.16 = (bf16[128,896]{1,0:T(8,128)(2,1)S(1)}, bf16[128,896]{1,0:T(8,128)(2,1)S(1)}, u32[]{:S(2)}, u32[]{:S(2)}) collective-permute-start(bf16[128,896]{1,0:T(8,128)(2,1)S(1)} %fusion), channel_id=1, source_target_pairs={{0,2},{2,0},{1,3},{3,1},{4,6},{6,4},{5,7},{7,5},{8,10},{10,8},{9,1... | collective-permute-start | bytes 688136 | tf_op jit(solution)/shard_map/ppermute | solution.py:328
  86.5 7.3 %collective-permute-start.19 = (bf16[48,896]{1,0:T(8,128)(2,1)S(1)}, bf16[48,896]{1,0:T(8,128)(2,1)S(1)}, u32[]{:S(2)}, u32[]{:S(2)}) collective-permute-start(bf16[48,896]{1,0:T(8,128)(2,1)S(1)} %convolution_convert_fusion), channel_id=1, source_target_pairs={{0,12},{4,8},{8,4},{12,0},{1,13},{5,9},{9,5},{13,1},{2,14},{6,10},... | collective-permute-start | bytes 258056 | tf_op jit(solution)/shard_map/ppermute | solution.py:328
  88.5 7.7 %collective-permute-start.18 = (bf16[48,896]{1,0:T(8,128)(2,1)S(1)}, bf16[48,896]{1,0:T(8,128)(2,1)S(1)}, u32[]{:S(2)}, u32[]{:S(2)}) collective-permute-start(bf16[48,896]{1,0:T(8,128)(2,1)S(1)} %convolution_convert_fusion.1), channel_id=1, source_target_pairs={{0,8},{4,12},{8,0},{12,4},{1,9},{5,13},{9,1},{13,5},{2,10},{6,14},... | collective-permute-start | bytes 258056 | tf_op jit(solution)/shard_map/ppermute | solution.py:328
  88.5 7.7 %collective-permute-start.17 = (bf16[48,896]{1,0:T(8,128)(2,1)S(1)}, bf16[48,896]{1,0:T(8,128)(2,1)S(1)}, u32[]{:S(2)}, u32[]{:S(2)}) collective-permute-start(bf16[48,896]{1,0:T(8,128)(2,1)S(1)} %convolution_convert_fusion.2), channel_id=1, source_target_pairs={{0,4},{4,0},{8,12},{12,8},{1,5},{5,1},{9,13},{13,9},{2,6},{6,2},{1... | collective-permute-start | bytes 258056 | tf_op jit(solution)/shard_map/ppermute | solution.py:328
  96.7 9.8 %collective-permute-start.21 = (bf16[48,3584]{1,0:T(8,128)(2,1)S(1)}, bf16[48,3584]{1,0:T(8,128)(2,1)S(1)}, u32[]{:S(2)}, u32[]{:S(2)}) collective-permute-start(bf16[48,3584]{1,0:T(8,128)(2,1)S(1)} %shard_map.105.refs_0_), channel_id=1, source_target_pairs={{0,2},{2,0},{1,3},{3,1},{4,6},{6,4},{5,7},{7,5},{8,10},{10,8},{9,1... | collective-permute-start | bytes 1032200 | tf_op jit(solution)/shard_map/ppermute | solution.py:328
  100.2 6.2 %collective-permute-start.20 = (bf16[48,3584]{1,0:T(8,128)(2,1)S(1)}, bf16[48,3584]{1,0:T(8,128)(2,1)S(1)}, u32[]{:S(2)}, u32[]{:S(2)}) collective-permute-start(bf16[48,3584]{1,0:T(8,128)(2,1)S(1)} %shard_map.105.refs_0_), channel_id=1, source_target_pairs={{0,1},{1,0},{2,3},{3,2},{4,5},{5,4},{6,7},{7,6},{8,9},{9,8},{10,11... | collective-permute-start | bytes 1032200 | tf_op jit(solution)/shard_map/ppermute | solution.py:328
  106.4 1.7 %collective-permute-start.22 = (bf16[48,3584]{1,0:T(8,128)(2,1)S(1)}, bf16[48,3584]{1,0:T(8,128)(2,1)S(1)}, u32[]{:S(2)}, u32[]{:S(2)}) collective-permute-start(bf16[48,3584]{1,0:T(8,128)(2,1)S(1)} %collective-permute-done.21.refs_2_), channel_id=1, source_target_pairs={{0,1},{1,0},{2,3},{3,2},{4,5},{5,4},{6,7},{7,6},{8,9},{9,8},{10,11... | collective-permute-start | bytes 1032200 | tf_op jit(solution)/shard_map/ppermute | solution.py:328

commit v5 on v4

--- a/solution.py
+++ b/solution.py
@@ -14,6 +14,7 @@
 F32 = jnp.float32
 I32 = jnp.int32
 PARAMS = pltpu.CompilerParams(vmem_limit_bytes=16 * 1024 * 1024)
+NORM_MB = 52
 PAIRWISE = True
 
 
@@ -55,38 +56,52 @@
     )(*args)
 
 
-def norm_kernel(student_ref, gain_ref, owner_ref, docs_ref, *refs):
-    *pieces, inverse_ref, hidden_ref = refs
+def inverse_rms(hidden):
+    width = hidden.shape[1]
+    return lax.rsqrt(jnp.sum(hidden * hidden, axis=1, keepdims=True) / width + 1e-06)
+
+
+def norm_kernel(student_any, small_ref, *refs):
+    *pieces, hidden_ref, arrived = refs
     me, mine = indices()
-    hidden_ref[...] = student_ref[mine]
-    rows, width = hidden_ref.shape
+    copies = [
+        pltpu.make_async_copy(student_any.at[mine ^ (2 * i)], hidden_ref.at[i], arrived.at[i])
+        for i in range(2)
+    ]
+    for copy in copies:
+        copy.start()
+    _, rows, width = hidden_ref.shape
     tiles = width // len(pieces) // LANES
     line = lax.broadcasted_iota(I32, (rows, LANES), 0)
-    owner_row, docs_row = owner_ref[...].astype(F32), docs_ref[...].astype(F32)
+    last = width // LANES
+    owner_row, docs_row = small_ref[last : last + 1, :], small_ref[last + 1 : last + 2, :]
     extra = jnp.where(line == 0, owner_row, jnp.where(line == 1, docs_row, 0.0)).astype(BF)
     for piece in pieces:
         piece[:, tiles * LANES :] = extra
-    hidden = hidden_ref[...].astype(F32)
-    inverse = lax.rsqrt(jnp.sum(hidden * hidden, axis=1, keepdims=True) / width + 1e-06)
-    inverse_ref[...] = inverse
+    copies[0].wait()
+    inverse = inverse_rms(hidden_ref[0].astype(F32))
     for k, piece in enumerate(pieces):
         for tile in range(tiles):
             at = (me ^ k) * tiles + tile
-            block = hidden_ref[:, pl.ds(pl.multiple_of(at * LANES, LANES), LANES)].astype(F32)
-            normed = block * inverse * gain_ref[pl.ds(at, 1), :]
+            columns = pl.ds(pl.multiple_of(at * LANES, LANES), LANES)
+            block = hidden_ref[0, :, columns].astype(F32)
+            normed = block * inverse * small_ref[pl.ds(at, 1), :]
             piece[:, tile * LANES : (tile + 1) * LANES] = normed.astype(BF)
-
-
-def norm_pieces(student, gain, owner, doc_ids):
+    copies[1].wait()
+
+
+def norm_pieces(student, small):
     n, rows, width = student.shape
     piece = jax.ShapeDtypeStruct((rows, width // n + LANES), BF)
     return call(
         norm_kernel,
-        [piece] * n
-        + [jax.ShapeDtypeStruct((rows, 1), F32), jax.ShapeDtypeStruct((rows, width), BF)],
-        (student, gain, owner, doc_ids),
+        [piece] * n + [jax.ShapeDtypeStruct((2, rows, width), BF)],
+        (student, small),
         6 * rows * width,
-        6 * rows * width,
+        8 * rows * width,
+        in_specs=[pl.BlockSpec(memory_space=pl.ANY), pl.BlockSpec(memory_space=pltpu.VMEM)],
+        scratch_shapes=[pltpu.SemaphoreType.DMA((2,))],
+        compiler_params=pltpu.CompilerParams(vmem_limit_bytes=NORM_MB * 1024 * 1024),
     )
 
 
@@ -254,48 +269,50 @@
     )
 
 
-def rows_kernel(hidden_ref, gain_ref, inverse_ref, *refs):
+def rows_kernel(hidden_ref, small_ref, *refs):
     *pieces, out_ref = refs
     me, _ = indices()
-    rows, width = hidden_ref.shape
-    tiles = width // len(pieces) // LANES
-    inverse = inverse_ref[...]
-    total = jnp.zeros((rows, LANES), F32)
-    for k, piece in enumerate(pieces):
-        for tile in range(tiles):
-            at = (me ^ k) * tiles + tile
-            block = hidden_ref[:, pl.ds(pl.multiple_of(at * LANES, LANES), LANES)].astype(F32)
+    blocks, rows, width = hidden_ref.shape
+    n = len(pieces) // blocks
+    tiles = width // n // LANES
+    for i in range(blocks):
+        inverse = inverse_rms(hidden_ref[i].astype(F32))
+        spots = [
+            (piece, tile, (me ^ k) * tiles + tile)
+            for k, piece in enumerate(pieces[i * n : (i + 1) * n])
+            for tile in range(tiles)
+        ]
+        total = jnp.zeros((rows, LANES), F32)
+        for piece, tile, at in spots:
+            columns = pl.ds(pl.multiple_of(at * LANES, LANES), LANES)
+            block = hidden_ref[i, :, columns].astype(F32)
             grad = piece[:, tile * LANES : (tile + 1) * LANES].astype(F32)
-            total = total + grad * gain_ref[pl.ds(at, 1), :] * block
-    mean = jnp.sum(total, axis=1, keepdims=True) / width
-    lean = inverse * inverse * inverse * mean
-    for k, piece in enumerate(pieces):
-        for tile in range(tiles):
-            at = (me ^ k) * tiles + tile
+            total = total + grad * small_ref[pl.ds(at, 1), :] * block
+        mean = jnp.sum(total, axis=1, keepdims=True) / width
+        lean = inverse * inverse * inverse * mean
+        for piece, tile, at in spots:
             columns = pl.ds(pl.multiple_of(at * LANES, LANES), LANES)
-            block = hidden_ref[:, columns].astype(F32)
+            block = hidden_ref[i, :, columns].astype(F32)
             grad = piece[:, tile * LANES : (tile + 1) * LANES].astype(F32)
-            grad = inverse * (grad * gain_ref[pl.ds(at, 1), :]) - lean * block
-            out_ref[:, columns] = grad.astype(BF)
-
-
-def grad_rows(hidden, gain, inverse, pieces):
-    rows, width = hidden.shape
+            grad = inverse * (grad * small_ref[pl.ds(at, 1), :]) - lean * block
+            out_ref[i, :, columns] = grad.astype(BF)
+
+
+def grad_rows(hidden, small, pieces):
     return call(
         rows_kernel,
-        jax.ShapeDtypeStruct((rows, width), BF),
-        (hidden, gain, inverse, *pieces),
-        12 * rows * width,
-        6 * rows * width,
-    )
-
-
-def write_kernel(first, *refs):
-    *blocks, out_ref, done = refs
+        jax.ShapeDtypeStruct(hidden.shape, BF),
+        (hidden, small, *pieces),
+        14 * hidden.size,
+        6 * hidden.size,
+    )
+
+
+def write_kernel(first, pair_ref, out_ref, done):
     _, mine = indices()
     copies = [
-        pltpu.make_async_copy(block, out_ref.at[mine ^ (first + q)], done.at[q])
-        for q, block in enumerate(blocks)
+        pltpu.make_async_copy(pair_ref.at[i], out_ref.at[mine ^ first ^ (2 * i)], done.at[i])
+        for i in range(2)
     ]
     for copy in copies:
         copy.start()
@@ -303,24 +320,24 @@
         copy.wait()
 
 
-def write_rows(blocks, first, target=None):
-    rows, width = blocks[0].shape
+def write_rows(pair, first, target=None):
+    _, rows, width = pair.shape
     hbm, vmem = pl.BlockSpec(memory_space=pltpu.HBM), pl.BlockSpec(memory_space=pltpu.VMEM)
     kernel = functools.partial(write_kernel, first)
-    args, specs, aliases = tuple(blocks), [vmem] * len(blocks), {}
+    args, specs, aliases = (pair,), [vmem], {}
     if target is not None:
         kernel = lambda t, *refs: write_kernel(first, *refs)
-        args, specs, aliases = (target, *args), [hbm] + specs, {0: 0}
+        args, specs, aliases = (target, pair), [hbm, vmem], {0: 0}
     return call(
         kernel,
         jax.ShapeDtypeStruct((4, rows, width), BF),
         args,
         0,
-        4 * len(blocks) * rows * width,
+        4 * pair.size,
         in_specs=specs,
         out_specs=hbm,
         input_output_aliases=aliases,
-        scratch_shapes=[pltpu.SemaphoreType.DMA((len(blocks),))],
+        scratch_shapes=[pltpu.SemaphoreType.DMA((2,))],
     )
 
 
@@ -350,9 +367,13 @@
     capacity, width = student_hidden.shape
     slots = capacity // n
     student = student_hidden.reshape(n, slots, width)
-    gain = norm_gain.reshape(width // LANES, LANES)
-
-    *made, inverse, hidden = norm_pieces(student, gain, owner.T, doc_ids[None, :])
+    tiles = width // LANES
+    line = lax.broadcasted_iota(I32, (tiles + 2, LANES), 0)
+    ids = jnp.where(line == tiles, owner[:, 0][None, :], doc_ids[None, :]).astype(F32)
+    gain = jnp.pad(norm_gain.reshape(tiles, LANES), ((0, 2), (0, 0)))
+    small = jnp.where(line < tiles, gain, ids)
+
+    *made, hidden = norm_pieces(student, small)
     pieces = [made[0]] + exchange(made)
     normed_own, drop = pick_rows(pieces, rows)
 
@@ -368,10 +389,10 @@
     far = swap(normed_own, "mp")
     mate = swap(after(normed_own, parcel), "side")
     parcels = [parcel] + exchange([parcel] * n)
-    far_mate = swap(after(far, mate, *parcels), "side")
+    far_mate = lax.ppermute(normed_own, ("mp", "side"), [(j, j ^ 3) for j in range(n)])
     entries = [far_mate, far, mate, normed_own]
 
-    away = away_partial(entries, proj)
+    away = away_partial([after(e, *parcels) for e in entries], proj)
     own, over_own, normed = kept_partials([after(e, away) for e in entries], proj)
     got_over = after(swap(away, "seq", 1), over_own)
     over = lax.optimization_barrier((over_own + got_over.astype(F32)).astype(BF))
@@ -393,20 +414,18 @@
     cross = lax.optimization_barrier((kept[1].astype(F32) + got[1].astype(F32)).astype(BF))
     crossed = swap(cross, "mp")
     near = lax.optimization_barrier(kept[0].astype(F32) + after(got[0], cross).astype(F32))
-    feature_rows = (near + crossed.astype(F32)).astype(BF)
+
+    factor = 1.0 / math.sqrt(rows * n)
+    deltas = after(jnp.concatenate([deltas[k] for k in (0, 2, 1, 3)]), cross)
+    grad_proj = lax.optimization_barrier(dot(normed, deltas, ((0,), (0,))) * factor)
+    feature_rows = (near + after(crossed, grad_proj).astype(F32)).astype(BF)
+
     leaving = [dot(drop[k * slots : (k + 1) * slots], feature_rows).astype(BF) for k in range(n)]
     arrived = [leaving[0]] + exchange(leaving)
-    grad_own = grad_rows(hidden, gain, inverse, arrived)
-
-    factor = 1.0 / math.sqrt(rows * n)
-    deltas = jnp.concatenate([deltas[k] for k in (0, 2, 1, 3)])
-    grad_proj = lax.optimization_barrier(dot(normed, after(deltas, cross), ((0,), (0,))) * factor)
-
-    grad_mate = swap(grad_own, "side")
-    grad_far = swap(grad_own, "mp")
-    grad_last = swap(after(grad_far, grad_proj), "side")
-    grad_hidden = write_rows([grad_own, grad_mate, grad_far], 0)
-    grad_hidden = write_rows([grad_last], 3, grad_hidden).reshape(capacity, width)
+    across = [swap(block, "mp") for block in arrived]
+    grad_pair = grad_rows(hidden, small, arrived + across)
+    grad_mates = swap(grad_pair, "side")
+    grad_hidden = write_rows(grad_mates, 1, write_rows(grad_pair, 0)).reshape(capacity, width)
     return (grad_hidden, grad_proj)
 
 

time: 109 us -> 106 us (0.972)
  waiting for transfers between devices: 66.1 us -> 61.9 us
  local copies, waits for them, and re-layouts: 4.3 us -> 0.81 us
  starting transfers between devices: 23.8 us -> 26.3 us
  Pallas kernels: 9.71 us -> 11 us
    ppermute x23 -> x24, waiting for transfers between devices: 66.1 us -> 61.9 us  [swap(): lax.ppermute(x, axis, [(i, i ^ k) for i in range(lax.axis_size(axis))])]
    unnamed x14 -> x4, local copies, waits for them, and re-layouts: 3.51 us -> 0.01 us
    ppermute x23 -> x24, starting transfers between devices: 23.8 us -> 26 us  [swap(): lax.ppermute(x, axis, [(i, i ^ k) for i in range(lax.axis_size(axis))])]
    pallas_call x13, Pallas kernels: 9.71 us -> 11 us  [call(): pl.pallas_call(kernel, out_shape=shapes, cost_estimate=pl.CostEstimate(fl...]
  transfers between devices with their start and end apart: 23 -> 25, of which waited for: 18 -> 18; matrix products, arithmetic and copies ran while one was open for 4% -> 4% of each run, Pallas kernels for 6% -> 6%
where the time goes in v5:
time: 106 us
  waiting for transfers between devices  61.9 us (58%)
  starting transfers between devices  26.3 us (25%)
  Pallas kernels  11 us (10%)
  matrix products  3.65 us (3%)
  other arithmetic  1.39 us (1%)
    ppermute x24, waiting for transfers between devices, swap(): lax.ppermute(x, axis, [(i, i ^ k) for i in range(lax.axis_size(axis))])  61.9 us
    ppermute x24, starting transfers between devices, swap(): lax.ppermute(x, axis, [(i, i ^ k) for i in range(lax.axis_size(axis))])  26 us
    pallas_call x13, Pallas kernels, call(): pl.pallas_call(kernel, out_shape=shapes, cost_estimate=pl.CostEstimate(fl...  11 us
    dot_general x5, matrix products, dot(): return lax.dot_general(a, b, (dims, ((), ())), preferred_element_type=F32)  3.65 us
  transfers between devices with their start and end apart: 25, of which 18 were waited for; matrix products, arithmetic and copies ran while one was open for 4% of the time, Pallas kernels for 6%

profile of v5, /device:TPU:0, one launch (start us, length us, event | category | flops | bytes accessed | tf_op | source)
XLA Modules:
  0.0 105.8 jit_solution(9863234634582907072)
XLA Ops:
  0.7 0.9 convert_select_fusion.small_ref
  1.6 1.2 %shard_map.95 = (bf16[48,1024]{1,0:T(8,128)(2,1)S(1)}, bf16[48,1024]{1,0:T(8,128)(2,1)S(1)}, bf16[48,1024]{1,0:T(8,128)(2,1)S(1)}, bf16[48,1024]{1,0:T(8,128)(2,1)S(1)}, bf16[2,48,3584]{2,1,0:T(8,128)(2,1)S(1)}) custom-call(bf16[4,48,3584]{2,1,0:T(8,128)(2,1)} %bitcast.18, f32[30,128]{1,0:T(8,128)S(1)} %convert_select_fusion.small_ref), custom_call_target="tpu_custom_call" | custom-call | flops 1032192 | bytes 1376256 | tf_op jit(solution)/shard_map/pallas_call | solution.py:49
  2.8 5.1 %collective-permute-start = (bf16[48,1024]{1,0:T(8,128)(2,1)S(1)}, bf16[48,1024]{1,0:T(8,128)(2,1)S(1)}, u32[]{:S(2)}, u32[]{:S(2)}) collective-permute-start(bf16[48,1024]{1,0:T(8,128)(2,1)S(1)} %get-tuple-element.32), channel_id=1, source_target_pairs={{0,12},{4,8},{8,4},{12,0},{1,13},{5,9},{9,5},{13,1},{2,14},{6,10},... | collective-permute-start | bytes 294920 | tf_op jit(solution)/shard_map/ppermute | solution.py:345
  7.9 0.6 collective-permute-start.2
  8.6 0.8 constant_dynamic-slice_fusion
  9.4 2.3 %collective-permute-done.refs_0_.refs_7_ = bf16[48,1024]{1,0:T(8,128)(2,1)S(1)} collective-permute-done((bf16[48,1024]{1,0:T(8,128)(2,1)S(1)}, bf16[48,1024]{1,0:T(8,128)(2,1)S(1)}, u32[]{:S(2)}, u32[]{:S(2)}) %collective-permute-start) | collective-permute-done | bytes 98336 | tf_op jit(solution)/shard_map/ppermute | solution.py:345
  11.6 4.6 %collective-permute-done.1.refs_1_.refs_6_ = bf16[48,1024]{1,0:T(8,128)(2,1)S(1)} collective-permute-done((bf16[48,1024]{1,0:T(8,128)(2,1)S(1)}, bf16[48,1024]{1,0:T(8,128)(2,1)S(1)}, u32[]{:S(2)}, u32[]{:S(2)}) %collective-permute-start.1) | collective-permute-done | bytes 98336 | tf_op jit(solution)/shard_map/ppermute | solution.py:345
  16.2 0.4 shard_map.96
  16.6 0.1 collective-permute-start.8
  16.7 1.6 %collective-permute-start.7 = (bf16[128,896]{1,0:T(8,128)(2,1)S(1)}, bf16[128,896]{1,0:T(8,128)(2,1)S(1)}, u32[]{:S(2)}, u32[]{:S(2)}) collective-permute-start(bf16[128,896]{1,0:T(8,128)(2,1)S(1)} %get-tuple-element.47.refs_3_), channel_id=1, source_target_pairs={{0,2},{2,0},{1,3},{3,1},{4,6},{6,4},{5,7},{7,5},{8,10},{10,8},{9,1... | collective-permute-start | bytes 688136 | tf_op jit(solution)/shard_map/ppermute | solution.py:345
  18.2 0.3 collective-permute-start.3
  18.5 2.5 %collective-permute-start.6 = (bf16[256,128]{1,0:T(8,128)(2,1)S(1)}, bf16[256,128]{1,0:T(8,128)(2,1)S(1)}, u32[]{:S(2)}, u32[]{:S(2)}) collective-permute-start(bf16[256,128]{1,0:T(8,128)(2,1)S(1)} %pad_maximum_fusion.1.refs_0_), channel_id=1, source_target_pairs={{0,12},{4,8},{8,4},{12,0},{1,13},{5,9},{9,5},{13,1},{2,14},{6,10},... | collective-permute-start | bytes 196616 | tf_op jit(solution)/shard_map/ppermute | solution.py:345
  21.1 4.2 %collective-permute-done.6.refs_3_ = bf16[256,128]{1,0:T(8,128)(2,1)S(1)} collective-permute-done((bf16[256,128]{1,0:T(8,128)(2,1)S(1)}, bf16[256,128]{1,0:T(8,128)(2,1)S(1)}, u32[]{:S(2)}, u32[]{:S(2)}) %collective-permute-start.6) | collective-permute-done | bytes 65568 | tf_op jit(solution)/shard_map/ppermute | solution.py:345
  25.3 2.2 %collective-permute-done.5.refs_2_ = bf16[256,128]{1,0:T(8,128)(2,1)S(1)} collective-permute-done((bf16[256,128]{1,0:T(8,128)(2,1)S(1)}, bf16[256,128]{1,0:T(8,128)(2,1)S(1)}, u32[]{:S(2)}, u32[]{:S(2)}) %collective-permute-start.5) | collective-permute-done | bytes 65568 | tf_op jit(solution)/shard_map/ppermute | solution.py:345
  27.6 2.0 %collective-permute-done.4.refs_1_ = bf16[256,128]{1,0:T(8,128)(2,1)S(1)} collective-permute-done((bf16[256,128]{1,0:T(8,128)(2,1)S(1)}, bf16[256,128]{1,0:T(8,128)(2,1)S(1)}, u32[]{:S(2)}, u32[]{:S(2)}) %collective-permute-start.4) | collective-permute-done | bytes 65568 | tf_op jit(solution)/shard_map/ppermute | solution.py:345
  29.6 0.5 shard_map.97
  30.1 0.2 collective-permute-start.9
  30.2 0.9 shard_map.98
  31.1 7.3 %collective-permute-done.9 = bf16[128,1024]{1,0:T(8,128)(2,1)S(1)} collective-permute-done((bf16[128,1024]{1,0:T(8,128)(2,1)S(1)}, bf16[128,1024]{1,0:T(8,128)(2,1)S(1)}, u32[]{:S(2)}, u32[]{:S(2)}) %collective-permute-start.9) | collective-permute-done | bytes 262176 | tf_op jit(solution)/shard_map/ppermute | solution.py:345
  38.4 0.1 add_convert_fusion
  38.5 1.4 %collective-permute-start.10 = (bf16[128,1024]{1,0:T(8,128)(2,1)S(1)}, bf16[128,1024]{1,0:T(8,128)(2,1)S(1)}, u32[]{:S(2)}, u32[]{:S(2)}) collective-permute-start(bf16[128,1024]{1,0:T(8,128)(2,1)S(1)} %add_convert_fusion), channel_id=1, source_target_pairs={{0,8},{4,12},{8,0},{12,4},{1,9},{5,13},{9,1},{13,5},{2,10},{6,14},... | collective-permute-start | bytes 786440 | tf_op jit(solution)/shard_map/ppermute | solution.py:345
  39.9 0.4 shard_map.99
  40.4 1.8 %collective-permute-start.11 = (bf16[128,1024]{1,0:T(8,128)(2,1)S(1)}, bf16[128,1024]{1,0:T(8,128)(2,1)S(1)}, u32[]{:S(2)}, u32[]{:S(2)}) collective-permute-start(bf16[128,1024]{1,0:T(8,128)(2,1)S(1)} %shard_map.99), channel_id=1, source_target_pairs={{0,4},{4,0},{8,12},{12,8},{1,5},{5,1},{9,13},{13,9},{2,6},{6,2},{1... | collective-permute-start | bytes 786440 | tf_op jit(solution)/shard_map/ppermute | solution.py:345
  42.2 2.3 %shard_map.100 = bf16[128,1024]{1,0:T(8,128)(2,1)S(1)} custom-call(bf16[128,1024]{1,0:T(8,128)(2,1)S(1)} %copy-done.1, bf16[256,128]{1,0:T(8,128)(2,1)S(1)} %pad_maximum_fusion.1.refs_0_, bf16[256,128]{1,0:T(8,128)(2,1)S(1)} %collective-permute-done.4.refs_1_, bf16[256,128]{1,0:T(8,128)(2,1)S(1)} %collective-permute-done.5.refs_2_, ...), custom_call_target="tpu_custom_call" | custom-call | bytes 524288 | tf_op jit(solution)/shard_map/pallas_call | solution.py:49
  44.5 8.1 %collective-permute-done.10 = bf16[128,1024]{1,0:T(8,128)(2,1)S(1)} collective-permute-done((bf16[128,1024]{1,0:T(8,128)(2,1)S(1)}, bf16[128,1024]{1,0:T(8,128)(2,1)S(1)}, u32[]{:S(2)}, u32[]{:S(2)}) %collective-permute-start.10) | collective-permute-done | bytes 262176 | tf_op jit(solution)/shard_map/ppermute | solution.py:345
  52.6 0.1 convert_add_fusion
  52.7 0.8 collective-permute-done.11
  53.5 0.1 subtract_convert_fusion.delta_ref
  53.6 0.1 collective-permute-start.13
  53.7 0.7 shard_map.101.first_ref
  54.4 2.3 %collective-permute-start.12 = (bf16[128,1024]{1,0:T(8,128)(2,1)S(1)}, bf16[128,1024]{1,0:T(8,128)(2,1)S(1)}, u32[]{:S(2)}, u32[]{:S(2)}) collective-permute-start(bf16[128,1024]{1,0:T(8,128)(2,1)S(1)} %subtract_convert_fusion.delta_ref), channel_id=1, source_target_pairs={{0,4},{4,0},{8,12},{12,8},{1,5},{5,1},{9,13},{13,9},{2,6},{6,2},{1... | collective-permute-start | bytes 786440 | tf_op jit(solution)/shard_map/ppermute | solution.py:345
  56.7 10.8 %collective-permute-done.13.delta_ref = bf16[128,1024]{1,0:T(8,128)(2,1)S(1)} collective-permute-done((bf16[128,1024]{1,0:T(8,128)(2,1)S(1)}, bf16[128,1024]{1,0:T(8,128)(2,1)S(1)}, u32[]{:S(2)}, u32[]{:S(2)}) %collective-permute-start.13) | collective-permute-done | bytes 262176 | tf_op jit(solution)/shard_map/ppermute | solution.py:345
  67.5 0.7 shard_map.103.third_ref
  68.2 0.1 collective-permute-done.12.delta_ref
  68.4 0.7 shard_map.102.second_ref
  69.1 6.6 %collective-permute-done.14.delta_ref = bf16[128,1024]{1,0:T(8,128)(2,1)S(1)} collective-permute-done((bf16[128,1024]{1,0:T(8,128)(2,1)S(1)}, bf16[128,1024]{1,0:T(8,128)(2,1)S(1)}, u32[]{:S(2)}, u32[]{:S(2)}) %collective-permute-start.14) | collective-permute-done | bytes 262176 | tf_op jit(solution)/shard_map/ppermute | solution.py:345
  75.7 0.8 shard_map.104
  76.5 0.1 collective-permute-start.15
  76.5 0.1 pad_maximum_fusion
  76.6 1.7 %collective-permute-done.15 = bf16[2,128,896]{2,1,0:T(8,128)(2,1)S(1)} collective-permute-done((bf16[2,128,896]{2,1,0:T(8,128)(2,1)S(1)}, bf16[2,128,896]{2,1,0:T(8,128)(2,1)S(1)}, u32[]{:S(2)}, u32[]{:S(2)}) %collective-permute-start.15) | collective-permute-done | bytes 458784 | tf_op jit(solution)/shard_map/ppermute | solution.py:345
  78.3 0.1 fusion
  78.4 1.6 %collective-permute-start.16 = (bf16[128,896]{1,0:T(8,128)(2,1)S(1)}, bf16[128,896]{1,0:T(8,128)(2,1)S(1)}, u32[]{:S(2)}, u32[]{:S(2)}) collective-permute-start(bf16[128,896]{1,0:T(8,128)(2,1)S(1)} %fusion), channel_id=1, source_target_pairs={{0,2},{2,0},{1,3},{3,1},{4,6},{6,4},{5,7},{7,5},{8,10},{10,8},{9,1... | collective-permute-start | bytes 688136 | tf_op jit(solution)/shard_map/ppermute | solution.py:345
  80.0 3.0 %convolution_multiply_fusion = f32[896,1024]{1,0:T(8,128)} fusion(bf16[512,896]{1,0:T(8,128)(2,1)S(1)} %get-tuple-element.52.normed_ref, bf16[512,1024]{1,0:T(8,128)(2,1)S(1)} %pad_maximum_fusion), kind=kOutput, calls=%fused_computation | convolution fusion | flops 940441600 | bytes 5636096 | tf_op jit(solution)/shard_map/dot_general | solution.py:22
  83.0 3.1 %collective-permute-done.16 = bf16[128,896]{1,0:T(8,128)(2,1)S(1)} collective-permute-done((bf16[128,896]{1,0:T(8,128)(2,1)S(1)}, bf16[128,896]{1,0:T(8,128)(2,1)S(1)}, u32[]{:S(2)}, u32[]{:S(2)}) %collective-permute-start.16) | collective-permute-done | bytes 229408 | tf_op jit(solution)/shard_map/ppermute | solution.py:345
  86.2 0.2 convolution_convert_fusion
  86.3 0.2 convolution_convert_fusion.1
  86.5 0.2 convolution_convert_fusion.2
  86.7 0.4 collective-permute-start.17
  87.1 1.6 %collective-permute-start.18 = (bf16[48,896]{1,0:T(8,128)(2,1)S(1)}, bf16[48,896]{1,0:T(8,128)(2,1)S(1)}, u32[]{:S(2)}, u32[]{:S(2)}) collective-permute-start(bf16[48,896]{1,0:T(8,128)(2,1)S(1)} %convolution_convert_fusion.1), channel_id=1, source_target_pairs={{0,8},{4,12},{8,0},{12,4},{1,9},{5,13},{9,1},{13,5},{2,10},{6,14},... | collective-permute-start | bytes 258056 | tf_op jit(solution)/shard_map/ppermute | solution.py:345
  88.6 2.5 %collective-permute-start.19 = (bf16[48,896]{1,0:T(8,128)(2,1)S(1)}, bf16[48,896]{1,0:T(8,128)(2,1)S(1)}, u32[]{:S(2)}, u32[]{:S(2)}) collective-permute-start(bf16[48,896]{1,0:T(8,128)(2,1)S(1)} %convolution_convert_fusion), channel_id=1, source_target_pairs={{0,12},{4,8},{8,4},{12,0},{1,13},{5,9},{9,5},{13,1},{2,14},{6,10},... | collective-permute-start | bytes 258056 | tf_op jit(solution)/shard_map/ppermute | solution.py:345
  91.2 0.2 convolution_convert_fusion.3.refs_0_
  91.3 1.6 %collective-permute-start.20 = (bf16[48,896]{1,0:T(8,128)(2,1)S(1)}, bf16[48,896]{1,0:T(8,128)(2,1)S(1)}, u32[]{:S(2)}, u32[]{:S(2)}) collective-permute-start(bf16[48,896]{1,0:T(8,128)(2,1)S(1)} %convolution_convert_fusion.3.refs_0_), channel_id=1, source_target_pairs={{0,2},{2,0},{1,3},{3,1},{4,6},{6,4},{5,7},{7,5},{8,10},{10,8},{9,1... | collective-permute-start | bytes 258056 | tf_op jit(solution)/shard_map/ppermute | solution.py:345
  92.9 0.5 collective-permute-start.21
  93.4 2.7 %collective-permute-done.18.refs_2_ = bf16[48,896]{1,0:T(8,128)(2,1)S(1)} collective-permute-done((bf16[48,896]{1,0:T(8,128)(2,1)S(1)}, bf16[48,896]{1,0:T(8,128)(2,1)S(1)}, u32[]{:S(2)}, u32[]{:S(2)}) %collective-permute-start.18) | collective-permute-done | bytes 86048 | tf_op jit(solution)/shard_map/ppermute | solution.py:345
  96.1 1.5 %collective-permute-start.22 = (bf16[48,896]{1,0:T(8,128)(2,1)S(1)}, bf16[48,896]{1,0:T(8,128)(2,1)S(1)}, u32[]{:S(2)}, u32[]{:S(2)}) collective-permute-start(bf16[48,896]{1,0:T(8,128)(2,1)S(1)} %collective-permute-done.18.refs_2_), channel_id=1, source_target_pairs={{0,2},{2,0},{1,3},{3,1},{4,6},{6,4},{5,7},{7,5},{8,10},{10,8},{9,1... | collective-permute-start | bytes 258056 | tf_op jit(solution)/shard_map/ppermute | solution.py:345
  97.6 0.5 collective-permute-start.23
  98.1 0.1 collective-permute-done.21.refs_5_
  98.3 2.3 %collective-permute-done.22.refs_6_ = bf16[48,896]{1,0:T(8,128)(2,1)S(1)} collective-permute-done((bf16[48,896]{1,0:T(8,128)(2,1)S(1)}, bf16[48,896]{1,0:T(8,128)(2,1)S(1)}, u32[]{:S(2)}, u32[]{:S(2)}) %collective-permute-start.22) | collective-permute-done | bytes 86048 | tf_op jit(solution)/shard_map/ppermute | solution.py:345
  100.6 1.5 %collective-permute-done.23.refs_7_ = bf16[48,896]{1,0:T(8,128)(2,1)S(1)} collective-permute-done((bf16[48,896]{1,0:T(8,128)(2,1)S(1)}, bf16[48,896]{1,0:T(8,128)(2,1)S(1)}, u32[]{:S(2)}, u32[]{:S(2)}) %collective-permute-start.23) | collective-permute-done | bytes 86048 | tf_op jit(solution)/shard_map/ppermute | solution.py:345
  102.1 0.7 shard_map.105.pair_ref
  102.8 0.1 collective-permute-start.24
  102.9 0.9 shard_map.106.t
  103.7 1.3 %collective-permute-done.24.refs_0_ = bf16[2,48,3584]{2,1,0:T(8,128)(2,1)S(1)} collective-permute-done((bf16[2,48,3584]{2,1,0:T(8,128)(2,1)S(1)}, bf16[2,48,3584]{2,1,0:T(8,128)(2,1)S(1)}, u32[]{:S(2)}, u32[]{:S(2)}) %collective-permute-start.24) | collective-permute-done | bytes 688160 | tf_op jit(solution)/shard_map/ppermute | solution.py:345
  105.0 0.9 shard_map.107
  (20 shorter events, 0.2 us)
Async XLA Ops:
  0.6 29.0 %copy-start = (bf16[896,1024]{1,0:T(8,128)(2,1)S(1)}, bf16[896,1024]{1,0:T(8,128)(2,1)}, u32[]{:S(2)}) copy-start(bf16[896,1024]{1,0:T(8,128)(2,1)} %proj_ref.9) | copy-start | bytes 5505028
  2.8 8.8 %collective-permute-start = (bf16[48,1024]{1,0:T(8,128)(2,1)S(1)}, bf16[48,1024]{1,0:T(8,128)(2,1)S(1)}, u32[]{:S(2)}, u32[]{:S(2)}) collective-permute-start(bf16[48,1024]{1,0:T(8,128)(2,1)S(1)} %get-tuple-element.32), channel_id=1, source_target_pairs={{0,12},{4,8},{8,4},{12,0},{1,13},{5,9},{9,5},{13,1},{2,14},{6,10},... | collective-permute-start | bytes 294920 | tf_op jit(solution)/shard_map/ppermute | solution.py:345
  7.9 8.3 %collective-permute-start.1 = (bf16[48,1024]{1,0:T(8,128)(2,1)S(1)}, bf16[48,1024]{1,0:T(8,128)(2,1)S(1)}, u32[]{:S(2)}, u32[]{:S(2)}) collective-permute-start(bf16[48,1024]{1,0:T(8,128)(2,1)S(1)} %get-tuple-element.33), channel_id=1, source_target_pairs={{0,8},{4,12},{8,0},{12,4},{1,9},{5,13},{9,1},{13,5},{2,10},{6,14},... | collective-permute-start | bytes 294920 | tf_op jit(solution)/shard_map/ppermute | solution.py:345
  7.9 8.3 %collective-permute-start.2 = (bf16[48,1024]{1,0:T(8,128)(2,1)S(1)}, bf16[48,1024]{1,0:T(8,128)(2,1)S(1)}, u32[]{:S(2)}, u32[]{:S(2)}) collective-permute-start(bf16[48,1024]{1,0:T(8,128)(2,1)S(1)} %get-tuple-element.34), channel_id=1, source_target_pairs={{0,4},{4,0},{8,12},{12,8},{1,5},{5,1},{9,13},{13,9},{2,6},{6,2},{1... | collective-permute-start | bytes 294920 | tf_op jit(solution)/shard_map/ppermute | solution.py:345
  16.6 13.0 %collective-permute-start.8 = (bf16[128,896]{1,0:T(8,128)(2,1)S(1)}, bf16[128,896]{1,0:T(8,128)(2,1)S(1)}, u32[]{:S(2)}, u32[]{:S(2)}) collective-permute-start(bf16[128,896]{1,0:T(8,128)(2,1)S(1)} %get-tuple-element.47.refs_3_), channel_id=1, source_target_pairs={{0,1},{1,0},{2,3},{3,2},{4,5},{5,4},{6,7},{7,6},{8,9},{9,8},{10,11... | collective-permute-start | bytes 688136 | tf_op jit(solution)/shard_map/ppermute | solution.py:345
  16.7 12.9 %collective-permute-start.7 = (bf16[128,896]{1,0:T(8,128)(2,1)S(1)}, bf16[128,896]{1,0:T(8,128)(2,1)S(1)}, u32[]{:S(2)}, u32[]{:S(2)}) collective-permute-start(bf16[128,896]{1,0:T(8,128)(2,1)S(1)} %get-tuple-element.47.refs_3_), channel_id=1, source_target_pairs={{0,2},{2,0},{1,3},{3,1},{4,6},{6,4},{5,7},{7,5},{8,10},{10,8},{9,1... | collective-permute-start | bytes 688136 | tf_op jit(solution)/shard_map/ppermute | solution.py:345
  18.2 11.4 %collective-permute-start.3 = (bf16[128,896]{1,0:T(8,128)(2,1)S(1)}, bf16[128,896]{1,0:T(8,128)(2,1)S(1)}, u32[]{:S(2)}, u32[]{:S(2)}) collective-permute-start(bf16[128,896]{1,0:T(8,128)(2,1)S(1)} %get-tuple-element.47.refs_3_), channel_id=1, source_target_pairs={{0,3},{1,2},{2,1},{3,0},{4,7},{5,6},{6,5},{7,4},{8,11},{9,10},{10,... | collective-permute-start | bytes 688136 | tf_op jit(solution)/shard_map/ppermute | solution.py:392
  18.5 6.8 %collective-permute-start.6 = (bf16[256,128]{1,0:T(8,128)(2,1)S(1)}, bf16[256,128]{1,0:T(8,128)(2,1)S(1)}, u32[]{:S(2)}, u32[]{:S(2)}) collective-permute-start(bf16[256,128]{1,0:T(8,128)(2,1)S(1)} %pad_maximum_fusion.1.refs_0_), channel_id=1, source_target_pairs={{0,12},{4,8},{8,4},{12,0},{1,13},{5,9},{9,5},{13,1},{2,14},{6,10},... | collective-permute-start | bytes 196616 | tf_op jit(solution)/shard_map/ppermute | solution.py:345
  21.1 6.5 %collective-permute-start.5 = (bf16[256,128]{1,0:T(8,128)(2,1)S(1)}, bf16[256,128]{1,0:T(8,128)(2,1)S(1)}, u32[]{:S(2)}, u32[]{:S(2)}) collective-permute-start(bf16[256,128]{1,0:T(8,128)(2,1)S(1)} %pad_maximum_fusion.1.refs_0_), channel_id=1, source_target_pairs={{0,8},{4,12},{8,0},{12,4},{1,9},{5,13},{9,1},{13,5},{2,10},{6,14},... | collective-permute-start | bytes 196616 | tf_op jit(solution)/shard_map/ppermute | solution.py:345
  25.3 4.3 %collective-permute-start.4 = (bf16[256,128]{1,0:T(8,128)(2,1)S(1)}, bf16[256,128]{1,0:T(8,128)(2,1)S(1)}, u32[]{:S(2)}, u32[]{:S(2)}) collective-permute-start(bf16[256,128]{1,0:T(8,128)(2,1)S(1)} %pad_maximum_fusion.1.refs_0_), channel_id=1, source_target_pairs={{0,4},{4,0},{8,12},{12,8},{1,5},{5,1},{9,13},{13,9},{2,6},{6,2},{1... | collective-permute-start | bytes 196616 | tf_op jit(solution)/shard_map/ppermute | solution.py:345
  30.1 8.4 %collective-permute-start.9 = (bf16[128,1024]{1,0:T(8,128)(2,1)S(1)}, bf16[128,1024]{1,0:T(8,128)(2,1)S(1)}, u32[]{:S(2)}, u32[]{:S(2)}) collective-permute-start(bf16[128,1024]{1,0:T(8,128)(2,1)S(1)} %shard_map.97), channel_id=1, source_target_pairs={{0,4},{4,0},{8,12},{12,8},{1,5},{5,1},{9,13},{13,9},{2,6},{6,2},{1... | collective-permute-start | bytes 786440 | tf_op jit(solution)/shard_map/ppermute | solution.py:345
  31.1 11.1 %copy-start.1 = (bf16[128,1024]{1,0:T(8,128)(2,1)S(1)}, bf16[128,1024]{1,0:T(8,128)(2,1)}, u32[]{:S(2)}) copy-start(bf16[128,1024]{1,0:T(8,128)(2,1)} %queries_ref) | copy-start | bytes 786436
  38.5 14.1 %collective-permute-start.10 = (bf16[128,1024]{1,0:T(8,128)(2,1)S(1)}, bf16[128,1024]{1,0:T(8,128)(2,1)S(1)}, u32[]{:S(2)}, u32[]{:S(2)}) collective-permute-start(bf16[128,1024]{1,0:T(8,128)(2,1)S(1)} %add_convert_fusion), channel_id=1, source_target_pairs={{0,8},{4,12},{8,0},{12,4},{1,9},{5,13},{9,1},{13,5},{2,10},{6,14},... | collective-permute-start | bytes 786440 | tf_op jit(solution)/shard_map/ppermute | solution.py:345
  40.4 13.1 %collective-permute-start.11 = (bf16[128,1024]{1,0:T(8,128)(2,1)S(1)}, bf16[128,1024]{1,0:T(8,128)(2,1)S(1)}, u32[]{:S(2)}, u32[]{:S(2)}) collective-permute-start(bf16[128,1024]{1,0:T(8,128)(2,1)S(1)} %shard_map.99), channel_id=1, source_target_pairs={{0,4},{4,0},{8,12},{12,8},{1,5},{5,1},{9,13},{13,9},{2,6},{6,2},{1... | collective-permute-start | bytes 786440 | tf_op jit(solution)/shard_map/ppermute | solution.py:345
  53.6 13.9 %collective-permute-start.13 = (bf16[128,1024]{1,0:T(8,128)(2,1)S(1)}, bf16[128,1024]{1,0:T(8,128)(2,1)S(1)}, u32[]{:S(2)}, u32[]{:S(2)}) collective-permute-start(bf16[128,1024]{1,0:T(8,128)(2,1)S(1)} %subtract_convert_fusion.delta_ref), channel_id=1, source_target_pairs={{0,8},{4,12},{8,0},{12,4},{1,9},{5,13},{9,1},{13,5},{2,10},{6,14},... | collective-permute-start | bytes 786440 | tf_op jit(solution)/shard_map/ppermute | solution.py:345
  54.4 14.0 %collective-permute-start.12 = (bf16[128,1024]{1,0:T(8,128)(2,1)S(1)}, bf16[128,1024]{1,0:T(8,128)(2,1)S(1)}, u32[]{:S(2)}, u32[]{:S(2)}) collective-permute-start(bf16[128,1024]{1,0:T(8,128)(2,1)S(1)} %subtract_convert_fusion.delta_ref), channel_id=1, source_target_pairs={{0,4},{4,0},{8,12},{12,8},{1,5},{5,1},{9,13},{13,9},{2,6},{6,2},{1... | collective-permute-start | bytes 786440 | tf_op jit(solution)/shard_map/ppermute | solution.py:345
  67.5 8.2 %collective-permute-start.14 = (bf16[128,1024]{1,0:T(8,128)(2,1)S(1)}, bf16[128,1024]{1,0:T(8,128)(2,1)S(1)}, u32[]{:S(2)}, u32[]{:S(2)}) collective-permute-start(bf16[128,1024]{1,0:T(8,128)(2,1)S(1)} %collective-permute-done.13.delta_ref), channel_id=1, source_target_pairs={{0,4},{4,0},{8,12},{12,8},{1,5},{5,1},{9,13},{13,9},{2,6},{6,2},{1... | collective-permute-start | bytes 786440 | tf_op jit(solution)/shard_map/ppermute | solution.py:345
  76.5 1.9 %collective-permute-start.15 = (bf16[2,128,896]{2,1,0:T(8,128)(2,1)S(1)}, bf16[2,128,896]{2,1,0:T(8,128)(2,1)S(1)}, u32[]{:S(2)}, u32[]{:S(2)}) collective-permute-start(bf16[2,128,896]{2,1,0:T(8,128)(2,1)S(1)} %get-tuple-element.56), channel_id=1, source_target_pairs={{0,1},{1,0},{2,3},{3,2},{4,5},{5,4},{6,7},{7,6},{8,9},{9,8},{10,11... | collective-permute-start | bytes 1376264 | tf_op jit(solution)/shard_map/ppermute | solution.py:345
  78.4 7.7 %collective-permute-start.16 = (bf16[128,896]{1,0:T(8,128)(2,1)S(1)}, bf16[128,896]{1,0:T(8,128)(2,1)S(1)}, u32[]{:S(2)}, u32[]{:S(2)}) collective-permute-start(bf16[128,896]{1,0:T(8,128)(2,1)S(1)} %fusion), channel_id=1, source_target_pairs={{0,2},{2,0},{1,3},{3,1},{4,6},{6,4},{5,7},{7,5},{8,10},{10,8},{9,1... | collective-permute-start | bytes 688136 | tf_op jit(solution)/shard_map/ppermute | solution.py:345
  86.7 6.2 %collective-permute-start.17 = (bf16[48,896]{1,0:T(8,128)(2,1)S(1)}, bf16[48,896]{1,0:T(8,128)(2,1)S(1)}, u32[]{:S(2)}, u32[]{:S(2)}) collective-permute-start(bf16[48,896]{1,0:T(8,128)(2,1)S(1)} %convolution_convert_fusion.2), channel_id=1, source_target_pairs={{0,4},{4,0},{8,12},{12,8},{1,5},{5,1},{9,13},{13,9},{2,6},{6,2},{1... | collective-permute-start | bytes 258056 | tf_op jit(solution)/shard_map/ppermute | solution.py:345
  87.1 9.0 %collective-permute-start.18 = (bf16[48,896]{1,0:T(8,128)(2,1)S(1)}, bf16[48,896]{1,0:T(8,128)(2,1)S(1)}, u32[]{:S(2)}, u32[]{:S(2)}) collective-permute-start(bf16[48,896]{1,0:T(8,128)(2,1)S(1)} %convolution_convert_fusion.1), channel_id=1, source_target_pairs={{0,8},{4,12},{8,0},{12,4},{1,9},{5,13},{9,1},{13,5},{2,10},{6,14},... | collective-permute-start | bytes 258056 | tf_op jit(solution)/shard_map/ppermute | solution.py:345
  88.6 8.9 %collective-permute-start.19 = (bf16[48,896]{1,0:T(8,128)(2,1)S(1)}, bf16[48,896]{1,0:T(8,128)(2,1)S(1)}, u32[]{:S(2)}, u32[]{:S(2)}) collective-permute-start(bf16[48,896]{1,0:T(8,128)(2,1)S(1)} %convolution_convert_fusion), channel_id=1, source_target_pairs={{0,12},{4,8},{8,4},{12,0},{1,13},{5,9},{9,5},{13,1},{2,14},{6,10},... | collective-permute-start | bytes 258056 | tf_op jit(solution)/shard_map/ppermute | solution.py:345
  91.3 6.8 %collective-permute-start.20 = (bf16[48,896]{1,0:T(8,128)(2,1)S(1)}, bf16[48,896]{1,0:T(8,128)(2,1)S(1)}, u32[]{:S(2)}, u32[]{:S(2)}) collective-permute-start(bf16[48,896]{1,0:T(8,128)(2,1)S(1)} %convolution_convert_fusion.3.refs_0_), channel_id=1, source_target_pairs={{0,2},{2,0},{1,3},{3,1},{4,6},{6,4},{5,7},{7,5},{8,10},{10,8},{9,1... | collective-permute-start | bytes 258056 | tf_op jit(solution)/shard_map/ppermute | solution.py:345
  92.9 5.4 %collective-permute-start.21 = (bf16[48,896]{1,0:T(8,128)(2,1)S(1)}, bf16[48,896]{1,0:T(8,128)(2,1)S(1)}, u32[]{:S(2)}, u32[]{:S(2)}) collective-permute-start(bf16[48,896]{1,0:T(8,128)(2,1)S(1)} %collective-permute-done.17.refs_1_), channel_id=1, source_target_pairs={{0,2},{2,0},{1,3},{3,1},{4,6},{6,4},{5,7},{7,5},{8,10},{10,8},{9,1... | collective-permute-start | bytes 258056 | tf_op jit(solution)/shard_map/ppermute | solution.py:345
  96.1 4.5 %collective-permute-start.22 = (bf16[48,896]{1,0:T(8,128)(2,1)S(1)}, bf16[48,896]{1,0:T(8,128)(2,1)S(1)}, u32[]{:S(2)}, u32[]{:S(2)}) collective-permute-start(bf16[48,896]{1,0:T(8,128)(2,1)S(1)} %collective-permute-done.18.refs_2_), channel_id=1, source_target_pairs={{0,2},{2,0},{1,3},{3,1},{4,6},{6,4},{5,7},{7,5},{8,10},{10,8},{9,1... | collective-permute-start | bytes 258056 | tf_op jit(solution)/shard_map/ppermute | solution.py:345
  97.6 4.5 %collective-permute-start.23 = (bf16[48,896]{1,0:T(8,128)(2,1)S(1)}, bf16[48,896]{1,0:T(8,128)(2,1)S(1)}, u32[]{:S(2)}, u32[]{:S(2)}) collective-permute-start(bf16[48,896]{1,0:T(8,128)(2,1)S(1)} %collective-permute-done.19.refs_3_), channel_id=1, source_target_pairs={{0,2},{2,0},{1,3},{3,1},{4,6},{6,4},{5,7},{7,5},{8,10},{10,8},{9,1... | collective-permute-start | bytes 258056 | tf_op jit(solution)/shard_map/ppermute | solution.py:345
  102.8 2.2 %collective-permute-start.24 = (bf16[2,48,3584]{2,1,0:T(8,128)(2,1)S(1)}, bf16[2,48,3584]{2,1,0:T(8,128)(2,1)S(1)}, u32[]{:S(2)}, u32[]{:S(2)}) collective-permute-start(bf16[2,48,3584]{2,1,0:T(8,128)(2,1)S(1)} %shard_map.105.pair_ref), channel_id=1, source_target_pairs={{0,1},{1,0},{2,3},{3,2},{4,5},{5,4},{6,7},{7,6},{8,9},{9,8},{10,11... | collective-permute-start | bytes 2064392 | tf_op jit(solution)/shard_map/ppermute | solution.py:345

commit v6 on v5

--- a/solution.py
+++ b/solution.py
@@ -159,8 +159,10 @@
     within = lax.broadcasted_iota(I32, (tokens, tokens), 1)
     masks = []
     for k in range(n):
-        near = (me ^ k) * tokens + within <= query_pos
-        masks.append(jnp.where(near & (docs[k] == doc_column), 1.0, 0.0))
+        block = (me - k + n) % n
+        doc_row = sum(jnp.where((me ^ block) == i, docs[i], 0.0) for i in range(n))
+        near = block * tokens + within <= query_pos
+        masks.append(jnp.where(near & (doc_row == doc_column), 1.0, 0.0))
     allowed = jnp.concatenate(masks, axis=1) > 0.5
     scale_factor = 1.0 / math.sqrt(HD)
     for h in range(queries_ref.shape[1] // HD):
@@ -345,6 +347,10 @@
     return lax.ppermute(x, axis, [(i, i ^ k) for i in range(lax.axis_size(axis))])
 
 
+def onward(x):
+    return lax.ppermute(x, "seq", [(i, i + 1) for i in range(lax.axis_size("seq") - 1)])
+
+
 def exchange(blocks):
     got = {k: swap(blocks[k], "seq", k) for k in reversed(range(1, len(blocks)))}
     return [got[k] for k in range(1, len(blocks))]
@@ -388,16 +394,18 @@
 
     far = swap(normed_own, "mp")
     mate = swap(after(normed_own, parcel), "side")
-    parcels = [parcel] + exchange([parcel] * n)
-    far_mate = lax.ppermute(normed_own, ("mp", "side"), [(j, j ^ 3) for j in range(n)])
+    parcels = [parcel, onward(parcel)]
+    far_mate = swap(after(far, mate, parcels[1]), "side")
     entries = [far_mate, far, mate, normed_own]
 
-    away = away_partial([after(e, *parcels) for e in entries], proj)
+    away = away_partial(entries, proj)
     own, over_own, normed = kept_partials([after(e, away) for e in entries], proj)
-    got_over = after(swap(away, "seq", 1), over_own)
+    parcels.append(onward(after(parcels[1], away)))
+    got_over = after(swap(away, "seq", 1), over_own, parcels[2])
     over = lax.optimization_barrier((over_own + got_over.astype(F32)).astype(BF))
     got_far = swap(over, "seq", 2)
     got_beside = swap(beside_partial(after(normed, over), proj), "seq", 1)
+    parcels.append(onward(after(parcels[2], over)))
     teacher_rows = attention_rows(after(teacher_queries, over), parcels, pieces)
     predicted = lax.optimization_barrier(own + got_far.astype(F32)) + got_beside.astype(F32)
     delta = (predicted - teacher_rows.astype(F32)).astype(BF)

time: 106 us -> 106 us (level)
  waiting for transfers between devices: 61.9 us -> 54.3 us
  starting transfers between devices: 26.3 us -> 33.7 us
    ppermute x24 -> x22, waiting for transfers between devices: 61.9 us -> 46.3 us  [swap(): lax.ppermute(x, axis, [(i, i ^ k) for i in range(lax.axis_size(axis))])]
    ppermute x1 -> x3, starting transfers between devices: 0.31 us -> 10.2 us  [onward(): lax.ppermute(x, 'seq', [(i, i + 1) for i in range(lax.axis_size('seq') -...]
    ppermute x1 -> x3, waiting for transfers between devices: 0.01 us -> 7.92 us  [onward(): lax.ppermute(x, 'seq', [(i, i + 1) for i in range(lax.axis_size('seq') -...]
    ppermute x24 -> x22, starting transfers between devices: 26 us -> 23.5 us  [swap(): lax.ppermute(x, axis, [(i, i ^ k) for i in range(lax.axis_size(axis))])]
  transfers between devices with their start and end apart: 25 -> 25, of which waited for: 18 -> 20; matrix products, arithmetic and copies ran while one was open for 4% -> 4% of each run, Pallas kernels for 6% -> 6%
where the time goes in v6:
time: 106 us
  waiting for transfers between devices  54.3 us (51%)
  starting transfers between devices  33.7 us (32%)
  Pallas kernels  11 us (10%)
  matrix products  3.65 us (3%)
  other arithmetic  1.39 us (1%)
    ppermute x22, waiting for transfers between devices, swap(): lax.ppermute(x, axis, [(i, i ^ k) for i in range(lax.axis_size(axis))])  46.3 us
    ppermute x22, starting transfers between devices, swap(): lax.ppermute(x, axis, [(i, i ^ k) for i in range(lax.axis_size(axis))])  23.5 us
    pallas_call x13, Pallas kernels, call(): pl.pallas_call(kernel, out_shape=shapes, cost_estimate=pl.CostEstimate(fl...  11 us
    ppermute x3, starting transfers between devices, onward(): lax.ppermute(x, 'seq', [(i, i + 1) for i in range(lax.axis_size('seq') -...  10.2 us
    ppermute x3, waiting for transfers between devices, onward(): lax.ppermute(x, 'seq', [(i, i + 1) for i in range(lax.axis_size('seq') -...  7.92 us
    dot_general x5, matrix products, dot(): return lax.dot_general(a, b, (dims, ((), ())), preferred_element_type=F32)  3.65 us
  transfers between devices with their start and end apart: 25, of which 20 were waited for; matrix products, arithmetic and copies ran while one was open for 4% of the time, Pallas kernels for 6%

profile of v6, /device:TPU:0, one launch (start us, length us, event | category | flops | bytes accessed | tf_op | source)
XLA Modules:
  0.0 105.7 jit_solution(14388760854130307867)
XLA Ops:
  0.7 0.9 convert_select_fusion.small_ref
  1.6 1.2 %shard_map.95 = (bf16[48,1024]{1,0:T(8,128)(2,1)S(1)}, bf16[48,1024]{1,0:T(8,128)(2,1)S(1)}, bf16[48,1024]{1,0:T(8,128)(2,1)S(1)}, bf16[48,1024]{1,0:T(8,128)(2,1)S(1)}, bf16[2,48,3584]{2,1,0:T(8,128)(2,1)S(1)}) custom-call(bf16[4,48,3584]{2,1,0:T(8,128)(2,1)} %bitcast.18, f32[30,128]{1,0:T(8,128)S(1)} %convert_select_fusion.small_ref), custom_call_target="tpu_custom_call" | custom-call | flops 1032192 | bytes 1376256 | tf_op jit(solution)/shard_map/pallas_call | solution.py:49
  2.8 5.1 %collective-permute-start = (bf16[48,1024]{1,0:T(8,128)(2,1)S(1)}, bf16[48,1024]{1,0:T(8,128)(2,1)S(1)}, u32[]{:S(2)}, u32[]{:S(2)}) collective-permute-start(bf16[48,1024]{1,0:T(8,128)(2,1)S(1)} %get-tuple-element.31), channel_id=1, source_target_pairs={{0,12},{4,8},{8,4},{12,0},{1,13},{5,9},{9,5},{13,1},{2,14},{6,10},... | collective-permute-start | bytes 294920 | tf_op jit(solution)/shard_map/ppermute | solution.py:347
  7.9 0.6 collective-permute-start.2
  8.6 0.8 constant_dynamic-slice_fusion
  9.4 2.3 %collective-permute-done.refs_0_.refs_7_ = bf16[48,1024]{1,0:T(8,128)(2,1)S(1)} collective-permute-done((bf16[48,1024]{1,0:T(8,128)(2,1)S(1)}, bf16[48,1024]{1,0:T(8,128)(2,1)S(1)}, u32[]{:S(2)}, u32[]{:S(2)}) %collective-permute-start) | collective-permute-done | bytes 98336 | tf_op jit(solution)/shard_map/ppermute | solution.py:347
  11.6 4.6 %collective-permute-done.1.refs_1_.refs_6_ = bf16[48,1024]{1,0:T(8,128)(2,1)S(1)} collective-permute-done((bf16[48,1024]{1,0:T(8,128)(2,1)S(1)}, bf16[48,1024]{1,0:T(8,128)(2,1)S(1)}, u32[]{:S(2)}, u32[]{:S(2)}) %collective-permute-start.1) | collective-permute-done | bytes 98336 | tf_op jit(solution)/shard_map/ppermute | solution.py:347
  16.2 0.4 shard_map.96
  16.6 0.1 collective-permute-start.4
  16.7 1.6 %collective-permute-start.3 = (bf16[128,896]{1,0:T(8,128)(2,1)S(1)}, bf16[128,896]{1,0:T(8,128)(2,1)S(1)}, u32[]{:S(2)}, u32[]{:S(2)}) collective-permute-start(bf16[128,896]{1,0:T(8,128)(2,1)S(1)} %get-tuple-element.43.refs_3_), channel_id=1, source_target_pairs={{0,2},{2,0},{1,3},{3,1},{4,6},{6,4},{5,7},{7,5},{8,10},{10,8},{9,1... | collective-permute-start | bytes 688136 | tf_op jit(solution)/shard_map/ppermute | solution.py:347
  18.2 2.4 %collective-permute-start.5 = (bf16[256,128]{1,0:T(8,128)(2,1)S(1)}, bf16[256,128]{1,0:T(8,128)(2,1)S(1)}, u32[]{:S(2)}, u32[]{:S(2)}) collective-permute-start(bf16[256,128]{1,0:T(8,128)(2,1)S(1)} %pad_maximum_fusion.1.refs_0_), channel_id=1, source_target_pairs={{0,4},{4,8},{8,12},{1,5},{5,9},{9,13},{2,6},{6,10},{10,14},{3,7},{... | collective-permute-start | bytes 196616 | tf_op jit(solution)/shard_map/ppermute | solution.py:351
  20.7 1.9 %collective-permute-done.5.refs_1_ = bf16[256,128]{1,0:T(8,128)(2,1)S(1)} collective-permute-done((bf16[256,128]{1,0:T(8,128)(2,1)S(1)}, bf16[256,128]{1,0:T(8,128)(2,1)S(1)}, u32[]{:S(2)}, u32[]{:S(2)}) %collective-permute-start.5) | collective-permute-done | bytes 65568 | tf_op jit(solution)/shard_map/ppermute | solution.py:351
  22.6 2.1 %collective-permute-done.3.refs_1_ = bf16[128,896]{1,0:T(8,128)(2,1)S(1)} collective-permute-done((bf16[128,896]{1,0:T(8,128)(2,1)S(1)}, bf16[128,896]{1,0:T(8,128)(2,1)S(1)}, u32[]{:S(2)}, u32[]{:S(2)}) %collective-permute-start.3) | collective-permute-done | bytes 229408 | tf_op jit(solution)/shard_map/ppermute | solution.py:347
  24.7 1.5 %collective-permute-done.6.refs_0_ = bf16[128,896]{1,0:T(8,128)(2,1)S(1)} collective-permute-done((bf16[128,896]{1,0:T(8,128)(2,1)S(1)}, bf16[128,896]{1,0:T(8,128)(2,1)S(1)}, u32[]{:S(2)}, u32[]{:S(2)}) %collective-permute-start.6) | collective-permute-done | bytes 229408 | tf_op jit(solution)/shard_map/ppermute | solution.py:347
  26.2 0.5 shard_map.97
  26.6 0.6 collective-permute-start.7
  27.2 3.4 %collective-permute-start.8 = (bf16[256,128]{1,0:T(8,128)(2,1)S(1)}, bf16[256,128]{1,0:T(8,128)(2,1)S(1)}, u32[]{:S(2)}, u32[]{:S(2)}) collective-permute-start(bf16[256,128]{1,0:T(8,128)(2,1)S(1)} %collective-permute-done.5.refs_1_), channel_id=1, source_target_pairs={{0,4},{4,8},{8,12},{1,5},{5,9},{9,13},{2,6},{6,10},{10,14},{3,7},{... | collective-permute-start | bytes 196616 | tf_op jit(solution)/shard_map/ppermute | solution.py:351
  30.6 0.9 shard_map.98
  31.5 3.0 %collective-permute-done.8.refs_2_ = bf16[256,128]{1,0:T(8,128)(2,1)S(1)} collective-permute-done((bf16[256,128]{1,0:T(8,128)(2,1)S(1)}, bf16[256,128]{1,0:T(8,128)(2,1)S(1)}, u32[]{:S(2)}, u32[]{:S(2)}) %collective-permute-start.8) | collective-permute-done | bytes 65568 | tf_op jit(solution)/shard_map/ppermute | solution.py:351
  34.5 0.5 collective-permute-done.7
  35.1 2.1 %collective-permute-start.9 = (bf16[128,1024]{1,0:T(8,128)(2,1)S(1)}, bf16[128,1024]{1,0:T(8,128)(2,1)S(1)}, u32[]{:S(2)}, u32[]{:S(2)}) collective-permute-start(bf16[128,1024]{1,0:T(8,128)(2,1)S(1)} %add_convert_fusion), channel_id=1, source_target_pairs={{0,8},{4,12},{8,0},{12,4},{1,9},{5,13},{9,1},{13,5},{2,10},{6,14},... | collective-permute-start | bytes 786440 | tf_op jit(solution)/shard_map/ppermute | solution.py:347
  37.2 4.4 %collective-permute-start.11 = (bf16[256,128]{1,0:T(8,128)(2,1)S(1)}, bf16[256,128]{1,0:T(8,128)(2,1)S(1)}, u32[]{:S(2)}, u32[]{:S(2)}) collective-permute-start(bf16[256,128]{1,0:T(8,128)(2,1)S(1)} %collective-permute-done.8.refs_2_), channel_id=1, source_target_pairs={{0,4},{4,8},{8,12},{1,5},{5,9},{9,13},{2,6},{6,10},{10,14},{3,7},{... | collective-permute-start | bytes 196616 | tf_op jit(solution)/shard_map/ppermute | solution.py:351
  41.6 0.4 shard_map.99
  42.0 0.1 collective-permute-start.10
  42.1 3.1 %collective-permute-done.11.refs_3_ = bf16[256,128]{1,0:T(8,128)(2,1)S(1)} collective-permute-done((bf16[256,128]{1,0:T(8,128)(2,1)S(1)}, bf16[256,128]{1,0:T(8,128)(2,1)S(1)}, u32[]{:S(2)}, u32[]{:S(2)}) %collective-permute-start.11) | collective-permute-done | bytes 65568 | tf_op jit(solution)/shard_map/ppermute | solution.py:351
  45.2 2.3 %shard_map.100 = bf16[128,1024]{1,0:T(8,128)(2,1)S(1)} custom-call(bf16[128,1024]{1,0:T(8,128)(2,1)S(1)} %copy-done.1, bf16[256,128]{1,0:T(8,128)(2,1)S(1)} %pad_maximum_fusion.1.refs_0_, bf16[256,128]{1,0:T(8,128)(2,1)S(1)} %collective-permute-done.5.refs_1_, bf16[256,128]{1,0:T(8,128)(2,1)S(1)} %collective-permute-done.8.refs_2_, ...), custom_call_target="tpu_custom_call" | custom-call | bytes 524288 | tf_op jit(solution)/shard_map/pallas_call | solution.py:49
  47.5 1.8 %collective-permute-done.9 = bf16[128,1024]{1,0:T(8,128)(2,1)S(1)} collective-permute-done((bf16[128,1024]{1,0:T(8,128)(2,1)S(1)}, bf16[128,1024]{1,0:T(8,128)(2,1)S(1)}, u32[]{:S(2)}, u32[]{:S(2)}) %collective-permute-start.9) | collective-permute-done | bytes 262176 | tf_op jit(solution)/shard_map/ppermute | solution.py:347
  49.4 3.8 %collective-permute-done.10 = bf16[128,1024]{1,0:T(8,128)(2,1)S(1)} collective-permute-done((bf16[128,1024]{1,0:T(8,128)(2,1)S(1)}, bf16[128,1024]{1,0:T(8,128)(2,1)S(1)}, u32[]{:S(2)}, u32[]{:S(2)}) %collective-permute-start.10) | collective-permute-done | bytes 262176 | tf_op jit(solution)/shard_map/ppermute | solution.py:347
  53.2 0.1 subtract_convert_fusion.delta_ref
  53.3 2.0 %collective-permute-start.13 = (bf16[128,1024]{1,0:T(8,128)(2,1)S(1)}, bf16[128,1024]{1,0:T(8,128)(2,1)S(1)}, u32[]{:S(2)}, u32[]{:S(2)}) collective-permute-start(bf16[128,1024]{1,0:T(8,128)(2,1)S(1)} %subtract_convert_fusion.delta_ref), channel_id=1, source_target_pairs={{0,8},{4,12},{8,0},{12,4},{1,9},{5,13},{9,1},{13,5},{2,10},{6,14},... | collective-permute-start | bytes 786440 | tf_op jit(solution)/shard_map/ppermute | solution.py:347
  55.3 0.7 shard_map.101.first_ref
  56.0 1.0 collective-permute-start.12
  57.0 10.4 %collective-permute-done.13.delta_ref = bf16[128,1024]{1,0:T(8,128)(2,1)S(1)} collective-permute-done((bf16[128,1024]{1,0:T(8,128)(2,1)S(1)}, bf16[128,1024]{1,0:T(8,128)(2,1)S(1)}, u32[]{:S(2)}, u32[]{:S(2)}) %collective-permute-start.13) | collective-permute-done | bytes 262176 | tf_op jit(solution)/shard_map/ppermute | solution.py:347
  67.5 0.7 shard_map.103.third_ref
  68.2 1.1 %collective-permute-done.12.delta_ref = bf16[128,1024]{1,0:T(8,128)(2,1)S(1)} collective-permute-done((bf16[128,1024]{1,0:T(8,128)(2,1)S(1)}, bf16[128,1024]{1,0:T(8,128)(2,1)S(1)}, u32[]{:S(2)}, u32[]{:S(2)}) %collective-permute-start.12) | collective-permute-done | bytes 262176 | tf_op jit(solution)/shard_map/ppermute | solution.py:347
  69.3 0.7 shard_map.102.second_ref
  70.0 5.4 %collective-permute-done.14.delta_ref = bf16[128,1024]{1,0:T(8,128)(2,1)S(1)} collective-permute-done((bf16[128,1024]{1,0:T(8,128)(2,1)S(1)}, bf16[128,1024]{1,0:T(8,128)(2,1)S(1)}, u32[]{:S(2)}, u32[]{:S(2)}) %collective-permute-start.14) | collective-permute-done | bytes 262176 | tf_op jit(solution)/shard_map/ppermute | solution.py:347
  75.5 0.8 shard_map.104
  76.2 0.1 collective-permute-start.15
  76.3 0.1 pad_maximum_fusion
  76.4 1.7 %collective-permute-done.15 = bf16[2,128,896]{2,1,0:T(8,128)(2,1)S(1)} collective-permute-done((bf16[2,128,896]{2,1,0:T(8,128)(2,1)S(1)}, bf16[2,128,896]{2,1,0:T(8,128)(2,1)S(1)}, u32[]{:S(2)}, u32[]{:S(2)}) %collective-permute-start.15) | collective-permute-done | bytes 458784 | tf_op jit(solution)/shard_map/ppermute | solution.py:347
  78.1 0.1 fusion
  78.2 1.6 %collective-permute-start.16 = (bf16[128,896]{1,0:T(8,128)(2,1)S(1)}, bf16[128,896]{1,0:T(8,128)(2,1)S(1)}, u32[]{:S(2)}, u32[]{:S(2)}) collective-permute-start(bf16[128,896]{1,0:T(8,128)(2,1)S(1)} %fusion), channel_id=1, source_target_pairs={{0,2},{2,0},{1,3},{3,1},{4,6},{6,4},{5,7},{7,5},{8,10},{10,8},{9,1... | collective-permute-start | bytes 688136 | tf_op jit(solution)/shard_map/ppermute | solution.py:347
  79.9 3.0 %convolution_multiply_fusion = f32[896,1024]{1,0:T(8,128)} fusion(bf16[512,896]{1,0:T(8,128)(2,1)S(1)} %get-tuple-element.49.normed_ref, bf16[512,1024]{1,0:T(8,128)(2,1)S(1)} %pad_maximum_fusion), kind=kOutput, calls=%fused_computation | convolution fusion | flops 940441600 | bytes 5636096 | tf_op jit(solution)/shard_map/dot_general | solution.py:22
  82.9 3.0 %collective-permute-done.16 = bf16[128,896]{1,0:T(8,128)(2,1)S(1)} collective-permute-done((bf16[128,896]{1,0:T(8,128)(2,1)S(1)}, bf16[128,896]{1,0:T(8,128)(2,1)S(1)}, u32[]{:S(2)}, u32[]{:S(2)}) %collective-permute-start.16) | collective-permute-done | bytes 229408 | tf_op jit(solution)/shard_map/ppermute | solution.py:347
  86.0 0.2 convolution_convert_fusion
  86.1 0.2 convolution_convert_fusion.1
  86.3 0.2 convolution_convert_fusion.2
  86.5 0.3 collective-permute-start.17
  86.8 4.1 %collective-permute-start.19 = (bf16[48,896]{1,0:T(8,128)(2,1)S(1)}, bf16[48,896]{1,0:T(8,128)(2,1)S(1)}, u32[]{:S(2)}, u32[]{:S(2)}) collective-permute-start(bf16[48,896]{1,0:T(8,128)(2,1)S(1)} %convolution_convert_fusion), channel_id=1, source_target_pairs={{0,12},{4,8},{8,4},{12,0},{1,13},{5,9},{9,5},{13,1},{2,14},{6,10},... | collective-permute-start | bytes 258056 | tf_op jit(solution)/shard_map/ppermute | solution.py:347
  90.9 0.2 convolution_convert_fusion.3.refs_0_
  91.1 1.6 %collective-permute-start.20 = (bf16[48,896]{1,0:T(8,128)(2,1)S(1)}, bf16[48,896]{1,0:T(8,128)(2,1)S(1)}, u32[]{:S(2)}, u32[]{:S(2)}) collective-permute-start(bf16[48,896]{1,0:T(8,128)(2,1)S(1)} %convolution_convert_fusion.3.refs_0_), channel_id=1, source_target_pairs={{0,2},{2,0},{1,3},{3,1},{4,6},{6,4},{5,7},{7,5},{8,10},{10,8},{9,1... | collective-permute-start | bytes 258056 | tf_op jit(solution)/shard_map/ppermute | solution.py:347
  92.7 0.5 collective-permute-start.21
  93.2 2.7 %collective-permute-done.18.refs_2_ = bf16[48,896]{1,0:T(8,128)(2,1)S(1)} collective-permute-done((bf16[48,896]{1,0:T(8,128)(2,1)S(1)}, bf16[48,896]{1,0:T(8,128)(2,1)S(1)}, u32[]{:S(2)}, u32[]{:S(2)}) %collective-permute-start.18) | collective-permute-done | bytes 86048 | tf_op jit(solution)/shard_map/ppermute | solution.py:347
  95.9 1.6 %collective-permute-start.22 = (bf16[48,896]{1,0:T(8,128)(2,1)S(1)}, bf16[48,896]{1,0:T(8,128)(2,1)S(1)}, u32[]{:S(2)}, u32[]{:S(2)}) collective-permute-start(bf16[48,896]{1,0:T(8,128)(2,1)S(1)} %collective-permute-done.18.refs_2_), channel_id=1, source_target_pairs={{0,2},{2,0},{1,3},{3,1},{4,6},{6,4},{5,7},{7,5},{8,10},{10,8},{9,1... | collective-permute-start | bytes 258056 | tf_op jit(solution)/shard_map/ppermute | solution.py:347
  97.4 0.5 collective-permute-start.23
  97.9 0.2 collective-permute-done.21.refs_5_
  98.1 2.2 %collective-permute-done.22.refs_6_ = bf16[48,896]{1,0:T(8,128)(2,1)S(1)} collective-permute-done((bf16[48,896]{1,0:T(8,128)(2,1)S(1)}, bf16[48,896]{1,0:T(8,128)(2,1)S(1)}, u32[]{:S(2)}, u32[]{:S(2)}) %collective-permute-start.22) | collective-permute-done | bytes 86048 | tf_op jit(solution)/shard_map/ppermute | solution.py:347
  100.4 1.6 %collective-permute-done.23.refs_7_ = bf16[48,896]{1,0:T(8,128)(2,1)S(1)} collective-permute-done((bf16[48,896]{1,0:T(8,128)(2,1)S(1)}, bf16[48,896]{1,0:T(8,128)(2,1)S(1)}, u32[]{:S(2)}, u32[]{:S(2)}) %collective-permute-start.23) | collective-permute-done | bytes 86048 | tf_op jit(solution)/shard_map/ppermute | solution.py:347
  101.9 0.7 shard_map.105.pair_ref
  102.6 0.1 collective-permute-start.24
  102.7 0.9 shard_map.106.t
  103.6 1.3 %collective-permute-done.24.refs_0_ = bf16[2,48,3584]{2,1,0:T(8,128)(2,1)S(1)} collective-permute-done((bf16[2,48,3584]{2,1,0:T(8,128)(2,1)S(1)}, bf16[2,48,3584]{2,1,0:T(8,128)(2,1)S(1)}, u32[]{:S(2)}, u32[]{:S(2)}) %collective-permute-start.24) | collective-permute-done | bytes 688160 | tf_op jit(solution)/shard_map/ppermute | solution.py:347
  104.8 0.9 shard_map.107
  (20 shorter events, 0.3 us)
Async XLA Ops:
  0.6 25.6 %copy-start = (bf16[896,1024]{1,0:T(8,128)(2,1)S(1)}, bf16[896,1024]{1,0:T(8,128)(2,1)}, u32[]{:S(2)}) copy-start(bf16[896,1024]{1,0:T(8,128)(2,1)} %proj_ref.9) | copy-start | bytes 5505028
  2.8 8.8 %collective-permute-start = (bf16[48,1024]{1,0:T(8,128)(2,1)S(1)}, bf16[48,1024]{1,0:T(8,128)(2,1)S(1)}, u32[]{:S(2)}, u32[]{:S(2)}) collective-permute-start(bf16[48,1024]{1,0:T(8,128)(2,1)S(1)} %get-tuple-element.31), channel_id=1, source_target_pairs={{0,12},{4,8},{8,4},{12,0},{1,13},{5,9},{9,5},{13,1},{2,14},{6,10},... | collective-permute-start | bytes 294920 | tf_op jit(solution)/shard_map/ppermute | solution.py:347
  7.9 8.3 %collective-permute-start.1 = (bf16[48,1024]{1,0:T(8,128)(2,1)S(1)}, bf16[48,1024]{1,0:T(8,128)(2,1)S(1)}, u32[]{:S(2)}, u32[]{:S(2)}) collective-permute-start(bf16[48,1024]{1,0:T(8,128)(2,1)S(1)} %get-tuple-element.32), channel_id=1, source_target_pairs={{0,8},{4,12},{8,0},{12,4},{1,9},{5,13},{9,1},{13,5},{2,10},{6,14},... | collective-permute-start | bytes 294920 | tf_op jit(solution)/shard_map/ppermute | solution.py:347
  7.9 8.3 %collective-permute-start.2 = (bf16[48,1024]{1,0:T(8,128)(2,1)S(1)}, bf16[48,1024]{1,0:T(8,128)(2,1)S(1)}, u32[]{:S(2)}, u32[]{:S(2)}) collective-permute-start(bf16[48,1024]{1,0:T(8,128)(2,1)S(1)} %get-tuple-element.33), channel_id=1, source_target_pairs={{0,4},{4,0},{8,12},{12,8},{1,5},{5,1},{9,13},{13,9},{2,6},{6,2},{1... | collective-permute-start | bytes 294920 | tf_op jit(solution)/shard_map/ppermute | solution.py:347
  16.6 6.0 %collective-permute-start.4 = (bf16[128,896]{1,0:T(8,128)(2,1)S(1)}, bf16[128,896]{1,0:T(8,128)(2,1)S(1)}, u32[]{:S(2)}, u32[]{:S(2)}) collective-permute-start(bf16[128,896]{1,0:T(8,128)(2,1)S(1)} %get-tuple-element.43.refs_3_), channel_id=1, source_target_pairs={{0,1},{1,0},{2,3},{3,2},{4,5},{5,4},{6,7},{7,6},{8,9},{9,8},{10,11... | collective-permute-start | bytes 688136 | tf_op jit(solution)/shard_map/ppermute | solution.py:347
  16.7 8.0 %collective-permute-start.3 = (bf16[128,896]{1,0:T(8,128)(2,1)S(1)}, bf16[128,896]{1,0:T(8,128)(2,1)S(1)}, u32[]{:S(2)}, u32[]{:S(2)}) collective-permute-start(bf16[128,896]{1,0:T(8,128)(2,1)S(1)} %get-tuple-element.43.refs_3_), channel_id=1, source_target_pairs={{0,2},{2,0},{1,3},{3,1},{4,6},{6,4},{5,7},{7,5},{8,10},{10,8},{9,1... | collective-permute-start | bytes 688136 | tf_op jit(solution)/shard_map/ppermute | solution.py:347
  18.2 4.3 %collective-permute-start.5 = (bf16[256,128]{1,0:T(8,128)(2,1)S(1)}, bf16[256,128]{1,0:T(8,128)(2,1)S(1)}, u32[]{:S(2)}, u32[]{:S(2)}) collective-permute-start(bf16[256,128]{1,0:T(8,128)(2,1)S(1)} %pad_maximum_fusion.1.refs_0_), channel_id=1, source_target_pairs={{0,4},{4,8},{8,12},{1,5},{5,9},{9,13},{2,6},{6,10},{10,14},{3,7},{... | collective-permute-start | bytes 196616 | tf_op jit(solution)/shard_map/ppermute | solution.py:351
  24.7 1.5 %collective-permute-start.6 = (bf16[128,896]{1,0:T(8,128)(2,1)S(1)}, bf16[128,896]{1,0:T(8,128)(2,1)S(1)}, u32[]{:S(2)}, u32[]{:S(2)}) collective-permute-start(bf16[128,896]{1,0:T(8,128)(2,1)S(1)} %collective-permute-done.3.refs_1_), channel_id=1, source_target_pairs={{0,1},{1,0},{2,3},{3,2},{4,5},{5,4},{6,7},{7,6},{8,9},{9,8},{10,11... | collective-permute-start | bytes 688136 | tf_op jit(solution)/shard_map/ppermute | solution.py:347
  26.6 8.4 %collective-permute-start.7 = (bf16[128,1024]{1,0:T(8,128)(2,1)S(1)}, bf16[128,1024]{1,0:T(8,128)(2,1)S(1)}, u32[]{:S(2)}, u32[]{:S(2)}) collective-permute-start(bf16[128,1024]{1,0:T(8,128)(2,1)S(1)} %shard_map.97), channel_id=1, source_target_pairs={{0,4},{4,0},{8,12},{12,8},{1,5},{5,1},{9,13},{13,9},{2,6},{6,2},{1... | collective-permute-start | bytes 786440 | tf_op jit(solution)/shard_map/ppermute | solution.py:347
  27.2 7.3 %collective-permute-start.8 = (bf16[256,128]{1,0:T(8,128)(2,1)S(1)}, bf16[256,128]{1,0:T(8,128)(2,1)S(1)}, u32[]{:S(2)}, u32[]{:S(2)}) collective-permute-start(bf16[256,128]{1,0:T(8,128)(2,1)S(1)} %collective-permute-done.5.refs_1_), channel_id=1, source_target_pairs={{0,4},{4,8},{8,12},{1,5},{5,9},{9,13},{2,6},{6,10},{10,14},{3,7},{... | collective-permute-start | bytes 196616 | tf_op jit(solution)/shard_map/ppermute | solution.py:351
  31.5 13.7 %copy-start.1 = (bf16[128,1024]{1,0:T(8,128)(2,1)S(1)}, bf16[128,1024]{1,0:T(8,128)(2,1)}, u32[]{:S(2)}) copy-start(bf16[128,1024]{1,0:T(8,128)(2,1)} %queries_ref) | copy-start | bytes 786436
  35.1 14.2 %collective-permute-start.9 = (bf16[128,1024]{1,0:T(8,128)(2,1)S(1)}, bf16[128,1024]{1,0:T(8,128)(2,1)S(1)}, u32[]{:S(2)}, u32[]{:S(2)}) collective-permute-start(bf16[128,1024]{1,0:T(8,128)(2,1)S(1)} %add_convert_fusion), channel_id=1, source_target_pairs={{0,8},{4,12},{8,0},{12,4},{1,9},{5,13},{9,1},{13,5},{2,10},{6,14},... | collective-permute-start | bytes 786440 | tf_op jit(solution)/shard_map/ppermute | solution.py:347
  37.2 8.0 %collective-permute-start.11 = (bf16[256,128]{1,0:T(8,128)(2,1)S(1)}, bf16[256,128]{1,0:T(8,128)(2,1)S(1)}, u32[]{:S(2)}, u32[]{:S(2)}) collective-permute-start(bf16[256,128]{1,0:T(8,128)(2,1)S(1)} %collective-permute-done.8.refs_2_), channel_id=1, source_target_pairs={{0,4},{4,8},{8,12},{1,5},{5,9},{9,13},{2,6},{6,10},{10,14},{3,7},{... | collective-permute-start | bytes 196616 | tf_op jit(solution)/shard_map/ppermute | solution.py:351
  42.0 11.2 %collective-permute-start.10 = (bf16[128,1024]{1,0:T(8,128)(2,1)S(1)}, bf16[128,1024]{1,0:T(8,128)(2,1)S(1)}, u32[]{:S(2)}, u32[]{:S(2)}) collective-permute-start(bf16[128,1024]{1,0:T(8,128)(2,1)S(1)} %shard_map.99), channel_id=1, source_target_pairs={{0,4},{4,0},{8,12},{12,8},{1,5},{5,1},{9,13},{13,9},{2,6},{6,2},{1... | collective-permute-start | bytes 786440 | tf_op jit(solution)/shard_map/ppermute | solution.py:347
  53.3 14.2 %collective-permute-start.13 = (bf16[128,1024]{1,0:T(8,128)(2,1)S(1)}, bf16[128,1024]{1,0:T(8,128)(2,1)S(1)}, u32[]{:S(2)}, u32[]{:S(2)}) collective-permute-start(bf16[128,1024]{1,0:T(8,128)(2,1)S(1)} %subtract_convert_fusion.delta_ref), channel_id=1, source_target_pairs={{0,8},{4,12},{8,0},{12,4},{1,9},{5,13},{9,1},{13,5},{2,10},{6,14},... | collective-permute-start | bytes 786440 | tf_op jit(solution)/shard_map/ppermute | solution.py:347
  56.0 13.3 %collective-permute-start.12 = (bf16[128,1024]{1,0:T(8,128)(2,1)S(1)}, bf16[128,1024]{1,0:T(8,128)(2,1)S(1)}, u32[]{:S(2)}, u32[]{:S(2)}) collective-permute-start(bf16[128,1024]{1,0:T(8,128)(2,1)S(1)} %subtract_convert_fusion.delta_ref), channel_id=1, source_target_pairs={{0,4},{4,0},{8,12},{12,8},{1,5},{5,1},{9,13},{13,9},{2,6},{6,2},{1... | collective-permute-start | bytes 786440 | tf_op jit(solution)/shard_map/ppermute | solution.py:347
  67.5 8.0 %collective-permute-start.14 = (bf16[128,1024]{1,0:T(8,128)(2,1)S(1)}, bf16[128,1024]{1,0:T(8,128)(2,1)S(1)}, u32[]{:S(2)}, u32[]{:S(2)}) collective-permute-start(bf16[128,1024]{1,0:T(8,128)(2,1)S(1)} %collective-permute-done.13.delta_ref), channel_id=1, source_target_pairs={{0,4},{4,0},{8,12},{12,8},{1,5},{5,1},{9,13},{13,9},{2,6},{6,2},{1... | collective-permute-start | bytes 786440 | tf_op jit(solution)/shard_map/ppermute | solution.py:347
  76.2 1.9 %collective-permute-start.15 = (bf16[2,128,896]{2,1,0:T(8,128)(2,1)S(1)}, bf16[2,128,896]{2,1,0:T(8,128)(2,1)S(1)}, u32[]{:S(2)}, u32[]{:S(2)}) collective-permute-start(bf16[2,128,896]{2,1,0:T(8,128)(2,1)S(1)} %get-tuple-element.54), channel_id=1, source_target_pairs={{0,1},{1,0},{2,3},{3,2},{4,5},{5,4},{6,7},{7,6},{8,9},{9,8},{10,11... | collective-permute-start | bytes 1376264 | tf_op jit(solution)/shard_map/ppermute | solution.py:347
  78.2 7.7 %collective-permute-start.16 = (bf16[128,896]{1,0:T(8,128)(2,1)S(1)}, bf16[128,896]{1,0:T(8,128)(2,1)S(1)}, u32[]{:S(2)}, u32[]{:S(2)}) collective-permute-start(bf16[128,896]{1,0:T(8,128)(2,1)S(1)} %fusion), channel_id=1, source_target_pairs={{0,2},{2,0},{1,3},{3,1},{4,6},{6,4},{5,7},{7,5},{8,10},{10,8},{9,1... | collective-permute-start | bytes 688136 | tf_op jit(solution)/shard_map/ppermute | solution.py:347
  86.5 6.3 %collective-permute-start.17 = (bf16[48,896]{1,0:T(8,128)(2,1)S(1)}, bf16[48,896]{1,0:T(8,128)(2,1)S(1)}, u32[]{:S(2)}, u32[]{:S(2)}) collective-permute-start(bf16[48,896]{1,0:T(8,128)(2,1)S(1)} %convolution_convert_fusion.2), channel_id=1, source_target_pairs={{0,4},{4,0},{8,12},{12,8},{1,5},{5,1},{9,13},{13,9},{2,6},{6,2},{1... | collective-permute-start | bytes 258056 | tf_op jit(solution)/shard_map/ppermute | solution.py:347
  86.8 9.1 %collective-permute-start.18 = (bf16[48,896]{1,0:T(8,128)(2,1)S(1)}, bf16[48,896]{1,0:T(8,128)(2,1)S(1)}, u32[]{:S(2)}, u32[]{:S(2)}) collective-permute-start(bf16[48,896]{1,0:T(8,128)(2,1)S(1)} %convolution_convert_fusion.1), channel_id=1, source_target_pairs={{0,8},{4,12},{8,0},{12,4},{1,9},{5,13},{9,1},{13,5},{2,10},{6,14},... | collective-permute-start | bytes 258056 | tf_op jit(solution)/shard_map/ppermute | solution.py:347
  86.8 10.6 %collective-permute-start.19 = (bf16[48,896]{1,0:T(8,128)(2,1)S(1)}, bf16[48,896]{1,0:T(8,128)(2,1)S(1)}, u32[]{:S(2)}, u32[]{:S(2)}) collective-permute-start(bf16[48,896]{1,0:T(8,128)(2,1)S(1)} %convolution_convert_fusion), channel_id=1, source_target_pairs={{0,12},{4,8},{8,4},{12,0},{1,13},{5,9},{9,5},{13,1},{2,14},{6,10},... | collective-permute-start | bytes 258056 | tf_op jit(solution)/shard_map/ppermute | solution.py:347
  91.1 6.8 %collective-permute-start.20 = (bf16[48,896]{1,0:T(8,128)(2,1)S(1)}, bf16[48,896]{1,0:T(8,128)(2,1)S(1)}, u32[]{:S(2)}, u32[]{:S(2)}) collective-permute-start(bf16[48,896]{1,0:T(8,128)(2,1)S(1)} %convolution_convert_fusion.3.refs_0_), channel_id=1, source_target_pairs={{0,2},{2,0},{1,3},{3,1},{4,6},{6,4},{5,7},{7,5},{8,10},{10,8},{9,1... | collective-permute-start | bytes 258056 | tf_op jit(solution)/shard_map/ppermute | solution.py:347
  92.7 5.4 %collective-permute-start.21 = (bf16[48,896]{1,0:T(8,128)(2,1)S(1)}, bf16[48,896]{1,0:T(8,128)(2,1)S(1)}, u32[]{:S(2)}, u32[]{:S(2)}) collective-permute-start(bf16[48,896]{1,0:T(8,128)(2,1)S(1)} %collective-permute-done.17.refs_1_), channel_id=1, source_target_pairs={{0,2},{2,0},{1,3},{3,1},{4,6},{6,4},{5,7},{7,5},{8,10},{10,8},{9,1... | collective-permute-start | bytes 258056 | tf_op jit(solution)/shard_map/ppermute | solution.py:347
  95.9 4.5 %collective-permute-start.22 = (bf16[48,896]{1,0:T(8,128)(2,1)S(1)}, bf16[48,896]{1,0:T(8,128)(2,1)S(1)}, u32[]{:S(2)}, u32[]{:S(2)}) collective-permute-start(bf16[48,896]{1,0:T(8,128)(2,1)S(1)} %collective-permute-done.18.refs_2_), channel_id=1, source_target_pairs={{0,2},{2,0},{1,3},{3,1},{4,6},{6,4},{5,7},{7,5},{8,10},{10,8},{9,1... | collective-permute-start | bytes 258056 | tf_op jit(solution)/shard_map/ppermute | solution.py:347
  97.4 4.5 %collective-permute-start.23 = (bf16[48,896]{1,0:T(8,128)(2,1)S(1)}, bf16[48,896]{1,0:T(8,128)(2,1)S(1)}, u32[]{:S(2)}, u32[]{:S(2)}) collective-permute-start(bf16[48,896]{1,0:T(8,128)(2,1)S(1)} %collective-permute-done.19.refs_3_), channel_id=1, source_target_pairs={{0,2},{2,0},{1,3},{3,1},{4,6},{6,4},{5,7},{7,5},{8,10},{10,8},{9,1... | collective-permute-start | bytes 258056 | tf_op jit(solution)/shard_map/ppermute | solution.py:347
  102.6 2.2 %collective-permute-start.24 = (bf16[2,48,3584]{2,1,0:T(8,128)(2,1)S(1)}, bf16[2,48,3584]{2,1,0:T(8,128)(2,1)S(1)}, u32[]{:S(2)}, u32[]{:S(2)}) collective-permute-start(bf16[2,48,3584]{2,1,0:T(8,128)(2,1)S(1)} %shard_map.105.pair_ref), channel_id=1, source_target_pairs={{0,1},{1,0},{2,3},{3,2},{4,5},{5,4},{6,7},{7,6},{8,9},{9,8},{10,11... | collective-permute-start | bytes 2064392 | tf_op jit(solution)/shard_map/ppermute | solution.py:347

commit v7 on v6

--- a/solution.py
+++ b/solution.py
@@ -144,15 +144,17 @@
     )
 
 
-def attention_kernel(queries_ref, *refs):
-    out_ref = refs[-1]
-    n = (len(refs) - 1) // 2
-    parcels, pieces = refs[:n], refs[n : 2 * n]
+def attention_kernel(queries_ref, near_ref, far_ref, *refs):
+    *pieces, out_ref = refs
+    n = len(pieces)
     tokens = queries_ref.shape[0]
     depth = pieces[0].shape[1] - LANES
     me, _ = indices()
-    keys = jnp.concatenate([parcel[:tokens, :] for parcel in parcels], axis=0)
-    values = jnp.concatenate([parcel[tokens:, :] for parcel in parcels], axis=0)
+    parcels = [(pair, 2 * tokens * i) for pair in (near_ref, far_ref) for i in range(2)]
+    keys = jnp.concatenate([pair[at : at + tokens, :] for pair, at in parcels], axis=0)
+    values = jnp.concatenate(
+        [pair[at + tokens : at + 2 * tokens, :] for pair, at in parcels], axis=0
+    )
     docs = [piece[0:16, depth:].astype(F32)[1:2] for piece in pieces]
     doc_column = to_column(docs[0])
     query_pos = me * tokens + lax.broadcasted_iota(I32, (tokens, tokens), 0)
@@ -175,13 +177,12 @@
         out_ref[:, columns] = (dot(probs.astype(BF), values) / total).astype(BF)
 
 
-def attention_rows(queries, parcels, pieces):
+def attention_rows(queries, pairs, pieces):
     tokens, width = queries.shape
-    n = len(parcels)
     return call(
         attention_kernel,
         jax.ShapeDtypeStruct((tokens, width), BF),
-        (queries, *parcels, *pieces),
+        (queries, *pairs, *pieces),
         0,
         4 * tokens * width,
     )
@@ -347,8 +348,9 @@
     return lax.ppermute(x, axis, [(i, i ^ k) for i in range(lax.axis_size(axis))])
 
 
-def onward(x):
-    return lax.ppermute(x, "seq", [(i, i + 1) for i in range(lax.axis_size("seq") - 1)])
+def onward(x, step):
+    n = lax.axis_size("seq")
+    return lax.ppermute(x, "seq", [(i, i + step) for i in range(n - step)])
 
 
 def exchange(blocks):
@@ -394,19 +396,19 @@
 
     far = swap(normed_own, "mp")
     mate = swap(after(normed_own, parcel), "side")
-    parcels = [parcel, onward(parcel)]
-    far_mate = swap(after(far, mate, parcels[1]), "side")
+    before = onward(parcel, 1)
+    far_mate = swap(after(far, mate, before), "side")
     entries = [far_mate, far, mate, normed_own]
 
     away = away_partial(entries, proj)
     own, over_own, normed = kept_partials([after(e, away) for e in entries], proj)
-    parcels.append(onward(after(parcels[1], away)))
-    got_over = after(swap(away, "seq", 1), over_own, parcels[2])
+    near_pair = lax.optimization_barrier(jnp.concatenate([parcel, before]))
+    far_pair = onward(after(near_pair, away), 2)
+    got_over = after(swap(away, "seq", 1), over_own, far_pair)
     over = lax.optimization_barrier((over_own + got_over.astype(F32)).astype(BF))
     got_far = swap(over, "seq", 2)
     got_beside = swap(beside_partial(after(normed, over), proj), "seq", 1)
-    parcels.append(onward(after(parcels[2], over)))
-    teacher_rows = attention_rows(after(teacher_queries, over), parcels, pieces)
+    teacher_rows = attention_rows(after(teacher_queries, over), [near_pair, far_pair], pieces)
     predicted = lax.optimization_barrier(own + got_far.astype(F32)) + got_beside.astype(F32)
     delta = (predicted - teacher_rows.astype(F32)).astype(BF)
 

time: 106 us -> 102 us (0.962)
  waiting for transfers between devices: 54.3 us -> 49.7 us
    ppermute x22, starting transfers between devices: 23.5 us -> 27.3 us  [swap(): lax.ppermute(x, axis, [(i, i ^ k) for i in range(lax.axis_size(axis))])]
    ppermute x3 -> x2, starting transfers between devices: 10.2 us -> 6.9 us  [onward(): return lax.ppermute(x, 'seq', [(i, i + step) for i in range(n - step)])]
    ppermute x3 -> x2, waiting for transfers between devices: 7.92 us -> 5.21 us  [onward(): return lax.ppermute(x, 'seq', [(i, i + step) for i in range(n - step)])]
    ppermute x22, waiting for transfers between devices: 46.3 us -> 44.5 us  [swap(): lax.ppermute(x, axis, [(i, i ^ k) for i in range(lax.axis_size(axis))])]
  transfers between devices with their start and end apart: 25 -> 24, of which waited for: 20 -> 17; matrix products, arithmetic and copies ran while one was open for 4% -> 4% of each run, Pallas kernels for 6% -> 7%
where the time goes in v7:
time: 102 us
  waiting for transfers between devices  49.7 us (49%)
  starting transfers between devices  34.2 us (34%)
  Pallas kernels  11 us (11%)
  matrix products  3.65 us (4%)
  other arithmetic  1.4 us (1%)
    ppermute x22, waiting for transfers between devices, swap(): lax.ppermute(x, axis, [(i, i ^ k) for i in range(lax.axis_size(axis))])  44.5 us
    ppermute x22, starting transfers between devices, swap(): lax.ppermute(x, axis, [(i, i ^ k) for i in range(lax.axis_size(axis))])  27.3 us
    pallas_call x13, Pallas kernels, call(): pl.pallas_call(kernel, out_shape=shapes, cost_estimate=pl.CostEstimate(fl...  11 us
    ppermute x2, starting transfers between devices, onward(): return lax.ppermute(x, 'seq', [(i, i + step) for i in range(n - step)])  6.9 us
    ppermute x2, waiting for transfers between devices, onward(): return lax.ppermute(x, 'seq', [(i, i + step) for i in range(n - step)])  5.21 us
    dot_general x5, matrix products, dot(): return lax.dot_general(a, b, (dims, ((), ())), preferred_element_type=F32)  3.65 us
  transfers between devices with their start and end apart: 24, of which 17 were waited for; matrix products, arithmetic and copies ran while one was open for 4% of the time, Pallas kernels for 7%

profile of v7, /device:TPU:0, one launch (start us, length us, event | category | flops | bytes accessed | tf_op | source)
XLA Modules:
  0.0 101.6 jit_solution(15066980259869506102)
XLA Ops:
  0.7 0.9 convert_select_fusion.small_ref
  1.6 1.2 %shard_map.95 = (bf16[48,1024]{1,0:T(8,128)(2,1)S(1)}, bf16[48,1024]{1,0:T(8,128)(2,1)S(1)}, bf16[48,1024]{1,0:T(8,128)(2,1)S(1)}, bf16[48,1024]{1,0:T(8,128)(2,1)S(1)}, bf16[2,48,3584]{2,1,0:T(8,128)(2,1)S(1)}) custom-call(bf16[4,48,3584]{2,1,0:T(8,128)(2,1)} %bitcast.18, f32[30,128]{1,0:T(8,128)S(1)} %convert_select_fusion.small_ref), custom_call_target="tpu_custom_call" | custom-call | flops 1032192 | bytes 1376256 | tf_op jit(solution)/shard_map/pallas_call | solution.py:49
  2.8 5.1 %collective-permute-start = (bf16[48,1024]{1,0:T(8,128)(2,1)S(1)}, bf16[48,1024]{1,0:T(8,128)(2,1)S(1)}, u32[]{:S(2)}, u32[]{:S(2)}) collective-permute-start(bf16[48,1024]{1,0:T(8,128)(2,1)S(1)} %get-tuple-element.30), channel_id=1, source_target_pairs={{0,12},{4,8},{8,4},{12,0},{1,13},{5,9},{9,5},{13,1},{2,14},{6,10},... | collective-permute-start | bytes 294920 | tf_op jit(solution)/shard_map/ppermute | solution.py:348
  7.9 0.6 collective-permute-start.2
  8.6 0.8 constant_dynamic-slice_fusion
  9.4 2.3 %collective-permute-done.refs_0_.refs_3_ = bf16[48,1024]{1,0:T(8,128)(2,1)S(1)} collective-permute-done((bf16[48,1024]{1,0:T(8,128)(2,1)S(1)}, bf16[48,1024]{1,0:T(8,128)(2,1)S(1)}, u32[]{:S(2)}, u32[]{:S(2)}) %collective-permute-start) | collective-permute-done | bytes 98336 | tf_op jit(solution)/shard_map/ppermute | solution.py:348
  11.6 4.6 %collective-permute-done.1.refs_1_.refs_2_ = bf16[48,1024]{1,0:T(8,128)(2,1)S(1)} collective-permute-done((bf16[48,1024]{1,0:T(8,128)(2,1)S(1)}, bf16[48,1024]{1,0:T(8,128)(2,1)S(1)}, u32[]{:S(2)}, u32[]{:S(2)}) %collective-permute-start.1) | collective-permute-done | bytes 98336 | tf_op jit(solution)/shard_map/ppermute | solution.py:348
  16.2 0.4 shard_map.96
  16.6 0.1 collective-permute-start.4
  16.7 1.6 %collective-permute-start.3 = (bf16[128,896]{1,0:T(8,128)(2,1)S(1)}, bf16[128,896]{1,0:T(8,128)(2,1)S(1)}, u32[]{:S(2)}, u32[]{:S(2)}) collective-permute-start(bf16[128,896]{1,0:T(8,128)(2,1)S(1)} %get-tuple-element.42.refs_3_), channel_id=1, source_target_pairs={{0,2},{2,0},{1,3},{3,1},{4,6},{6,4},{5,7},{7,5},{8,10},{10,8},{9,1... | collective-permute-start | bytes 688136 | tf_op jit(solution)/shard_map/ppermute | solution.py:348
  18.2 2.4 %collective-permute-start.5 = (bf16[256,128]{1,0:T(8,128)(2,1)S(1)}, bf16[256,128]{1,0:T(8,128)(2,1)S(1)}, u32[]{:S(2)}, u32[]{:S(2)}) collective-permute-start(bf16[256,128]{1,0:T(8,128)(2,1)S(1)} %pad_maximum_fusion.2), channel_id=1, source_target_pairs={{0,4},{4,8},{8,12},{1,5},{5,9},{9,13},{2,6},{6,10},{10,14},{3,7},{... | collective-permute-start | bytes 196616 | tf_op jit(solution)/shard_map/ppermute | solution.py:353
  20.7 1.9 %collective-permute-done.5 = bf16[256,128]{1,0:T(8,128)(2,1)S(1)} collective-permute-done((bf16[256,128]{1,0:T(8,128)(2,1)S(1)}, bf16[256,128]{1,0:T(8,128)(2,1)S(1)}, u32[]{:S(2)}, u32[]{:S(2)}) %collective-permute-start.5) | collective-permute-done | bytes 65568 | tf_op jit(solution)/shard_map/ppermute | solution.py:353
  22.6 2.1 %collective-permute-done.3.refs_1_ = bf16[128,896]{1,0:T(8,128)(2,1)S(1)} collective-permute-done((bf16[128,896]{1,0:T(8,128)(2,1)S(1)}, bf16[128,896]{1,0:T(8,128)(2,1)S(1)}, u32[]{:S(2)}, u32[]{:S(2)}) %collective-permute-start.3) | collective-permute-done | bytes 229408 | tf_op jit(solution)/shard_map/ppermute | solution.py:348
  24.7 1.5 %collective-permute-done.6.refs_0_ = bf16[128,896]{1,0:T(8,128)(2,1)S(1)} collective-permute-done((bf16[128,896]{1,0:T(8,128)(2,1)S(1)}, bf16[128,896]{1,0:T(8,128)(2,1)S(1)}, u32[]{:S(2)}, u32[]{:S(2)}) %collective-permute-start.6) | collective-permute-done | bytes 229408 | tf_op jit(solution)/shard_map/ppermute | solution.py:348
  26.2 0.5 shard_map.97
  26.6 0.6 collective-permute-start.7
  27.2 4.5 %collective-permute-start.8 = (bf16[512,128]{1,0:T(8,128)(2,1)S(1)}, bf16[512,128]{1,0:T(8,128)(2,1)S(1)}, u32[]{:S(2)}, u32[]{:S(2)}) collective-permute-start(bf16[512,128]{1,0:T(8,128)(2,1)S(1)} %pad_maximum_fusion.1.near_ref), channel_id=1, source_target_pairs={{0,8},{4,12},{1,9},{5,13},{2,10},{6,14},{3,11},{7,15},{16,24},{20,... | collective-permute-start | bytes 393224 | tf_op jit(solution)/shard_map/ppermute | solution.py:353
  31.7 0.9 shard_map.98
  32.6 0.0 copy-start.1
  32.6 3.3 %collective-permute-done.8.far_ref = bf16[512,128]{1,0:T(8,128)(2,1)S(1)} collective-permute-done((bf16[512,128]{1,0:T(8,128)(2,1)S(1)}, bf16[512,128]{1,0:T(8,128)(2,1)S(1)}, u32[]{:S(2)}, u32[]{:S(2)}) %collective-permute-start.8) | collective-permute-done | bytes 131104 | tf_op jit(solution)/shard_map/ppermute | solution.py:353
  36.0 0.1 add_convert_fusion
  36.0 3.5 %collective-permute-start.9 = (bf16[128,1024]{1,0:T(8,128)(2,1)S(1)}, bf16[128,1024]{1,0:T(8,128)(2,1)S(1)}, u32[]{:S(2)}, u32[]{:S(2)}) collective-permute-start(bf16[128,1024]{1,0:T(8,128)(2,1)S(1)} %add_convert_fusion), channel_id=1, source_target_pairs={{0,8},{4,12},{8,0},{12,4},{1,9},{5,13},{9,1},{13,5},{2,10},{6,14},... | collective-permute-start | bytes 786440 | tf_op jit(solution)/shard_map/ppermute | solution.py:348
  39.5 0.4 shard_map.99
  40.0 1.7 %collective-permute-start.10 = (bf16[128,1024]{1,0:T(8,128)(2,1)S(1)}, bf16[128,1024]{1,0:T(8,128)(2,1)S(1)}, u32[]{:S(2)}, u32[]{:S(2)}) collective-permute-start(bf16[128,1024]{1,0:T(8,128)(2,1)S(1)} %shard_map.99), channel_id=1, source_target_pairs={{0,4},{4,0},{8,12},{12,8},{1,5},{5,1},{9,13},{13,9},{2,6},{6,2},{1... | collective-permute-start | bytes 786440 | tf_op jit(solution)/shard_map/ppermute | solution.py:348
  41.7 2.3 %shard_map.100 = bf16[128,1024]{1,0:T(8,128)(2,1)S(1)} custom-call(bf16[128,1024]{1,0:T(8,128)(2,1)S(1)} %copy-done.1, bf16[512,128]{1,0:T(8,128)(2,1)S(1)} %pad_maximum_fusion.1.near_ref, bf16[512,128]{1,0:T(8,128)(2,1)S(1)} %collective-permute-done.8.far_ref, bf16[48,1024]{1,0:T(8,128)(2,1)S(1)} %get-tuple-element.33.refs_3_.refs_0_, ...), custom_call_target="tpu_custom_call" | custom-call | bytes 524288 | tf_op jit(solution)/shard_map/pallas_call | solution.py:49
  44.0 7.0 %collective-permute-done.9 = bf16[128,1024]{1,0:T(8,128)(2,1)S(1)} collective-permute-done((bf16[128,1024]{1,0:T(8,128)(2,1)S(1)}, bf16[128,1024]{1,0:T(8,128)(2,1)S(1)}, u32[]{:S(2)}, u32[]{:S(2)}) %collective-permute-start.9) | collective-permute-done | bytes 262176 | tf_op jit(solution)/shard_map/ppermute | solution.py:348
  51.0 0.1 convert_add_fusion
  51.0 0.8 collective-permute-done.10
  51.9 0.1 subtract_convert_fusion.delta_ref
  52.0 0.6 collective-permute-start.12
  52.5 0.7 shard_map.101.first_ref
  53.2 2.7 %collective-permute-start.11 = (bf16[128,1024]{1,0:T(8,128)(2,1)S(1)}, bf16[128,1024]{1,0:T(8,128)(2,1)S(1)}, u32[]{:S(2)}, u32[]{:S(2)}) collective-permute-start(bf16[128,1024]{1,0:T(8,128)(2,1)S(1)} %subtract_convert_fusion.delta_ref), channel_id=1, source_target_pairs={{0,4},{4,0},{8,12},{12,8},{1,5},{5,1},{9,13},{13,9},{2,6},{6,2},{1... | collective-permute-start | bytes 786440 | tf_op jit(solution)/shard_map/ppermute | solution.py:348
  56.0 9.1 %collective-permute-done.12.delta_ref = bf16[128,1024]{1,0:T(8,128)(2,1)S(1)} collective-permute-done((bf16[128,1024]{1,0:T(8,128)(2,1)S(1)}, bf16[128,1024]{1,0:T(8,128)(2,1)S(1)}, u32[]{:S(2)}, u32[]{:S(2)}) %collective-permute-start.12) | collective-permute-done | bytes 262176 | tf_op jit(solution)/shard_map/ppermute | solution.py:348
  65.1 0.7 shard_map.103.third_ref
  65.8 0.2 collective-permute-done.11.delta_ref
  66.0 0.7 shard_map.102.second_ref
  66.7 4.8 %collective-permute-done.13.delta_ref = bf16[128,1024]{1,0:T(8,128)(2,1)S(1)} collective-permute-done((bf16[128,1024]{1,0:T(8,128)(2,1)S(1)}, bf16[128,1024]{1,0:T(8,128)(2,1)S(1)}, u32[]{:S(2)}, u32[]{:S(2)}) %collective-permute-start.13) | collective-permute-done | bytes 262176 | tf_op jit(solution)/shard_map/ppermute | solution.py:348
  71.5 0.8 shard_map.104
  72.3 0.1 collective-permute-start.14
  72.4 0.1 pad_maximum_fusion
  72.5 1.7 %collective-permute-done.14 = bf16[2,128,896]{2,1,0:T(8,128)(2,1)S(1)} collective-permute-done((bf16[2,128,896]{2,1,0:T(8,128)(2,1)S(1)}, bf16[2,128,896]{2,1,0:T(8,128)(2,1)S(1)}, u32[]{:S(2)}, u32[]{:S(2)}) %collective-permute-start.14) | collective-permute-done | bytes 458784 | tf_op jit(solution)/shard_map/ppermute | solution.py:348
  74.2 0.1 fusion
  74.3 1.5 %collective-permute-start.15 = (bf16[128,896]{1,0:T(8,128)(2,1)S(1)}, bf16[128,896]{1,0:T(8,128)(2,1)S(1)}, u32[]{:S(2)}, u32[]{:S(2)}) collective-permute-start(bf16[128,896]{1,0:T(8,128)(2,1)S(1)} %fusion), channel_id=1, source_target_pairs={{0,2},{2,0},{1,3},{3,1},{4,6},{6,4},{5,7},{7,5},{8,10},{10,8},{9,1... | collective-permute-start | bytes 688136 | tf_op jit(solution)/shard_map/ppermute | solution.py:348
  75.9 3.0 %convolution_multiply_fusion = f32[896,1024]{1,0:T(8,128)} fusion(bf16[512,896]{1,0:T(8,128)(2,1)S(1)} %get-tuple-element.48.normed_ref, bf16[512,1024]{1,0:T(8,128)(2,1)S(1)} %pad_maximum_fusion), kind=kOutput, calls=%fused_computation | convolution fusion | flops 940441600 | bytes 5636096 | tf_op jit(solution)/shard_map/dot_general | solution.py:22
  78.8 3.1 %collective-permute-done.15 = bf16[128,896]{1,0:T(8,128)(2,1)S(1)} collective-permute-done((bf16[128,896]{1,0:T(8,128)(2,1)S(1)}, bf16[128,896]{1,0:T(8,128)(2,1)S(1)}, u32[]{:S(2)}, u32[]{:S(2)}) %collective-permute-start.15) | collective-permute-done | bytes 229408 | tf_op jit(solution)/shard_map/ppermute | solution.py:348
  82.0 0.2 convolution_convert_fusion
  82.2 0.2 convolution_convert_fusion.1
  82.4 0.2 convolution_convert_fusion.2
  82.5 0.7 collective-permute-start.16
  83.2 3.4 %collective-permute-start.17 = (bf16[48,896]{1,0:T(8,128)(2,1)S(1)}, bf16[48,896]{1,0:T(8,128)(2,1)S(1)}, u32[]{:S(2)}, u32[]{:S(2)}) collective-permute-start(bf16[48,896]{1,0:T(8,128)(2,1)S(1)} %convolution_convert_fusion.1), channel_id=1, source_target_pairs={{0,8},{4,12},{8,0},{12,4},{1,9},{5,13},{9,1},{13,5},{2,10},{6,14},... | collective-permute-start | bytes 258056 | tf_op jit(solution)/shard_map/ppermute | solution.py:348
  86.6 0.4 collective-permute-start.18
  87.0 0.2 convolution_convert_fusion.3.refs_0_
  87.2 1.5 %collective-permute-start.19 = (bf16[48,896]{1,0:T(8,128)(2,1)S(1)}, bf16[48,896]{1,0:T(8,128)(2,1)S(1)}, u32[]{:S(2)}, u32[]{:S(2)}) collective-permute-start(bf16[48,896]{1,0:T(8,128)(2,1)S(1)} %convolution_convert_fusion.3.refs_0_), channel_id=1, source_target_pairs={{0,2},{2,0},{1,3},{3,1},{4,6},{6,4},{5,7},{7,5},{8,10},{10,8},{9,1... | collective-permute-start | bytes 258056 | tf_op jit(solution)/shard_map/ppermute | solution.py:348
  88.7 0.6 collective-permute-start.20
  89.3 2.6 %collective-permute-done.17.refs_2_ = bf16[48,896]{1,0:T(8,128)(2,1)S(1)} collective-permute-done((bf16[48,896]{1,0:T(8,128)(2,1)S(1)}, bf16[48,896]{1,0:T(8,128)(2,1)S(1)}, u32[]{:S(2)}, u32[]{:S(2)}) %collective-permute-start.17) | collective-permute-done | bytes 86048 | tf_op jit(solution)/shard_map/ppermute | solution.py:348
  91.9 1.5 %collective-permute-start.21 = (bf16[48,896]{1,0:T(8,128)(2,1)S(1)}, bf16[48,896]{1,0:T(8,128)(2,1)S(1)}, u32[]{:S(2)}, u32[]{:S(2)}) collective-permute-start(bf16[48,896]{1,0:T(8,128)(2,1)S(1)} %collective-permute-done.17.refs_2_), channel_id=1, source_target_pairs={{0,2},{2,0},{1,3},{3,1},{4,6},{6,4},{5,7},{7,5},{8,10},{10,8},{9,1... | collective-permute-start | bytes 258056 | tf_op jit(solution)/shard_map/ppermute | solution.py:348
  93.4 1.1 %collective-permute-start.22 = (bf16[48,896]{1,0:T(8,128)(2,1)S(1)}, bf16[48,896]{1,0:T(8,128)(2,1)S(1)}, u32[]{:S(2)}, u32[]{:S(2)}) collective-permute-start(bf16[48,896]{1,0:T(8,128)(2,1)S(1)} %collective-permute-done.18.refs_3_), channel_id=1, source_target_pairs={{0,2},{2,0},{1,3},{3,1},{4,6},{6,4},{5,7},{7,5},{8,10},{10,8},{9,1... | collective-permute-start | bytes 258056 | tf_op jit(solution)/shard_map/ppermute | solution.py:348
  94.5 1.9 %collective-permute-done.21.refs_6_ = bf16[48,896]{1,0:T(8,128)(2,1)S(1)} collective-permute-done((bf16[48,896]{1,0:T(8,128)(2,1)S(1)}, bf16[48,896]{1,0:T(8,128)(2,1)S(1)}, u32[]{:S(2)}, u32[]{:S(2)}) %collective-permute-start.21) | collective-permute-done | bytes 86048 | tf_op jit(solution)/shard_map/ppermute | solution.py:348
  96.4 1.5 %collective-permute-done.22.refs_7_ = bf16[48,896]{1,0:T(8,128)(2,1)S(1)} collective-permute-done((bf16[48,896]{1,0:T(8,128)(2,1)S(1)}, bf16[48,896]{1,0:T(8,128)(2,1)S(1)}, u32[]{:S(2)}, u32[]{:S(2)}) %collective-permute-start.22) | collective-permute-done | bytes 86048 | tf_op jit(solution)/shard_map/ppermute | solution.py:348
  97.9 0.7 shard_map.105.pair_ref
  98.6 0.1 collective-permute-start.23
  98.7 0.9 shard_map.106.t
  99.5 1.3 %collective-permute-done.23.refs_0_ = bf16[2,48,3584]{2,1,0:T(8,128)(2,1)S(1)} collective-permute-done((bf16[2,48,3584]{2,1,0:T(8,128)(2,1)S(1)}, bf16[2,48,3584]{2,1,0:T(8,128)(2,1)S(1)}, u32[]{:S(2)}, u32[]{:S(2)}) %collective-permute-start.23) | collective-permute-done | bytes 688160 | tf_op jit(solution)/shard_map/ppermute | solution.py:348
  100.8 0.9 shard_map.107
  (19 shorter events, 0.2 us)
Async XLA Ops:
  0.6 25.6 %copy-start = (bf16[896,1024]{1,0:T(8,128)(2,1)S(1)}, bf16[896,1024]{1,0:T(8,128)(2,1)}, u32[]{:S(2)}) copy-start(bf16[896,1024]{1,0:T(8,128)(2,1)} %proj_ref.9) | copy-start | bytes 5505028
  2.8 8.8 %collective-permute-start = (bf16[48,1024]{1,0:T(8,128)(2,1)S(1)}, bf16[48,1024]{1,0:T(8,128)(2,1)S(1)}, u32[]{:S(2)}, u32[]{:S(2)}) collective-permute-start(bf16[48,1024]{1,0:T(8,128)(2,1)S(1)} %get-tuple-element.30), channel_id=1, source_target_pairs={{0,12},{4,8},{8,4},{12,0},{1,13},{5,9},{9,5},{13,1},{2,14},{6,10},... | collective-permute-start | bytes 294920 | tf_op jit(solution)/shard_map/ppermute | solution.py:348
  7.9 8.3 %collective-permute-start.1 = (bf16[48,1024]{1,0:T(8,128)(2,1)S(1)}, bf16[48,1024]{1,0:T(8,128)(2,1)S(1)}, u32[]{:S(2)}, u32[]{:S(2)}) collective-permute-start(bf16[48,1024]{1,0:T(8,128)(2,1)S(1)} %get-tuple-element.31), channel_id=1, source_target_pairs={{0,8},{4,12},{8,0},{12,4},{1,9},{5,13},{9,1},{13,5},{2,10},{6,14},... | collective-permute-start | bytes 294920 | tf_op jit(solution)/shard_map/ppermute | solution.py:348
  7.9 8.3 %collective-permute-start.2 = (bf16[48,1024]{1,0:T(8,128)(2,1)S(1)}, bf16[48,1024]{1,0:T(8,128)(2,1)S(1)}, u32[]{:S(2)}, u32[]{:S(2)}) collective-permute-start(bf16[48,1024]{1,0:T(8,128)(2,1)S(1)} %get-tuple-element.32), channel_id=1, source_target_pairs={{0,4},{4,0},{8,12},{12,8},{1,5},{5,1},{9,13},{13,9},{2,6},{6,2},{1... | collective-permute-start | bytes 294920 | tf_op jit(solution)/shard_map/ppermute | solution.py:348
  16.6 6.0 %collective-permute-start.4 = (bf16[128,896]{1,0:T(8,128)(2,1)S(1)}, bf16[128,896]{1,0:T(8,128)(2,1)S(1)}, u32[]{:S(2)}, u32[]{:S(2)}) collective-permute-start(bf16[128,896]{1,0:T(8,128)(2,1)S(1)} %get-tuple-element.42.refs_3_), channel_id=1, source_target_pairs={{0,1},{1,0},{2,3},{3,2},{4,5},{5,4},{6,7},{7,6},{8,9},{9,8},{10,11... | collective-permute-start | bytes 688136 | tf_op jit(solution)/shard_map/ppermute | solution.py:348
  16.7 8.0 %collective-permute-start.3 = (bf16[128,896]{1,0:T(8,128)(2,1)S(1)}, bf16[128,896]{1,0:T(8,128)(2,1)S(1)}, u32[]{:S(2)}, u32[]{:S(2)}) collective-permute-start(bf16[128,896]{1,0:T(8,128)(2,1)S(1)} %get-tuple-element.42.refs_3_), channel_id=1, source_target_pairs={{0,2},{2,0},{1,3},{3,1},{4,6},{6,4},{5,7},{7,5},{8,10},{10,8},{9,1... | collective-permute-start | bytes 688136 | tf_op jit(solution)/shard_map/ppermute | solution.py:348
  18.2 4.3 %collective-permute-start.5 = (bf16[256,128]{1,0:T(8,128)(2,1)S(1)}, bf16[256,128]{1,0:T(8,128)(2,1)S(1)}, u32[]{:S(2)}, u32[]{:S(2)}) collective-permute-start(bf16[256,128]{1,0:T(8,128)(2,1)S(1)} %pad_maximum_fusion.2), channel_id=1, source_target_pairs={{0,4},{4,8},{8,12},{1,5},{5,9},{9,13},{2,6},{6,10},{10,14},{3,7},{... | collective-permute-start | bytes 196616 | tf_op jit(solution)/shard_map/ppermute | solution.py:353
  24.7 1.5 %collective-permute-start.6 = (bf16[128,896]{1,0:T(8,128)(2,1)S(1)}, bf16[128,896]{1,0:T(8,128)(2,1)S(1)}, u32[]{:S(2)}, u32[]{:S(2)}) collective-permute-start(bf16[128,896]{1,0:T(8,128)(2,1)S(1)} %collective-permute-done.3.refs_1_), channel_id=1, source_target_pairs={{0,1},{1,0},{2,3},{3,2},{4,5},{5,4},{6,7},{7,6},{8,9},{9,8},{10,11... | collective-permute-start | bytes 688136 | tf_op jit(solution)/shard_map/ppermute | solution.py:348
  26.6 9.3 %collective-permute-start.7 = (bf16[128,1024]{1,0:T(8,128)(2,1)S(1)}, bf16[128,1024]{1,0:T(8,128)(2,1)S(1)}, u32[]{:S(2)}, u32[]{:S(2)}) collective-permute-start(bf16[128,1024]{1,0:T(8,128)(2,1)S(1)} %shard_map.97), channel_id=1, source_target_pairs={{0,4},{4,0},{8,12},{12,8},{1,5},{5,1},{9,13},{13,9},{2,6},{6,2},{1... | collective-permute-start | bytes 786440 | tf_op jit(solution)/shard_map/ppermute | solution.py:348
  27.2 8.7 %collective-permute-start.8 = (bf16[512,128]{1,0:T(8,128)(2,1)S(1)}, bf16[512,128]{1,0:T(8,128)(2,1)S(1)}, u32[]{:S(2)}, u32[]{:S(2)}) collective-permute-start(bf16[512,128]{1,0:T(8,128)(2,1)S(1)} %pad_maximum_fusion.1.near_ref), channel_id=1, source_target_pairs={{0,8},{4,12},{1,9},{5,13},{2,10},{6,14},{3,11},{7,15},{16,24},{20,... | collective-permute-start | bytes 393224 | tf_op jit(solution)/shard_map/ppermute | solution.py:353
  32.6 9.0 %copy-start.1 = (bf16[128,1024]{1,0:T(8,128)(2,1)S(1)}, bf16[128,1024]{1,0:T(8,128)(2,1)}, u32[]{:S(2)}) copy-start(bf16[128,1024]{1,0:T(8,128)(2,1)} %queries_ref) | copy-start | bytes 786436
  36.0 15.0 %collective-permute-start.9 = (bf16[128,1024]{1,0:T(8,128)(2,1)S(1)}, bf16[128,1024]{1,0:T(8,128)(2,1)S(1)}, u32[]{:S(2)}, u32[]{:S(2)}) collective-permute-start(bf16[128,1024]{1,0:T(8,128)(2,1)S(1)} %add_convert_fusion), channel_id=1, source_target_pairs={{0,8},{4,12},{8,0},{12,4},{1,9},{5,13},{9,1},{13,5},{2,10},{6,14},... | collective-permute-start | bytes 786440 | tf_op jit(solution)/shard_map/ppermute | solution.py:348
  40.0 11.9 %collective-permute-start.10 = (bf16[128,1024]{1,0:T(8,128)(2,1)S(1)}, bf16[128,1024]{1,0:T(8,128)(2,1)S(1)}, u32[]{:S(2)}, u32[]{:S(2)}) collective-permute-start(bf16[128,1024]{1,0:T(8,128)(2,1)S(1)} %shard_map.99), channel_id=1, source_target_pairs={{0,4},{4,0},{8,12},{12,8},{1,5},{5,1},{9,13},{13,9},{2,6},{6,2},{1... | collective-permute-start | bytes 786440 | tf_op jit(solution)/shard_map/ppermute | solution.py:348
  52.0 13.1 %collective-permute-start.12 = (bf16[128,1024]{1,0:T(8,128)(2,1)S(1)}, bf16[128,1024]{1,0:T(8,128)(2,1)S(1)}, u32[]{:S(2)}, u32[]{:S(2)}) collective-permute-start(bf16[128,1024]{1,0:T(8,128)(2,1)S(1)} %subtract_convert_fusion.delta_ref), channel_id=1, source_target_pairs={{0,8},{4,12},{8,0},{12,4},{1,9},{5,13},{9,1},{13,5},{2,10},{6,14},... | collective-permute-start | bytes 786440 | tf_op jit(solution)/shard_map/ppermute | solution.py:348
  53.2 12.8 %collective-permute-start.11 = (bf16[128,1024]{1,0:T(8,128)(2,1)S(1)}, bf16[128,1024]{1,0:T(8,128)(2,1)S(1)}, u32[]{:S(2)}, u32[]{:S(2)}) collective-permute-start(bf16[128,1024]{1,0:T(8,128)(2,1)S(1)} %subtract_convert_fusion.delta_ref), channel_id=1, source_target_pairs={{0,4},{4,0},{8,12},{12,8},{1,5},{5,1},{9,13},{13,9},{2,6},{6,2},{1... | collective-permute-start | bytes 786440 | tf_op jit(solution)/shard_map/ppermute | solution.py:348
  65.1 6.5 %collective-permute-start.13 = (bf16[128,1024]{1,0:T(8,128)(2,1)S(1)}, bf16[128,1024]{1,0:T(8,128)(2,1)S(1)}, u32[]{:S(2)}, u32[]{:S(2)}) collective-permute-start(bf16[128,1024]{1,0:T(8,128)(2,1)S(1)} %collective-permute-done.12.delta_ref), channel_id=1, source_target_pairs={{0,4},{4,0},{8,12},{12,8},{1,5},{5,1},{9,13},{13,9},{2,6},{6,2},{1... | collective-permute-start | bytes 786440 | tf_op jit(solution)/shard_map/ppermute | solution.py:348
  72.3 1.9 %collective-permute-start.14 = (bf16[2,128,896]{2,1,0:T(8,128)(2,1)S(1)}, bf16[2,128,896]{2,1,0:T(8,128)(2,1)S(1)}, u32[]{:S(2)}, u32[]{:S(2)}) collective-permute-start(bf16[2,128,896]{2,1,0:T(8,128)(2,1)S(1)} %get-tuple-element.52), channel_id=1, source_target_pairs={{0,1},{1,0},{2,3},{3,2},{4,5},{5,4},{6,7},{7,6},{8,9},{9,8},{10,11... | collective-permute-start | bytes 1376264 | tf_op jit(solution)/shard_map/ppermute | solution.py:348
  74.3 7.7 %collective-permute-start.15 = (bf16[128,896]{1,0:T(8,128)(2,1)S(1)}, bf16[128,896]{1,0:T(8,128)(2,1)S(1)}, u32[]{:S(2)}, u32[]{:S(2)}) collective-permute-start(bf16[128,896]{1,0:T(8,128)(2,1)S(1)} %fusion), channel_id=1, source_target_pairs={{0,2},{2,0},{1,3},{3,1},{4,6},{6,4},{5,7},{7,5},{8,10},{10,8},{9,1... | collective-permute-start | bytes 688136 | tf_op jit(solution)/shard_map/ppermute | solution.py:348
  82.5 6.2 %collective-permute-start.16 = (bf16[48,896]{1,0:T(8,128)(2,1)S(1)}, bf16[48,896]{1,0:T(8,128)(2,1)S(1)}, u32[]{:S(2)}, u32[]{:S(2)}) collective-permute-start(bf16[48,896]{1,0:T(8,128)(2,1)S(1)} %convolution_convert_fusion.2), channel_id=1, source_target_pairs={{0,4},{4,0},{8,12},{12,8},{1,5},{5,1},{9,13},{13,9},{2,6},{6,2},{1... | collective-permute-start | bytes 258056 | tf_op jit(solution)/shard_map/ppermute | solution.py:348
  83.2 8.7 %collective-permute-start.17 = (bf16[48,896]{1,0:T(8,128)(2,1)S(1)}, bf16[48,896]{1,0:T(8,128)(2,1)S(1)}, u32[]{:S(2)}, u32[]{:S(2)}) collective-permute-start(bf16[48,896]{1,0:T(8,128)(2,1)S(1)} %convolution_convert_fusion.1), channel_id=1, source_target_pairs={{0,8},{4,12},{8,0},{12,4},{1,9},{5,13},{9,1},{13,5},{2,10},{6,14},... | collective-permute-start | bytes 258056 | tf_op jit(solution)/shard_map/ppermute | solution.py:348
  86.6 6.8 %collective-permute-start.18 = (bf16[48,896]{1,0:T(8,128)(2,1)S(1)}, bf16[48,896]{1,0:T(8,128)(2,1)S(1)}, u32[]{:S(2)}, u32[]{:S(2)}) collective-permute-start(bf16[48,896]{1,0:T(8,128)(2,1)S(1)} %convolution_convert_fusion), channel_id=1, source_target_pairs={{0,12},{4,8},{8,4},{12,0},{1,13},{5,9},{9,5},{13,1},{2,14},{6,10},... | collective-permute-start | bytes 258056 | tf_op jit(solution)/shard_map/ppermute | solution.py:348
  87.2 7.3 %collective-permute-start.19 = (bf16[48,896]{1,0:T(8,128)(2,1)S(1)}, bf16[48,896]{1,0:T(8,128)(2,1)S(1)}, u32[]{:S(2)}, u32[]{:S(2)}) collective-permute-start(bf16[48,896]{1,0:T(8,128)(2,1)S(1)} %convolution_convert_fusion.3.refs_0_), channel_id=1, source_target_pairs={{0,2},{2,0},{1,3},{3,1},{4,6},{6,4},{5,7},{7,5},{8,10},{10,8},{9,1... | collective-permute-start | bytes 258056 | tf_op jit(solution)/shard_map/ppermute | solution.py:348
  88.7 5.8 %collective-permute-start.20 = (bf16[48,896]{1,0:T(8,128)(2,1)S(1)}, bf16[48,896]{1,0:T(8,128)(2,1)S(1)}, u32[]{:S(2)}, u32[]{:S(2)}) collective-permute-start(bf16[48,896]{1,0:T(8,128)(2,1)S(1)} %collective-permute-done.16.refs_1_), channel_id=1, source_target_pairs={{0,2},{2,0},{1,3},{3,1},{4,6},{6,4},{5,7},{7,5},{8,10},{10,8},{9,1... | collective-permute-start | bytes 258056 | tf_op jit(solution)/shard_map/ppermute | solution.py:348
  91.9 4.5 %collective-permute-start.21 = (bf16[48,896]{1,0:T(8,128)(2,1)S(1)}, bf16[48,896]{1,0:T(8,128)(2,1)S(1)}, u32[]{:S(2)}, u32[]{:S(2)}) collective-permute-start(bf16[48,896]{1,0:T(8,128)(2,1)S(1)} %collective-permute-done.17.refs_2_), channel_id=1, source_target_pairs={{0,2},{2,0},{1,3},{3,1},{4,6},{6,4},{5,7},{7,5},{8,10},{10,8},{9,1... | collective-permute-start | bytes 258056 | tf_op jit(solution)/shard_map/ppermute | solution.py:348
  93.4 4.5 %collective-permute-start.22 = (bf16[48,896]{1,0:T(8,128)(2,1)S(1)}, bf16[48,896]{1,0:T(8,128)(2,1)S(1)}, u32[]{:S(2)}, u32[]{:S(2)}) collective-permute-start(bf16[48,896]{1,0:T(8,128)(2,1)S(1)} %collective-permute-done.18.refs_3_), channel_id=1, source_target_pairs={{0,2},{2,0},{1,3},{3,1},{4,6},{6,4},{5,7},{7,5},{8,10},{10,8},{9,1... | collective-permute-start | bytes 258056 | tf_op jit(solution)/shard_map/ppermute | solution.py:348
  98.6 2.2 %collective-permute-start.23 = (bf16[2,48,3584]{2,1,0:T(8,128)(2,1)S(1)}, bf16[2,48,3584]{2,1,0:T(8,128)(2,1)S(1)}, u32[]{:S(2)}, u32[]{:S(2)}) collective-permute-start(bf16[2,48,3584]{2,1,0:T(8,128)(2,1)S(1)} %shard_map.105.pair_ref), channel_id=1, source_target_pairs={{0,1},{1,0},{2,3},{3,2},{4,5},{5,4},{6,7},{7,6},{8,9},{9,8},{10,11... | collective-permute-start | bytes 2064392 | tf_op jit(solution)/shard_map/ppermute | solution.py:348

commit v8 on v6

--- a/solution.py
+++ b/solution.py
@@ -177,7 +177,6 @@
 
 def attention_rows(queries, parcels, pieces):
     tokens, width = queries.shape
-    n = len(parcels)
     return call(
         attention_kernel,
         jax.ShapeDtypeStruct((tokens, width), BF),
@@ -269,6 +268,20 @@
         0,
         scratch_shapes=[pltpu.VMEM((4, tokens, depth), BF)],
     )
+
+
+def leave_kernel(peers, drop_ref, kept_ref, got_ref, crossed_ref, *outs):
+    near = kept_ref[0].astype(F32) + got_ref[0].astype(F32)
+    rows = (near + crossed_ref[...].astype(F32)).astype(BF)
+    slots = outs[0].shape[0]
+    for k, out in zip(peers, outs):
+        out[...] = dot(drop_ref[k * slots : (k + 1) * slots, :], rows).astype(BF)
+
+
+def leaving_rows(peers, drop, kept, got, crossed):
+    out = jax.ShapeDtypeStruct((drop.shape[0] // 4, crossed.shape[1]), BF)
+    kernel = functools.partial(leave_kernel, peers)
+    return call(kernel, [out] * len(peers), (drop, kept, got, crossed), 0, 0)
 
 
 def rows_kernel(hidden_ref, small_ref, *refs):
@@ -381,7 +394,6 @@
 
     *made, hidden = norm_pieces(student, small)
     pieces = [made[0]] + exchange(made)
-    normed_own, drop = pick_rows(pieces, rows)
 
     head = side * heads // group
     parcel = jnp.concatenate(
@@ -390,22 +402,23 @@
             lax.dynamic_slice_in_dim(teacher_values, head * HD, HD, 1),
         ]
     )
-    parcel = after(lax.optimization_barrier(parcel), normed_own)
+    parcels = [after(lax.optimization_barrier(parcel), made[0])]
+    parcels.append(onward(parcels[0]))
+    normed_own, drop = pick_rows([after(piece, parcels[1]) for piece in pieces], rows)
 
     far = swap(normed_own, "mp")
-    mate = swap(after(normed_own, parcel), "side")
-    parcels = [parcel, onward(parcel)]
-    far_mate = swap(after(far, mate, parcels[1]), "side")
+    mate = swap(normed_own, "side")
+    parcels.append(onward(after(parcels[1], normed_own)))
+    far_mate = swap(after(far, mate, parcels[2]), "side")
     entries = [far_mate, far, mate, normed_own]
 
     away = away_partial(entries, proj)
     own, over_own, normed = kept_partials([after(e, away) for e in entries], proj)
-    parcels.append(onward(after(parcels[1], away)))
-    got_over = after(swap(away, "seq", 1), over_own, parcels[2])
+    parcels.append(onward(after(parcels[2], away)))
+    got_over = after(swap(away, "seq", 1), over_own, parcels[3])
     over = lax.optimization_barrier((over_own + got_over.astype(F32)).astype(BF))
     got_far = swap(over, "seq", 2)
     got_beside = swap(beside_partial(after(normed, over), proj), "seq", 1)
-    parcels.append(onward(after(parcels[2], over)))
     teacher_rows = attention_rows(after(teacher_queries, over), parcels, pieces)
     predicted = lax.optimization_barrier(own + got_far.astype(F32)) + got_beside.astype(F32)
     delta = (predicted - teacher_rows.astype(F32)).astype(BF)
@@ -421,14 +434,13 @@
     got = swap(sent, "side")
     cross = lax.optimization_barrier((kept[1].astype(F32) + got[1].astype(F32)).astype(BF))
     crossed = swap(cross, "mp")
-    near = lax.optimization_barrier(kept[0].astype(F32) + after(got[0], cross).astype(F32))
 
     factor = 1.0 / math.sqrt(rows * n)
     deltas = after(jnp.concatenate([deltas[k] for k in (0, 2, 1, 3)]), cross)
     grad_proj = lax.optimization_barrier(dot(normed, deltas, ((0,), (0,))) * factor)
-    feature_rows = (near + after(crossed, grad_proj).astype(F32)).astype(BF)
-
-    leaving = [dot(drop[k * slots : (k + 1) * slots], feature_rows).astype(BF) for k in range(n)]
+    crossed = after(crossed, grad_proj)
+    leaving = leaving_rows(range(n), drop, kept, got, crossed)
+
     arrived = [leaving[0]] + exchange(leaving)
     across = [swap(block, "mp") for block in arrived]
     grad_pair = grad_rows(hidden, small, arrived + across)

time: 106 us -> 102 us (0.962)
  waiting for transfers between devices: 54.3 us -> 44.4 us
  starting transfers between devices: 33.7 us -> 39.9 us
    ppermute x22, waiting for transfers between devices: 46.3 us -> 35.1 us  [swap(): lax.ppermute(x, axis, [(i, i ^ k) for i in range(lax.axis_size(axis))])]
    ppermute x22, starting transfers between devices: 23.5 us -> 30.8 us  [swap(): lax.ppermute(x, axis, [(i, i ^ k) for i in range(lax.axis_size(axis))])]
    ppermute x3, waiting for transfers between devices: 7.92 us -> 9.25 us  [onward(): lax.ppermute(x, 'seq', [(i, i + 1) for i in range(lax.axis_size('seq') -...]
    ppermute x3, starting transfers between devices: 10.2 us -> 9.11 us  [onward(): lax.ppermute(x, 'seq', [(i, i + 1) for i in range(lax.axis_size('seq') -...]
    dot_general x5 -> x1, matrix products: 3.65 us -> 2.98 us  [dot(): return lax.dot_general(a, b, (dims, ((), ())), preferred_element_type=F32)]
    pallas_call x13 -> x14, Pallas kernels: 11 us -> 11.4 us  [call(): pl.pallas_call(kernel, out_shape=shapes, cost_estimate=pl.CostEstimate(fl...]
  transfers between devices with their start and end apart: 25 -> 25, of which waited for: 20 -> 16; matrix products, arithmetic and copies ran while one was open for 4% -> 4% of each run, Pallas kernels for 6% -> 7%
where the time goes in v8:
time: 102 us
  waiting for transfers between devices  44.4 us (44%)
  starting transfers between devices  39.9 us (39%)
  Pallas kernels  11.4 us (11%)
  matrix products  2.98 us (3%)
  other arithmetic  1.29 us (1%)
    ppermute x22, waiting for transfers between devices, swap(): lax.ppermute(x, axis, [(i, i ^ k) for i in range(lax.axis_size(axis))])  35.1 us
    ppermute x22, starting transfers between devices, swap(): lax.ppermute(x, axis, [(i, i ^ k) for i in range(lax.axis_size(axis))])  30.8 us
    pallas_call x14, Pallas kernels, call(): pl.pallas_call(kernel, out_shape=shapes, cost_estimate=pl.CostEstimate(fl...  11.4 us
    ppermute x3, waiting for transfers between devices, onward(): lax.ppermute(x, 'seq', [(i, i + 1) for i in range(lax.axis_size('seq') -...  9.25 us
    ppermute x3, starting transfers between devices, onward(): lax.ppermute(x, 'seq', [(i, i + 1) for i in range(lax.axis_size('seq') -...  9.11 us
    dot_general x1, matrix products, dot(): return lax.dot_general(a, b, (dims, ((), ())), preferred_element_type=F32)  2.98 us
  transfers between devices with their start and end apart: 25, of which 16 were waited for; matrix products, arithmetic and copies ran while one was open for 4% of the time, Pallas kernels for 7%

profile of v8, /device:TPU:0, one launch (start us, length us, event | category | flops | bytes accessed | tf_op | source)
XLA Modules:
  0.0 101.6 jit_solution(8622242675290051837)
XLA Ops:
  0.7 0.9 convert_select_fusion.small_ref
  1.6 1.2 %shard_map.95 = (bf16[48,1024]{1,0:T(8,128)(2,1)S(1)}, bf16[48,1024]{1,0:T(8,128)(2,1)S(1)}, bf16[48,1024]{1,0:T(8,128)(2,1)S(1)}, bf16[48,1024]{1,0:T(8,128)(2,1)S(1)}, bf16[2,48,3584]{2,1,0:T(8,128)(2,1)S(1)}) custom-call(bf16[4,48,3584]{2,1,0:T(8,128)(2,1)} %bitcast.9, f32[30,128]{1,0:T(8,128)S(1)} %convert_select_fusion.small_ref), custom_call_target="tpu_custom_call" | custom-call | flops 1032192 | bytes 1376256 | tf_op jit(solution)/shard_map/pallas_call | solution.py:49
  2.8 5.1 %collective-permute-start = (bf16[48,1024]{1,0:T(8,128)(2,1)S(1)}, bf16[48,1024]{1,0:T(8,128)(2,1)S(1)}, u32[]{:S(2)}, u32[]{:S(2)}) collective-permute-start(bf16[48,1024]{1,0:T(8,128)(2,1)S(1)} %get-tuple-element.37), channel_id=1, source_target_pairs={{0,12},{4,8},{8,4},{12,0},{1,13},{5,9},{9,5},{13,1},{2,14},{6,10},... | collective-permute-start | bytes 294920 | tf_op jit(solution)/shard_map/ppermute | solution.py:360
  7.9 0.6 collective-permute-start.3
  8.6 0.8 constant_dynamic-slice_fusion
  9.4 3.3 %collective-permute-start.1 = (bf16[256,128]{1,0:T(8,128)(2,1)S(1)}, bf16[256,128]{1,0:T(8,128)(2,1)S(1)}, u32[]{:S(2)}, u32[]{:S(2)}) collective-permute-start(bf16[256,128]{1,0:T(8,128)(2,1)S(1)} %pad_maximum_fusion.1.refs_0_), channel_id=1, source_target_pairs={{0,4},{4,8},{8,12},{1,5},{5,9},{9,13},{2,6},{6,10},{10,14},{3,7},{... | collective-permute-start | bytes 196616 | tf_op jit(solution)/shard_map/ppermute | solution.py:364
  12.7 3.0 %collective-permute-done.1.refs_1_ = bf16[256,128]{1,0:T(8,128)(2,1)S(1)} collective-permute-done((bf16[256,128]{1,0:T(8,128)(2,1)S(1)}, bf16[256,128]{1,0:T(8,128)(2,1)S(1)}, u32[]{:S(2)}, u32[]{:S(2)}) %collective-permute-start.1) | collective-permute-done | bytes 65568 | tf_op jit(solution)/shard_map/ppermute | solution.py:364
  15.7 0.0 collective-permute-done.refs_0_.refs_7_
  15.7 0.5 collective-permute-done.2.refs_1_.refs_6_
  16.2 0.4 shard_map.96
  16.6 0.1 collective-permute-start.5
  16.7 1.6 %collective-permute-start.4 = (bf16[128,896]{1,0:T(8,128)(2,1)S(1)}, bf16[128,896]{1,0:T(8,128)(2,1)S(1)}, u32[]{:S(2)}, u32[]{:S(2)}) collective-permute-start(bf16[128,896]{1,0:T(8,128)(2,1)S(1)} %get-tuple-element.53.refs_3_), channel_id=1, source_target_pairs={{0,2},{2,0},{1,3},{3,1},{4,6},{6,4},{5,7},{7,5},{8,10},{10,8},{9,1... | collective-permute-start | bytes 688136 | tf_op jit(solution)/shard_map/ppermute | solution.py:360
  18.2 3.8 %collective-permute-start.6 = (bf16[256,128]{1,0:T(8,128)(2,1)S(1)}, bf16[256,128]{1,0:T(8,128)(2,1)S(1)}, u32[]{:S(2)}, u32[]{:S(2)}) collective-permute-start(bf16[256,128]{1,0:T(8,128)(2,1)S(1)} %collective-permute-done.1.refs_1_), channel_id=1, source_target_pairs={{0,4},{4,8},{8,12},{1,5},{5,9},{9,13},{2,6},{6,10},{10,14},{3,7},{... | collective-permute-start | bytes 196616 | tf_op jit(solution)/shard_map/ppermute | solution.py:364
  22.1 1.9 %collective-permute-done.6.refs_2_ = bf16[256,128]{1,0:T(8,128)(2,1)S(1)} collective-permute-done((bf16[256,128]{1,0:T(8,128)(2,1)S(1)}, bf16[256,128]{1,0:T(8,128)(2,1)S(1)}, u32[]{:S(2)}, u32[]{:S(2)}) %collective-permute-start.6) | collective-permute-done | bytes 65568 | tf_op jit(solution)/shard_map/ppermute | solution.py:364
  24.0 0.7 collective-permute-done.4.refs_1_
  24.7 1.5 %collective-permute-done.7.refs_0_ = bf16[128,896]{1,0:T(8,128)(2,1)S(1)} collective-permute-done((bf16[128,896]{1,0:T(8,128)(2,1)S(1)}, bf16[128,896]{1,0:T(8,128)(2,1)S(1)}, u32[]{:S(2)}, u32[]{:S(2)}) %collective-permute-start.7) | collective-permute-done | bytes 229408 | tf_op jit(solution)/shard_map/ppermute | solution.py:360
  26.2 0.5 shard_map.97
  26.6 2.0 %collective-permute-start.8 = (bf16[128,1024]{1,0:T(8,128)(2,1)S(1)}, bf16[128,1024]{1,0:T(8,128)(2,1)S(1)}, u32[]{:S(2)}, u32[]{:S(2)}) collective-permute-start(bf16[128,1024]{1,0:T(8,128)(2,1)S(1)} %shard_map.97), channel_id=1, source_target_pairs={{0,4},{4,0},{8,12},{12,8},{1,5},{5,1},{9,13},{13,9},{2,6},{6,2},{1... | collective-permute-start | bytes 786440 | tf_op jit(solution)/shard_map/ppermute | solution.py:360
  28.7 2.0 %collective-permute-start.9 = (bf16[256,128]{1,0:T(8,128)(2,1)S(1)}, bf16[256,128]{1,0:T(8,128)(2,1)S(1)}, u32[]{:S(2)}, u32[]{:S(2)}) collective-permute-start(bf16[256,128]{1,0:T(8,128)(2,1)S(1)} %collective-permute-done.6.refs_2_), channel_id=1, source_target_pairs={{0,4},{4,8},{8,12},{1,5},{5,9},{9,13},{2,6},{6,10},{10,14},{3,7},{... | collective-permute-start | bytes 196616 | tf_op jit(solution)/shard_map/ppermute | solution.py:364
  30.6 0.9 shard_map.98
  31.5 0.0 copy-start.1
  31.6 4.4 %collective-permute-done.9.refs_3_ = bf16[256,128]{1,0:T(8,128)(2,1)S(1)} collective-permute-done((bf16[256,128]{1,0:T(8,128)(2,1)S(1)}, bf16[256,128]{1,0:T(8,128)(2,1)S(1)}, u32[]{:S(2)}, u32[]{:S(2)}) %collective-permute-start.9) | collective-permute-done | bytes 65568 | tf_op jit(solution)/shard_map/ppermute | solution.py:364
  35.9 0.0 collective-permute-done.8
  35.9 0.1 add_convert_fusion
  36.0 2.4 %collective-permute-start.10 = (bf16[128,1024]{1,0:T(8,128)(2,1)S(1)}, bf16[128,1024]{1,0:T(8,128)(2,1)S(1)}, u32[]{:S(2)}, u32[]{:S(2)}) collective-permute-start(bf16[128,1024]{1,0:T(8,128)(2,1)S(1)} %add_convert_fusion), channel_id=1, source_target_pairs={{0,8},{4,12},{8,0},{12,4},{1,9},{5,13},{9,1},{13,5},{2,10},{6,14},... | collective-permute-start | bytes 786440 | tf_op jit(solution)/shard_map/ppermute | solution.py:360
  38.4 0.4 shard_map.99
  38.8 2.5 %collective-permute-start.11 = (bf16[128,1024]{1,0:T(8,128)(2,1)S(1)}, bf16[128,1024]{1,0:T(8,128)(2,1)S(1)}, u32[]{:S(2)}, u32[]{:S(2)}) collective-permute-start(bf16[128,1024]{1,0:T(8,128)(2,1)S(1)} %shard_map.99), channel_id=1, source_target_pairs={{0,4},{4,0},{8,12},{12,8},{1,5},{5,1},{9,13},{13,9},{2,6},{6,2},{1... | collective-permute-start | bytes 786440 | tf_op jit(solution)/shard_map/ppermute | solution.py:360
  41.4 2.4 %shard_map.100 = bf16[128,1024]{1,0:T(8,128)(2,1)S(1)} custom-call(bf16[128,1024]{1,0:T(8,128)(2,1)S(1)} %copy-done.1, bf16[256,128]{1,0:T(8,128)(2,1)S(1)} %pad_maximum_fusion.1.refs_0_, bf16[256,128]{1,0:T(8,128)(2,1)S(1)} %collective-permute-done.1.refs_1_, bf16[256,128]{1,0:T(8,128)(2,1)S(1)} %collective-permute-done.6.refs_2_, ...), custom_call_target="tpu_custom_call" | custom-call | bytes 524288 | tf_op jit(solution)/shard_map/pallas_call | solution.py:49
  43.7 6.5 %collective-permute-done.10 = bf16[128,1024]{1,0:T(8,128)(2,1)S(1)} collective-permute-done((bf16[128,1024]{1,0:T(8,128)(2,1)S(1)}, bf16[128,1024]{1,0:T(8,128)(2,1)S(1)}, u32[]{:S(2)}, u32[]{:S(2)}) %collective-permute-start.10) | collective-permute-done | bytes 262176 | tf_op jit(solution)/shard_map/ppermute | solution.py:360
  50.2 0.1 convert_add_fusion
  50.3 0.2 collective-permute-done.11
  50.5 0.1 subtract_convert_fusion.delta_ref
  50.6 2.2 %collective-permute-start.13 = (bf16[128,1024]{1,0:T(8,128)(2,1)S(1)}, bf16[128,1024]{1,0:T(8,128)(2,1)S(1)}, u32[]{:S(2)}, u32[]{:S(2)}) collective-permute-start(bf16[128,1024]{1,0:T(8,128)(2,1)S(1)} %subtract_convert_fusion.delta_ref), channel_id=1, source_target_pairs={{0,8},{4,12},{8,0},{12,4},{1,9},{5,13},{9,1},{13,5},{2,10},{6,14},... | collective-permute-start | bytes 786440 | tf_op jit(solution)/shard_map/ppermute | solution.py:360
  52.8 0.7 shard_map.101.first_ref
  53.5 2.3 %collective-permute-start.12 = (bf16[128,1024]{1,0:T(8,128)(2,1)S(1)}, bf16[128,1024]{1,0:T(8,128)(2,1)S(1)}, u32[]{:S(2)}, u32[]{:S(2)}) collective-permute-start(bf16[128,1024]{1,0:T(8,128)(2,1)S(1)} %subtract_convert_fusion.delta_ref), channel_id=1, source_target_pairs={{0,4},{4,0},{8,12},{12,8},{1,5},{5,1},{9,13},{13,9},{2,6},{6,2},{1... | collective-permute-start | bytes 786440 | tf_op jit(solution)/shard_map/ppermute | solution.py:360
  55.8 7.8 %collective-permute-done.13.delta_ref = bf16[128,1024]{1,0:T(8,128)(2,1)S(1)} collective-permute-done((bf16[128,1024]{1,0:T(8,128)(2,1)S(1)}, bf16[128,1024]{1,0:T(8,128)(2,1)S(1)}, u32[]{:S(2)}, u32[]{:S(2)}) %collective-permute-start.13) | collective-permute-done | bytes 262176 | tf_op jit(solution)/shard_map/ppermute | solution.py:360
  63.5 0.5 collective-permute-start.14
  64.1 0.7 shard_map.103.third_ref
  64.8 0.0 collective-permute-done.12.delta_ref
  64.8 0.7 shard_map.102.second_ref
  65.5 5.1 %collective-permute-done.14.delta_ref = bf16[128,1024]{1,0:T(8,128)(2,1)S(1)} collective-permute-done((bf16[128,1024]{1,0:T(8,128)(2,1)S(1)}, bf16[128,1024]{1,0:T(8,128)(2,1)S(1)}, u32[]{:S(2)}, u32[]{:S(2)}) %collective-permute-start.14) | collective-permute-done | bytes 262176 | tf_op jit(solution)/shard_map/ppermute | solution.py:360
  70.6 0.8 shard_map.104
  71.3 0.1 collective-permute-start.15
  71.4 0.1 pad_maximum_fusion
  71.5 1.7 %collective-permute-done.15.got_ref = bf16[2,128,896]{2,1,0:T(8,128)(2,1)S(1)} collective-permute-done((bf16[2,128,896]{2,1,0:T(8,128)(2,1)S(1)}, bf16[2,128,896]{2,1,0:T(8,128)(2,1)S(1)}, u32[]{:S(2)}, u32[]{:S(2)}) %collective-permute-start.15) | collective-permute-done | bytes 458784 | tf_op jit(solution)/shard_map/ppermute | solution.py:360
  73.2 0.1 fusion
  73.3 1.5 %collective-permute-start.16 = (bf16[128,896]{1,0:T(8,128)(2,1)S(1)}, bf16[128,896]{1,0:T(8,128)(2,1)S(1)}, u32[]{:S(2)}, u32[]{:S(2)}) collective-permute-start(bf16[128,896]{1,0:T(8,128)(2,1)S(1)} %fusion), channel_id=1, source_target_pairs={{0,2},{2,0},{1,3},{3,1},{4,6},{6,4},{5,7},{7,5},{8,10},{10,8},{9,1... | collective-permute-start | bytes 688136 | tf_op jit(solution)/shard_map/ppermute | solution.py:360
  74.8 3.0 %convolution_multiply_fusion = f32[896,1024]{1,0:T(8,128)} fusion(bf16[512,896]{1,0:T(8,128)(2,1)S(1)} %get-tuple-element.59.normed_ref, bf16[512,1024]{1,0:T(8,128)(2,1)S(1)} %pad_maximum_fusion), kind=kOutput, calls=%fused_computation | convolution fusion | flops 940441600 | bytes 5636096 | tf_op jit(solution)/shard_map/dot_general | solution.py:22
  77.8 3.2 %collective-permute-done.16.crossed_ref = bf16[128,896]{1,0:T(8,128)(2,1)S(1)} collective-permute-done((bf16[128,896]{1,0:T(8,128)(2,1)S(1)}, bf16[128,896]{1,0:T(8,128)(2,1)S(1)}, u32[]{:S(2)}, u32[]{:S(2)}) %collective-permute-start.16) | collective-permute-done | bytes 229408 | tf_op jit(solution)/shard_map/ppermute | solution.py:360
  81.0 0.3 shard_map.105
  81.3 1.8 %collective-permute-start.17 = (bf16[48,896]{1,0:T(8,128)(2,1)S(1)}, bf16[48,896]{1,0:T(8,128)(2,1)S(1)}, u32[]{:S(2)}, u32[]{:S(2)}) collective-permute-start(bf16[48,896]{1,0:T(8,128)(2,1)S(1)} %get-tuple-element.67), channel_id=1, source_target_pairs={{0,4},{4,0},{8,12},{12,8},{1,5},{5,1},{9,13},{13,9},{2,6},{6,2},{1... | collective-permute-start | bytes 258056 | tf_op jit(solution)/shard_map/ppermute | solution.py:360
  83.2 3.4 %collective-permute-start.18 = (bf16[48,896]{1,0:T(8,128)(2,1)S(1)}, bf16[48,896]{1,0:T(8,128)(2,1)S(1)}, u32[]{:S(2)}, u32[]{:S(2)}) collective-permute-start(bf16[48,896]{1,0:T(8,128)(2,1)S(1)} %get-tuple-element.68), channel_id=1, source_target_pairs={{0,8},{4,12},{8,0},{12,4},{1,9},{5,13},{9,1},{13,5},{2,10},{6,14},... | collective-permute-start | bytes 258056 | tf_op jit(solution)/shard_map/ppermute | solution.py:360
  86.5 1.5 %collective-permute-start.20 = (bf16[48,896]{1,0:T(8,128)(2,1)S(1)}, bf16[48,896]{1,0:T(8,128)(2,1)S(1)}, u32[]{:S(2)}, u32[]{:S(2)}) collective-permute-start(bf16[48,896]{1,0:T(8,128)(2,1)S(1)} %get-tuple-element.66.refs_0_), channel_id=1, source_target_pairs={{0,2},{2,0},{1,3},{3,1},{4,6},{6,4},{5,7},{7,5},{8,10},{10,8},{9,1... | collective-permute-start | bytes 258056 | tf_op jit(solution)/shard_map/ppermute | solution.py:360
  88.0 0.5 collective-permute-start.21
  88.6 3.3 %collective-permute-done.18.refs_2_ = bf16[48,896]{1,0:T(8,128)(2,1)S(1)} collective-permute-done((bf16[48,896]{1,0:T(8,128)(2,1)S(1)}, bf16[48,896]{1,0:T(8,128)(2,1)S(1)}, u32[]{:S(2)}, u32[]{:S(2)}) %collective-permute-start.18) | collective-permute-done | bytes 86048 | tf_op jit(solution)/shard_map/ppermute | solution.py:360
  91.8 1.5 %collective-permute-start.22 = (bf16[48,896]{1,0:T(8,128)(2,1)S(1)}, bf16[48,896]{1,0:T(8,128)(2,1)S(1)}, u32[]{:S(2)}, u32[]{:S(2)}) collective-permute-start(bf16[48,896]{1,0:T(8,128)(2,1)S(1)} %collective-permute-done.18.refs_2_), channel_id=1, source_target_pairs={{0,2},{2,0},{1,3},{3,1},{4,6},{6,4},{5,7},{7,5},{8,10},{10,8},{9,1... | collective-permute-start | bytes 258056 | tf_op jit(solution)/shard_map/ppermute | solution.py:360
  93.3 1.1 %collective-permute-start.23 = (bf16[48,896]{1,0:T(8,128)(2,1)S(1)}, bf16[48,896]{1,0:T(8,128)(2,1)S(1)}, u32[]{:S(2)}, u32[]{:S(2)}) collective-permute-start(bf16[48,896]{1,0:T(8,128)(2,1)S(1)} %collective-permute-done.19.refs_3_), channel_id=1, source_target_pairs={{0,2},{2,0},{1,3},{3,1},{4,6},{6,4},{5,7},{7,5},{8,10},{10,8},{9,1... | collective-permute-start | bytes 258056 | tf_op jit(solution)/shard_map/ppermute | solution.py:360
  94.4 1.9 %collective-permute-done.22.refs_6_ = bf16[48,896]{1,0:T(8,128)(2,1)S(1)} collective-permute-done((bf16[48,896]{1,0:T(8,128)(2,1)S(1)}, bf16[48,896]{1,0:T(8,128)(2,1)S(1)}, u32[]{:S(2)}, u32[]{:S(2)}) %collective-permute-start.22) | collective-permute-done | bytes 86048 | tf_op jit(solution)/shard_map/ppermute | solution.py:360
  96.3 1.5 %collective-permute-done.23.refs_7_ = bf16[48,896]{1,0:T(8,128)(2,1)S(1)} collective-permute-done((bf16[48,896]{1,0:T(8,128)(2,1)S(1)}, bf16[48,896]{1,0:T(8,128)(2,1)S(1)}, u32[]{:S(2)}, u32[]{:S(2)}) %collective-permute-start.23) | collective-permute-done | bytes 86048 | tf_op jit(solution)/shard_map/ppermute | solution.py:360
  97.8 0.7 shard_map.106.pair_ref
  98.5 0.1 collective-permute-start.24
  98.6 0.9 shard_map.107.t
  99.5 1.3 %collective-permute-done.24.refs_0_ = bf16[2,48,3584]{2,1,0:T(8,128)(2,1)S(1)} collective-permute-done((bf16[2,48,3584]{2,1,0:T(8,128)(2,1)S(1)}, bf16[2,48,3584]{2,1,0:T(8,128)(2,1)S(1)}, u32[]{:S(2)}, u32[]{:S(2)}) %collective-permute-start.24) | collective-permute-done | bytes 688160 | tf_op jit(solution)/shard_map/ppermute | solution.py:360
  100.7 0.9 shard_map.108
  (14 shorter events, 0.0 us)
Async XLA Ops:
  0.6 25.6 %copy-start = (bf16[896,1024]{1,0:T(8,128)(2,1)S(1)}, bf16[896,1024]{1,0:T(8,128)(2,1)}, u32[]{:S(2)}) copy-start(bf16[896,1024]{1,0:T(8,128)(2,1)} %proj_ref.9) | copy-start | bytes 5505028
  2.8 12.8 %collective-permute-start = (bf16[48,1024]{1,0:T(8,128)(2,1)S(1)}, bf16[48,1024]{1,0:T(8,128)(2,1)S(1)}, u32[]{:S(2)}, u32[]{:S(2)}) collective-permute-start(bf16[48,1024]{1,0:T(8,128)(2,1)S(1)} %get-tuple-element.37), channel_id=1, source_target_pairs={{0,12},{4,8},{8,4},{12,0},{1,13},{5,9},{9,5},{13,1},{2,14},{6,10},... | collective-permute-start | bytes 294920 | tf_op jit(solution)/shard_map/ppermute | solution.py:360
  7.9 8.3 %collective-permute-start.2 = (bf16[48,1024]{1,0:T(8,128)(2,1)S(1)}, bf16[48,1024]{1,0:T(8,128)(2,1)S(1)}, u32[]{:S(2)}, u32[]{:S(2)}) collective-permute-start(bf16[48,1024]{1,0:T(8,128)(2,1)S(1)} %get-tuple-element.41), channel_id=1, source_target_pairs={{0,8},{4,12},{8,0},{12,4},{1,9},{5,13},{9,1},{13,5},{2,10},{6,14},... | collective-permute-start | bytes 294920 | tf_op jit(solution)/shard_map/ppermute | solution.py:360
  7.9 8.3 %collective-permute-start.3 = (bf16[48,1024]{1,0:T(8,128)(2,1)S(1)}, bf16[48,1024]{1,0:T(8,128)(2,1)S(1)}, u32[]{:S(2)}, u32[]{:S(2)}) collective-permute-start(bf16[48,1024]{1,0:T(8,128)(2,1)S(1)} %get-tuple-element.43), channel_id=1, source_target_pairs={{0,4},{4,0},{8,12},{12,8},{1,5},{5,1},{9,13},{13,9},{2,6},{6,2},{1... | collective-permute-start | bytes 294920 | tf_op jit(solution)/shard_map/ppermute | solution.py:360
  9.4 6.3 %collective-permute-start.1 = (bf16[256,128]{1,0:T(8,128)(2,1)S(1)}, bf16[256,128]{1,0:T(8,128)(2,1)S(1)}, u32[]{:S(2)}, u32[]{:S(2)}) collective-permute-start(bf16[256,128]{1,0:T(8,128)(2,1)S(1)} %pad_maximum_fusion.1.refs_0_), channel_id=1, source_target_pairs={{0,4},{4,8},{8,12},{1,5},{5,9},{9,13},{2,6},{6,10},{10,14},{3,7},{... | collective-permute-start | bytes 196616 | tf_op jit(solution)/shard_map/ppermute | solution.py:364
  16.6 7.4 %collective-permute-start.5 = (bf16[128,896]{1,0:T(8,128)(2,1)S(1)}, bf16[128,896]{1,0:T(8,128)(2,1)S(1)}, u32[]{:S(2)}, u32[]{:S(2)}) collective-permute-start(bf16[128,896]{1,0:T(8,128)(2,1)S(1)} %get-tuple-element.53.refs_3_), channel_id=1, source_target_pairs={{0,1},{1,0},{2,3},{3,2},{4,5},{5,4},{6,7},{7,6},{8,9},{9,8},{10,11... | collective-permute-start | bytes 688136 | tf_op jit(solution)/shard_map/ppermute | solution.py:360
  16.7 8.0 %collective-permute-start.4 = (bf16[128,896]{1,0:T(8,128)(2,1)S(1)}, bf16[128,896]{1,0:T(8,128)(2,1)S(1)}, u32[]{:S(2)}, u32[]{:S(2)}) collective-permute-start(bf16[128,896]{1,0:T(8,128)(2,1)S(1)} %get-tuple-element.53.refs_3_), channel_id=1, source_target_pairs={{0,2},{2,0},{1,3},{3,1},{4,6},{6,4},{5,7},{7,5},{8,10},{10,8},{9,1... | collective-permute-start | bytes 688136 | tf_op jit(solution)/shard_map/ppermute | solution.py:360
  18.2 5.7 %collective-permute-start.6 = (bf16[256,128]{1,0:T(8,128)(2,1)S(1)}, bf16[256,128]{1,0:T(8,128)(2,1)S(1)}, u32[]{:S(2)}, u32[]{:S(2)}) collective-permute-start(bf16[256,128]{1,0:T(8,128)(2,1)S(1)} %collective-permute-done.1.refs_1_), channel_id=1, source_target_pairs={{0,4},{4,8},{8,12},{1,5},{5,9},{9,13},{2,6},{6,10},{10,14},{3,7},{... | collective-permute-start | bytes 196616 | tf_op jit(solution)/shard_map/ppermute | solution.py:364
  24.7 1.5 %collective-permute-start.7 = (bf16[128,896]{1,0:T(8,128)(2,1)S(1)}, bf16[128,896]{1,0:T(8,128)(2,1)S(1)}, u32[]{:S(2)}, u32[]{:S(2)}) collective-permute-start(bf16[128,896]{1,0:T(8,128)(2,1)S(1)} %collective-permute-done.4.refs_1_), channel_id=1, source_target_pairs={{0,1},{1,0},{2,3},{3,2},{4,5},{5,4},{6,7},{7,6},{8,9},{9,8},{10,11... | collective-permute-start | bytes 688136 | tf_op jit(solution)/shard_map/ppermute | solution.py:360
  26.6 9.3 %collective-permute-start.8 = (bf16[128,1024]{1,0:T(8,128)(2,1)S(1)}, bf16[128,1024]{1,0:T(8,128)(2,1)S(1)}, u32[]{:S(2)}, u32[]{:S(2)}) collective-permute-start(bf16[128,1024]{1,0:T(8,128)(2,1)S(1)} %shard_map.97), channel_id=1, source_target_pairs={{0,4},{4,0},{8,12},{12,8},{1,5},{5,1},{9,13},{13,9},{2,6},{6,2},{1... | collective-permute-start | bytes 786440 | tf_op jit(solution)/shard_map/ppermute | solution.py:360
  28.7 7.3 %collective-permute-start.9 = (bf16[256,128]{1,0:T(8,128)(2,1)S(1)}, bf16[256,128]{1,0:T(8,128)(2,1)S(1)}, u32[]{:S(2)}, u32[]{:S(2)}) collective-permute-start(bf16[256,128]{1,0:T(8,128)(2,1)S(1)} %collective-permute-done.6.refs_2_), channel_id=1, source_target_pairs={{0,4},{4,8},{8,12},{1,5},{5,9},{9,13},{2,6},{6,10},{10,14},{3,7},{... | collective-permute-start | bytes 196616 | tf_op jit(solution)/shard_map/ppermute | solution.py:364
  31.5 9.8 %copy-start.1 = (bf16[128,1024]{1,0:T(8,128)(2,1)S(1)}, bf16[128,1024]{1,0:T(8,128)(2,1)}, u32[]{:S(2)}) copy-start(bf16[128,1024]{1,0:T(8,128)(2,1)} %queries_ref) | copy-start | bytes 786436
  36.0 14.2 %collective-permute-start.10 = (bf16[128,1024]{1,0:T(8,128)(2,1)S(1)}, bf16[128,1024]{1,0:T(8,128)(2,1)S(1)}, u32[]{:S(2)}, u32[]{:S(2)}) collective-permute-start(bf16[128,1024]{1,0:T(8,128)(2,1)S(1)} %add_convert_fusion), channel_id=1, source_target_pairs={{0,8},{4,12},{8,0},{12,4},{1,9},{5,13},{9,1},{13,5},{2,10},{6,14},... | collective-permute-start | bytes 786440 | tf_op jit(solution)/shard_map/ppermute | solution.py:360
  38.8 11.6 %collective-permute-start.11 = (bf16[128,1024]{1,0:T(8,128)(2,1)S(1)}, bf16[128,1024]{1,0:T(8,128)(2,1)S(1)}, u32[]{:S(2)}, u32[]{:S(2)}) collective-permute-start(bf16[128,1024]{1,0:T(8,128)(2,1)S(1)} %shard_map.99), channel_id=1, source_target_pairs={{0,4},{4,0},{8,12},{12,8},{1,5},{5,1},{9,13},{13,9},{2,6},{6,2},{1... | collective-permute-start | bytes 786440 | tf_op jit(solution)/shard_map/ppermute | solution.py:360
  50.6 13.0 %collective-permute-start.13 = (bf16[128,1024]{1,0:T(8,128)(2,1)S(1)}, bf16[128,1024]{1,0:T(8,128)(2,1)S(1)}, u32[]{:S(2)}, u32[]{:S(2)}) collective-permute-start(bf16[128,1024]{1,0:T(8,128)(2,1)S(1)} %subtract_convert_fusion.delta_ref), channel_id=1, source_target_pairs={{0,8},{4,12},{8,0},{12,4},{1,9},{5,13},{9,1},{13,5},{2,10},{6,14},... | collective-permute-start | bytes 786440 | tf_op jit(solution)/shard_map/ppermute | solution.py:360
  53.5 11.3 %collective-permute-start.12 = (bf16[128,1024]{1,0:T(8,128)(2,1)S(1)}, bf16[128,1024]{1,0:T(8,128)(2,1)S(1)}, u32[]{:S(2)}, u32[]{:S(2)}) collective-permute-start(bf16[128,1024]{1,0:T(8,128)(2,1)S(1)} %subtract_convert_fusion.delta_ref), channel_id=1, source_target_pairs={{0,4},{4,0},{8,12},{12,8},{1,5},{5,1},{9,13},{13,9},{2,6},{6,2},{1... | collective-permute-start | bytes 786440 | tf_op jit(solution)/shard_map/ppermute | solution.py:360
  63.5 7.0 %collective-permute-start.14 = (bf16[128,1024]{1,0:T(8,128)(2,1)S(1)}, bf16[128,1024]{1,0:T(8,128)(2,1)S(1)}, u32[]{:S(2)}, u32[]{:S(2)}) collective-permute-start(bf16[128,1024]{1,0:T(8,128)(2,1)S(1)} %collective-permute-done.13.delta_ref), channel_id=1, source_target_pairs={{0,4},{4,0},{8,12},{12,8},{1,5},{5,1},{9,13},{13,9},{2,6},{6,2},{1... | collective-permute-start | bytes 786440 | tf_op jit(solution)/shard_map/ppermute | solution.py:360
  71.3 1.9 %collective-permute-start.15 = (bf16[2,128,896]{2,1,0:T(8,128)(2,1)S(1)}, bf16[2,128,896]{2,1,0:T(8,128)(2,1)S(1)}, u32[]{:S(2)}, u32[]{:S(2)}) collective-permute-start(bf16[2,128,896]{2,1,0:T(8,128)(2,1)S(1)} %get-tuple-element.63), channel_id=1, source_target_pairs={{0,1},{1,0},{2,3},{3,2},{4,5},{5,4},{6,7},{7,6},{8,9},{9,8},{10,11... | collective-permute-start | bytes 1376264 | tf_op jit(solution)/shard_map/ppermute | solution.py:360
  73.3 7.7 %collective-permute-start.16 = (bf16[128,896]{1,0:T(8,128)(2,1)S(1)}, bf16[128,896]{1,0:T(8,128)(2,1)S(1)}, u32[]{:S(2)}, u32[]{:S(2)}) collective-permute-start(bf16[128,896]{1,0:T(8,128)(2,1)S(1)} %fusion), channel_id=1, source_target_pairs={{0,2},{2,0},{1,3},{3,1},{4,6},{6,4},{5,7},{7,5},{8,10},{10,8},{9,1... | collective-permute-start | bytes 688136 | tf_op jit(solution)/shard_map/ppermute | solution.py:360
  81.3 6.7 %collective-permute-start.17 = (bf16[48,896]{1,0:T(8,128)(2,1)S(1)}, bf16[48,896]{1,0:T(8,128)(2,1)S(1)}, u32[]{:S(2)}, u32[]{:S(2)}) collective-permute-start(bf16[48,896]{1,0:T(8,128)(2,1)S(1)} %get-tuple-element.67), channel_id=1, source_target_pairs={{0,4},{4,0},{8,12},{12,8},{1,5},{5,1},{9,13},{13,9},{2,6},{6,2},{1... | collective-permute-start | bytes 258056 | tf_op jit(solution)/shard_map/ppermute | solution.py:360
  83.2 8.7 %collective-permute-start.18 = (bf16[48,896]{1,0:T(8,128)(2,1)S(1)}, bf16[48,896]{1,0:T(8,128)(2,1)S(1)}, u32[]{:S(2)}, u32[]{:S(2)}) collective-permute-start(bf16[48,896]{1,0:T(8,128)(2,1)S(1)} %get-tuple-element.68), channel_id=1, source_target_pairs={{0,8},{4,12},{8,0},{12,4},{1,9},{5,13},{9,1},{13,5},{2,10},{6,14},... | collective-permute-start | bytes 258056 | tf_op jit(solution)/shard_map/ppermute | solution.py:360
  86.5 6.8 %collective-permute-start.19 = (bf16[48,896]{1,0:T(8,128)(2,1)S(1)}, bf16[48,896]{1,0:T(8,128)(2,1)S(1)}, u32[]{:S(2)}, u32[]{:S(2)}) collective-permute-start(bf16[48,896]{1,0:T(8,128)(2,1)S(1)} %get-tuple-element.69), channel_id=1, source_target_pairs={{0,12},{4,8},{8,4},{12,0},{1,13},{5,9},{9,5},{13,1},{2,14},{6,10},... | collective-permute-start | bytes 258056 | tf_op jit(solution)/shard_map/ppermute | solution.py:360
  86.5 7.9 %collective-permute-start.20 = (bf16[48,896]{1,0:T(8,128)(2,1)S(1)}, bf16[48,896]{1,0:T(8,128)(2,1)S(1)}, u32[]{:S(2)}, u32[]{:S(2)}) collective-permute-start(bf16[48,896]{1,0:T(8,128)(2,1)S(1)} %get-tuple-element.66.refs_0_), channel_id=1, source_target_pairs={{0,2},{2,0},{1,3},{3,1},{4,6},{6,4},{5,7},{7,5},{8,10},{10,8},{9,1... | collective-permute-start | bytes 258056 | tf_op jit(solution)/shard_map/ppermute | solution.py:360
  88.0 6.4 %collective-permute-start.21 = (bf16[48,896]{1,0:T(8,128)(2,1)S(1)}, bf16[48,896]{1,0:T(8,128)(2,1)S(1)}, u32[]{:S(2)}, u32[]{:S(2)}) collective-permute-start(bf16[48,896]{1,0:T(8,128)(2,1)S(1)} %collective-permute-done.17.refs_1_), channel_id=1, source_target_pairs={{0,2},{2,0},{1,3},{3,1},{4,6},{6,4},{5,7},{7,5},{8,10},{10,8},{9,1... | collective-permute-start | bytes 258056 | tf_op jit(solution)/shard_map/ppermute | solution.py:360
  91.8 4.5 %collective-permute-start.22 = (bf16[48,896]{1,0:T(8,128)(2,1)S(1)}, bf16[48,896]{1,0:T(8,128)(2,1)S(1)}, u32[]{:S(2)}, u32[]{:S(2)}) collective-permute-start(bf16[48,896]{1,0:T(8,128)(2,1)S(1)} %collective-permute-done.18.refs_2_), channel_id=1, source_target_pairs={{0,2},{2,0},{1,3},{3,1},{4,6},{6,4},{5,7},{7,5},{8,10},{10,8},{9,1... | collective-permute-start | bytes 258056 | tf_op jit(solution)/shard_map/ppermute | solution.py:360
  93.3 4.5 %collective-permute-start.23 = (bf16[48,896]{1,0:T(8,128)(2,1)S(1)}, bf16[48,896]{1,0:T(8,128)(2,1)S(1)}, u32[]{:S(2)}, u32[]{:S(2)}) collective-permute-start(bf16[48,896]{1,0:T(8,128)(2,1)S(1)} %collective-permute-done.19.refs_3_), channel_id=1, source_target_pairs={{0,2},{2,0},{1,3},{3,1},{4,6},{6,4},{5,7},{7,5},{8,10},{10,8},{9,1... | collective-permute-start | bytes 258056 | tf_op jit(solution)/shard_map/ppermute | solution.py:360
  98.5 2.2 %collective-permute-start.24 = (bf16[2,48,3584]{2,1,0:T(8,128)(2,1)S(1)}, bf16[2,48,3584]{2,1,0:T(8,128)(2,1)S(1)}, u32[]{:S(2)}, u32[]{:S(2)}) collective-permute-start(bf16[2,48,3584]{2,1,0:T(8,128)(2,1)S(1)} %shard_map.106.pair_ref), channel_id=1, source_target_pairs={{0,1},{1,0},{2,3},{3,2},{4,5},{5,4},{6,7},{7,6},{8,9},{9,8},{10,11... | collective-permute-start | bytes 2064392 | tf_op jit(solution)/shard_map/ppermute | solution.py:360

commit v9 on v8

--- a/solution.py
+++ b/solution.py
@@ -360,8 +360,9 @@
     return lax.ppermute(x, axis, [(i, i ^ k) for i in range(lax.axis_size(axis))])
 
 
-def onward(x):
-    return lax.ppermute(x, "seq", [(i, i + 1) for i in range(lax.axis_size("seq") - 1)])
+def onward(x, step):
+    n = lax.axis_size("seq")
+    return lax.ppermute(x, "seq", [(i, i + step) for i in range(n - step)])
 
 
 def exchange(blocks):
@@ -403,19 +404,18 @@
         ]
     )
     parcels = [after(lax.optimization_barrier(parcel), made[0])]
-    parcels.append(onward(parcels[0]))
+    parcels.append(onward(parcels[0], 1))
     normed_own, drop = pick_rows([after(piece, parcels[1]) for piece in pieces], rows)
 
     far = swap(normed_own, "mp")
     mate = swap(normed_own, "side")
-    parcels.append(onward(after(parcels[1], normed_own)))
-    far_mate = swap(after(far, mate, parcels[2]), "side")
+    parcels += [onward(after(parcels[0], normed_own), step) for step in (2, 3)]
+    far_mate = swap(after(far, mate, *parcels[2:]), "side")
     entries = [far_mate, far, mate, normed_own]
 
     away = away_partial(entries, proj)
     own, over_own, normed = kept_partials([after(e, away) for e in entries], proj)
-    parcels.append(onward(after(parcels[2], away)))
-    got_over = after(swap(away, "seq", 1), over_own, parcels[3])
+    got_over = after(swap(away, "seq", 1), over_own)
     over = lax.optimization_barrier((over_own + got_over.astype(F32)).astype(BF))
     got_far = swap(over, "seq", 2)
     got_beside = swap(beside_partial(after(normed, over), proj), "seq", 1)

time: 102 us -> 104 us (1.020)
  waiting for transfers between devices: 44.4 us -> 49.4 us
  starting transfers between devices: 39.9 us -> 37.3 us
    ppermute x22, waiting for transfers between devices: 35.1 us -> 44.5 us  [swap(): lax.ppermute(x, axis, [(i, i ^ k) for i in range(lax.axis_size(axis))])]
    ppermute x3, waiting for transfers between devices: 9.25 us -> 4.87 us  [onward(): return lax.ppermute(x, 'seq', [(i, i + step) for i in range(n - step)])]
    ppermute x22, starting transfers between devices: 30.8 us -> 27.1 us  [swap(): lax.ppermute(x, axis, [(i, i ^ k) for i in range(lax.axis_size(axis))])]
    ppermute x3, starting transfers between devices: 9.11 us -> 10.2 us  [onward(): return lax.ppermute(x, 'seq', [(i, i + step) for i in range(n - step)])]
  transfers between devices with their start and end apart: 25 -> 25, of which waited for: 16 -> 19; matrix products, arithmetic and copies ran while one was open for 4% -> 4% of each run, Pallas kernels for 7% -> 6%
where the time goes in v9:
time: 104 us
  waiting for transfers between devices  49.4 us (48%)
  starting transfers between devices  37.3 us (36%)
  Pallas kernels  11.3 us (11%)
  matrix products  2.98 us (3%)
  other arithmetic  1.29 us (1%)
    ppermute x22, waiting for transfers between devices, swap(): lax.ppermute(x, axis, [(i, i ^ k) for i in range(lax.axis_size(axis))])  44.5 us
    ppermute x22, starting transfers between devices, swap(): lax.ppermute(x, axis, [(i, i ^ k) for i in range(lax.axis_size(axis))])  27.1 us
    pallas_call x14, Pallas kernels, call(): pl.pallas_call(kernel, out_shape=shapes, cost_estimate=pl.CostEstimate(fl...  11.3 us
    ppermute x3, starting transfers between devices, onward(): return lax.ppermute(x, 'seq', [(i, i + step) for i in range(n - step)])  10.2 us
    ppermute x3, waiting for transfers between devices, onward(): return lax.ppermute(x, 'seq', [(i, i + step) for i in range(n - step)])  4.87 us
    dot_general x1, matrix products, dot(): return lax.dot_general(a, b, (dims, ((), ())), preferred_element_type=F32)  2.98 us
  transfers between devices with their start and end apart: 25, of which 19 were waited for; matrix products, arithmetic and copies ran while one was open for 4% of the time, Pallas kernels for 6%

profile of v9, /device:TPU:0, one launch (start us, length us, event | category | flops | bytes accessed | tf_op | source)
XLA Modules:
  0.0 104.0 jit_solution(5289309111156572412)
XLA Ops:
  0.7 0.9 convert_select_fusion.small_ref
  1.6 1.2 %shard_map.95 = (bf16[48,1024]{1,0:T(8,128)(2,1)S(1)}, bf16[48,1024]{1,0:T(8,128)(2,1)S(1)}, bf16[48,1024]{1,0:T(8,128)(2,1)S(1)}, bf16[48,1024]{1,0:T(8,128)(2,1)S(1)}, bf16[2,48,3584]{2,1,0:T(8,128)(2,1)S(1)}) custom-call(bf16[4,48,3584]{2,1,0:T(8,128)(2,1)} %bitcast.9, f32[30,128]{1,0:T(8,128)S(1)} %convert_select_fusion.small_ref), custom_call_target="tpu_custom_call" | custom-call | flops 1032192 | bytes 1376256 | tf_op jit(solution)/shard_map/pallas_call | solution.py:49
  2.8 5.1 %collective-permute-start = (bf16[48,1024]{1,0:T(8,128)(2,1)S(1)}, bf16[48,1024]{1,0:T(8,128)(2,1)S(1)}, u32[]{:S(2)}, u32[]{:S(2)}) collective-permute-start(bf16[48,1024]{1,0:T(8,128)(2,1)S(1)} %get-tuple-element.36), channel_id=1, source_target_pairs={{0,12},{4,8},{8,4},{12,0},{1,13},{5,9},{9,5},{13,1},{2,14},{6,10},... | collective-permute-start | bytes 294920 | tf_op jit(solution)/shard_map/ppermute | solution.py:360
  7.9 0.6 collective-permute-start.3
  8.6 0.8 constant_dynamic-slice_fusion
  9.4 3.3 %collective-permute-start.1 = (bf16[256,128]{1,0:T(8,128)(2,1)S(1)}, bf16[256,128]{1,0:T(8,128)(2,1)S(1)}, u32[]{:S(2)}, u32[]{:S(2)}) collective-permute-start(bf16[256,128]{1,0:T(8,128)(2,1)S(1)} %pad_maximum_fusion.1.refs_0_), channel_id=1, source_target_pairs={{0,4},{4,8},{8,12},{1,5},{5,9},{9,13},{2,6},{6,10},{10,14},{3,7},{... | collective-permute-start | bytes 196616 | tf_op jit(solution)/shard_map/ppermute | solution.py:365
  12.7 3.0 %collective-permute-done.1.refs_1_ = bf16[256,128]{1,0:T(8,128)(2,1)S(1)} collective-permute-done((bf16[256,128]{1,0:T(8,128)(2,1)S(1)}, bf16[256,128]{1,0:T(8,128)(2,1)S(1)}, u32[]{:S(2)}, u32[]{:S(2)}) %collective-permute-start.1) | collective-permute-done | bytes 65568 | tf_op jit(solution)/shard_map/ppermute | solution.py:365
  15.7 0.5 collective-permute-done.2.refs_1_.refs_6_
  16.2 0.4 shard_map.96
  16.6 0.1 collective-permute-start.5
  16.7 1.6 %collective-permute-start.4 = (bf16[128,896]{1,0:T(8,128)(2,1)S(1)}, bf16[128,896]{1,0:T(8,128)(2,1)S(1)}, u32[]{:S(2)}, u32[]{:S(2)}) collective-permute-start(bf16[128,896]{1,0:T(8,128)(2,1)S(1)} %get-tuple-element.52.refs_3_), channel_id=1, source_target_pairs={{0,2},{2,0},{1,3},{3,1},{4,6},{6,4},{5,7},{7,5},{8,10},{10,8},{9,1... | collective-permute-start | bytes 688136 | tf_op jit(solution)/shard_map/ppermute | solution.py:360
  18.2 5.6 %collective-permute-start.7 = (bf16[256,128]{1,0:T(8,128)(2,1)S(1)}, bf16[256,128]{1,0:T(8,128)(2,1)S(1)}, u32[]{:S(2)}, u32[]{:S(2)}) collective-permute-start(bf16[256,128]{1,0:T(8,128)(2,1)S(1)} %pad_maximum_fusion.1.refs_0_), channel_id=1, source_target_pairs={{0,12},{1,13},{2,14},{3,15},{16,28},{17,29},{18,30},{19,31}} | collective-permute-start | bytes 196616 | tf_op jit(solution)/shard_map/ppermute | solution.py:365
  23.8 1.3 %collective-permute-start.6 = (bf16[256,128]{1,0:T(8,128)(2,1)S(1)}, bf16[256,128]{1,0:T(8,128)(2,1)S(1)}, u32[]{:S(2)}, u32[]{:S(2)}) collective-permute-start(bf16[256,128]{1,0:T(8,128)(2,1)S(1)} %pad_maximum_fusion.1.refs_0_), channel_id=1, source_target_pairs={{0,8},{4,12},{1,9},{5,13},{2,10},{6,14},{3,11},{7,15},{16,24},{20,... | collective-permute-start | bytes 196616 | tf_op jit(solution)/shard_map/ppermute | solution.py:365
  25.1 0.7 collective-permute-done.7.refs_3_
  25.9 1.1 %collective-permute-done.6.refs_2_ = bf16[256,128]{1,0:T(8,128)(2,1)S(1)} collective-permute-done((bf16[256,128]{1,0:T(8,128)(2,1)S(1)}, bf16[256,128]{1,0:T(8,128)(2,1)S(1)}, u32[]{:S(2)}, u32[]{:S(2)}) %collective-permute-start.6) | collective-permute-done | bytes 65568 | tf_op jit(solution)/shard_map/ppermute | solution.py:365
  27.0 1.5 %collective-permute-done.8.refs_0_ = bf16[128,896]{1,0:T(8,128)(2,1)S(1)} collective-permute-done((bf16[128,896]{1,0:T(8,128)(2,1)S(1)}, bf16[128,896]{1,0:T(8,128)(2,1)S(1)}, u32[]{:S(2)}, u32[]{:S(2)}) %collective-permute-start.8) | collective-permute-done | bytes 229408 | tf_op jit(solution)/shard_map/ppermute | solution.py:360
  28.5 0.5 shard_map.97
  29.0 2.8 %collective-permute-start.9 = (bf16[128,1024]{1,0:T(8,128)(2,1)S(1)}, bf16[128,1024]{1,0:T(8,128)(2,1)S(1)}, u32[]{:S(2)}, u32[]{:S(2)}) collective-permute-start(bf16[128,1024]{1,0:T(8,128)(2,1)S(1)} %shard_map.97), channel_id=1, source_target_pairs={{0,4},{4,0},{8,12},{12,8},{1,5},{5,1},{9,13},{13,9},{2,6},{6,2},{1... | collective-permute-start | bytes 786440 | tf_op jit(solution)/shard_map/ppermute | solution.py:360
  31.8 0.9 shard_map.98
  32.7 0.0 copy-start.1
  32.7 5.7 %collective-permute-done.9 = bf16[128,1024]{1,0:T(8,128)(2,1)S(1)} collective-permute-done((bf16[128,1024]{1,0:T(8,128)(2,1)S(1)}, bf16[128,1024]{1,0:T(8,128)(2,1)S(1)}, u32[]{:S(2)}, u32[]{:S(2)}) %collective-permute-start.9) | collective-permute-done | bytes 262176 | tf_op jit(solution)/shard_map/ppermute | solution.py:360
  38.4 0.1 add_convert_fusion
  38.5 3.5 %collective-permute-start.10 = (bf16[128,1024]{1,0:T(8,128)(2,1)S(1)}, bf16[128,1024]{1,0:T(8,128)(2,1)S(1)}, u32[]{:S(2)}, u32[]{:S(2)}) collective-permute-start(bf16[128,1024]{1,0:T(8,128)(2,1)S(1)} %add_convert_fusion), channel_id=1, source_target_pairs={{0,8},{4,12},{8,0},{12,4},{1,9},{5,13},{9,1},{13,5},{2,10},{6,14},... | collective-permute-start | bytes 786440 | tf_op jit(solution)/shard_map/ppermute | solution.py:360
  41.9 0.4 shard_map.99
  42.4 1.8 %collective-permute-start.11 = (bf16[128,1024]{1,0:T(8,128)(2,1)S(1)}, bf16[128,1024]{1,0:T(8,128)(2,1)S(1)}, u32[]{:S(2)}, u32[]{:S(2)}) collective-permute-start(bf16[128,1024]{1,0:T(8,128)(2,1)S(1)} %shard_map.99), channel_id=1, source_target_pairs={{0,4},{4,0},{8,12},{12,8},{1,5},{5,1},{9,13},{13,9},{2,6},{6,2},{1... | collective-permute-start | bytes 786440 | tf_op jit(solution)/shard_map/ppermute | solution.py:360
  44.2 2.3 %shard_map.100 = bf16[128,1024]{1,0:T(8,128)(2,1)S(1)} custom-call(bf16[128,1024]{1,0:T(8,128)(2,1)S(1)} %copy-done.1, bf16[256,128]{1,0:T(8,128)(2,1)S(1)} %pad_maximum_fusion.1.refs_0_, bf16[256,128]{1,0:T(8,128)(2,1)S(1)} %collective-permute-done.1.refs_1_, bf16[256,128]{1,0:T(8,128)(2,1)S(1)} %collective-permute-done.6.refs_2_, ...), custom_call_target="tpu_custom_call" | custom-call | bytes 524288 | tf_op jit(solution)/shard_map/pallas_call | solution.py:49
  46.5 7.2 %collective-permute-done.10 = bf16[128,1024]{1,0:T(8,128)(2,1)S(1)} collective-permute-done((bf16[128,1024]{1,0:T(8,128)(2,1)S(1)}, bf16[128,1024]{1,0:T(8,128)(2,1)S(1)}, u32[]{:S(2)}, u32[]{:S(2)}) %collective-permute-start.10) | collective-permute-done | bytes 262176 | tf_op jit(solution)/shard_map/ppermute | solution.py:360
  53.7 0.1 convert_add_fusion
  53.8 0.9 collective-permute-done.11
  54.7 0.1 subtract_convert_fusion.delta_ref
  54.8 0.5 collective-permute-start.13
  55.3 0.7 shard_map.101.first_ref
  56.0 2.7 %collective-permute-start.12 = (bf16[128,1024]{1,0:T(8,128)(2,1)S(1)}, bf16[128,1024]{1,0:T(8,128)(2,1)S(1)}, u32[]{:S(2)}, u32[]{:S(2)}) collective-permute-start(bf16[128,1024]{1,0:T(8,128)(2,1)S(1)} %subtract_convert_fusion.delta_ref), channel_id=1, source_target_pairs={{0,4},{4,0},{8,12},{12,8},{1,5},{5,1},{9,13},{13,9},{2,6},{6,2},{1... | collective-permute-start | bytes 786440 | tf_op jit(solution)/shard_map/ppermute | solution.py:360
  58.7 9.2 %collective-permute-done.13.delta_ref = bf16[128,1024]{1,0:T(8,128)(2,1)S(1)} collective-permute-done((bf16[128,1024]{1,0:T(8,128)(2,1)S(1)}, bf16[128,1024]{1,0:T(8,128)(2,1)S(1)}, u32[]{:S(2)}, u32[]{:S(2)}) %collective-permute-start.13) | collective-permute-done | bytes 262176 | tf_op jit(solution)/shard_map/ppermute | solution.py:360
  67.9 0.7 shard_map.103.third_ref
  68.6 0.1 collective-permute-done.12.delta_ref
  68.8 0.7 shard_map.102.second_ref
  69.5 4.9 %collective-permute-done.14.delta_ref = bf16[128,1024]{1,0:T(8,128)(2,1)S(1)} collective-permute-done((bf16[128,1024]{1,0:T(8,128)(2,1)S(1)}, bf16[128,1024]{1,0:T(8,128)(2,1)S(1)}, u32[]{:S(2)}, u32[]{:S(2)}) %collective-permute-start.14) | collective-permute-done | bytes 262176 | tf_op jit(solution)/shard_map/ppermute | solution.py:360
  74.4 0.8 shard_map.104
  75.1 0.1 collective-permute-start.15
  75.2 0.1 pad_maximum_fusion
  75.3 1.7 %collective-permute-done.15.got_ref = bf16[2,128,896]{2,1,0:T(8,128)(2,1)S(1)} collective-permute-done((bf16[2,128,896]{2,1,0:T(8,128)(2,1)S(1)}, bf16[2,128,896]{2,1,0:T(8,128)(2,1)S(1)}, u32[]{:S(2)}, u32[]{:S(2)}) %collective-permute-start.15) | collective-permute-done | bytes 458784 | tf_op jit(solution)/shard_map/ppermute | solution.py:360
  77.0 0.1 fusion
  77.1 0.6 collective-permute-start.16
  77.7 3.0 %convolution_multiply_fusion = f32[896,1024]{1,0:T(8,128)} fusion(bf16[512,896]{1,0:T(8,128)(2,1)S(1)} %get-tuple-element.57.normed_ref, bf16[512,1024]{1,0:T(8,128)(2,1)S(1)} %pad_maximum_fusion), kind=kOutput, calls=%fused_computation | convolution fusion | flops 940441600 | bytes 5636096 | tf_op jit(solution)/shard_map/dot_general | solution.py:22
  80.7 4.1 %collective-permute-done.16.crossed_ref = bf16[128,896]{1,0:T(8,128)(2,1)S(1)} collective-permute-done((bf16[128,896]{1,0:T(8,128)(2,1)S(1)}, bf16[128,896]{1,0:T(8,128)(2,1)S(1)}, u32[]{:S(2)}, u32[]{:S(2)}) %collective-permute-start.16) | collective-permute-done | bytes 229408 | tf_op jit(solution)/shard_map/ppermute | solution.py:360
  84.8 0.3 shard_map.105
  85.2 0.8 collective-permute-start.17
  85.9 3.4 %collective-permute-start.18 = (bf16[48,896]{1,0:T(8,128)(2,1)S(1)}, bf16[48,896]{1,0:T(8,128)(2,1)S(1)}, u32[]{:S(2)}, u32[]{:S(2)}) collective-permute-start(bf16[48,896]{1,0:T(8,128)(2,1)S(1)} %get-tuple-element.66), channel_id=1, source_target_pairs={{0,8},{4,12},{8,0},{12,4},{1,9},{5,13},{9,1},{13,5},{2,10},{6,14},... | collective-permute-start | bytes 258056 | tf_op jit(solution)/shard_map/ppermute | solution.py:360
  89.3 0.3 collective-permute-start.19
  89.6 0.5 collective-permute-start.20
  90.2 0.3 collective-permute-done.17.refs_1_
  90.4 1.2 %collective-permute-start.21 = (bf16[48,896]{1,0:T(8,128)(2,1)S(1)}, bf16[48,896]{1,0:T(8,128)(2,1)S(1)}, u32[]{:S(2)}, u32[]{:S(2)}) collective-permute-start(bf16[48,896]{1,0:T(8,128)(2,1)S(1)} %collective-permute-done.17.refs_1_), channel_id=1, source_target_pairs={{0,2},{2,0},{1,3},{3,1},{4,6},{6,4},{5,7},{7,5},{8,10},{10,8},{9,1... | collective-permute-start | bytes 258056 | tf_op jit(solution)/shard_map/ppermute | solution.py:360
  91.6 3.0 %collective-permute-done.18.refs_2_ = bf16[48,896]{1,0:T(8,128)(2,1)S(1)} collective-permute-done((bf16[48,896]{1,0:T(8,128)(2,1)S(1)}, bf16[48,896]{1,0:T(8,128)(2,1)S(1)}, u32[]{:S(2)}, u32[]{:S(2)}) %collective-permute-start.18) | collective-permute-done | bytes 86048 | tf_op jit(solution)/shard_map/ppermute | solution.py:360
  94.6 0.5 collective-permute-start.22
  95.2 0.5 collective-permute-done.19.refs_3_
  95.7 0.9 collective-permute-start.23
  96.7 2.4 %collective-permute-done.22.refs_6_ = bf16[48,896]{1,0:T(8,128)(2,1)S(1)} collective-permute-done((bf16[48,896]{1,0:T(8,128)(2,1)S(1)}, bf16[48,896]{1,0:T(8,128)(2,1)S(1)}, u32[]{:S(2)}, u32[]{:S(2)}) %collective-permute-start.22) | collective-permute-done | bytes 86048 | tf_op jit(solution)/shard_map/ppermute | solution.py:360
  99.1 1.1 %collective-permute-done.23.refs_7_ = bf16[48,896]{1,0:T(8,128)(2,1)S(1)} collective-permute-done((bf16[48,896]{1,0:T(8,128)(2,1)S(1)}, bf16[48,896]{1,0:T(8,128)(2,1)S(1)}, u32[]{:S(2)}, u32[]{:S(2)}) %collective-permute-start.23) | collective-permute-done | bytes 86048 | tf_op jit(solution)/shard_map/ppermute | solution.py:360
  100.2 0.7 shard_map.106.pair_ref
  100.9 0.1 collective-permute-start.24
  101.0 0.9 shard_map.107.t
  101.9 1.3 %collective-permute-done.24.refs_0_ = bf16[2,48,3584]{2,1,0:T(8,128)(2,1)S(1)} collective-permute-done((bf16[2,48,3584]{2,1,0:T(8,128)(2,1)S(1)}, bf16[2,48,3584]{2,1,0:T(8,128)(2,1)S(1)}, u32[]{:S(2)}, u32[]{:S(2)}) %collective-permute-start.24) | collective-permute-done | bytes 688160 | tf_op jit(solution)/shard_map/ppermute | solution.py:360
  103.1 0.9 shard_map.108
  (14 shorter events, 0.0 us)
Async XLA Ops:
  0.6 27.9 %copy-start = (bf16[896,1024]{1,0:T(8,128)(2,1)S(1)}, bf16[896,1024]{1,0:T(8,128)(2,1)}, u32[]{:S(2)}) copy-start(bf16[896,1024]{1,0:T(8,128)(2,1)} %proj_ref.9) | copy-start | bytes 5505028
  2.8 12.8 %collective-permute-start = (bf16[48,1024]{1,0:T(8,128)(2,1)S(1)}, bf16[48,1024]{1,0:T(8,128)(2,1)S(1)}, u32[]{:S(2)}, u32[]{:S(2)}) collective-permute-start(bf16[48,1024]{1,0:T(8,128)(2,1)S(1)} %get-tuple-element.36), channel_id=1, source_target_pairs={{0,12},{4,8},{8,4},{12,0},{1,13},{5,9},{9,5},{13,1},{2,14},{6,10},... | collective-permute-start | bytes 294920 | tf_op jit(solution)/shard_map/ppermute | solution.py:360
  7.9 8.3 %collective-permute-start.2 = (bf16[48,1024]{1,0:T(8,128)(2,1)S(1)}, bf16[48,1024]{1,0:T(8,128)(2,1)S(1)}, u32[]{:S(2)}, u32[]{:S(2)}) collective-permute-start(bf16[48,1024]{1,0:T(8,128)(2,1)S(1)} %get-tuple-element.40), channel_id=1, source_target_pairs={{0,8},{4,12},{8,0},{12,4},{1,9},{5,13},{9,1},{13,5},{2,10},{6,14},... | collective-permute-start | bytes 294920 | tf_op jit(solution)/shard_map/ppermute | solution.py:360
  7.9 8.3 %collective-permute-start.3 = (bf16[48,1024]{1,0:T(8,128)(2,1)S(1)}, bf16[48,1024]{1,0:T(8,128)(2,1)S(1)}, u32[]{:S(2)}, u32[]{:S(2)}) collective-permute-start(bf16[48,1024]{1,0:T(8,128)(2,1)S(1)} %get-tuple-element.42), channel_id=1, source_target_pairs={{0,4},{4,0},{8,12},{12,8},{1,5},{5,1},{9,13},{13,9},{2,6},{6,2},{1... | collective-permute-start | bytes 294920 | tf_op jit(solution)/shard_map/ppermute | solution.py:360
  9.4 6.3 %collective-permute-start.1 = (bf16[256,128]{1,0:T(8,128)(2,1)S(1)}, bf16[256,128]{1,0:T(8,128)(2,1)S(1)}, u32[]{:S(2)}, u32[]{:S(2)}) collective-permute-start(bf16[256,128]{1,0:T(8,128)(2,1)S(1)} %pad_maximum_fusion.1.refs_0_), channel_id=1, source_target_pairs={{0,4},{4,8},{8,12},{1,5},{5,9},{9,13},{2,6},{6,10},{10,14},{3,7},{... | collective-permute-start | bytes 196616 | tf_op jit(solution)/shard_map/ppermute | solution.py:365
  16.6 10.4 %collective-permute-start.5 = (bf16[128,896]{1,0:T(8,128)(2,1)S(1)}, bf16[128,896]{1,0:T(8,128)(2,1)S(1)}, u32[]{:S(2)}, u32[]{:S(2)}) collective-permute-start(bf16[128,896]{1,0:T(8,128)(2,1)S(1)} %get-tuple-element.52.refs_3_), channel_id=1, source_target_pairs={{0,1},{1,0},{2,3},{3,2},{4,5},{5,4},{6,7},{7,6},{8,9},{9,8},{10,11... | collective-permute-start | bytes 688136 | tf_op jit(solution)/shard_map/ppermute | solution.py:360
  16.7 10.4 %collective-permute-start.4 = (bf16[128,896]{1,0:T(8,128)(2,1)S(1)}, bf16[128,896]{1,0:T(8,128)(2,1)S(1)}, u32[]{:S(2)}, u32[]{:S(2)}) collective-permute-start(bf16[128,896]{1,0:T(8,128)(2,1)S(1)} %get-tuple-element.52.refs_3_), channel_id=1, source_target_pairs={{0,2},{2,0},{1,3},{3,1},{4,6},{6,4},{5,7},{7,5},{8,10},{10,8},{9,1... | collective-permute-start | bytes 688136 | tf_op jit(solution)/shard_map/ppermute | solution.py:360
  18.2 7.6 %collective-permute-start.7 = (bf16[256,128]{1,0:T(8,128)(2,1)S(1)}, bf16[256,128]{1,0:T(8,128)(2,1)S(1)}, u32[]{:S(2)}, u32[]{:S(2)}) collective-permute-start(bf16[256,128]{1,0:T(8,128)(2,1)S(1)} %pad_maximum_fusion.1.refs_0_), channel_id=1, source_target_pairs={{0,12},{1,13},{2,14},{3,15},{16,28},{17,29},{18,30},{19,31}} | collective-permute-start | bytes 196616 | tf_op jit(solution)/shard_map/ppermute | solution.py:365
  23.8 3.2 %collective-permute-start.6 = (bf16[256,128]{1,0:T(8,128)(2,1)S(1)}, bf16[256,128]{1,0:T(8,128)(2,1)S(1)}, u32[]{:S(2)}, u32[]{:S(2)}) collective-permute-start(bf16[256,128]{1,0:T(8,128)(2,1)S(1)} %pad_maximum_fusion.1.refs_0_), channel_id=1, source_target_pairs={{0,8},{4,12},{1,9},{5,13},{2,10},{6,14},{3,11},{7,15},{16,24},{20,... | collective-permute-start | bytes 196616 | tf_op jit(solution)/shard_map/ppermute | solution.py:365
  27.0 1.5 %collective-permute-start.8 = (bf16[128,896]{1,0:T(8,128)(2,1)S(1)}, bf16[128,896]{1,0:T(8,128)(2,1)S(1)}, u32[]{:S(2)}, u32[]{:S(2)}) collective-permute-start(bf16[128,896]{1,0:T(8,128)(2,1)S(1)} %collective-permute-done.4.refs_1_), channel_id=1, source_target_pairs={{0,1},{1,0},{2,3},{3,2},{4,5},{5,4},{6,7},{7,6},{8,9},{9,8},{10,11... | collective-permute-start | bytes 688136 | tf_op jit(solution)/shard_map/ppermute | solution.py:360
  29.0 9.4 %collective-permute-start.9 = (bf16[128,1024]{1,0:T(8,128)(2,1)S(1)}, bf16[128,1024]{1,0:T(8,128)(2,1)S(1)}, u32[]{:S(2)}, u32[]{:S(2)}) collective-permute-start(bf16[128,1024]{1,0:T(8,128)(2,1)S(1)} %shard_map.97), channel_id=1, source_target_pairs={{0,4},{4,0},{8,12},{12,8},{1,5},{5,1},{9,13},{13,9},{2,6},{6,2},{1... | collective-permute-start | bytes 786440 | tf_op jit(solution)/shard_map/ppermute | solution.py:360
  32.7 11.5 %copy-start.1 = (bf16[128,1024]{1,0:T(8,128)(2,1)S(1)}, bf16[128,1024]{1,0:T(8,128)(2,1)}, u32[]{:S(2)}) copy-start(bf16[128,1024]{1,0:T(8,128)(2,1)} %queries_ref) | copy-start | bytes 786436
  38.5 15.3 %collective-permute-start.10 = (bf16[128,1024]{1,0:T(8,128)(2,1)S(1)}, bf16[128,1024]{1,0:T(8,128)(2,1)S(1)}, u32[]{:S(2)}, u32[]{:S(2)}) collective-permute-start(bf16[128,1024]{1,0:T(8,128)(2,1)S(1)} %add_convert_fusion), channel_id=1, source_target_pairs={{0,8},{4,12},{8,0},{12,4},{1,9},{5,13},{9,1},{13,5},{2,10},{6,14},... | collective-permute-start | bytes 786440 | tf_op jit(solution)/shard_map/ppermute | solution.py:360
  42.4 12.3 %collective-permute-start.11 = (bf16[128,1024]{1,0:T(8,128)(2,1)S(1)}, bf16[128,1024]{1,0:T(8,128)(2,1)S(1)}, u32[]{:S(2)}, u32[]{:S(2)}) collective-permute-start(bf16[128,1024]{1,0:T(8,128)(2,1)S(1)} %shard_map.99), channel_id=1, source_target_pairs={{0,4},{4,0},{8,12},{12,8},{1,5},{5,1},{9,13},{13,9},{2,6},{6,2},{1... | collective-permute-start | bytes 786440 | tf_op jit(solution)/shard_map/ppermute | solution.py:360
  54.8 13.1 %collective-permute-start.13 = (bf16[128,1024]{1,0:T(8,128)(2,1)S(1)}, bf16[128,1024]{1,0:T(8,128)(2,1)S(1)}, u32[]{:S(2)}, u32[]{:S(2)}) collective-permute-start(bf16[128,1024]{1,0:T(8,128)(2,1)S(1)} %subtract_convert_fusion.delta_ref), channel_id=1, source_target_pairs={{0,8},{4,12},{8,0},{12,4},{1,9},{5,13},{9,1},{13,5},{2,10},{6,14},... | collective-permute-start | bytes 786440 | tf_op jit(solution)/shard_map/ppermute | solution.py:360
  56.0 12.8 %collective-permute-start.12 = (bf16[128,1024]{1,0:T(8,128)(2,1)S(1)}, bf16[128,1024]{1,0:T(8,128)(2,1)S(1)}, u32[]{:S(2)}, u32[]{:S(2)}) collective-permute-start(bf16[128,1024]{1,0:T(8,128)(2,1)S(1)} %subtract_convert_fusion.delta_ref), channel_id=1, source_target_pairs={{0,4},{4,0},{8,12},{12,8},{1,5},{5,1},{9,13},{13,9},{2,6},{6,2},{1... | collective-permute-start | bytes 786440 | tf_op jit(solution)/shard_map/ppermute | solution.py:360
  67.9 6.5 %collective-permute-start.14 = (bf16[128,1024]{1,0:T(8,128)(2,1)S(1)}, bf16[128,1024]{1,0:T(8,128)(2,1)S(1)}, u32[]{:S(2)}, u32[]{:S(2)}) collective-permute-start(bf16[128,1024]{1,0:T(8,128)(2,1)S(1)} %collective-permute-done.13.delta_ref), channel_id=1, source_target_pairs={{0,4},{4,0},{8,12},{12,8},{1,5},{5,1},{9,13},{13,9},{2,6},{6,2},{1... | collective-permute-start | bytes 786440 | tf_op jit(solution)/shard_map/ppermute | solution.py:360
  75.1 1.9 %collective-permute-start.15 = (bf16[2,128,896]{2,1,0:T(8,128)(2,1)S(1)}, bf16[2,128,896]{2,1,0:T(8,128)(2,1)S(1)}, u32[]{:S(2)}, u32[]{:S(2)}) collective-permute-start(bf16[2,128,896]{2,1,0:T(8,128)(2,1)S(1)} %get-tuple-element.61), channel_id=1, source_target_pairs={{0,1},{1,0},{2,3},{3,2},{4,5},{5,4},{6,7},{7,6},{8,9},{9,8},{10,11... | collective-permute-start | bytes 1376264 | tf_op jit(solution)/shard_map/ppermute | solution.py:360
  77.1 7.7 %collective-permute-start.16 = (bf16[128,896]{1,0:T(8,128)(2,1)S(1)}, bf16[128,896]{1,0:T(8,128)(2,1)S(1)}, u32[]{:S(2)}, u32[]{:S(2)}) collective-permute-start(bf16[128,896]{1,0:T(8,128)(2,1)S(1)} %fusion), channel_id=1, source_target_pairs={{0,2},{2,0},{1,3},{3,1},{4,6},{6,4},{5,7},{7,5},{8,10},{10,8},{9,1... | collective-permute-start | bytes 688136 | tf_op jit(solution)/shard_map/ppermute | solution.py:360
  85.2 5.3 %collective-permute-start.17 = (bf16[48,896]{1,0:T(8,128)(2,1)S(1)}, bf16[48,896]{1,0:T(8,128)(2,1)S(1)}, u32[]{:S(2)}, u32[]{:S(2)}) collective-permute-start(bf16[48,896]{1,0:T(8,128)(2,1)S(1)} %get-tuple-element.65), channel_id=1, source_target_pairs={{0,4},{4,0},{8,12},{12,8},{1,5},{5,1},{9,13},{13,9},{2,6},{6,2},{1... | collective-permute-start | bytes 258056 | tf_op jit(solution)/shard_map/ppermute | solution.py:360
  85.9 8.7 %collective-permute-start.18 = (bf16[48,896]{1,0:T(8,128)(2,1)S(1)}, bf16[48,896]{1,0:T(8,128)(2,1)S(1)}, u32[]{:S(2)}, u32[]{:S(2)}) collective-permute-start(bf16[48,896]{1,0:T(8,128)(2,1)S(1)} %get-tuple-element.66), channel_id=1, source_target_pairs={{0,8},{4,12},{8,0},{12,4},{1,9},{5,13},{9,1},{13,5},{2,10},{6,14},... | collective-permute-start | bytes 258056 | tf_op jit(solution)/shard_map/ppermute | solution.py:360
  89.3 6.4 %collective-permute-start.19 = (bf16[48,896]{1,0:T(8,128)(2,1)S(1)}, bf16[48,896]{1,0:T(8,128)(2,1)S(1)}, u32[]{:S(2)}, u32[]{:S(2)}) collective-permute-start(bf16[48,896]{1,0:T(8,128)(2,1)S(1)} %get-tuple-element.67), channel_id=1, source_target_pairs={{0,12},{4,8},{8,4},{12,0},{1,13},{5,9},{9,5},{13,1},{2,14},{6,10},... | collective-permute-start | bytes 258056 | tf_op jit(solution)/shard_map/ppermute | solution.py:360
  89.6 7.0 %collective-permute-start.20 = (bf16[48,896]{1,0:T(8,128)(2,1)S(1)}, bf16[48,896]{1,0:T(8,128)(2,1)S(1)}, u32[]{:S(2)}, u32[]{:S(2)}) collective-permute-start(bf16[48,896]{1,0:T(8,128)(2,1)S(1)} %get-tuple-element.64.refs_0_), channel_id=1, source_target_pairs={{0,2},{2,0},{1,3},{3,1},{4,6},{6,4},{5,7},{7,5},{8,10},{10,8},{9,1... | collective-permute-start | bytes 258056 | tf_op jit(solution)/shard_map/ppermute | solution.py:360
  90.4 6.2 %collective-permute-start.21 = (bf16[48,896]{1,0:T(8,128)(2,1)S(1)}, bf16[48,896]{1,0:T(8,128)(2,1)S(1)}, u32[]{:S(2)}, u32[]{:S(2)}) collective-permute-start(bf16[48,896]{1,0:T(8,128)(2,1)S(1)} %collective-permute-done.17.refs_1_), channel_id=1, source_target_pairs={{0,2},{2,0},{1,3},{3,1},{4,6},{6,4},{5,7},{7,5},{8,10},{10,8},{9,1... | collective-permute-start | bytes 258056 | tf_op jit(solution)/shard_map/ppermute | solution.py:360
  94.6 4.5 %collective-permute-start.22 = (bf16[48,896]{1,0:T(8,128)(2,1)S(1)}, bf16[48,896]{1,0:T(8,128)(2,1)S(1)}, u32[]{:S(2)}, u32[]{:S(2)}) collective-permute-start(bf16[48,896]{1,0:T(8,128)(2,1)S(1)} %collective-permute-done.18.refs_2_), channel_id=1, source_target_pairs={{0,2},{2,0},{1,3},{3,1},{4,6},{6,4},{5,7},{7,5},{8,10},{10,8},{9,1... | collective-permute-start | bytes 258056 | tf_op jit(solution)/shard_map/ppermute | solution.py:360
  95.7 4.5 %collective-permute-start.23 = (bf16[48,896]{1,0:T(8,128)(2,1)S(1)}, bf16[48,896]{1,0:T(8,128)(2,1)S(1)}, u32[]{:S(2)}, u32[]{:S(2)}) collective-permute-start(bf16[48,896]{1,0:T(8,128)(2,1)S(1)} %collective-permute-done.19.refs_3_), channel_id=1, source_target_pairs={{0,2},{2,0},{1,3},{3,1},{4,6},{6,4},{5,7},{7,5},{8,10},{10,8},{9,1... | collective-permute-start | bytes 258056 | tf_op jit(solution)/shard_map/ppermute | solution.py:360
  100.9 2.2 %collective-permute-start.24 = (bf16[2,48,3584]{2,1,0:T(8,128)(2,1)S(1)}, bf16[2,48,3584]{2,1,0:T(8,128)(2,1)S(1)}, u32[]{:S(2)}, u32[]{:S(2)}) collective-permute-start(bf16[2,48,3584]{2,1,0:T(8,128)(2,1)S(1)} %shard_map.106.pair_ref), channel_id=1, source_target_pairs={{0,1},{1,0},{2,3},{3,2},{4,5},{5,4},{6,7},{7,6},{8,9},{9,8},{10,11... | collective-permute-start | bytes 2064392 | tf_op jit(solution)/shard_map/ppermute | solution.py:360

commit v10 on v8

--- a/solution.py
+++ b/solution.py
@@ -192,48 +192,33 @@
     return jnp.where(at >= 2, jnp.where(odd, d, c), jnp.where(odd, b, a))
 
 
-def away_kernel(*refs):
+def away_kernel(peer, *refs):
     *entries, proj_ref, out_ref = refs
     me, mine = indices()
-    block = pick_entry(entries, me ^ mine ^ 3)
+    block = pick_entry(entries, me ^ mine ^ peer)
     out_ref[...] = dot(block, proj_ref[...]).astype(BF)
 
 
 def kept_kernel(*refs):
-    *entries, proj_ref, own_ref, over_ref, normed_ref = refs
+    *entries, proj_ref, own_ref, normed_ref = refs
     me, mine = indices()
     rows = entries[0].shape[0]
     for k, spot in enumerate((0, 2, 1, 3)):
         normed_ref[spot * rows : (spot + 1) * rows, :] = pick_entry(entries, me ^ mine ^ k)
-    columns = 256
-    for first in range(0, proj_ref.shape[1], columns):
-        part = slice(first, first + columns)
-        product = dot(normed_ref[: 2 * rows, :], proj_ref[:, part])
-        own_ref[:, part] = product[:rows]
-        over_ref[:, part] = product[rows:]
-
-
-def beside_kernel(normed_ref, proj_ref, out_ref):
-    rows = out_ref.shape[0]
-    out_ref[...] = dot(normed_ref[2 * rows : 3 * rows, :], proj_ref[...]).astype(BF)
-
-
-def away_partial(entries, proj):
+    own_ref[...] = dot(normed_ref[:rows, :], proj_ref[...])
+
+
+def away_partial(peer, entries, proj):
     rows, depth = entries[0].shape
     out = jax.ShapeDtypeStruct((rows, proj.shape[1]), BF)
-    return call(away_kernel, out, (*entries, proj), 0, 0)
-
-
-def kept_partials(entries, proj):
+    return call(functools.partial(away_kernel, peer), out, (*entries, proj), 0, 0)
+
+
+def kept_partial(entries, proj):
     rows, depth = entries[0].shape
     out = jax.ShapeDtypeStruct((rows, proj.shape[1]), F32)
-    shapes = [out, out, jax.ShapeDtypeStruct((4 * rows, depth), BF)]
+    shapes = [out, jax.ShapeDtypeStruct((4 * rows, depth), BF)]
     return call(kept_kernel, shapes, (*entries, proj), 0, 0)
-
-
-def beside_partial(normed, proj):
-    out = jax.ShapeDtypeStruct((normed.shape[0] // 4, proj.shape[1]), BF)
-    return call(beside_kernel, out, (normed, proj), 0, 0)
 
 
 def product_kernel(delta_ref, proj_ref, out_ref):
@@ -412,15 +397,16 @@
     far_mate = swap(after(far, mate, parcels[2]), "side")
     entries = [far_mate, far, mate, normed_own]
 
-    away = away_partial(entries, proj)
-    own, over_own, normed = kept_partials([after(e, away) for e in entries], proj)
-    parcels.append(onward(after(parcels[2], away)))
-    got_over = after(swap(away, "seq", 1), over_own, parcels[3])
-    over = lax.optimization_barrier((over_own + got_over.astype(F32)).astype(BF))
-    got_far = swap(over, "seq", 2)
-    got_beside = swap(beside_partial(after(normed, over), proj), "seq", 1)
-    teacher_rows = attention_rows(after(teacher_queries, over), parcels, pieces)
-    predicted = lax.optimization_barrier(own + got_far.astype(F32)) + got_beside.astype(F32)
+    got, last = [], []
+    for k in (3, 2, 1):
+        partial = away_partial(k, [after(e, *last) for e in entries], proj)
+        last = [partial]
+        got.append(swap(partial, "seq", k).astype(F32))
+    own, normed = kept_partial([after(e, *last) for e in entries], proj)
+    parcels.append(onward(after(parcels[2], own)))
+    teacher_rows = attention_rows(after(teacher_queries, own), parcels, pieces)
+    predicted = lax.optimization_barrier(own + got[0])
+    predicted = lax.optimization_barrier(predicted + got[1]) + got[2]
     delta = (predicted - teacher_rows.astype(F32)).astype(BF)
 
     delta_far = swap(delta, "seq", 2)

time: 102 us -> 105 us (1.029)
  waiting for transfers between devices: 44.4 us -> 51.5 us
  starting transfers between devices: 39.9 us -> 35.8 us
    ppermute x22, waiting for transfers between devices: 35.1 us -> 42.8 us  [swap(): lax.ppermute(x, axis, [(i, i ^ k) for i in range(lax.axis_size(axis))])]
    ppermute x22, starting transfers between devices: 30.8 us -> 26.9 us  [swap(): lax.ppermute(x, axis, [(i, i ^ k) for i in range(lax.axis_size(axis))])]
    pallas_call x14 -> x15, Pallas kernels: 11.4 us -> 11.6 us  [call(): pl.pallas_call(kernel, out_shape=shapes, cost_estimate=pl.CostEstimate(fl...]
where the time goes in v10:
time: 105 us
  waiting for transfers between devices  51.5 us (49%)
  starting transfers between devices  35.8 us (34%)
  Pallas kernels  11.6 us (11%)
  matrix products  2.98 us (3%)
  other arithmetic  1.3 us (1%)
    ppermute x22, waiting for transfers between devices, swap(): lax.ppermute(x, axis, [(i, i ^ k) for i in range(lax.axis_size(axis))])  42.8 us
    ppermute x22, starting transfers between devices, swap(): lax.ppermute(x, axis, [(i, i ^ k) for i in range(lax.axis_size(axis))])  26.9 us
    pallas_call x15, Pallas kernels, call(): pl.pallas_call(kernel, out_shape=shapes, cost_estimate=pl.CostEstimate(fl...  11.6 us
    ppermute x3, starting transfers between devices, onward(): lax.ppermute(x, 'seq', [(i, i + 1) for i in range(lax.axis_size('seq') -...  8.95 us
    ppermute x3, waiting for transfers between devices, onward(): lax.ppermute(x, 'seq', [(i, i + 1) for i in range(lax.axis_size('seq') -...  8.74 us
    dot_general x1, matrix products, dot(): return lax.dot_general(a, b, (dims, ((), ())), preferred_element_type=F32)  2.98 us
  transfers between devices with their start and end apart: 25, of which 16 were waited for; matrix products, arithmetic and copies ran while one was open for 4% of the time, Pallas kernels for 7%

profile of v10, /device:TPU:0, one launch (start us, length us, event | category | flops | bytes accessed | tf_op | source)
XLA Modules:
  0.0 104.9 jit_solution(6728548365303657496)
XLA Ops:
  0.7 0.9 convert_select_fusion.small_ref
  1.6 1.2 %shard_map.95 = (bf16[48,1024]{1,0:T(8,128)(2,1)S(1)}, bf16[48,1024]{1,0:T(8,128)(2,1)S(1)}, bf16[48,1024]{1,0:T(8,128)(2,1)S(1)}, bf16[48,1024]{1,0:T(8,128)(2,1)S(1)}, bf16[2,48,3584]{2,1,0:T(8,128)(2,1)S(1)}) custom-call(bf16[4,48,3584]{2,1,0:T(8,128)(2,1)} %bitcast.9, f32[30,128]{1,0:T(8,128)S(1)} %convert_select_fusion.small_ref), custom_call_target="tpu_custom_call" | custom-call | flops 1032192 | bytes 1376256 | tf_op jit(solution)/shard_map/pallas_call | solution.py:49
  2.8 5.1 %collective-permute-start = (bf16[48,1024]{1,0:T(8,128)(2,1)S(1)}, bf16[48,1024]{1,0:T(8,128)(2,1)S(1)}, u32[]{:S(2)}, u32[]{:S(2)}) collective-permute-start(bf16[48,1024]{1,0:T(8,128)(2,1)S(1)} %get-tuple-element.42), channel_id=1, source_target_pairs={{0,12},{4,8},{8,4},{12,0},{1,13},{5,9},{9,5},{13,1},{2,14},{6,10},... | collective-permute-start | bytes 294920 | tf_op jit(solution)/shard_map/ppermute | solution.py:345
  7.9 0.6 collective-permute-start.3
  8.6 0.8 constant_dynamic-slice_fusion
  9.4 3.3 %collective-permute-start.1 = (bf16[256,128]{1,0:T(8,128)(2,1)S(1)}, bf16[256,128]{1,0:T(8,128)(2,1)S(1)}, u32[]{:S(2)}, u32[]{:S(2)}) collective-permute-start(bf16[256,128]{1,0:T(8,128)(2,1)S(1)} %pad_maximum_fusion.1.refs_0_), channel_id=1, source_target_pairs={{0,4},{4,8},{8,12},{1,5},{5,9},{9,13},{2,6},{6,10},{10,14},{3,7},{... | collective-permute-start | bytes 196616 | tf_op jit(solution)/shard_map/ppermute | solution.py:349
  12.7 3.0 %collective-permute-done.1.refs_1_ = bf16[256,128]{1,0:T(8,128)(2,1)S(1)} collective-permute-done((bf16[256,128]{1,0:T(8,128)(2,1)S(1)}, bf16[256,128]{1,0:T(8,128)(2,1)S(1)}, u32[]{:S(2)}, u32[]{:S(2)}) %collective-permute-start.1) | collective-permute-done | bytes 65568 | tf_op jit(solution)/shard_map/ppermute | solution.py:349
  15.7 0.0 collective-permute-done.refs_0_.refs_7_
  15.7 0.5 collective-permute-done.2.refs_1_.refs_6_
  16.2 0.0 collective-permute-done.3.refs_2_.refs_5_
  16.2 0.4 shard_map.96
  16.6 0.1 collective-permute-start.5
  16.7 1.6 %collective-permute-start.4 = (bf16[128,896]{1,0:T(8,128)(2,1)S(1)}, bf16[128,896]{1,0:T(8,128)(2,1)S(1)}, u32[]{:S(2)}, u32[]{:S(2)}) collective-permute-start(bf16[128,896]{1,0:T(8,128)(2,1)S(1)} %get-tuple-element.66.refs_3_), channel_id=1, source_target_pairs={{0,2},{2,0},{1,3},{3,1},{4,6},{6,4},{5,7},{7,5},{8,10},{10,8},{9,1... | collective-permute-start | bytes 688136 | tf_op jit(solution)/shard_map/ppermute | solution.py:345
  18.2 3.8 %collective-permute-start.6 = (bf16[256,128]{1,0:T(8,128)(2,1)S(1)}, bf16[256,128]{1,0:T(8,128)(2,1)S(1)}, u32[]{:S(2)}, u32[]{:S(2)}) collective-permute-start(bf16[256,128]{1,0:T(8,128)(2,1)S(1)} %collective-permute-done.1.refs_1_), channel_id=1, source_target_pairs={{0,4},{4,8},{8,12},{1,5},{5,9},{9,13},{2,6},{6,10},{10,14},{3,7},{... | collective-permute-start | bytes 196616 | tf_op jit(solution)/shard_map/ppermute | solution.py:349
  22.1 1.9 %collective-permute-done.6.refs_2_ = bf16[256,128]{1,0:T(8,128)(2,1)S(1)} collective-permute-done((bf16[256,128]{1,0:T(8,128)(2,1)S(1)}, bf16[256,128]{1,0:T(8,128)(2,1)S(1)}, u32[]{:S(2)}, u32[]{:S(2)}) %collective-permute-start.6) | collective-permute-done | bytes 65568 | tf_op jit(solution)/shard_map/ppermute | solution.py:349
  24.0 0.7 collective-permute-done.4.refs_1_
  24.7 0.0 collective-permute-start.7
  24.7 1.5 %collective-permute-done.7.refs_0_ = bf16[128,896]{1,0:T(8,128)(2,1)S(1)} collective-permute-done((bf16[128,896]{1,0:T(8,128)(2,1)S(1)}, bf16[128,896]{1,0:T(8,128)(2,1)S(1)}, u32[]{:S(2)}, u32[]{:S(2)}) %collective-permute-start.7) | collective-permute-done | bytes 229408 | tf_op jit(solution)/shard_map/ppermute | solution.py:345
  26.2 0.5 shard_map.97
  26.6 3.8 %collective-permute-start.8 = (bf16[128,1024]{1,0:T(8,128)(2,1)S(1)}, bf16[128,1024]{1,0:T(8,128)(2,1)S(1)}, u32[]{:S(2)}, u32[]{:S(2)}) collective-permute-start(bf16[128,1024]{1,0:T(8,128)(2,1)S(1)} %shard_map.97), channel_id=1, source_target_pairs={{0,12},{4,8},{8,4},{12,0},{1,13},{5,9},{9,5},{13,1},{2,14},{6,10},... | collective-permute-start | bytes 786440 | tf_op jit(solution)/shard_map/ppermute | solution.py:345
  30.4 0.4 shard_map.98
  30.9 0.5 shard_map.99
  31.3 0.0 copy-start.1
  31.3 0.7 shard_map.100
  32.0 1.8 %collective-permute-start.11 = (bf16[256,128]{1,0:T(8,128)(2,1)S(1)}, bf16[256,128]{1,0:T(8,128)(2,1)S(1)}, u32[]{:S(2)}, u32[]{:S(2)}) collective-permute-start(bf16[256,128]{1,0:T(8,128)(2,1)S(1)} %collective-permute-done.6.refs_2_), channel_id=1, source_target_pairs={{0,4},{4,8},{8,12},{1,5},{5,9},{9,13},{2,6},{6,10},{10,14},{3,7},{... | collective-permute-start | bytes 196616 | tf_op jit(solution)/shard_map/ppermute | solution.py:349
  33.9 0.8 collective-permute-start.9
  34.7 3.9 %collective-permute-done.11.refs_3_ = bf16[256,128]{1,0:T(8,128)(2,1)S(1)} collective-permute-done((bf16[256,128]{1,0:T(8,128)(2,1)S(1)}, bf16[256,128]{1,0:T(8,128)(2,1)S(1)}, u32[]{:S(2)}, u32[]{:S(2)}) %collective-permute-start.11) | collective-permute-done | bytes 65568 | tf_op jit(solution)/shard_map/ppermute | solution.py:349
  38.6 2.3 %shard_map.101 = bf16[128,1024]{1,0:T(8,128)(2,1)S(1)} custom-call(bf16[128,1024]{1,0:T(8,128)(2,1)S(1)} %copy-done.1, bf16[256,128]{1,0:T(8,128)(2,1)S(1)} %pad_maximum_fusion.1.refs_0_, bf16[256,128]{1,0:T(8,128)(2,1)S(1)} %collective-permute-done.1.refs_1_, bf16[256,128]{1,0:T(8,128)(2,1)S(1)} %collective-permute-done.6.refs_2_, ...), custom_call_target="tpu_custom_call" | custom-call | bytes 524288 | tf_op jit(solution)/shard_map/pallas_call | solution.py:49
  40.9 0.1 convert_add_fusion.1
  41.0 12.3 %collective-permute-done.9 = bf16[128,1024]{1,0:T(8,128)(2,1)S(1)} collective-permute-done((bf16[128,1024]{1,0:T(8,128)(2,1)S(1)}, bf16[128,1024]{1,0:T(8,128)(2,1)S(1)}, u32[]{:S(2)}, u32[]{:S(2)}) %collective-permute-start.9) | collective-permute-done | bytes 262176 | tf_op jit(solution)/shard_map/ppermute | solution.py:345
  53.3 0.1 convert_add_fusion
  53.4 0.1 subtract_convert_fusion.delta_ref
  53.5 0.7 collective-permute-start.13
  54.2 0.7 shard_map.102.first_ref
  54.9 3.9 %collective-permute-start.12 = (bf16[128,1024]{1,0:T(8,128)(2,1)S(1)}, bf16[128,1024]{1,0:T(8,128)(2,1)S(1)}, u32[]{:S(2)}, u32[]{:S(2)}) collective-permute-start(bf16[128,1024]{1,0:T(8,128)(2,1)S(1)} %subtract_convert_fusion.delta_ref), channel_id=1, source_target_pairs={{0,4},{4,0},{8,12},{12,8},{1,5},{5,1},{9,13},{13,9},{2,6},{6,2},{1... | collective-permute-start | bytes 786440 | tf_op jit(solution)/shard_map/ppermute | solution.py:345
  58.8 9.0 %collective-permute-done.13.delta_ref = bf16[128,1024]{1,0:T(8,128)(2,1)S(1)} collective-permute-done((bf16[128,1024]{1,0:T(8,128)(2,1)S(1)}, bf16[128,1024]{1,0:T(8,128)(2,1)S(1)}, u32[]{:S(2)}, u32[]{:S(2)}) %collective-permute-start.13) | collective-permute-done | bytes 262176 | tf_op jit(solution)/shard_map/ppermute | solution.py:345
  67.8 0.7 shard_map.104.third_ref
  68.5 0.1 collective-permute-done.12.delta_ref
  68.7 0.7 shard_map.103.second_ref
  69.4 5.4 %collective-permute-done.14.delta_ref = bf16[128,1024]{1,0:T(8,128)(2,1)S(1)} collective-permute-done((bf16[128,1024]{1,0:T(8,128)(2,1)S(1)}, bf16[128,1024]{1,0:T(8,128)(2,1)S(1)}, u32[]{:S(2)}, u32[]{:S(2)}) %collective-permute-start.14) | collective-permute-done | bytes 262176 | tf_op jit(solution)/shard_map/ppermute | solution.py:345
  74.8 0.8 shard_map.105
  75.5 0.1 collective-permute-start.15
  75.6 0.1 pad_maximum_fusion
  75.7 1.7 %collective-permute-done.15.got_ref = bf16[2,128,896]{2,1,0:T(8,128)(2,1)S(1)} collective-permute-done((bf16[2,128,896]{2,1,0:T(8,128)(2,1)S(1)}, bf16[2,128,896]{2,1,0:T(8,128)(2,1)S(1)}, u32[]{:S(2)}, u32[]{:S(2)}) %collective-permute-start.15) | collective-permute-done | bytes 458784 | tf_op jit(solution)/shard_map/ppermute | solution.py:345
  77.4 0.1 fusion
  77.5 1.6 %collective-permute-start.16 = (bf16[128,896]{1,0:T(8,128)(2,1)S(1)}, bf16[128,896]{1,0:T(8,128)(2,1)S(1)}, u32[]{:S(2)}, u32[]{:S(2)}) collective-permute-start(bf16[128,896]{1,0:T(8,128)(2,1)S(1)} %fusion), channel_id=1, source_target_pairs={{0,2},{2,0},{1,3},{3,1},{4,6},{6,4},{5,7},{7,5},{8,10},{10,8},{9,1... | collective-permute-start | bytes 688136 | tf_op jit(solution)/shard_map/ppermute | solution.py:345
  79.0 3.0 %convolution_multiply_fusion = f32[896,1024]{1,0:T(8,128)} fusion(bf16[512,896]{1,0:T(8,128)(2,1)S(1)} %get-tuple-element.73, bf16[512,1024]{1,0:T(8,128)(2,1)S(1)} %pad_maximum_fusion), kind=kOutput, calls=%fused_computation | convolution fusion | flops 940441600 | bytes 5636096 | tf_op jit(solution)/shard_map/dot_general | solution.py:22
  82.0 3.2 %collective-permute-done.16.crossed_ref = bf16[128,896]{1,0:T(8,128)(2,1)S(1)} collective-permute-done((bf16[128,896]{1,0:T(8,128)(2,1)S(1)}, bf16[128,896]{1,0:T(8,128)(2,1)S(1)}, u32[]{:S(2)}, u32[]{:S(2)}) %collective-permute-start.16) | collective-permute-done | bytes 229408 | tf_op jit(solution)/shard_map/ppermute | solution.py:345
  85.2 0.3 shard_map.106
  85.6 0.3 collective-permute-start.17
  85.9 2.7 %collective-permute-start.18 = (bf16[48,896]{1,0:T(8,128)(2,1)S(1)}, bf16[48,896]{1,0:T(8,128)(2,1)S(1)}, u32[]{:S(2)}, u32[]{:S(2)}) collective-permute-start(bf16[48,896]{1,0:T(8,128)(2,1)S(1)} %get-tuple-element.78), channel_id=1, source_target_pairs={{0,8},{4,12},{8,0},{12,4},{1,9},{5,13},{9,1},{13,5},{2,10},{6,14},... | collective-permute-start | bytes 258056 | tf_op jit(solution)/shard_map/ppermute | solution.py:345
  88.6 1.4 %collective-permute-start.19 = (bf16[48,896]{1,0:T(8,128)(2,1)S(1)}, bf16[48,896]{1,0:T(8,128)(2,1)S(1)}, u32[]{:S(2)}, u32[]{:S(2)}) collective-permute-start(bf16[48,896]{1,0:T(8,128)(2,1)S(1)} %get-tuple-element.79), channel_id=1, source_target_pairs={{0,12},{4,8},{8,4},{12,0},{1,13},{5,9},{9,5},{13,1},{2,14},{6,10},... | collective-permute-start | bytes 258056 | tf_op jit(solution)/shard_map/ppermute | solution.py:345
  90.0 1.5 %collective-permute-start.20 = (bf16[48,896]{1,0:T(8,128)(2,1)S(1)}, bf16[48,896]{1,0:T(8,128)(2,1)S(1)}, u32[]{:S(2)}, u32[]{:S(2)}) collective-permute-start(bf16[48,896]{1,0:T(8,128)(2,1)S(1)} %get-tuple-element.76.refs_0_), channel_id=1, source_target_pairs={{0,2},{2,0},{1,3},{3,1},{4,6},{6,4},{5,7},{7,5},{8,10},{10,8},{9,1... | collective-permute-start | bytes 258056 | tf_op jit(solution)/shard_map/ppermute | solution.py:345
  91.5 0.5 collective-permute-start.21
  92.0 3.1 %collective-permute-done.18.refs_2_ = bf16[48,896]{1,0:T(8,128)(2,1)S(1)} collective-permute-done((bf16[48,896]{1,0:T(8,128)(2,1)S(1)}, bf16[48,896]{1,0:T(8,128)(2,1)S(1)}, u32[]{:S(2)}, u32[]{:S(2)}) %collective-permute-start.18) | collective-permute-done | bytes 86048 | tf_op jit(solution)/shard_map/ppermute | solution.py:345
  95.1 1.5 %collective-permute-start.22 = (bf16[48,896]{1,0:T(8,128)(2,1)S(1)}, bf16[48,896]{1,0:T(8,128)(2,1)S(1)}, u32[]{:S(2)}, u32[]{:S(2)}) collective-permute-start(bf16[48,896]{1,0:T(8,128)(2,1)S(1)} %collective-permute-done.18.refs_2_), channel_id=1, source_target_pairs={{0,2},{2,0},{1,3},{3,1},{4,6},{6,4},{5,7},{7,5},{8,10},{10,8},{9,1... | collective-permute-start | bytes 258056 | tf_op jit(solution)/shard_map/ppermute | solution.py:345
  96.6 0.5 collective-permute-start.23
  97.2 2.4 %collective-permute-done.22.refs_6_ = bf16[48,896]{1,0:T(8,128)(2,1)S(1)} collective-permute-done((bf16[48,896]{1,0:T(8,128)(2,1)S(1)}, bf16[48,896]{1,0:T(8,128)(2,1)S(1)}, u32[]{:S(2)}, u32[]{:S(2)}) %collective-permute-start.22) | collective-permute-done | bytes 86048 | tf_op jit(solution)/shard_map/ppermute | solution.py:345
  99.6 1.5 %collective-permute-done.23.refs_7_ = bf16[48,896]{1,0:T(8,128)(2,1)S(1)} collective-permute-done((bf16[48,896]{1,0:T(8,128)(2,1)S(1)}, bf16[48,896]{1,0:T(8,128)(2,1)S(1)}, u32[]{:S(2)}, u32[]{:S(2)}) %collective-permute-start.23) | collective-permute-done | bytes 86048 | tf_op jit(solution)/shard_map/ppermute | solution.py:345
  101.1 0.7 shard_map.107.pair_ref
  101.8 0.1 collective-permute-start.24
  101.9 0.9 shard_map.108.t
  102.8 1.3 %collective-permute-done.24.refs_0_ = bf16[2,48,3584]{2,1,0:T(8,128)(2,1)S(1)} collective-permute-done((bf16[2,48,3584]{2,1,0:T(8,128)(2,1)S(1)}, bf16[2,48,3584]{2,1,0:T(8,128)(2,1)S(1)}, u32[]{:S(2)}, u32[]{:S(2)}) %collective-permute-start.24) | collective-permute-done | bytes 688160 | tf_op jit(solution)/shard_map/ppermute | solution.py:345
  104.0 0.9 shard_map.109
  (15 shorter events, 0.0 us)
Async XLA Ops:
  0.6 25.6 %copy-start = (bf16[896,1024]{1,0:T(8,128)(2,1)S(1)}, bf16[896,1024]{1,0:T(8,128)(2,1)}, u32[]{:S(2)}) copy-start(bf16[896,1024]{1,0:T(8,128)(2,1)} %proj_ref.7) | copy-start | bytes 5505028
  2.8 12.8 %collective-permute-start = (bf16[48,1024]{1,0:T(8,128)(2,1)S(1)}, bf16[48,1024]{1,0:T(8,128)(2,1)S(1)}, u32[]{:S(2)}, u32[]{:S(2)}) collective-permute-start(bf16[48,1024]{1,0:T(8,128)(2,1)S(1)} %get-tuple-element.42), channel_id=1, source_target_pairs={{0,12},{4,8},{8,4},{12,0},{1,13},{5,9},{9,5},{13,1},{2,14},{6,10},... | collective-permute-start | bytes 294920 | tf_op jit(solution)/shard_map/ppermute | solution.py:345
  7.9 8.3 %collective-permute-start.2 = (bf16[48,1024]{1,0:T(8,128)(2,1)S(1)}, bf16[48,1024]{1,0:T(8,128)(2,1)S(1)}, u32[]{:S(2)}, u32[]{:S(2)}) collective-permute-start(bf16[48,1024]{1,0:T(8,128)(2,1)S(1)} %get-tuple-element.46), channel_id=1, source_target_pairs={{0,8},{4,12},{8,0},{12,4},{1,9},{5,13},{9,1},{13,5},{2,10},{6,14},... | collective-permute-start | bytes 294920 | tf_op jit(solution)/shard_map/ppermute | solution.py:345
  7.9 8.3 %collective-permute-start.3 = (bf16[48,1024]{1,0:T(8,128)(2,1)S(1)}, bf16[48,1024]{1,0:T(8,128)(2,1)S(1)}, u32[]{:S(2)}, u32[]{:S(2)}) collective-permute-start(bf16[48,1024]{1,0:T(8,128)(2,1)S(1)} %get-tuple-element.48), channel_id=1, source_target_pairs={{0,4},{4,0},{8,12},{12,8},{1,5},{5,1},{9,13},{13,9},{2,6},{6,2},{1... | collective-permute-start | bytes 294920 | tf_op jit(solution)/shard_map/ppermute | solution.py:345
  9.4 6.3 %collective-permute-start.1 = (bf16[256,128]{1,0:T(8,128)(2,1)S(1)}, bf16[256,128]{1,0:T(8,128)(2,1)S(1)}, u32[]{:S(2)}, u32[]{:S(2)}) collective-permute-start(bf16[256,128]{1,0:T(8,128)(2,1)S(1)} %pad_maximum_fusion.1.refs_0_), channel_id=1, source_target_pairs={{0,4},{4,8},{8,12},{1,5},{5,9},{9,13},{2,6},{6,10},{10,14},{3,7},{... | collective-permute-start | bytes 196616 | tf_op jit(solution)/shard_map/ppermute | solution.py:349
  16.6 7.4 %collective-permute-start.5 = (bf16[128,896]{1,0:T(8,128)(2,1)S(1)}, bf16[128,896]{1,0:T(8,128)(2,1)S(1)}, u32[]{:S(2)}, u32[]{:S(2)}) collective-permute-start(bf16[128,896]{1,0:T(8,128)(2,1)S(1)} %get-tuple-element.66.refs_3_), channel_id=1, source_target_pairs={{0,1},{1,0},{2,3},{3,2},{4,5},{5,4},{6,7},{7,6},{8,9},{9,8},{10,11... | collective-permute-start | bytes 688136 | tf_op jit(solution)/shard_map/ppermute | solution.py:345
  16.7 8.0 %collective-permute-start.4 = (bf16[128,896]{1,0:T(8,128)(2,1)S(1)}, bf16[128,896]{1,0:T(8,128)(2,1)S(1)}, u32[]{:S(2)}, u32[]{:S(2)}) collective-permute-start(bf16[128,896]{1,0:T(8,128)(2,1)S(1)} %get-tuple-element.66.refs_3_), channel_id=1, source_target_pairs={{0,2},{2,0},{1,3},{3,1},{4,6},{6,4},{5,7},{7,5},{8,10},{10,8},{9,1... | collective-permute-start | bytes 688136 | tf_op jit(solution)/shard_map/ppermute | solution.py:345
  18.2 5.7 %collective-permute-start.6 = (bf16[256,128]{1,0:T(8,128)(2,1)S(1)}, bf16[256,128]{1,0:T(8,128)(2,1)S(1)}, u32[]{:S(2)}, u32[]{:S(2)}) collective-permute-start(bf16[256,128]{1,0:T(8,128)(2,1)S(1)} %collective-permute-done.1.refs_1_), channel_id=1, source_target_pairs={{0,4},{4,8},{8,12},{1,5},{5,9},{9,13},{2,6},{6,10},{10,14},{3,7},{... | collective-permute-start | bytes 196616 | tf_op jit(solution)/shard_map/ppermute | solution.py:349
  24.7 1.5 %collective-permute-start.7 = (bf16[128,896]{1,0:T(8,128)(2,1)S(1)}, bf16[128,896]{1,0:T(8,128)(2,1)S(1)}, u32[]{:S(2)}, u32[]{:S(2)}) collective-permute-start(bf16[128,896]{1,0:T(8,128)(2,1)S(1)} %collective-permute-done.4.refs_1_), channel_id=1, source_target_pairs={{0,1},{1,0},{2,3},{3,2},{4,5},{5,4},{6,7},{7,6},{8,9},{9,8},{10,11... | collective-permute-start | bytes 688136 | tf_op jit(solution)/shard_map/ppermute | solution.py:345
  26.6 14.3 %collective-permute-start.8 = (bf16[128,1024]{1,0:T(8,128)(2,1)S(1)}, bf16[128,1024]{1,0:T(8,128)(2,1)S(1)}, u32[]{:S(2)}, u32[]{:S(2)}) collective-permute-start(bf16[128,1024]{1,0:T(8,128)(2,1)S(1)} %shard_map.97), channel_id=1, source_target_pairs={{0,12},{4,8},{8,4},{12,0},{1,13},{5,9},{9,5},{13,1},{2,14},{6,10},... | collective-permute-start | bytes 786440 | tf_op jit(solution)/shard_map/ppermute | solution.py:345
  31.3 7.3 %copy-start.1 = (bf16[128,1024]{1,0:T(8,128)(2,1)S(1)}, bf16[128,1024]{1,0:T(8,128)(2,1)}, u32[]{:S(2)}) copy-start(bf16[128,1024]{1,0:T(8,128)(2,1)} %queries_ref) | copy-start | bytes 786436
  32.0 6.5 %collective-permute-start.11 = (bf16[256,128]{1,0:T(8,128)(2,1)S(1)}, bf16[256,128]{1,0:T(8,128)(2,1)S(1)}, u32[]{:S(2)}, u32[]{:S(2)}) collective-permute-start(bf16[256,128]{1,0:T(8,128)(2,1)S(1)} %collective-permute-done.6.refs_2_), channel_id=1, source_target_pairs={{0,4},{4,8},{8,12},{1,5},{5,9},{9,13},{2,6},{6,10},{10,14},{3,7},{... | collective-permute-start | bytes 196616 | tf_op jit(solution)/shard_map/ppermute | solution.py:349
  33.9 19.4 %collective-permute-start.9 = (bf16[128,1024]{1,0:T(8,128)(2,1)S(1)}, bf16[128,1024]{1,0:T(8,128)(2,1)S(1)}, u32[]{:S(2)}, u32[]{:S(2)}) collective-permute-start(bf16[128,1024]{1,0:T(8,128)(2,1)S(1)} %shard_map.98), channel_id=1, source_target_pairs={{0,8},{4,12},{8,0},{12,4},{1,9},{5,13},{9,1},{13,5},{2,10},{6,14},... | collective-permute-start | bytes 786440 | tf_op jit(solution)/shard_map/ppermute | solution.py:345
  34.7 18.7 %collective-permute-start.10 = (bf16[128,1024]{1,0:T(8,128)(2,1)S(1)}, bf16[128,1024]{1,0:T(8,128)(2,1)S(1)}, u32[]{:S(2)}, u32[]{:S(2)}) collective-permute-start(bf16[128,1024]{1,0:T(8,128)(2,1)S(1)} %shard_map.99), channel_id=1, source_target_pairs={{0,4},{4,0},{8,12},{12,8},{1,5},{5,1},{9,13},{13,9},{2,6},{6,2},{1... | collective-permute-start | bytes 786440 | tf_op jit(solution)/shard_map/ppermute | solution.py:345
  53.5 14.4 %collective-permute-start.13 = (bf16[128,1024]{1,0:T(8,128)(2,1)S(1)}, bf16[128,1024]{1,0:T(8,128)(2,1)S(1)}, u32[]{:S(2)}, u32[]{:S(2)}) collective-permute-start(bf16[128,1024]{1,0:T(8,128)(2,1)S(1)} %subtract_convert_fusion.delta_ref), channel_id=1, source_target_pairs={{0,8},{4,12},{8,0},{12,4},{1,9},{5,13},{9,1},{13,5},{2,10},{6,14},... | collective-permute-start | bytes 786440 | tf_op jit(solution)/shard_map/ppermute | solution.py:345
  54.9 13.7 %collective-permute-start.12 = (bf16[128,1024]{1,0:T(8,128)(2,1)S(1)}, bf16[128,1024]{1,0:T(8,128)(2,1)S(1)}, u32[]{:S(2)}, u32[]{:S(2)}) collective-permute-start(bf16[128,1024]{1,0:T(8,128)(2,1)S(1)} %subtract_convert_fusion.delta_ref), channel_id=1, source_target_pairs={{0,4},{4,0},{8,12},{12,8},{1,5},{5,1},{9,13},{13,9},{2,6},{6,2},{1... | collective-permute-start | bytes 786440 | tf_op jit(solution)/shard_map/ppermute | solution.py:345
  67.8 6.9 %collective-permute-start.14 = (bf16[128,1024]{1,0:T(8,128)(2,1)S(1)}, bf16[128,1024]{1,0:T(8,128)(2,1)S(1)}, u32[]{:S(2)}, u32[]{:S(2)}) collective-permute-start(bf16[128,1024]{1,0:T(8,128)(2,1)S(1)} %collective-permute-done.13.delta_ref), channel_id=1, source_target_pairs={{0,4},{4,0},{8,12},{12,8},{1,5},{5,1},{9,13},{13,9},{2,6},{6,2},{1... | collective-permute-start | bytes 786440 | tf_op jit(solution)/shard_map/ppermute | solution.py:345
  75.5 1.9 %collective-permute-start.15 = (bf16[2,128,896]{2,1,0:T(8,128)(2,1)S(1)}, bf16[2,128,896]{2,1,0:T(8,128)(2,1)S(1)}, u32[]{:S(2)}, u32[]{:S(2)}) collective-permute-start(bf16[2,128,896]{2,1,0:T(8,128)(2,1)S(1)} %get-tuple-element.72), channel_id=1, source_target_pairs={{0,1},{1,0},{2,3},{3,2},{4,5},{5,4},{6,7},{7,6},{8,9},{9,8},{10,11... | collective-permute-start | bytes 1376264 | tf_op jit(solution)/shard_map/ppermute | solution.py:345
  77.5 7.7 %collective-permute-start.16 = (bf16[128,896]{1,0:T(8,128)(2,1)S(1)}, bf16[128,896]{1,0:T(8,128)(2,1)S(1)}, u32[]{:S(2)}, u32[]{:S(2)}) collective-permute-start(bf16[128,896]{1,0:T(8,128)(2,1)S(1)} %fusion), channel_id=1, source_target_pairs={{0,2},{2,0},{1,3},{3,1},{4,6},{6,4},{5,7},{7,5},{8,10},{10,8},{9,1... | collective-permute-start | bytes 688136 | tf_op jit(solution)/shard_map/ppermute | solution.py:345
  85.6 5.9 %collective-permute-start.17 = (bf16[48,896]{1,0:T(8,128)(2,1)S(1)}, bf16[48,896]{1,0:T(8,128)(2,1)S(1)}, u32[]{:S(2)}, u32[]{:S(2)}) collective-permute-start(bf16[48,896]{1,0:T(8,128)(2,1)S(1)} %get-tuple-element.77), channel_id=1, source_target_pairs={{0,4},{4,0},{8,12},{12,8},{1,5},{5,1},{9,13},{13,9},{2,6},{6,2},{1... | collective-permute-start | bytes 258056 | tf_op jit(solution)/shard_map/ppermute | solution.py:345
  85.9 9.2 %collective-permute-start.18 = (bf16[48,896]{1,0:T(8,128)(2,1)S(1)}, bf16[48,896]{1,0:T(8,128)(2,1)S(1)}, u32[]{:S(2)}, u32[]{:S(2)}) collective-permute-start(bf16[48,896]{1,0:T(8,128)(2,1)S(1)} %get-tuple-element.78), channel_id=1, source_target_pairs={{0,8},{4,12},{8,0},{12,4},{1,9},{5,13},{9,1},{13,5},{2,10},{6,14},... | collective-permute-start | bytes 258056 | tf_op jit(solution)/shard_map/ppermute | solution.py:345
  88.6 8.0 %collective-permute-start.19 = (bf16[48,896]{1,0:T(8,128)(2,1)S(1)}, bf16[48,896]{1,0:T(8,128)(2,1)S(1)}, u32[]{:S(2)}, u32[]{:S(2)}) collective-permute-start(bf16[48,896]{1,0:T(8,128)(2,1)S(1)} %get-tuple-element.79), channel_id=1, source_target_pairs={{0,12},{4,8},{8,4},{12,0},{1,13},{5,9},{9,5},{13,1},{2,14},{6,10},... | collective-permute-start | bytes 258056 | tf_op jit(solution)/shard_map/ppermute | solution.py:345
  90.0 7.2 %collective-permute-start.20 = (bf16[48,896]{1,0:T(8,128)(2,1)S(1)}, bf16[48,896]{1,0:T(8,128)(2,1)S(1)}, u32[]{:S(2)}, u32[]{:S(2)}) collective-permute-start(bf16[48,896]{1,0:T(8,128)(2,1)S(1)} %get-tuple-element.76.refs_0_), channel_id=1, source_target_pairs={{0,2},{2,0},{1,3},{3,1},{4,6},{6,4},{5,7},{7,5},{8,10},{10,8},{9,1... | collective-permute-start | bytes 258056 | tf_op jit(solution)/shard_map/ppermute | solution.py:345
  91.5 5.7 %collective-permute-start.21 = (bf16[48,896]{1,0:T(8,128)(2,1)S(1)}, bf16[48,896]{1,0:T(8,128)(2,1)S(1)}, u32[]{:S(2)}, u32[]{:S(2)}) collective-permute-start(bf16[48,896]{1,0:T(8,128)(2,1)S(1)} %collective-permute-done.17.refs_1_), channel_id=1, source_target_pairs={{0,2},{2,0},{1,3},{3,1},{4,6},{6,4},{5,7},{7,5},{8,10},{10,8},{9,1... | collective-permute-start | bytes 258056 | tf_op jit(solution)/shard_map/ppermute | solution.py:345
  95.1 4.5 %collective-permute-start.22 = (bf16[48,896]{1,0:T(8,128)(2,1)S(1)}, bf16[48,896]{1,0:T(8,128)(2,1)S(1)}, u32[]{:S(2)}, u32[]{:S(2)}) collective-permute-start(bf16[48,896]{1,0:T(8,128)(2,1)S(1)} %collective-permute-done.18.refs_2_), channel_id=1, source_target_pairs={{0,2},{2,0},{1,3},{3,1},{4,6},{6,4},{5,7},{7,5},{8,10},{10,8},{9,1... | collective-permute-start | bytes 258056 | tf_op jit(solution)/shard_map/ppermute | solution.py:345
  96.6 4.5 %collective-permute-start.23 = (bf16[48,896]{1,0:T(8,128)(2,1)S(1)}, bf16[48,896]{1,0:T(8,128)(2,1)S(1)}, u32[]{:S(2)}, u32[]{:S(2)}) collective-permute-start(bf16[48,896]{1,0:T(8,128)(2,1)S(1)} %collective-permute-done.19.refs_3_), channel_id=1, source_target_pairs={{0,2},{2,0},{1,3},{3,1},{4,6},{6,4},{5,7},{7,5},{8,10},{10,8},{9,1... | collective-permute-start | bytes 258056 | tf_op jit(solution)/shard_map/ppermute | solution.py:345
  101.8 2.2 %collective-permute-start.24 = (bf16[2,48,3584]{2,1,0:T(8,128)(2,1)S(1)}, bf16[2,48,3584]{2,1,0:T(8,128)(2,1)S(1)}, u32[]{:S(2)}, u32[]{:S(2)}) collective-permute-start(bf16[2,48,3584]{2,1,0:T(8,128)(2,1)S(1)} %shard_map.107.pair_ref), channel_id=1, source_target_pairs={{0,1},{1,0},{2,3},{3,2},{4,5},{5,4},{6,7},{7,6},{8,9},{9,8},{10,11... | collective-permute-start | bytes 2064392 | tf_op jit(solution)/shard_map/ppermute | solution.py:345

commit v11 on v8

--- a/solution.py
+++ b/solution.py
@@ -284,50 +284,44 @@
     return call(kernel, [out] * len(peers), (drop, kept, got, crossed), 0, 0)
 
 
-def rows_kernel(hidden_ref, small_ref, *refs):
+def rows_kernel(which, hidden_ref, small_ref, *refs):
     *pieces, out_ref = refs
     me, _ = indices()
-    blocks, rows, width = hidden_ref.shape
-    n = len(pieces) // blocks
-    tiles = width // n // LANES
-    for i in range(blocks):
-        inverse = inverse_rms(hidden_ref[i].astype(F32))
-        spots = [
-            (piece, tile, (me ^ k) * tiles + tile)
-            for k, piece in enumerate(pieces[i * n : (i + 1) * n])
-            for tile in range(tiles)
-        ]
-        total = jnp.zeros((rows, LANES), F32)
-        for piece, tile, at in spots:
-            columns = pl.ds(pl.multiple_of(at * LANES, LANES), LANES)
-            block = hidden_ref[i, :, columns].astype(F32)
-            grad = piece[:, tile * LANES : (tile + 1) * LANES].astype(F32)
-            total = total + grad * small_ref[pl.ds(at, 1), :] * block
-        mean = jnp.sum(total, axis=1, keepdims=True) / width
-        lean = inverse * inverse * inverse * mean
-        for piece, tile, at in spots:
-            columns = pl.ds(pl.multiple_of(at * LANES, LANES), LANES)
-            block = hidden_ref[i, :, columns].astype(F32)
-            grad = piece[:, tile * LANES : (tile + 1) * LANES].astype(F32)
-            grad = inverse * (grad * small_ref[pl.ds(at, 1), :]) - lean * block
-            out_ref[i, :, columns] = grad.astype(BF)
-
-
-def grad_rows(hidden, small, pieces):
-    return call(
-        rows_kernel,
-        jax.ShapeDtypeStruct(hidden.shape, BF),
-        (hidden, small, *pieces),
-        14 * hidden.size,
-        6 * hidden.size,
-    )
-
-
-def write_kernel(first, pair_ref, out_ref, done):
+    _, rows, width = hidden_ref.shape
+    tiles = width // len(pieces) // LANES
+    inverse = inverse_rms(hidden_ref[which].astype(F32))
+    spots = [
+        (piece, tile, (me ^ k) * tiles + tile)
+        for k, piece in enumerate(pieces)
+        for tile in range(tiles)
+    ]
+    total = jnp.zeros((rows, LANES), F32)
+    for piece, tile, at in spots:
+        columns = pl.ds(pl.multiple_of(at * LANES, LANES), LANES)
+        block = hidden_ref[which, :, columns].astype(F32)
+        grad = piece[:, tile * LANES : (tile + 1) * LANES].astype(F32)
+        total = total + grad * small_ref[pl.ds(at, 1), :] * block
+    mean = jnp.sum(total, axis=1, keepdims=True) / width
+    lean = inverse * inverse * inverse * mean
+    for piece, tile, at in spots:
+        columns = pl.ds(pl.multiple_of(at * LANES, LANES), LANES)
+        block = hidden_ref[which, :, columns].astype(F32)
+        grad = piece[:, tile * LANES : (tile + 1) * LANES].astype(F32)
+        grad = inverse * (grad * small_ref[pl.ds(at, 1), :]) - lean * block
+        out_ref[:, columns] = grad.astype(BF)
+
+
+def grad_rows(which, hidden, small, pieces):
+    out = jax.ShapeDtypeStruct(hidden.shape[1:], BF)
+    return call(functools.partial(rows_kernel, which), out, (hidden, small, *pieces), 0, 0)
+
+
+def write_kernel(places, *refs):
+    *blocks, out_ref, done = refs
     _, mine = indices()
     copies = [
-        pltpu.make_async_copy(pair_ref.at[i], out_ref.at[mine ^ first ^ (2 * i)], done.at[i])
-        for i in range(2)
+        pltpu.make_async_copy(block, out_ref.at[mine ^ place], done.at[i])
+        for i, (block, place) in enumerate(zip(blocks, places))
     ]
     for copy in copies:
         copy.start()
@@ -335,24 +329,24 @@
         copy.wait()
 
 
-def write_rows(pair, first, target=None):
-    _, rows, width = pair.shape
+def write_rows(blocks, places, target=None):
+    rows, width = blocks[0].shape
     hbm, vmem = pl.BlockSpec(memory_space=pltpu.HBM), pl.BlockSpec(memory_space=pltpu.VMEM)
-    kernel = functools.partial(write_kernel, first)
-    args, specs, aliases = (pair,), [vmem], {}
+    kernel = functools.partial(write_kernel, places)
+    args, specs, aliases = tuple(blocks), [vmem] * len(blocks), {}
     if target is not None:
-        kernel = lambda t, *refs: write_kernel(first, *refs)
-        args, specs, aliases = (target, pair), [hbm, vmem], {0: 0}
+        kernel = lambda t, *refs: write_kernel(places, *refs)
+        args, specs, aliases = (target, *args), [hbm] + specs, {0: 0}
     return call(
         kernel,
         jax.ShapeDtypeStruct((4, rows, width), BF),
         args,
         0,
-        4 * pair.size,
+        4 * len(blocks) * rows * width,
         in_specs=specs,
         out_specs=hbm,
         input_output_aliases=aliases,
-        scratch_shapes=[pltpu.SemaphoreType.DMA((2,))],
+        scratch_shapes=[pltpu.SemaphoreType.DMA((len(blocks),))],
     )
 
 
@@ -443,9 +437,13 @@
 
     arrived = [leaving[0]] + exchange(leaving)
     across = [swap(block, "mp") for block in arrived]
-    grad_pair = grad_rows(hidden, small, arrived + across)
-    grad_mates = swap(grad_pair, "side")
-    grad_hidden = write_rows(grad_mates, 1, write_rows(grad_pair, 0)).reshape(capacity, width)
+    own_ready = [after(block, leaving[0]) for block in arrived]
+    grad_own = grad_rows(0, hidden, small, own_ready)
+    grad_mate = swap(grad_own, "side")
+    grad_far = grad_rows(1, hidden, small, across)
+    grad_last = swap(grad_far, "side")
+    grad_hidden = write_rows([grad_own, grad_mate, grad_far], (0, 1, 2))
+    grad_hidden = write_rows([grad_last], (3,), grad_hidden).reshape(capacity, width)
     return (grad_hidden, grad_proj)
 
 

time: 102 us -> 101 us (level)
  waiting for transfers between devices: 44.4 us -> 43.3 us
    ppermute x22 -> x23, waiting for transfers between devices: 35.1 us -> 34 us  [swap(): lax.ppermute(x, axis, [(i, i ^ k) for i in range(lax.axis_size(axis))])]
    ppermute x22 -> x23, starting transfers between devices: 30.8 us -> 30.9 us  [swap(): lax.ppermute(x, axis, [(i, i ^ k) for i in range(lax.axis_size(axis))])]
    pallas_call x14 -> x15, Pallas kernels: 11.4 us -> 11.4 us  [call(): pl.pallas_call(kernel, out_shape=shapes, cost_estimate=pl.CostEstimate(fl...]
  transfers between devices with their start and end apart: 25 -> 26, of which waited for: 16 -> 16; matrix products, arithmetic and copies ran while one was open for 4% -> 4% of each run, Pallas kernels for 7% -> 7%
where the time goes in v11:
time: 101 us
  waiting for transfers between devices  43.3 us (43%)
  starting transfers between devices  40 us (40%)
  Pallas kernels  11.4 us (11%)
  matrix products  2.98 us (3%)
  other arithmetic  1.29 us (1%)
    ppermute x23, waiting for transfers between devices, swap(): lax.ppermute(x, axis, [(i, i ^ k) for i in range(lax.axis_size(axis))])  34 us
    ppermute x23, starting transfers between devices, swap(): lax.ppermute(x, axis, [(i, i ^ k) for i in range(lax.axis_size(axis))])  30.9 us
    pallas_call x15, Pallas kernels, call(): pl.pallas_call(kernel, out_shape=shapes, cost_estimate=pl.CostEstimate(fl...  11.4 us
    ppermute x3, waiting for transfers between devices, onward(): lax.ppermute(x, 'seq', [(i, i + 1) for i in range(lax.axis_size('seq') -...  9.25 us
    ppermute x3, starting transfers between devices, onward(): lax.ppermute(x, 'seq', [(i, i + 1) for i in range(lax.axis_size('seq') -...  9.11 us
    dot_general x1, matrix products, dot(): return lax.dot_general(a, b, (dims, ((), ())), preferred_element_type=F32)  2.98 us
  transfers between devices with their start and end apart: 26, of which 16 were waited for; matrix products, arithmetic and copies ran while one was open for 4% of the time, Pallas kernels for 7%

profile of v11, /device:TPU:0, one launch (start us, length us, event | category | flops | bytes accessed | tf_op | source)
XLA Modules:
  0.0 100.6 jit_solution(5356255067452755244)
XLA Ops:
  0.7 0.9 convert_select_fusion.small_ref
  1.6 1.2 %shard_map.95 = (bf16[48,1024]{1,0:T(8,128)(2,1)S(1)}, bf16[48,1024]{1,0:T(8,128)(2,1)S(1)}, bf16[48,1024]{1,0:T(8,128)(2,1)S(1)}, bf16[48,1024]{1,0:T(8,128)(2,1)S(1)}, bf16[2,48,3584]{2,1,0:T(8,128)(2,1)S(1)}) custom-call(bf16[4,48,3584]{2,1,0:T(8,128)(2,1)} %bitcast.9, f32[30,128]{1,0:T(8,128)S(1)} %convert_select_fusion.small_ref), custom_call_target="tpu_custom_call" | custom-call | flops 1032192 | bytes 1376256 | tf_op jit(solution)/shard_map/pallas_call | solution.py:49
  2.8 5.1 %collective-permute-start = (bf16[48,1024]{1,0:T(8,128)(2,1)S(1)}, bf16[48,1024]{1,0:T(8,128)(2,1)S(1)}, u32[]{:S(2)}, u32[]{:S(2)}) collective-permute-start(bf16[48,1024]{1,0:T(8,128)(2,1)S(1)} %get-tuple-element.41), channel_id=1, source_target_pairs={{0,12},{4,8},{8,4},{12,0},{1,13},{5,9},{9,5},{13,1},{2,14},{6,10},... | collective-permute-start | bytes 294920 | tf_op jit(solution)/shard_map/ppermute | solution.py:354
  7.9 0.6 collective-permute-start.3
  8.6 0.8 constant_dynamic-slice_fusion
  9.4 3.3 %collective-permute-start.1 = (bf16[256,128]{1,0:T(8,128)(2,1)S(1)}, bf16[256,128]{1,0:T(8,128)(2,1)S(1)}, u32[]{:S(2)}, u32[]{:S(2)}) collective-permute-start(bf16[256,128]{1,0:T(8,128)(2,1)S(1)} %pad_maximum_fusion.1.refs_0_), channel_id=1, source_target_pairs={{0,4},{4,8},{8,12},{1,5},{5,9},{9,13},{2,6},{6,10},{10,14},{3,7},{... | collective-permute-start | bytes 196616 | tf_op jit(solution)/shard_map/ppermute | solution.py:358
  12.7 3.0 %collective-permute-done.1.refs_1_ = bf16[256,128]{1,0:T(8,128)(2,1)S(1)} collective-permute-done((bf16[256,128]{1,0:T(8,128)(2,1)S(1)}, bf16[256,128]{1,0:T(8,128)(2,1)S(1)}, u32[]{:S(2)}, u32[]{:S(2)}) %collective-permute-start.1) | collective-permute-done | bytes 65568 | tf_op jit(solution)/shard_map/ppermute | solution.py:358
  15.7 0.0 collective-permute-done.refs_0_.refs_7_
  15.7 0.5 collective-permute-done.2.refs_1_.refs_6_
  16.2 0.4 shard_map.96
  16.6 0.1 collective-permute-start.5
  16.7 1.6 %collective-permute-start.4 = (bf16[128,896]{1,0:T(8,128)(2,1)S(1)}, bf16[128,896]{1,0:T(8,128)(2,1)S(1)}, u32[]{:S(2)}, u32[]{:S(2)}) collective-permute-start(bf16[128,896]{1,0:T(8,128)(2,1)S(1)} %get-tuple-element.57.refs_3_), channel_id=1, source_target_pairs={{0,2},{2,0},{1,3},{3,1},{4,6},{6,4},{5,7},{7,5},{8,10},{10,8},{9,1... | collective-permute-start | bytes 688136 | tf_op jit(solution)/shard_map/ppermute | solution.py:354
  18.2 3.8 %collective-permute-start.6 = (bf16[256,128]{1,0:T(8,128)(2,1)S(1)}, bf16[256,128]{1,0:T(8,128)(2,1)S(1)}, u32[]{:S(2)}, u32[]{:S(2)}) collective-permute-start(bf16[256,128]{1,0:T(8,128)(2,1)S(1)} %collective-permute-done.1.refs_1_), channel_id=1, source_target_pairs={{0,4},{4,8},{8,12},{1,5},{5,9},{9,13},{2,6},{6,10},{10,14},{3,7},{... | collective-permute-start | bytes 196616 | tf_op jit(solution)/shard_map/ppermute | solution.py:358
  22.1 1.9 %collective-permute-done.6.refs_2_ = bf16[256,128]{1,0:T(8,128)(2,1)S(1)} collective-permute-done((bf16[256,128]{1,0:T(8,128)(2,1)S(1)}, bf16[256,128]{1,0:T(8,128)(2,1)S(1)}, u32[]{:S(2)}, u32[]{:S(2)}) %collective-permute-start.6) | collective-permute-done | bytes 65568 | tf_op jit(solution)/shard_map/ppermute | solution.py:358
  24.0 0.7 collective-permute-done.4.refs_1_
  24.7 1.5 %collective-permute-done.7.refs_0_ = bf16[128,896]{1,0:T(8,128)(2,1)S(1)} collective-permute-done((bf16[128,896]{1,0:T(8,128)(2,1)S(1)}, bf16[128,896]{1,0:T(8,128)(2,1)S(1)}, u32[]{:S(2)}, u32[]{:S(2)}) %collective-permute-start.7) | collective-permute-done | bytes 229408 | tf_op jit(solution)/shard_map/ppermute | solution.py:354
  26.2 0.5 shard_map.97
  26.6 2.0 %collective-permute-start.8 = (bf16[128,1024]{1,0:T(8,128)(2,1)S(1)}, bf16[128,1024]{1,0:T(8,128)(2,1)S(1)}, u32[]{:S(2)}, u32[]{:S(2)}) collective-permute-start(bf16[128,1024]{1,0:T(8,128)(2,1)S(1)} %shard_map.97), channel_id=1, source_target_pairs={{0,4},{4,0},{8,12},{12,8},{1,5},{5,1},{9,13},{13,9},{2,6},{6,2},{1... | collective-permute-start | bytes 786440 | tf_op jit(solution)/shard_map/ppermute | solution.py:354
  28.7 2.0 %collective-permute-start.9 = (bf16[256,128]{1,0:T(8,128)(2,1)S(1)}, bf16[256,128]{1,0:T(8,128)(2,1)S(1)}, u32[]{:S(2)}, u32[]{:S(2)}) collective-permute-start(bf16[256,128]{1,0:T(8,128)(2,1)S(1)} %collective-permute-done.6.refs_2_), channel_id=1, source_target_pairs={{0,4},{4,8},{8,12},{1,5},{5,9},{9,13},{2,6},{6,10},{10,14},{3,7},{... | collective-permute-start | bytes 196616 | tf_op jit(solution)/shard_map/ppermute | solution.py:358
  30.6 0.9 shard_map.98
  31.5 0.0 copy-start.1
  31.6 4.4 %collective-permute-done.9.refs_3_ = bf16[256,128]{1,0:T(8,128)(2,1)S(1)} collective-permute-done((bf16[256,128]{1,0:T(8,128)(2,1)S(1)}, bf16[256,128]{1,0:T(8,128)(2,1)S(1)}, u32[]{:S(2)}, u32[]{:S(2)}) %collective-permute-start.9) | collective-permute-done | bytes 65568 | tf_op jit(solution)/shard_map/ppermute | solution.py:358
  35.9 0.1 add_convert_fusion
  36.0 2.4 %collective-permute-start.10 = (bf16[128,1024]{1,0:T(8,128)(2,1)S(1)}, bf16[128,1024]{1,0:T(8,128)(2,1)S(1)}, u32[]{:S(2)}, u32[]{:S(2)}) collective-permute-start(bf16[128,1024]{1,0:T(8,128)(2,1)S(1)} %add_convert_fusion), channel_id=1, source_target_pairs={{0,8},{4,12},{8,0},{12,4},{1,9},{5,13},{9,1},{13,5},{2,10},{6,14},... | collective-permute-start | bytes 786440 | tf_op jit(solution)/shard_map/ppermute | solution.py:354
  38.4 0.4 shard_map.99
  38.8 2.5 %collective-permute-start.11 = (bf16[128,1024]{1,0:T(8,128)(2,1)S(1)}, bf16[128,1024]{1,0:T(8,128)(2,1)S(1)}, u32[]{:S(2)}, u32[]{:S(2)}) collective-permute-start(bf16[128,1024]{1,0:T(8,128)(2,1)S(1)} %shard_map.99), channel_id=1, source_target_pairs={{0,4},{4,0},{8,12},{12,8},{1,5},{5,1},{9,13},{13,9},{2,6},{6,2},{1... | collective-permute-start | bytes 786440 | tf_op jit(solution)/shard_map/ppermute | solution.py:354
  41.4 2.4 %shard_map.100 = bf16[128,1024]{1,0:T(8,128)(2,1)S(1)} custom-call(bf16[128,1024]{1,0:T(8,128)(2,1)S(1)} %copy-done.1, bf16[256,128]{1,0:T(8,128)(2,1)S(1)} %pad_maximum_fusion.1.refs_0_, bf16[256,128]{1,0:T(8,128)(2,1)S(1)} %collective-permute-done.1.refs_1_, bf16[256,128]{1,0:T(8,128)(2,1)S(1)} %collective-permute-done.6.refs_2_, ...), custom_call_target="tpu_custom_call" | custom-call | bytes 524288 | tf_op jit(solution)/shard_map/pallas_call | solution.py:49
  43.7 6.5 %collective-permute-done.10 = bf16[128,1024]{1,0:T(8,128)(2,1)S(1)} collective-permute-done((bf16[128,1024]{1,0:T(8,128)(2,1)S(1)}, bf16[128,1024]{1,0:T(8,128)(2,1)S(1)}, u32[]{:S(2)}, u32[]{:S(2)}) %collective-permute-start.10) | collective-permute-done | bytes 262176 | tf_op jit(solution)/shard_map/ppermute | solution.py:354
  50.2 0.1 convert_add_fusion
  50.3 0.2 collective-permute-done.11
  50.5 0.1 subtract_convert_fusion.delta_ref
  50.6 2.2 %collective-permute-start.13 = (bf16[128,1024]{1,0:T(8,128)(2,1)S(1)}, bf16[128,1024]{1,0:T(8,128)(2,1)S(1)}, u32[]{:S(2)}, u32[]{:S(2)}) collective-permute-start(bf16[128,1024]{1,0:T(8,128)(2,1)S(1)} %subtract_convert_fusion.delta_ref), channel_id=1, source_target_pairs={{0,8},{4,12},{8,0},{12,4},{1,9},{5,13},{9,1},{13,5},{2,10},{6,14},... | collective-permute-start | bytes 786440 | tf_op jit(solution)/shard_map/ppermute | solution.py:354
  52.8 0.7 shard_map.101.first_ref
  53.5 2.3 %collective-permute-start.12 = (bf16[128,1024]{1,0:T(8,128)(2,1)S(1)}, bf16[128,1024]{1,0:T(8,128)(2,1)S(1)}, u32[]{:S(2)}, u32[]{:S(2)}) collective-permute-start(bf16[128,1024]{1,0:T(8,128)(2,1)S(1)} %subtract_convert_fusion.delta_ref), channel_id=1, source_target_pairs={{0,4},{4,0},{8,12},{12,8},{1,5},{5,1},{9,13},{13,9},{2,6},{6,2},{1... | collective-permute-start | bytes 786440 | tf_op jit(solution)/shard_map/ppermute | solution.py:354
  55.8 7.8 %collective-permute-done.13.delta_ref = bf16[128,1024]{1,0:T(8,128)(2,1)S(1)} collective-permute-done((bf16[128,1024]{1,0:T(8,128)(2,1)S(1)}, bf16[128,1024]{1,0:T(8,128)(2,1)S(1)}, u32[]{:S(2)}, u32[]{:S(2)}) %collective-permute-start.13) | collective-permute-done | bytes 262176 | tf_op jit(solution)/shard_map/ppermute | solution.py:354
  63.5 0.5 collective-permute-start.14
  64.1 0.7 shard_map.103.third_ref
  64.8 0.7 shard_map.102.second_ref
  65.5 5.1 %collective-permute-done.14.delta_ref = bf16[128,1024]{1,0:T(8,128)(2,1)S(1)} collective-permute-done((bf16[128,1024]{1,0:T(8,128)(2,1)S(1)}, bf16[128,1024]{1,0:T(8,128)(2,1)S(1)}, u32[]{:S(2)}, u32[]{:S(2)}) %collective-permute-start.14) | collective-permute-done | bytes 262176 | tf_op jit(solution)/shard_map/ppermute | solution.py:354
  70.6 0.8 shard_map.104
  71.3 0.1 collective-permute-start.15
  71.4 0.1 pad_maximum_fusion
  71.5 1.7 %collective-permute-done.15.got_ref = bf16[2,128,896]{2,1,0:T(8,128)(2,1)S(1)} collective-permute-done((bf16[2,128,896]{2,1,0:T(8,128)(2,1)S(1)}, bf16[2,128,896]{2,1,0:T(8,128)(2,1)S(1)}, u32[]{:S(2)}, u32[]{:S(2)}) %collective-permute-start.15) | collective-permute-done | bytes 458784 | tf_op jit(solution)/shard_map/ppermute | solution.py:354
  73.2 0.1 fusion
  73.3 1.5 %collective-permute-start.16 = (bf16[128,896]{1,0:T(8,128)(2,1)S(1)}, bf16[128,896]{1,0:T(8,128)(2,1)S(1)}, u32[]{:S(2)}, u32[]{:S(2)}) collective-permute-start(bf16[128,896]{1,0:T(8,128)(2,1)S(1)} %fusion), channel_id=1, source_target_pairs={{0,2},{2,0},{1,3},{3,1},{4,6},{6,4},{5,7},{7,5},{8,10},{10,8},{9,1... | collective-permute-start | bytes 688136 | tf_op jit(solution)/shard_map/ppermute | solution.py:354
  74.8 3.0 %convolution_multiply_fusion = f32[896,1024]{1,0:T(8,128)} fusion(bf16[512,896]{1,0:T(8,128)(2,1)S(1)} %get-tuple-element.63.normed_ref, bf16[512,1024]{1,0:T(8,128)(2,1)S(1)} %pad_maximum_fusion), kind=kOutput, calls=%fused_computation | convolution fusion | flops 940441600 | bytes 5636096 | tf_op jit(solution)/shard_map/dot_general | solution.py:22
  77.8 3.2 %collective-permute-done.16.crossed_ref = bf16[128,896]{1,0:T(8,128)(2,1)S(1)} collective-permute-done((bf16[128,896]{1,0:T(8,128)(2,1)S(1)}, bf16[128,896]{1,0:T(8,128)(2,1)S(1)}, u32[]{:S(2)}, u32[]{:S(2)}) %collective-permute-start.16) | collective-permute-done | bytes 229408 | tf_op jit(solution)/shard_map/ppermute | solution.py:354
  81.0 0.3 shard_map.105
  81.4 1.8 %collective-permute-start.17 = (bf16[48,896]{1,0:T(8,128)(2,1)S(1)}, bf16[48,896]{1,0:T(8,128)(2,1)S(1)}, u32[]{:S(2)}, u32[]{:S(2)}) collective-permute-start(bf16[48,896]{1,0:T(8,128)(2,1)S(1)} %get-tuple-element.72), channel_id=1, source_target_pairs={{0,4},{4,0},{8,12},{12,8},{1,5},{5,1},{9,13},{13,9},{2,6},{6,2},{1... | collective-permute-start | bytes 258056 | tf_op jit(solution)/shard_map/ppermute | solution.py:354
  83.2 3.4 %collective-permute-start.18 = (bf16[48,896]{1,0:T(8,128)(2,1)S(1)}, bf16[48,896]{1,0:T(8,128)(2,1)S(1)}, u32[]{:S(2)}, u32[]{:S(2)}) collective-permute-start(bf16[48,896]{1,0:T(8,128)(2,1)S(1)} %get-tuple-element.74), channel_id=1, source_target_pairs={{0,8},{4,12},{8,0},{12,4},{1,9},{5,13},{9,1},{13,5},{2,10},{6,14},... | collective-permute-start | bytes 258056 | tf_op jit(solution)/shard_map/ppermute | solution.py:354
  86.5 1.5 %collective-permute-start.21 = (bf16[48,896]{1,0:T(8,128)(2,1)S(1)}, bf16[48,896]{1,0:T(8,128)(2,1)S(1)}, u32[]{:S(2)}, u32[]{:S(2)}) collective-permute-start(bf16[48,896]{1,0:T(8,128)(2,1)S(1)} %get-tuple-element.71.refs_0_), channel_id=1, source_target_pairs={{0,2},{2,0},{1,3},{3,1},{4,6},{6,4},{5,7},{7,5},{8,10},{10,8},{9,1... | collective-permute-start | bytes 258056 | tf_op jit(solution)/shard_map/ppermute | solution.py:354
  88.0 0.5 collective-permute-start.22
  88.6 3.3 %collective-permute-done.18.refs_2_ = bf16[48,896]{1,0:T(8,128)(2,1)S(1)} collective-permute-done((bf16[48,896]{1,0:T(8,128)(2,1)S(1)}, bf16[48,896]{1,0:T(8,128)(2,1)S(1)}, u32[]{:S(2)}, u32[]{:S(2)}) %collective-permute-start.18) | collective-permute-done | bytes 86048 | tf_op jit(solution)/shard_map/ppermute | solution.py:354
  91.8 1.5 %collective-permute-start.23 = (bf16[48,896]{1,0:T(8,128)(2,1)S(1)}, bf16[48,896]{1,0:T(8,128)(2,1)S(1)}, u32[]{:S(2)}, u32[]{:S(2)}) collective-permute-start(bf16[48,896]{1,0:T(8,128)(2,1)S(1)} %collective-permute-done.18.refs_2_), channel_id=1, source_target_pairs={{0,2},{2,0},{1,3},{3,1},{4,6},{6,4},{5,7},{7,5},{8,10},{10,8},{9,1... | collective-permute-start | bytes 258056 | tf_op jit(solution)/shard_map/ppermute | solution.py:354
  93.3 1.1 %collective-permute-start.24 = (bf16[48,896]{1,0:T(8,128)(2,1)S(1)}, bf16[48,896]{1,0:T(8,128)(2,1)S(1)}, u32[]{:S(2)}, u32[]{:S(2)}) collective-permute-start(bf16[48,896]{1,0:T(8,128)(2,1)S(1)} %collective-permute-done.19.refs_3_), channel_id=1, source_target_pairs={{0,2},{2,0},{1,3},{3,1},{4,6},{6,4},{5,7},{7,5},{8,10},{10,8},{9,1... | collective-permute-start | bytes 258056 | tf_op jit(solution)/shard_map/ppermute | solution.py:354
  94.4 0.4 shard_map.106.refs_0_
  94.8 0.1 collective-permute-start.20
  94.9 1.4 %collective-permute-done.23.refs_2_ = bf16[48,896]{1,0:T(8,128)(2,1)S(1)} collective-permute-done((bf16[48,896]{1,0:T(8,128)(2,1)S(1)}, bf16[48,896]{1,0:T(8,128)(2,1)S(1)}, u32[]{:S(2)}, u32[]{:S(2)}) %collective-permute-start.23) | collective-permute-done | bytes 86048 | tf_op jit(solution)/shard_map/ppermute | solution.py:354
  96.3 1.5 %collective-permute-done.24.refs_3_ = bf16[48,896]{1,0:T(8,128)(2,1)S(1)} collective-permute-done((bf16[48,896]{1,0:T(8,128)(2,1)S(1)}, bf16[48,896]{1,0:T(8,128)(2,1)S(1)}, u32[]{:S(2)}, u32[]{:S(2)}) %collective-permute-start.24) | collective-permute-done | bytes 86048 | tf_op jit(solution)/shard_map/ppermute | solution.py:354
  97.8 0.4 shard_map.107.refs_2_
  98.2 0.1 collective-permute-start.25
  98.3 1.0 shard_map.108.t
  99.3 0.6 collective-permute-done.25.refs_0_
  99.9 0.7 shard_map.109
  (17 shorter events, 0.0 us)
Async XLA Ops:
  0.6 25.6 %copy-start = (bf16[896,1024]{1,0:T(8,128)(2,1)S(1)}, bf16[896,1024]{1,0:T(8,128)(2,1)}, u32[]{:S(2)}) copy-start(bf16[896,1024]{1,0:T(8,128)(2,1)} %proj_ref.9) | copy-start | bytes 5505028
  2.8 12.8 %collective-permute-start = (bf16[48,1024]{1,0:T(8,128)(2,1)S(1)}, bf16[48,1024]{1,0:T(8,128)(2,1)S(1)}, u32[]{:S(2)}, u32[]{:S(2)}) collective-permute-start(bf16[48,1024]{1,0:T(8,128)(2,1)S(1)} %get-tuple-element.41), channel_id=1, source_target_pairs={{0,12},{4,8},{8,4},{12,0},{1,13},{5,9},{9,5},{13,1},{2,14},{6,10},... | collective-permute-start | bytes 294920 | tf_op jit(solution)/shard_map/ppermute | solution.py:354
  7.9 8.3 %collective-permute-start.2 = (bf16[48,1024]{1,0:T(8,128)(2,1)S(1)}, bf16[48,1024]{1,0:T(8,128)(2,1)S(1)}, u32[]{:S(2)}, u32[]{:S(2)}) collective-permute-start(bf16[48,1024]{1,0:T(8,128)(2,1)S(1)} %get-tuple-element.45), channel_id=1, source_target_pairs={{0,8},{4,12},{8,0},{12,4},{1,9},{5,13},{9,1},{13,5},{2,10},{6,14},... | collective-permute-start | bytes 294920 | tf_op jit(solution)/shard_map/ppermute | solution.py:354
  7.9 8.3 %collective-permute-start.3 = (bf16[48,1024]{1,0:T(8,128)(2,1)S(1)}, bf16[48,1024]{1,0:T(8,128)(2,1)S(1)}, u32[]{:S(2)}, u32[]{:S(2)}) collective-permute-start(bf16[48,1024]{1,0:T(8,128)(2,1)S(1)} %get-tuple-element.47), channel_id=1, source_target_pairs={{0,4},{4,0},{8,12},{12,8},{1,5},{5,1},{9,13},{13,9},{2,6},{6,2},{1... | collective-permute-start | bytes 294920 | tf_op jit(solution)/shard_map/ppermute | solution.py:354
  9.4 6.3 %collective-permute-start.1 = (bf16[256,128]{1,0:T(8,128)(2,1)S(1)}, bf16[256,128]{1,0:T(8,128)(2,1)S(1)}, u32[]{:S(2)}, u32[]{:S(2)}) collective-permute-start(bf16[256,128]{1,0:T(8,128)(2,1)S(1)} %pad_maximum_fusion.1.refs_0_), channel_id=1, source_target_pairs={{0,4},{4,8},{8,12},{1,5},{5,9},{9,13},{2,6},{6,10},{10,14},{3,7},{... | collective-permute-start | bytes 196616 | tf_op jit(solution)/shard_map/ppermute | solution.py:358
  16.6 7.4 %collective-permute-start.5 = (bf16[128,896]{1,0:T(8,128)(2,1)S(1)}, bf16[128,896]{1,0:T(8,128)(2,1)S(1)}, u32[]{:S(2)}, u32[]{:S(2)}) collective-permute-start(bf16[128,896]{1,0:T(8,128)(2,1)S(1)} %get-tuple-element.57.refs_3_), channel_id=1, source_target_pairs={{0,1},{1,0},{2,3},{3,2},{4,5},{5,4},{6,7},{7,6},{8,9},{9,8},{10,11... | collective-permute-start | bytes 688136 | tf_op jit(solution)/shard_map/ppermute | solution.py:354
  16.7 8.0 %collective-permute-start.4 = (bf16[128,896]{1,0:T(8,128)(2,1)S(1)}, bf16[128,896]{1,0:T(8,128)(2,1)S(1)}, u32[]{:S(2)}, u32[]{:S(2)}) collective-permute-start(bf16[128,896]{1,0:T(8,128)(2,1)S(1)} %get-tuple-element.57.refs_3_), channel_id=1, source_target_pairs={{0,2},{2,0},{1,3},{3,1},{4,6},{6,4},{5,7},{7,5},{8,10},{10,8},{9,1... | collective-permute-start | bytes 688136 | tf_op jit(solution)/shard_map/ppermute | solution.py:354
  18.2 5.7 %collective-permute-start.6 = (bf16[256,128]{1,0:T(8,128)(2,1)S(1)}, bf16[256,128]{1,0:T(8,128)(2,1)S(1)}, u32[]{:S(2)}, u32[]{:S(2)}) collective-permute-start(bf16[256,128]{1,0:T(8,128)(2,1)S(1)} %collective-permute-done.1.refs_1_), channel_id=1, source_target_pairs={{0,4},{4,8},{8,12},{1,5},{5,9},{9,13},{2,6},{6,10},{10,14},{3,7},{... | collective-permute-start | bytes 196616 | tf_op jit(solution)/shard_map/ppermute | solution.py:358
  24.7 1.5 %collective-permute-start.7 = (bf16[128,896]{1,0:T(8,128)(2,1)S(1)}, bf16[128,896]{1,0:T(8,128)(2,1)S(1)}, u32[]{:S(2)}, u32[]{:S(2)}) collective-permute-start(bf16[128,896]{1,0:T(8,128)(2,1)S(1)} %collective-permute-done.4.refs_1_), channel_id=1, source_target_pairs={{0,1},{1,0},{2,3},{3,2},{4,5},{5,4},{6,7},{7,6},{8,9},{9,8},{10,11... | collective-permute-start | bytes 688136 | tf_op jit(solution)/shard_map/ppermute | solution.py:354
  26.6 9.3 %collective-permute-start.8 = (bf16[128,1024]{1,0:T(8,128)(2,1)S(1)}, bf16[128,1024]{1,0:T(8,128)(2,1)S(1)}, u32[]{:S(2)}, u32[]{:S(2)}) collective-permute-start(bf16[128,1024]{1,0:T(8,128)(2,1)S(1)} %shard_map.97), channel_id=1, source_target_pairs={{0,4},{4,0},{8,12},{12,8},{1,5},{5,1},{9,13},{13,9},{2,6},{6,2},{1... | collective-permute-start | bytes 786440 | tf_op jit(solution)/shard_map/ppermute | solution.py:354
  28.7 7.3 %collective-permute-start.9 = (bf16[256,128]{1,0:T(8,128)(2,1)S(1)}, bf16[256,128]{1,0:T(8,128)(2,1)S(1)}, u32[]{:S(2)}, u32[]{:S(2)}) collective-permute-start(bf16[256,128]{1,0:T(8,128)(2,1)S(1)} %collective-permute-done.6.refs_2_), channel_id=1, source_target_pairs={{0,4},{4,8},{8,12},{1,5},{5,9},{9,13},{2,6},{6,10},{10,14},{3,7},{... | collective-permute-start | bytes 196616 | tf_op jit(solution)/shard_map/ppermute | solution.py:358
  31.5 9.8 %copy-start.1 = (bf16[128,1024]{1,0:T(8,128)(2,1)S(1)}, bf16[128,1024]{1,0:T(8,128)(2,1)}, u32[]{:S(2)}) copy-start(bf16[128,1024]{1,0:T(8,128)(2,1)} %queries_ref) | copy-start | bytes 786436
  36.0 14.2 %collective-permute-start.10 = (bf16[128,1024]{1,0:T(8,128)(2,1)S(1)}, bf16[128,1024]{1,0:T(8,128)(2,1)S(1)}, u32[]{:S(2)}, u32[]{:S(2)}) collective-permute-start(bf16[128,1024]{1,0:T(8,128)(2,1)S(1)} %add_convert_fusion), channel_id=1, source_target_pairs={{0,8},{4,12},{8,0},{12,4},{1,9},{5,13},{9,1},{13,5},{2,10},{6,14},... | collective-permute-start | bytes 786440 | tf_op jit(solution)/shard_map/ppermute | solution.py:354
  38.8 11.6 %collective-permute-start.11 = (bf16[128,1024]{1,0:T(8,128)(2,1)S(1)}, bf16[128,1024]{1,0:T(8,128)(2,1)S(1)}, u32[]{:S(2)}, u32[]{:S(2)}) collective-permute-start(bf16[128,1024]{1,0:T(8,128)(2,1)S(1)} %shard_map.99), channel_id=1, source_target_pairs={{0,4},{4,0},{8,12},{12,8},{1,5},{5,1},{9,13},{13,9},{2,6},{6,2},{1... | collective-permute-start | bytes 786440 | tf_op jit(solution)/shard_map/ppermute | solution.py:354
  50.6 13.0 %collective-permute-start.13 = (bf16[128,1024]{1,0:T(8,128)(2,1)S(1)}, bf16[128,1024]{1,0:T(8,128)(2,1)S(1)}, u32[]{:S(2)}, u32[]{:S(2)}) collective-permute-start(bf16[128,1024]{1,0:T(8,128)(2,1)S(1)} %subtract_convert_fusion.delta_ref), channel_id=1, source_target_pairs={{0,8},{4,12},{8,0},{12,4},{1,9},{5,13},{9,1},{13,5},{2,10},{6,14},... | collective-permute-start | bytes 786440 | tf_op jit(solution)/shard_map/ppermute | solution.py:354
  53.5 11.3 %collective-permute-start.12 = (bf16[128,1024]{1,0:T(8,128)(2,1)S(1)}, bf16[128,1024]{1,0:T(8,128)(2,1)S(1)}, u32[]{:S(2)}, u32[]{:S(2)}) collective-permute-start(bf16[128,1024]{1,0:T(8,128)(2,1)S(1)} %subtract_convert_fusion.delta_ref), channel_id=1, source_target_pairs={{0,4},{4,0},{8,12},{12,8},{1,5},{5,1},{9,13},{13,9},{2,6},{6,2},{1... | collective-permute-start | bytes 786440 | tf_op jit(solution)/shard_map/ppermute | solution.py:354
  63.5 7.0 %collective-permute-start.14 = (bf16[128,1024]{1,0:T(8,128)(2,1)S(1)}, bf16[128,1024]{1,0:T(8,128)(2,1)S(1)}, u32[]{:S(2)}, u32[]{:S(2)}) collective-permute-start(bf16[128,1024]{1,0:T(8,128)(2,1)S(1)} %collective-permute-done.13.delta_ref), channel_id=1, source_target_pairs={{0,4},{4,0},{8,12},{12,8},{1,5},{5,1},{9,13},{13,9},{2,6},{6,2},{1... | collective-permute-start | bytes 786440 | tf_op jit(solution)/shard_map/ppermute | solution.py:354
  71.3 1.9 %collective-permute-start.15 = (bf16[2,128,896]{2,1,0:T(8,128)(2,1)S(1)}, bf16[2,128,896]{2,1,0:T(8,128)(2,1)S(1)}, u32[]{:S(2)}, u32[]{:S(2)}) collective-permute-start(bf16[2,128,896]{2,1,0:T(8,128)(2,1)S(1)} %get-tuple-element.67), channel_id=1, source_target_pairs={{0,1},{1,0},{2,3},{3,2},{4,5},{5,4},{6,7},{7,6},{8,9},{9,8},{10,11... | collective-permute-start | bytes 1376264 | tf_op jit(solution)/shard_map/ppermute | solution.py:354
  73.3 7.7 %collective-permute-start.16 = (bf16[128,896]{1,0:T(8,128)(2,1)S(1)}, bf16[128,896]{1,0:T(8,128)(2,1)S(1)}, u32[]{:S(2)}, u32[]{:S(2)}) collective-permute-start(bf16[128,896]{1,0:T(8,128)(2,1)S(1)} %fusion), channel_id=1, source_target_pairs={{0,2},{2,0},{1,3},{3,1},{4,6},{6,4},{5,7},{7,5},{8,10},{10,8},{9,1... | collective-permute-start | bytes 688136 | tf_op jit(solution)/shard_map/ppermute | solution.py:354
  81.4 6.7 %collective-permute-start.17 = (bf16[48,896]{1,0:T(8,128)(2,1)S(1)}, bf16[48,896]{1,0:T(8,128)(2,1)S(1)}, u32[]{:S(2)}, u32[]{:S(2)}) collective-permute-start(bf16[48,896]{1,0:T(8,128)(2,1)S(1)} %get-tuple-element.72), channel_id=1, source_target_pairs={{0,4},{4,0},{8,12},{12,8},{1,5},{5,1},{9,13},{13,9},{2,6},{6,2},{1... | collective-permute-start | bytes 258056 | tf_op jit(solution)/shard_map/ppermute | solution.py:354
  83.2 8.7 %collective-permute-start.18 = (bf16[48,896]{1,0:T(8,128)(2,1)S(1)}, bf16[48,896]{1,0:T(8,128)(2,1)S(1)}, u32[]{:S(2)}, u32[]{:S(2)}) collective-permute-start(bf16[48,896]{1,0:T(8,128)(2,1)S(1)} %get-tuple-element.74), channel_id=1, source_target_pairs={{0,8},{4,12},{8,0},{12,4},{1,9},{5,13},{9,1},{13,5},{2,10},{6,14},... | collective-permute-start | bytes 258056 | tf_op jit(solution)/shard_map/ppermute | solution.py:354
  86.5 6.8 %collective-permute-start.19 = (bf16[48,896]{1,0:T(8,128)(2,1)S(1)}, bf16[48,896]{1,0:T(8,128)(2,1)S(1)}, u32[]{:S(2)}, u32[]{:S(2)}) collective-permute-start(bf16[48,896]{1,0:T(8,128)(2,1)S(1)} %get-tuple-element.76), channel_id=1, source_target_pairs={{0,12},{4,8},{8,4},{12,0},{1,13},{5,9},{9,5},{13,1},{2,14},{6,10},... | collective-permute-start | bytes 258056 | tf_op jit(solution)/shard_map/ppermute | solution.py:354
  86.5 8.3 %collective-permute-start.21 = (bf16[48,896]{1,0:T(8,128)(2,1)S(1)}, bf16[48,896]{1,0:T(8,128)(2,1)S(1)}, u32[]{:S(2)}, u32[]{:S(2)}) collective-permute-start(bf16[48,896]{1,0:T(8,128)(2,1)S(1)} %get-tuple-element.71.refs_0_), channel_id=1, source_target_pairs={{0,2},{2,0},{1,3},{3,1},{4,6},{6,4},{5,7},{7,5},{8,10},{10,8},{9,1... | collective-permute-start | bytes 258056 | tf_op jit(solution)/shard_map/ppermute | solution.py:354
  88.0 6.8 %collective-permute-start.22 = (bf16[48,896]{1,0:T(8,128)(2,1)S(1)}, bf16[48,896]{1,0:T(8,128)(2,1)S(1)}, u32[]{:S(2)}, u32[]{:S(2)}) collective-permute-start(bf16[48,896]{1,0:T(8,128)(2,1)S(1)} %collective-permute-done.17.refs_1_), channel_id=1, source_target_pairs={{0,2},{2,0},{1,3},{3,1},{4,6},{6,4},{5,7},{7,5},{8,10},{10,8},{9,1... | collective-permute-start | bytes 258056 | tf_op jit(solution)/shard_map/ppermute | solution.py:354
  91.8 4.5 %collective-permute-start.23 = (bf16[48,896]{1,0:T(8,128)(2,1)S(1)}, bf16[48,896]{1,0:T(8,128)(2,1)S(1)}, u32[]{:S(2)}, u32[]{:S(2)}) collective-permute-start(bf16[48,896]{1,0:T(8,128)(2,1)S(1)} %collective-permute-done.18.refs_2_), channel_id=1, source_target_pairs={{0,2},{2,0},{1,3},{3,1},{4,6},{6,4},{5,7},{7,5},{8,10},{10,8},{9,1... | collective-permute-start | bytes 258056 | tf_op jit(solution)/shard_map/ppermute | solution.py:354
  93.3 4.5 %collective-permute-start.24 = (bf16[48,896]{1,0:T(8,128)(2,1)S(1)}, bf16[48,896]{1,0:T(8,128)(2,1)S(1)}, u32[]{:S(2)}, u32[]{:S(2)}) collective-permute-start(bf16[48,896]{1,0:T(8,128)(2,1)S(1)} %collective-permute-done.19.refs_3_), channel_id=1, source_target_pairs={{0,2},{2,0},{1,3},{3,1},{4,6},{6,4},{5,7},{7,5},{8,10},{10,8},{9,1... | collective-permute-start | bytes 258056 | tf_op jit(solution)/shard_map/ppermute | solution.py:354
  94.8 3.5 %collective-permute-start.20 = (bf16[48,3584]{1,0:T(8,128)(2,1)S(1)}, bf16[48,3584]{1,0:T(8,128)(2,1)S(1)}, u32[]{:S(2)}, u32[]{:S(2)}) collective-permute-start(bf16[48,3584]{1,0:T(8,128)(2,1)S(1)} %shard_map.106.refs_0_), channel_id=1, source_target_pairs={{0,1},{1,0},{2,3},{3,2},{4,5},{5,4},{6,7},{7,6},{8,9},{9,8},{10,11... | collective-permute-start | bytes 1032200 | tf_op jit(solution)/shard_map/ppermute | solution.py:354
  98.2 1.7 %collective-permute-start.25 = (bf16[48,3584]{1,0:T(8,128)(2,1)S(1)}, bf16[48,3584]{1,0:T(8,128)(2,1)S(1)}, u32[]{:S(2)}, u32[]{:S(2)}) collective-permute-start(bf16[48,3584]{1,0:T(8,128)(2,1)S(1)} %shard_map.107.refs_2_), channel_id=1, source_target_pairs={{0,1},{1,0},{2,3},{3,2},{4,5},{5,4},{6,7},{7,6},{8,9},{9,8},{10,11... | collective-permute-start | bytes 1032200 | tf_op jit(solution)/shard_map/ppermute | solution.py:354

commit v12 on v11

--- a/solution.py
+++ b/solution.py
@@ -245,24 +245,22 @@
     return call(product_kernel, out, (delta, proj), 0, 0)
 
 
-def route_kernel(first_ref, second_ref, third_ref, delta_ref, proj_ref, sent_ref, kept_ref, held):
+def route_kernel(first_ref, second_ref, third_ref, delta_ref, proj_ref, *refs):
+    *outs, held = refs
     me, mine = indices()
     last = dot(delta_ref[...], proj_ref[...], ((1,), (1,))).astype(BF)
     for k, block in enumerate((first_ref[...], second_ref[...], third_ref[...], last)):
         held[k] = block
-    off = me ^ mine
-    kept_ref[0] = held[off]
-    sent_ref[0] = held[off ^ 1]
-    kept_ref[1] = held[off ^ 2]
-    sent_ref[1] = held[off ^ 3]
+    for k, out in enumerate(outs):
+        out[...] = held[me ^ mine ^ k]
 
 
 def route_products(products, delta, proj):
     tokens, depth = products[0].shape
-    pair = jax.ShapeDtypeStruct((2, tokens, depth), BF)
+    out = jax.ShapeDtypeStruct((tokens, depth), BF)
     return call(
         route_kernel,
-        [pair, pair],
+        [out] * 4,
         (*products, delta, proj),
         0,
         0,
@@ -271,7 +269,7 @@
 
 
 def leave_kernel(peers, drop_ref, kept_ref, got_ref, crossed_ref, *outs):
-    near = kept_ref[0].astype(F32) + got_ref[0].astype(F32)
+    near = kept_ref[...].astype(F32) + got_ref[...].astype(F32)
     rows = (near + crossed_ref[...].astype(F32)).astype(BF)
     slots = outs[0].shape[0]
     for k, out in zip(peers, outs):
@@ -424,16 +422,17 @@
     deltas = [delta, delta_beside, delta_far, delta_last]
     products = [own_product, product(delta_beside, proj), product(delta_far, proj)]
 
-    sent, kept = route_products(products, delta_last, proj)
-    got = swap(sent, "side")
-    cross = lax.optimization_barrier((kept[1].astype(F32) + got[1].astype(F32)).astype(BF))
+    near, mates_near, over, mates_over = route_products(products, delta_last, proj)
+    got_cross = swap(mates_over, "side")
+    cross = lax.optimization_barrier((over.astype(F32) + got_cross.astype(F32)).astype(BF))
+    got_near = swap(after(mates_near, cross), "side")
     crossed = swap(cross, "mp")
 
     factor = 1.0 / math.sqrt(rows * n)
     deltas = after(jnp.concatenate([deltas[k] for k in (0, 2, 1, 3)]), cross)
     grad_proj = lax.optimization_barrier(dot(normed, deltas, ((0,), (0,))) * factor)
     crossed = after(crossed, grad_proj)
-    leaving = leaving_rows(range(n), drop, kept, got, crossed)
+    leaving = leaving_rows(range(n), drop, near, got_near, crossed)
 
     arrived = [leaving[0]] + exchange(leaving)
     across = [swap(block, "mp") for block in arrived]

time: 101 us -> 101 us (level)
    ppermute x23 -> x24, waiting for transfers between devices: 34 us -> 33.7 us  [swap(): lax.ppermute(x, axis, [(i, i ^ k) for i in range(lax.axis_size(axis))])]
    ppermute x23 -> x24, starting transfers between devices: 30.9 us -> 30.9 us  [swap(): lax.ppermute(x, axis, [(i, i ^ k) for i in range(lax.axis_size(axis))])]
  transfers between devices with their start and end apart: 26 -> 27, of which waited for: 16 -> 16; matrix products, arithmetic and copies ran while one was open for 4% -> 4% of each run, Pallas kernels for 7% -> 7%
where the time goes in v12:
time: 101 us; the launch traced here: 100 us
  waiting for transfers between devices  43 us (43%)
  starting transfers between devices  40 us (40%)
  Pallas kernels  11.4 us (11%)
  matrix products  2.98 us (3%)
  other arithmetic  1.29 us (1%)
    ppermute x24, waiting for transfers between devices, swap(): lax.ppermute(x, axis, [(i, i ^ k) for i in range(lax.axis_size(axis))])  33.7 us
    ppermute x24, starting transfers between devices, swap(): lax.ppermute(x, axis, [(i, i ^ k) for i in range(lax.axis_size(axis))])  30.9 us
    pallas_call x15, Pallas kernels, call(): pl.pallas_call(kernel, out_shape=shapes, cost_estimate=pl.CostEstimate(fl...  11.4 us
    ppermute x3, waiting for transfers between devices, onward(): lax.ppermute(x, 'seq', [(i, i + 1) for i in range(lax.axis_size('seq') -...  9.25 us
    ppermute x3, starting transfers between devices, onward(): lax.ppermute(x, 'seq', [(i, i + 1) for i in range(lax.axis_size('seq') -...  9.11 us
    dot_general x1, matrix products, dot(): return lax.dot_general(a, b, (dims, ((), ())), preferred_element_type=F32)  2.98 us
  transfers between devices with their start and end apart: 27, of which 16 were waited for; matrix products, arithmetic and copies ran while one was open for 4% of the time, Pallas kernels for 7%

profile of v12, /device:TPU:0, one launch (start us, length us, event | category | flops | bytes accessed | tf_op | source)
XLA Modules:
  0.0 100.3 jit_solution(9801785642363049178)
XLA Ops:
  0.7 0.9 convert_select_fusion.small_ref
  1.6 1.2 %shard_map.95 = (bf16[48,1024]{1,0:T(8,128)(2,1)S(1)}, bf16[48,1024]{1,0:T(8,128)(2,1)S(1)}, bf16[48,1024]{1,0:T(8,128)(2,1)S(1)}, bf16[48,1024]{1,0:T(8,128)(2,1)S(1)}, bf16[2,48,3584]{2,1,0:T(8,128)(2,1)S(1)}) custom-call(bf16[4,48,3584]{2,1,0:T(8,128)(2,1)} %bitcast.7, f32[30,128]{1,0:T(8,128)S(1)} %convert_select_fusion.small_ref), custom_call_target="tpu_custom_call" | custom-call | flops 1032192 | bytes 1376256 | tf_op jit(solution)/shard_map/pallas_call | solution.py:49
  2.8 5.1 %collective-permute-start = (bf16[48,1024]{1,0:T(8,128)(2,1)S(1)}, bf16[48,1024]{1,0:T(8,128)(2,1)S(1)}, u32[]{:S(2)}, u32[]{:S(2)}) collective-permute-start(bf16[48,1024]{1,0:T(8,128)(2,1)S(1)} %get-tuple-element.44), channel_id=1, source_target_pairs={{0,12},{4,8},{8,4},{12,0},{1,13},{5,9},{9,5},{13,1},{2,14},{6,10},... | collective-permute-start | bytes 294920 | tf_op jit(solution)/shard_map/ppermute | solution.py:352
  7.9 0.0 collective-permute-start.2
  7.9 0.6 collective-permute-start.3
  8.6 0.8 constant_dynamic-slice_fusion
  9.4 3.3 %collective-permute-start.1 = (bf16[256,128]{1,0:T(8,128)(2,1)S(1)}, bf16[256,128]{1,0:T(8,128)(2,1)S(1)}, u32[]{:S(2)}, u32[]{:S(2)}) collective-permute-start(bf16[256,128]{1,0:T(8,128)(2,1)S(1)} %pad_maximum_fusion.1.refs_0_), channel_id=1, source_target_pairs={{0,4},{4,8},{8,12},{1,5},{5,9},{9,13},{2,6},{6,10},{10,14},{3,7},{... | collective-permute-start | bytes 196616 | tf_op jit(solution)/shard_map/ppermute | solution.py:356
  12.7 3.0 %collective-permute-done.1.refs_1_ = bf16[256,128]{1,0:T(8,128)(2,1)S(1)} collective-permute-done((bf16[256,128]{1,0:T(8,128)(2,1)S(1)}, bf16[256,128]{1,0:T(8,128)(2,1)S(1)}, u32[]{:S(2)}, u32[]{:S(2)}) %collective-permute-start.1) | collective-permute-done | bytes 65568 | tf_op jit(solution)/shard_map/ppermute | solution.py:356
  15.7 0.5 collective-permute-done.2.refs_1_.refs_6_
  16.2 0.4 shard_map.96
  16.6 0.1 collective-permute-start.5
  16.7 1.6 %collective-permute-start.4 = (bf16[128,896]{1,0:T(8,128)(2,1)S(1)}, bf16[128,896]{1,0:T(8,128)(2,1)S(1)}, u32[]{:S(2)}, u32[]{:S(2)}) collective-permute-start(bf16[128,896]{1,0:T(8,128)(2,1)S(1)} %get-tuple-element.60.refs_3_), channel_id=1, source_target_pairs={{0,2},{2,0},{1,3},{3,1},{4,6},{6,4},{5,7},{7,5},{8,10},{10,8},{9,1... | collective-permute-start | bytes 688136 | tf_op jit(solution)/shard_map/ppermute | solution.py:352
  18.2 3.8 %collective-permute-start.6 = (bf16[256,128]{1,0:T(8,128)(2,1)S(1)}, bf16[256,128]{1,0:T(8,128)(2,1)S(1)}, u32[]{:S(2)}, u32[]{:S(2)}) collective-permute-start(bf16[256,128]{1,0:T(8,128)(2,1)S(1)} %collective-permute-done.1.refs_1_), channel_id=1, source_target_pairs={{0,4},{4,8},{8,12},{1,5},{5,9},{9,13},{2,6},{6,10},{10,14},{3,7},{... | collective-permute-start | bytes 196616 | tf_op jit(solution)/shard_map/ppermute | solution.py:356
  22.1 1.9 %collective-permute-done.6.refs_2_ = bf16[256,128]{1,0:T(8,128)(2,1)S(1)} collective-permute-done((bf16[256,128]{1,0:T(8,128)(2,1)S(1)}, bf16[256,128]{1,0:T(8,128)(2,1)S(1)}, u32[]{:S(2)}, u32[]{:S(2)}) %collective-permute-start.6) | collective-permute-done | bytes 65568 | tf_op jit(solution)/shard_map/ppermute | solution.py:356
  24.0 0.7 collective-permute-done.4.refs_1_
  24.7 1.5 %collective-permute-done.7.refs_0_ = bf16[128,896]{1,0:T(8,128)(2,1)S(1)} collective-permute-done((bf16[128,896]{1,0:T(8,128)(2,1)S(1)}, bf16[128,896]{1,0:T(8,128)(2,1)S(1)}, u32[]{:S(2)}, u32[]{:S(2)}) %collective-permute-start.7) | collective-permute-done | bytes 229408 | tf_op jit(solution)/shard_map/ppermute | solution.py:352
  26.2 0.5 shard_map.97
  26.6 2.0 %collective-permute-start.8 = (bf16[128,1024]{1,0:T(8,128)(2,1)S(1)}, bf16[128,1024]{1,0:T(8,128)(2,1)S(1)}, u32[]{:S(2)}, u32[]{:S(2)}) collective-permute-start(bf16[128,1024]{1,0:T(8,128)(2,1)S(1)} %shard_map.97), channel_id=1, source_target_pairs={{0,4},{4,0},{8,12},{12,8},{1,5},{5,1},{9,13},{13,9},{2,6},{6,2},{1... | collective-permute-start | bytes 786440 | tf_op jit(solution)/shard_map/ppermute | solution.py:352
  28.7 2.0 %collective-permute-start.9 = (bf16[256,128]{1,0:T(8,128)(2,1)S(1)}, bf16[256,128]{1,0:T(8,128)(2,1)S(1)}, u32[]{:S(2)}, u32[]{:S(2)}) collective-permute-start(bf16[256,128]{1,0:T(8,128)(2,1)S(1)} %collective-permute-done.6.refs_2_), channel_id=1, source_target_pairs={{0,4},{4,8},{8,12},{1,5},{5,9},{9,13},{2,6},{6,10},{10,14},{3,7},{... | collective-permute-start | bytes 196616 | tf_op jit(solution)/shard_map/ppermute | solution.py:356
  30.6 0.9 shard_map.98
  31.5 0.0 copy-start.1
  31.6 4.4 %collective-permute-done.9.refs_3_ = bf16[256,128]{1,0:T(8,128)(2,1)S(1)} collective-permute-done((bf16[256,128]{1,0:T(8,128)(2,1)S(1)}, bf16[256,128]{1,0:T(8,128)(2,1)S(1)}, u32[]{:S(2)}, u32[]{:S(2)}) %collective-permute-start.9) | collective-permute-done | bytes 65568 | tf_op jit(solution)/shard_map/ppermute | solution.py:356
  35.9 0.1 add_convert_fusion
  36.0 2.4 %collective-permute-start.10 = (bf16[128,1024]{1,0:T(8,128)(2,1)S(1)}, bf16[128,1024]{1,0:T(8,128)(2,1)S(1)}, u32[]{:S(2)}, u32[]{:S(2)}) collective-permute-start(bf16[128,1024]{1,0:T(8,128)(2,1)S(1)} %add_convert_fusion), channel_id=1, source_target_pairs={{0,8},{4,12},{8,0},{12,4},{1,9},{5,13},{9,1},{13,5},{2,10},{6,14},... | collective-permute-start | bytes 786440 | tf_op jit(solution)/shard_map/ppermute | solution.py:352
  38.4 0.4 shard_map.99
  38.8 2.5 %collective-permute-start.11 = (bf16[128,1024]{1,0:T(8,128)(2,1)S(1)}, bf16[128,1024]{1,0:T(8,128)(2,1)S(1)}, u32[]{:S(2)}, u32[]{:S(2)}) collective-permute-start(bf16[128,1024]{1,0:T(8,128)(2,1)S(1)} %shard_map.99), channel_id=1, source_target_pairs={{0,4},{4,0},{8,12},{12,8},{1,5},{5,1},{9,13},{13,9},{2,6},{6,2},{1... | collective-permute-start | bytes 786440 | tf_op jit(solution)/shard_map/ppermute | solution.py:352
  41.4 2.4 %shard_map.100 = bf16[128,1024]{1,0:T(8,128)(2,1)S(1)} custom-call(bf16[128,1024]{1,0:T(8,128)(2,1)S(1)} %copy-done.1, bf16[256,128]{1,0:T(8,128)(2,1)S(1)} %pad_maximum_fusion.1.refs_0_, bf16[256,128]{1,0:T(8,128)(2,1)S(1)} %collective-permute-done.1.refs_1_, bf16[256,128]{1,0:T(8,128)(2,1)S(1)} %collective-permute-done.6.refs_2_, ...), custom_call_target="tpu_custom_call" | custom-call | bytes 524288 | tf_op jit(solution)/shard_map/pallas_call | solution.py:49
  43.7 6.5 %collective-permute-done.10 = bf16[128,1024]{1,0:T(8,128)(2,1)S(1)} collective-permute-done((bf16[128,1024]{1,0:T(8,128)(2,1)S(1)}, bf16[128,1024]{1,0:T(8,128)(2,1)S(1)}, u32[]{:S(2)}, u32[]{:S(2)}) %collective-permute-start.10) | collective-permute-done | bytes 262176 | tf_op jit(solution)/shard_map/ppermute | solution.py:352
  50.2 0.1 convert_add_fusion
  50.3 0.2 collective-permute-done.11
  50.5 0.1 subtract_convert_fusion.delta_ref
  50.6 2.2 %collective-permute-start.13 = (bf16[128,1024]{1,0:T(8,128)(2,1)S(1)}, bf16[128,1024]{1,0:T(8,128)(2,1)S(1)}, u32[]{:S(2)}, u32[]{:S(2)}) collective-permute-start(bf16[128,1024]{1,0:T(8,128)(2,1)S(1)} %subtract_convert_fusion.delta_ref), channel_id=1, source_target_pairs={{0,8},{4,12},{8,0},{12,4},{1,9},{5,13},{9,1},{13,5},{2,10},{6,14},... | collective-permute-start | bytes 786440 | tf_op jit(solution)/shard_map/ppermute | solution.py:352
  52.8 0.7 shard_map.101.first_ref
  53.5 2.3 %collective-permute-start.12 = (bf16[128,1024]{1,0:T(8,128)(2,1)S(1)}, bf16[128,1024]{1,0:T(8,128)(2,1)S(1)}, u32[]{:S(2)}, u32[]{:S(2)}) collective-permute-start(bf16[128,1024]{1,0:T(8,128)(2,1)S(1)} %subtract_convert_fusion.delta_ref), channel_id=1, source_target_pairs={{0,4},{4,0},{8,12},{12,8},{1,5},{5,1},{9,13},{13,9},{2,6},{6,2},{1... | collective-permute-start | bytes 786440 | tf_op jit(solution)/shard_map/ppermute | solution.py:352
  55.8 7.8 %collective-permute-done.13.delta_ref = bf16[128,1024]{1,0:T(8,128)(2,1)S(1)} collective-permute-done((bf16[128,1024]{1,0:T(8,128)(2,1)S(1)}, bf16[128,1024]{1,0:T(8,128)(2,1)S(1)}, u32[]{:S(2)}, u32[]{:S(2)}) %collective-permute-start.13) | collective-permute-done | bytes 262176 | tf_op jit(solution)/shard_map/ppermute | solution.py:352
  63.5 0.5 collective-permute-start.14
  64.1 0.7 shard_map.103.third_ref
  64.8 0.7 shard_map.102.second_ref
  65.5 5.1 %collective-permute-done.14.delta_ref = bf16[128,1024]{1,0:T(8,128)(2,1)S(1)} collective-permute-done((bf16[128,1024]{1,0:T(8,128)(2,1)S(1)}, bf16[128,1024]{1,0:T(8,128)(2,1)S(1)}, u32[]{:S(2)}, u32[]{:S(2)}) %collective-permute-start.14) | collective-permute-done | bytes 262176 | tf_op jit(solution)/shard_map/ppermute | solution.py:352
  70.6 0.8 shard_map.104
  71.3 0.1 collective-permute-start.15
  71.4 0.1 pad_maximum_fusion
  71.5 1.4 %collective-permute-done.15 = bf16[128,896]{1,0:T(8,128)(2,1)S(1)} collective-permute-done((bf16[128,896]{1,0:T(8,128)(2,1)S(1)}, bf16[128,896]{1,0:T(8,128)(2,1)S(1)}, u32[]{:S(2)}, u32[]{:S(2)}) %collective-permute-start.15) | collective-permute-done | bytes 229408 | tf_op jit(solution)/shard_map/ppermute | solution.py:352
  72.9 0.1 add_convert_fusion.1
  73.0 1.5 %collective-permute-start.17 = (bf16[128,896]{1,0:T(8,128)(2,1)S(1)}, bf16[128,896]{1,0:T(8,128)(2,1)S(1)}, u32[]{:S(2)}, u32[]{:S(2)}) collective-permute-start(bf16[128,896]{1,0:T(8,128)(2,1)S(1)} %add_convert_fusion.1), channel_id=1, source_target_pairs={{0,2},{2,0},{1,3},{3,1},{4,6},{6,4},{5,7},{7,5},{8,10},{10,8},{9,1... | collective-permute-start | bytes 688136 | tf_op jit(solution)/shard_map/ppermute | solution.py:352
  74.5 3.0 %convolution_multiply_fusion = f32[896,1024]{1,0:T(8,128)} fusion(bf16[512,896]{1,0:T(8,128)(2,1)S(1)} %get-tuple-element.66.normed_ref, bf16[512,1024]{1,0:T(8,128)(2,1)S(1)} %pad_maximum_fusion), kind=kOutput, calls=%fused_computation | convolution fusion | flops 940441600 | bytes 5636096 | tf_op jit(solution)/shard_map/dot_general | solution.py:22
  77.5 3.2 %collective-permute-done.17.crossed_ref = bf16[128,896]{1,0:T(8,128)(2,1)S(1)} collective-permute-done((bf16[128,896]{1,0:T(8,128)(2,1)S(1)}, bf16[128,896]{1,0:T(8,128)(2,1)S(1)}, u32[]{:S(2)}, u32[]{:S(2)}) %collective-permute-start.17) | collective-permute-done | bytes 229408 | tf_op jit(solution)/shard_map/ppermute | solution.py:352
  80.7 0.3 shard_map.105
  81.0 1.8 %collective-permute-start.18 = (bf16[48,896]{1,0:T(8,128)(2,1)S(1)}, bf16[48,896]{1,0:T(8,128)(2,1)S(1)}, u32[]{:S(2)}, u32[]{:S(2)}) collective-permute-start(bf16[48,896]{1,0:T(8,128)(2,1)S(1)} %get-tuple-element.78), channel_id=1, source_target_pairs={{0,4},{4,0},{8,12},{12,8},{1,5},{5,1},{9,13},{13,9},{2,6},{6,2},{1... | collective-permute-start | bytes 258056 | tf_op jit(solution)/shard_map/ppermute | solution.py:352
  82.8 3.4 %collective-permute-start.19 = (bf16[48,896]{1,0:T(8,128)(2,1)S(1)}, bf16[48,896]{1,0:T(8,128)(2,1)S(1)}, u32[]{:S(2)}, u32[]{:S(2)}) collective-permute-start(bf16[48,896]{1,0:T(8,128)(2,1)S(1)} %get-tuple-element.80), channel_id=1, source_target_pairs={{0,8},{4,12},{8,0},{12,4},{1,9},{5,13},{9,1},{13,5},{2,10},{6,14},... | collective-permute-start | bytes 258056 | tf_op jit(solution)/shard_map/ppermute | solution.py:352
  86.2 1.5 %collective-permute-start.22 = (bf16[48,896]{1,0:T(8,128)(2,1)S(1)}, bf16[48,896]{1,0:T(8,128)(2,1)S(1)}, u32[]{:S(2)}, u32[]{:S(2)}) collective-permute-start(bf16[48,896]{1,0:T(8,128)(2,1)S(1)} %get-tuple-element.77.refs_0_), channel_id=1, source_target_pairs={{0,2},{2,0},{1,3},{3,1},{4,6},{6,4},{5,7},{7,5},{8,10},{10,8},{9,1... | collective-permute-start | bytes 258056 | tf_op jit(solution)/shard_map/ppermute | solution.py:352
  87.7 0.5 collective-permute-start.23
  88.2 3.3 %collective-permute-done.19.refs_2_ = bf16[48,896]{1,0:T(8,128)(2,1)S(1)} collective-permute-done((bf16[48,896]{1,0:T(8,128)(2,1)S(1)}, bf16[48,896]{1,0:T(8,128)(2,1)S(1)}, u32[]{:S(2)}, u32[]{:S(2)}) %collective-permute-start.19) | collective-permute-done | bytes 86048 | tf_op jit(solution)/shard_map/ppermute | solution.py:352
  91.5 1.5 %collective-permute-start.24 = (bf16[48,896]{1,0:T(8,128)(2,1)S(1)}, bf16[48,896]{1,0:T(8,128)(2,1)S(1)}, u32[]{:S(2)}, u32[]{:S(2)}) collective-permute-start(bf16[48,896]{1,0:T(8,128)(2,1)S(1)} %collective-permute-done.19.refs_2_), channel_id=1, source_target_pairs={{0,2},{2,0},{1,3},{3,1},{4,6},{6,4},{5,7},{7,5},{8,10},{10,8},{9,1... | collective-permute-start | bytes 258056 | tf_op jit(solution)/shard_map/ppermute | solution.py:352
  93.0 1.1 %collective-permute-start.25 = (bf16[48,896]{1,0:T(8,128)(2,1)S(1)}, bf16[48,896]{1,0:T(8,128)(2,1)S(1)}, u32[]{:S(2)}, u32[]{:S(2)}) collective-permute-start(bf16[48,896]{1,0:T(8,128)(2,1)S(1)} %collective-permute-done.20.refs_3_), channel_id=1, source_target_pairs={{0,2},{2,0},{1,3},{3,1},{4,6},{6,4},{5,7},{7,5},{8,10},{10,8},{9,1... | collective-permute-start | bytes 258056 | tf_op jit(solution)/shard_map/ppermute | solution.py:352
  94.1 0.4 shard_map.106.refs_0_
  94.5 0.1 collective-permute-start.21
  94.6 1.4 %collective-permute-done.24.refs_2_ = bf16[48,896]{1,0:T(8,128)(2,1)S(1)} collective-permute-done((bf16[48,896]{1,0:T(8,128)(2,1)S(1)}, bf16[48,896]{1,0:T(8,128)(2,1)S(1)}, u32[]{:S(2)}, u32[]{:S(2)}) %collective-permute-start.24) | collective-permute-done | bytes 86048 | tf_op jit(solution)/shard_map/ppermute | solution.py:352
  96.0 1.5 %collective-permute-done.25.refs_3_ = bf16[48,896]{1,0:T(8,128)(2,1)S(1)} collective-permute-done((bf16[48,896]{1,0:T(8,128)(2,1)S(1)}, bf16[48,896]{1,0:T(8,128)(2,1)S(1)}, u32[]{:S(2)}, u32[]{:S(2)}) %collective-permute-start.25) | collective-permute-done | bytes 86048 | tf_op jit(solution)/shard_map/ppermute | solution.py:352
  97.5 0.4 shard_map.107.refs_2_
  97.9 0.1 collective-permute-start.26
  98.0 1.0 shard_map.108.t
  99.0 0.6 collective-permute-done.26.refs_0_
  99.6 0.7 shard_map.109
  (19 shorter events, 0.1 us)
Async XLA Ops:
  0.6 25.6 %copy-start = (bf16[896,1024]{1,0:T(8,128)(2,1)S(1)}, bf16[896,1024]{1,0:T(8,128)(2,1)}, u32[]{:S(2)}) copy-start(bf16[896,1024]{1,0:T(8,128)(2,1)} %proj_ref.9) | copy-start | bytes 5505028
  2.8 12.8 %collective-permute-start = (bf16[48,1024]{1,0:T(8,128)(2,1)S(1)}, bf16[48,1024]{1,0:T(8,128)(2,1)S(1)}, u32[]{:S(2)}, u32[]{:S(2)}) collective-permute-start(bf16[48,1024]{1,0:T(8,128)(2,1)S(1)} %get-tuple-element.44), channel_id=1, source_target_pairs={{0,12},{4,8},{8,4},{12,0},{1,13},{5,9},{9,5},{13,1},{2,14},{6,10},... | collective-permute-start | bytes 294920 | tf_op jit(solution)/shard_map/ppermute | solution.py:352
  7.9 8.3 %collective-permute-start.2 = (bf16[48,1024]{1,0:T(8,128)(2,1)S(1)}, bf16[48,1024]{1,0:T(8,128)(2,1)S(1)}, u32[]{:S(2)}, u32[]{:S(2)}) collective-permute-start(bf16[48,1024]{1,0:T(8,128)(2,1)S(1)} %get-tuple-element.48), channel_id=1, source_target_pairs={{0,8},{4,12},{8,0},{12,4},{1,9},{5,13},{9,1},{13,5},{2,10},{6,14},... | collective-permute-start | bytes 294920 | tf_op jit(solution)/shard_map/ppermute | solution.py:352
  7.9 8.3 %collective-permute-start.3 = (bf16[48,1024]{1,0:T(8,128)(2,1)S(1)}, bf16[48,1024]{1,0:T(8,128)(2,1)S(1)}, u32[]{:S(2)}, u32[]{:S(2)}) collective-permute-start(bf16[48,1024]{1,0:T(8,128)(2,1)S(1)} %get-tuple-element.50), channel_id=1, source_target_pairs={{0,4},{4,0},{8,12},{12,8},{1,5},{5,1},{9,13},{13,9},{2,6},{6,2},{1... | collective-permute-start | bytes 294920 | tf_op jit(solution)/shard_map/ppermute | solution.py:352
  9.4 6.3 %collective-permute-start.1 = (bf16[256,128]{1,0:T(8,128)(2,1)S(1)}, bf16[256,128]{1,0:T(8,128)(2,1)S(1)}, u32[]{:S(2)}, u32[]{:S(2)}) collective-permute-start(bf16[256,128]{1,0:T(8,128)(2,1)S(1)} %pad_maximum_fusion.1.refs_0_), channel_id=1, source_target_pairs={{0,4},{4,8},{8,12},{1,5},{5,9},{9,13},{2,6},{6,10},{10,14},{3,7},{... | collective-permute-start | bytes 196616 | tf_op jit(solution)/shard_map/ppermute | solution.py:356
  16.6 7.4 %collective-permute-start.5 = (bf16[128,896]{1,0:T(8,128)(2,1)S(1)}, bf16[128,896]{1,0:T(8,128)(2,1)S(1)}, u32[]{:S(2)}, u32[]{:S(2)}) collective-permute-start(bf16[128,896]{1,0:T(8,128)(2,1)S(1)} %get-tuple-element.60.refs_3_), channel_id=1, source_target_pairs={{0,1},{1,0},{2,3},{3,2},{4,5},{5,4},{6,7},{7,6},{8,9},{9,8},{10,11... | collective-permute-start | bytes 688136 | tf_op jit(solution)/shard_map/ppermute | solution.py:352
  16.7 8.0 %collective-permute-start.4 = (bf16[128,896]{1,0:T(8,128)(2,1)S(1)}, bf16[128,896]{1,0:T(8,128)(2,1)S(1)}, u32[]{:S(2)}, u32[]{:S(2)}) collective-permute-start(bf16[128,896]{1,0:T(8,128)(2,1)S(1)} %get-tuple-element.60.refs_3_), channel_id=1, source_target_pairs={{0,2},{2,0},{1,3},{3,1},{4,6},{6,4},{5,7},{7,5},{8,10},{10,8},{9,1... | collective-permute-start | bytes 688136 | tf_op jit(solution)/shard_map/ppermute | solution.py:352
  18.2 5.7 %collective-permute-start.6 = (bf16[256,128]{1,0:T(8,128)(2,1)S(1)}, bf16[256,128]{1,0:T(8,128)(2,1)S(1)}, u32[]{:S(2)}, u32[]{:S(2)}) collective-permute-start(bf16[256,128]{1,0:T(8,128)(2,1)S(1)} %collective-permute-done.1.refs_1_), channel_id=1, source_target_pairs={{0,4},{4,8},{8,12},{1,5},{5,9},{9,13},{2,6},{6,10},{10,14},{3,7},{... | collective-permute-start | bytes 196616 | tf_op jit(solution)/shard_map/ppermute | solution.py:356
  24.7 1.5 %collective-permute-start.7 = (bf16[128,896]{1,0:T(8,128)(2,1)S(1)}, bf16[128,896]{1,0:T(8,128)(2,1)S(1)}, u32[]{:S(2)}, u32[]{:S(2)}) collective-permute-start(bf16[128,896]{1,0:T(8,128)(2,1)S(1)} %collective-permute-done.4.refs_1_), channel_id=1, source_target_pairs={{0,1},{1,0},{2,3},{3,2},{4,5},{5,4},{6,7},{7,6},{8,9},{9,8},{10,11... | collective-permute-start | bytes 688136 | tf_op jit(solution)/shard_map/ppermute | solution.py:352
  26.6 9.3 %collective-permute-start.8 = (bf16[128,1024]{1,0:T(8,128)(2,1)S(1)}, bf16[128,1024]{1,0:T(8,128)(2,1)S(1)}, u32[]{:S(2)}, u32[]{:S(2)}) collective-permute-start(bf16[128,1024]{1,0:T(8,128)(2,1)S(1)} %shard_map.97), channel_id=1, source_target_pairs={{0,4},{4,0},{8,12},{12,8},{1,5},{5,1},{9,13},{13,9},{2,6},{6,2},{1... | collective-permute-start | bytes 786440 | tf_op jit(solution)/shard_map/ppermute | solution.py:352
  28.7 7.3 %collective-permute-start.9 = (bf16[256,128]{1,0:T(8,128)(2,1)S(1)}, bf16[256,128]{1,0:T(8,128)(2,1)S(1)}, u32[]{:S(2)}, u32[]{:S(2)}) collective-permute-start(bf16[256,128]{1,0:T(8,128)(2,1)S(1)} %collective-permute-done.6.refs_2_), channel_id=1, source_target_pairs={{0,4},{4,8},{8,12},{1,5},{5,9},{9,13},{2,6},{6,10},{10,14},{3,7},{... | collective-permute-start | bytes 196616 | tf_op jit(solution)/shard_map/ppermute | solution.py:356
  31.5 9.8 %copy-start.1 = (bf16[128,1024]{1,0:T(8,128)(2,1)S(1)}, bf16[128,1024]{1,0:T(8,128)(2,1)}, u32[]{:S(2)}) copy-start(bf16[128,1024]{1,0:T(8,128)(2,1)} %queries_ref) | copy-start | bytes 786436
  36.0 14.2 %collective-permute-start.10 = (bf16[128,1024]{1,0:T(8,128)(2,1)S(1)}, bf16[128,1024]{1,0:T(8,128)(2,1)S(1)}, u32[]{:S(2)}, u32[]{:S(2)}) collective-permute-start(bf16[128,1024]{1,0:T(8,128)(2,1)S(1)} %add_convert_fusion), channel_id=1, source_target_pairs={{0,8},{4,12},{8,0},{12,4},{1,9},{5,13},{9,1},{13,5},{2,10},{6,14},... | collective-permute-start | bytes 786440 | tf_op jit(solution)/shard_map/ppermute | solution.py:352
  38.8 11.6 %collective-permute-start.11 = (bf16[128,1024]{1,0:T(8,128)(2,1)S(1)}, bf16[128,1024]{1,0:T(8,128)(2,1)S(1)}, u32[]{:S(2)}, u32[]{:S(2)}) collective-permute-start(bf16[128,1024]{1,0:T(8,128)(2,1)S(1)} %shard_map.99), channel_id=1, source_target_pairs={{0,4},{4,0},{8,12},{12,8},{1,5},{5,1},{9,13},{13,9},{2,6},{6,2},{1... | collective-permute-start | bytes 786440 | tf_op jit(solution)/shard_map/ppermute | solution.py:352
  50.6 13.0 %collective-permute-start.13 = (bf16[128,1024]{1,0:T(8,128)(2,1)S(1)}, bf16[128,1024]{1,0:T(8,128)(2,1)S(1)}, u32[]{:S(2)}, u32[]{:S(2)}) collective-permute-start(bf16[128,1024]{1,0:T(8,128)(2,1)S(1)} %subtract_convert_fusion.delta_ref), channel_id=1, source_target_pairs={{0,8},{4,12},{8,0},{12,4},{1,9},{5,13},{9,1},{13,5},{2,10},{6,14},... | collective-permute-start | bytes 786440 | tf_op jit(solution)/shard_map/ppermute | solution.py:352
  53.5 11.3 %collective-permute-start.12 = (bf16[128,1024]{1,0:T(8,128)(2,1)S(1)}, bf16[128,1024]{1,0:T(8,128)(2,1)S(1)}, u32[]{:S(2)}, u32[]{:S(2)}) collective-permute-start(bf16[128,1024]{1,0:T(8,128)(2,1)S(1)} %subtract_convert_fusion.delta_ref), channel_id=1, source_target_pairs={{0,4},{4,0},{8,12},{12,8},{1,5},{5,1},{9,13},{13,9},{2,6},{6,2},{1... | collective-permute-start | bytes 786440 | tf_op jit(solution)/shard_map/ppermute | solution.py:352
  63.5 7.0 %collective-permute-start.14 = (bf16[128,1024]{1,0:T(8,128)(2,1)S(1)}, bf16[128,1024]{1,0:T(8,128)(2,1)S(1)}, u32[]{:S(2)}, u32[]{:S(2)}) collective-permute-start(bf16[128,1024]{1,0:T(8,128)(2,1)S(1)} %collective-permute-done.13.delta_ref), channel_id=1, source_target_pairs={{0,4},{4,0},{8,12},{12,8},{1,5},{5,1},{9,13},{13,9},{2,6},{6,2},{1... | collective-permute-start | bytes 786440 | tf_op jit(solution)/shard_map/ppermute | solution.py:352
  71.3 1.6 %collective-permute-start.15 = (bf16[128,896]{1,0:T(8,128)(2,1)S(1)}, bf16[128,896]{1,0:T(8,128)(2,1)S(1)}, u32[]{:S(2)}, u32[]{:S(2)}) collective-permute-start(bf16[128,896]{1,0:T(8,128)(2,1)S(1)} %get-tuple-element.72), channel_id=1, source_target_pairs={{0,1},{1,0},{2,3},{3,2},{4,5},{5,4},{6,7},{7,6},{8,9},{9,8},{10,11... | collective-permute-start | bytes 688136 | tf_op jit(solution)/shard_map/ppermute | solution.py:352
  73.0 7.7 %collective-permute-start.17 = (bf16[128,896]{1,0:T(8,128)(2,1)S(1)}, bf16[128,896]{1,0:T(8,128)(2,1)S(1)}, u32[]{:S(2)}, u32[]{:S(2)}) collective-permute-start(bf16[128,896]{1,0:T(8,128)(2,1)S(1)} %add_convert_fusion.1), channel_id=1, source_target_pairs={{0,2},{2,0},{1,3},{3,1},{4,6},{6,4},{5,7},{7,5},{8,10},{10,8},{9,1... | collective-permute-start | bytes 688136 | tf_op jit(solution)/shard_map/ppermute | solution.py:352
  74.5 6.2 %collective-permute-start.16 = (bf16[128,896]{1,0:T(8,128)(2,1)S(1)}, bf16[128,896]{1,0:T(8,128)(2,1)S(1)}, u32[]{:S(2)}, u32[]{:S(2)}) collective-permute-start(bf16[128,896]{1,0:T(8,128)(2,1)S(1)} %get-tuple-element.73), channel_id=1, source_target_pairs={{0,1},{1,0},{2,3},{3,2},{4,5},{5,4},{6,7},{7,6},{8,9},{9,8},{10,11... | collective-permute-start | bytes 688136 | tf_op jit(solution)/shard_map/ppermute | solution.py:352
  81.0 6.7 %collective-permute-start.18 = (bf16[48,896]{1,0:T(8,128)(2,1)S(1)}, bf16[48,896]{1,0:T(8,128)(2,1)S(1)}, u32[]{:S(2)}, u32[]{:S(2)}) collective-permute-start(bf16[48,896]{1,0:T(8,128)(2,1)S(1)} %get-tuple-element.78), channel_id=1, source_target_pairs={{0,4},{4,0},{8,12},{12,8},{1,5},{5,1},{9,13},{13,9},{2,6},{6,2},{1... | collective-permute-start | bytes 258056 | tf_op jit(solution)/shard_map/ppermute | solution.py:352
  82.8 8.7 %collective-permute-start.19 = (bf16[48,896]{1,0:T(8,128)(2,1)S(1)}, bf16[48,896]{1,0:T(8,128)(2,1)S(1)}, u32[]{:S(2)}, u32[]{:S(2)}) collective-permute-start(bf16[48,896]{1,0:T(8,128)(2,1)S(1)} %get-tuple-element.80), channel_id=1, source_target_pairs={{0,8},{4,12},{8,0},{12,4},{1,9},{5,13},{9,1},{13,5},{2,10},{6,14},... | collective-permute-start | bytes 258056 | tf_op jit(solution)/shard_map/ppermute | solution.py:352
  86.2 6.8 %collective-permute-start.20 = (bf16[48,896]{1,0:T(8,128)(2,1)S(1)}, bf16[48,896]{1,0:T(8,128)(2,1)S(1)}, u32[]{:S(2)}, u32[]{:S(2)}) collective-permute-start(bf16[48,896]{1,0:T(8,128)(2,1)S(1)} %get-tuple-element.82), channel_id=1, source_target_pairs={{0,12},{4,8},{8,4},{12,0},{1,13},{5,9},{9,5},{13,1},{2,14},{6,10},... | collective-permute-start | bytes 258056 | tf_op jit(solution)/shard_map/ppermute | solution.py:352
  86.2 8.3 %collective-permute-start.22 = (bf16[48,896]{1,0:T(8,128)(2,1)S(1)}, bf16[48,896]{1,0:T(8,128)(2,1)S(1)}, u32[]{:S(2)}, u32[]{:S(2)}) collective-permute-start(bf16[48,896]{1,0:T(8,128)(2,1)S(1)} %get-tuple-element.77.refs_0_), channel_id=1, source_target_pairs={{0,2},{2,0},{1,3},{3,1},{4,6},{6,4},{5,7},{7,5},{8,10},{10,8},{9,1... | collective-permute-start | bytes 258056 | tf_op jit(solution)/shard_map/ppermute | solution.py:352
  87.7 6.8 %collective-permute-start.23 = (bf16[48,896]{1,0:T(8,128)(2,1)S(1)}, bf16[48,896]{1,0:T(8,128)(2,1)S(1)}, u32[]{:S(2)}, u32[]{:S(2)}) collective-permute-start(bf16[48,896]{1,0:T(8,128)(2,1)S(1)} %collective-permute-done.18.refs_1_), channel_id=1, source_target_pairs={{0,2},{2,0},{1,3},{3,1},{4,6},{6,4},{5,7},{7,5},{8,10},{10,8},{9,1... | collective-permute-start | bytes 258056 | tf_op jit(solution)/shard_map/ppermute | solution.py:352
  91.5 4.5 %collective-permute-start.24 = (bf16[48,896]{1,0:T(8,128)(2,1)S(1)}, bf16[48,896]{1,0:T(8,128)(2,1)S(1)}, u32[]{:S(2)}, u32[]{:S(2)}) collective-permute-start(bf16[48,896]{1,0:T(8,128)(2,1)S(1)} %collective-permute-done.19.refs_2_), channel_id=1, source_target_pairs={{0,2},{2,0},{1,3},{3,1},{4,6},{6,4},{5,7},{7,5},{8,10},{10,8},{9,1... | collective-permute-start | bytes 258056 | tf_op jit(solution)/shard_map/ppermute | solution.py:352
  93.0 4.5 %collective-permute-start.25 = (bf16[48,896]{1,0:T(8,128)(2,1)S(1)}, bf16[48,896]{1,0:T(8,128)(2,1)S(1)}, u32[]{:S(2)}, u32[]{:S(2)}) collective-permute-start(bf16[48,896]{1,0:T(8,128)(2,1)S(1)} %collective-permute-done.20.refs_3_), channel_id=1, source_target_pairs={{0,2},{2,0},{1,3},{3,1},{4,6},{6,4},{5,7},{7,5},{8,10},{10,8},{9,1... | collective-permute-start | bytes 258056 | tf_op jit(solution)/shard_map/ppermute | solution.py:352
  94.5 3.5 %collective-permute-start.21 = (bf16[48,3584]{1,0:T(8,128)(2,1)S(1)}, bf16[48,3584]{1,0:T(8,128)(2,1)S(1)}, u32[]{:S(2)}, u32[]{:S(2)}) collective-permute-start(bf16[48,3584]{1,0:T(8,128)(2,1)S(1)} %shard_map.106.refs_0_), channel_id=1, source_target_pairs={{0,1},{1,0},{2,3},{3,2},{4,5},{5,4},{6,7},{7,6},{8,9},{9,8},{10,11... | collective-permute-start | bytes 1032200 | tf_op jit(solution)/shard_map/ppermute | solution.py:352
  97.9 1.7 %collective-permute-start.26 = (bf16[48,3584]{1,0:T(8,128)(2,1)S(1)}, bf16[48,3584]{1,0:T(8,128)(2,1)S(1)}, u32[]{:S(2)}, u32[]{:S(2)}) collective-permute-start(bf16[48,3584]{1,0:T(8,128)(2,1)S(1)} %shard_map.107.refs_2_), channel_id=1, source_target_pairs={{0,1},{1,0},{2,3},{3,2},{4,5},{5,4},{6,7},{7,6},{8,9},{9,8},{10,11... | collective-permute-start | bytes 1032200 | tf_op jit(solution)/shard_map/ppermute | solution.py:352

commit v13 on v12

--- a/solution.py
+++ b/solution.py
@@ -399,9 +399,9 @@
     normed_own, drop = pick_rows([after(piece, parcels[1]) for piece in pieces], rows)
 
     far = swap(normed_own, "mp")
-    mate = swap(normed_own, "side")
+    mate = swap(after(normed_own, far, *parcels[2:]), "side")
     parcels.append(onward(after(parcels[1], normed_own)))
-    far_mate = swap(after(far, mate, parcels[2]), "side")
+    far_mate = swap(after(far, parcels[2]), "side")
     entries = [far_mate, far, mate, normed_own]
 
     away = away_partial(entries, proj)

time: 101 us -> 100 us (0.990)
  starting transfers between devices: 40 us -> 38.8 us
    ppermute x24, waiting for transfers between devices: 33.7 us -> 35.8 us  [swap(): lax.ppermute(x, axis, [(i, i ^ k) for i in range(lax.axis_size(axis))])]
    ppermute x3, waiting for transfers between devices: 9.25 us -> 8.03 us  [onward(): lax.ppermute(x, 'seq', [(i, i + 1) for i in range(lax.axis_size('seq') -...]
    ppermute x24, starting transfers between devices: 30.9 us -> 29.7 us  [swap(): lax.ppermute(x, axis, [(i, i ^ k) for i in range(lax.axis_size(axis))])]
  transfers between devices with their start and end apart: 27 -> 27, of which waited for: 16 -> 18; matrix products, arithmetic and copies ran while one was open for 4% -> 4% of each run, Pallas kernels for 7% -> 8%
where the time goes in v13:
time: 100 us
  waiting for transfers between devices  43.8 us (44%)
  starting transfers between devices  38.8 us (39%)
  Pallas kernels  11.4 us (11%)
  matrix products  2.98 us (3%)
  other arithmetic  1.29 us (1%)
    ppermute x24, waiting for transfers between devices, swap(): lax.ppermute(x, axis, [(i, i ^ k) for i in range(lax.axis_size(axis))])  35.8 us
    ppermute x24, starting transfers between devices, swap(): lax.ppermute(x, axis, [(i, i ^ k) for i in range(lax.axis_size(axis))])  29.7 us
    pallas_call x15, Pallas kernels, call(): pl.pallas_call(kernel, out_shape=shapes, cost_estimate=pl.CostEstimate(fl...  11.4 us
    ppermute x3, starting transfers between devices, onward(): lax.ppermute(x, 'seq', [(i, i + 1) for i in range(lax.axis_size('seq') -...  9.06 us
    ppermute x3, waiting for transfers between devices, onward(): lax.ppermute(x, 'seq', [(i, i + 1) for i in range(lax.axis_size('seq') -...  8.03 us
    dot_general x1, matrix products, dot(): return lax.dot_general(a, b, (dims, ((), ())), preferred_element_type=F32)  2.98 us
  transfers between devices with their start and end apart: 27, of which 18 were waited for; matrix products, arithmetic and copies ran while one was open for 4% of the time, Pallas kernels for 8%

profile of v13, /device:TPU:0, one launch (start us, length us, event | category | flops | bytes accessed | tf_op | source)
XLA Modules:
  0.0 100.0 jit_solution(13174713536438153480)
XLA Ops:
  0.7 0.9 convert_select_fusion.small_ref
  1.6 1.2 %shard_map.95 = (bf16[48,1024]{1,0:T(8,128)(2,1)S(1)}, bf16[48,1024]{1,0:T(8,128)(2,1)S(1)}, bf16[48,1024]{1,0:T(8,128)(2,1)S(1)}, bf16[48,1024]{1,0:T(8,128)(2,1)S(1)}, bf16[2,48,3584]{2,1,0:T(8,128)(2,1)S(1)}) custom-call(bf16[4,48,3584]{2,1,0:T(8,128)(2,1)} %bitcast.7, f32[30,128]{1,0:T(8,128)S(1)} %convert_select_fusion.small_ref), custom_call_target="tpu_custom_call" | custom-call | flops 1032192 | bytes 1376256 | tf_op jit(solution)/shard_map/pallas_call | solution.py:49
  2.8 5.1 %collective-permute-start = (bf16[48,1024]{1,0:T(8,128)(2,1)S(1)}, bf16[48,1024]{1,0:T(8,128)(2,1)S(1)}, u32[]{:S(2)}, u32[]{:S(2)}) collective-permute-start(bf16[48,1024]{1,0:T(8,128)(2,1)S(1)} %get-tuple-element.45), channel_id=1, source_target_pairs={{0,12},{4,8},{8,4},{12,0},{1,13},{5,9},{9,5},{13,1},{2,14},{6,10},... | collective-permute-start | bytes 294920 | tf_op jit(solution)/shard_map/ppermute | solution.py:352
  7.9 0.6 collective-permute-start.3
  8.6 0.8 constant_dynamic-slice_fusion
  9.4 3.3 %collective-permute-start.1 = (bf16[256,128]{1,0:T(8,128)(2,1)S(1)}, bf16[256,128]{1,0:T(8,128)(2,1)S(1)}, u32[]{:S(2)}, u32[]{:S(2)}) collective-permute-start(bf16[256,128]{1,0:T(8,128)(2,1)S(1)} %pad_maximum_fusion.1.refs_0_), channel_id=1, source_target_pairs={{0,4},{4,8},{8,12},{1,5},{5,9},{9,13},{2,6},{6,10},{10,14},{3,7},{... | collective-permute-start | bytes 196616 | tf_op jit(solution)/shard_map/ppermute | solution.py:356
  12.7 3.0 %collective-permute-done.1.refs_1_ = bf16[256,128]{1,0:T(8,128)(2,1)S(1)} collective-permute-done((bf16[256,128]{1,0:T(8,128)(2,1)S(1)}, bf16[256,128]{1,0:T(8,128)(2,1)S(1)}, u32[]{:S(2)}, u32[]{:S(2)}) %collective-permute-start.1) | collective-permute-done | bytes 65568 | tf_op jit(solution)/shard_map/ppermute | solution.py:356
  15.7 0.5 collective-permute-done.2.refs_1_.refs_6_
  16.2 0.4 shard_map.96
  16.6 1.6 %collective-permute-start.4 = (bf16[128,896]{1,0:T(8,128)(2,1)S(1)}, bf16[128,896]{1,0:T(8,128)(2,1)S(1)}, u32[]{:S(2)}, u32[]{:S(2)}) collective-permute-start(bf16[128,896]{1,0:T(8,128)(2,1)S(1)} %get-tuple-element.62.refs_3_), channel_id=1, source_target_pairs={{0,2},{2,0},{1,3},{3,1},{4,6},{6,4},{5,7},{7,5},{8,10},{10,8},{9,1... | collective-permute-start | bytes 688136 | tf_op jit(solution)/shard_map/ppermute | solution.py:352
  18.2 3.8 %collective-permute-start.5 = (bf16[256,128]{1,0:T(8,128)(2,1)S(1)}, bf16[256,128]{1,0:T(8,128)(2,1)S(1)}, u32[]{:S(2)}, u32[]{:S(2)}) collective-permute-start(bf16[256,128]{1,0:T(8,128)(2,1)S(1)} %collective-permute-done.1.refs_1_), channel_id=1, source_target_pairs={{0,4},{4,8},{8,12},{1,5},{5,9},{9,13},{2,6},{6,10},{10,14},{3,7},{... | collective-permute-start | bytes 196616 | tf_op jit(solution)/shard_map/ppermute | solution.py:356
  22.0 1.3 %collective-permute-done.4.refs_1_ = bf16[128,896]{1,0:T(8,128)(2,1)S(1)} collective-permute-done((bf16[128,896]{1,0:T(8,128)(2,1)S(1)}, bf16[128,896]{1,0:T(8,128)(2,1)S(1)}, u32[]{:S(2)}, u32[]{:S(2)}) %collective-permute-start.4) | collective-permute-done | bytes 229408 | tf_op jit(solution)/shard_map/ppermute | solution.py:352
  23.3 0.6 collective-permute-done.5.refs_2_
  23.9 0.5 collective-permute-start.7
  24.4 1.0 collective-permute-done.6.refs_0_
  25.4 0.3 collective-permute-done.7.refs_2_
  25.7 0.5 shard_map.97
  26.2 2.4 %collective-permute-start.8 = (bf16[128,1024]{1,0:T(8,128)(2,1)S(1)}, bf16[128,1024]{1,0:T(8,128)(2,1)S(1)}, u32[]{:S(2)}, u32[]{:S(2)}) collective-permute-start(bf16[128,1024]{1,0:T(8,128)(2,1)S(1)} %shard_map.97), channel_id=1, source_target_pairs={{0,4},{4,0},{8,12},{12,8},{1,5},{5,1},{9,13},{13,9},{2,6},{6,2},{1... | collective-permute-start | bytes 786440 | tf_op jit(solution)/shard_map/ppermute | solution.py:352
  28.6 1.9 %collective-permute-start.9 = (bf16[256,128]{1,0:T(8,128)(2,1)S(1)}, bf16[256,128]{1,0:T(8,128)(2,1)S(1)}, u32[]{:S(2)}, u32[]{:S(2)}) collective-permute-start(bf16[256,128]{1,0:T(8,128)(2,1)S(1)} %collective-permute-done.5.refs_2_), channel_id=1, source_target_pairs={{0,4},{4,8},{8,12},{1,5},{5,9},{9,13},{2,6},{6,10},{10,14},{3,7},{... | collective-permute-start | bytes 196616 | tf_op jit(solution)/shard_map/ppermute | solution.py:356
  30.5 0.9 shard_map.98
  31.4 4.5 %collective-permute-done.9.refs_3_ = bf16[256,128]{1,0:T(8,128)(2,1)S(1)} collective-permute-done((bf16[256,128]{1,0:T(8,128)(2,1)S(1)}, bf16[256,128]{1,0:T(8,128)(2,1)S(1)}, u32[]{:S(2)}, u32[]{:S(2)}) %collective-permute-start.9) | collective-permute-done | bytes 65568 | tf_op jit(solution)/shard_map/ppermute | solution.py:356
  35.9 0.1 add_convert_fusion
  36.0 2.4 %collective-permute-start.10 = (bf16[128,1024]{1,0:T(8,128)(2,1)S(1)}, bf16[128,1024]{1,0:T(8,128)(2,1)S(1)}, u32[]{:S(2)}, u32[]{:S(2)}) collective-permute-start(bf16[128,1024]{1,0:T(8,128)(2,1)S(1)} %add_convert_fusion), channel_id=1, source_target_pairs={{0,8},{4,12},{8,0},{12,4},{1,9},{5,13},{9,1},{13,5},{2,10},{6,14},... | collective-permute-start | bytes 786440 | tf_op jit(solution)/shard_map/ppermute | solution.py:352
  38.4 0.4 shard_map.99
  38.8 2.5 %collective-permute-start.11 = (bf16[128,1024]{1,0:T(8,128)(2,1)S(1)}, bf16[128,1024]{1,0:T(8,128)(2,1)S(1)}, u32[]{:S(2)}, u32[]{:S(2)}) collective-permute-start(bf16[128,1024]{1,0:T(8,128)(2,1)S(1)} %shard_map.99), channel_id=1, source_target_pairs={{0,4},{4,0},{8,12},{12,8},{1,5},{5,1},{9,13},{13,9},{2,6},{6,2},{1... | collective-permute-start | bytes 786440 | tf_op jit(solution)/shard_map/ppermute | solution.py:352
  41.4 2.4 %shard_map.100 = bf16[128,1024]{1,0:T(8,128)(2,1)S(1)} custom-call(bf16[128,1024]{1,0:T(8,128)(2,1)S(1)} %copy-done.1, bf16[256,128]{1,0:T(8,128)(2,1)S(1)} %pad_maximum_fusion.1.refs_0_, bf16[256,128]{1,0:T(8,128)(2,1)S(1)} %collective-permute-done.1.refs_1_, bf16[256,128]{1,0:T(8,128)(2,1)S(1)} %collective-permute-done.5.refs_2_, ...), custom_call_target="tpu_custom_call" | custom-call | bytes 524288 | tf_op jit(solution)/shard_map/pallas_call | solution.py:49
  43.7 6.5 %collective-permute-done.10 = bf16[128,1024]{1,0:T(8,128)(2,1)S(1)} collective-permute-done((bf16[128,1024]{1,0:T(8,128)(2,1)S(1)}, bf16[128,1024]{1,0:T(8,128)(2,1)S(1)}, u32[]{:S(2)}, u32[]{:S(2)}) %collective-permute-start.10) | collective-permute-done | bytes 262176 | tf_op jit(solution)/shard_map/ppermute | solution.py:352
  50.2 0.1 convert_add_fusion
  50.3 0.2 collective-permute-done.11
  50.5 0.1 subtract_convert_fusion.delta_ref
  50.6 2.2 %collective-permute-start.13 = (bf16[128,1024]{1,0:T(8,128)(2,1)S(1)}, bf16[128,1024]{1,0:T(8,128)(2,1)S(1)}, u32[]{:S(2)}, u32[]{:S(2)}) collective-permute-start(bf16[128,1024]{1,0:T(8,128)(2,1)S(1)} %subtract_convert_fusion.delta_ref), channel_id=1, source_target_pairs={{0,8},{4,12},{8,0},{12,4},{1,9},{5,13},{9,1},{13,5},{2,10},{6,14},... | collective-permute-start | bytes 786440 | tf_op jit(solution)/shard_map/ppermute | solution.py:352
  52.8 0.7 shard_map.101.first_ref
  53.5 2.3 %collective-permute-start.12 = (bf16[128,1024]{1,0:T(8,128)(2,1)S(1)}, bf16[128,1024]{1,0:T(8,128)(2,1)S(1)}, u32[]{:S(2)}, u32[]{:S(2)}) collective-permute-start(bf16[128,1024]{1,0:T(8,128)(2,1)S(1)} %subtract_convert_fusion.delta_ref), channel_id=1, source_target_pairs={{0,4},{4,0},{8,12},{12,8},{1,5},{5,1},{9,13},{13,9},{2,6},{6,2},{1... | collective-permute-start | bytes 786440 | tf_op jit(solution)/shard_map/ppermute | solution.py:352
  55.8 7.8 %collective-permute-done.13.delta_ref = bf16[128,1024]{1,0:T(8,128)(2,1)S(1)} collective-permute-done((bf16[128,1024]{1,0:T(8,128)(2,1)S(1)}, bf16[128,1024]{1,0:T(8,128)(2,1)S(1)}, u32[]{:S(2)}, u32[]{:S(2)}) %collective-permute-start.13) | collective-permute-done | bytes 262176 | tf_op jit(solution)/shard_map/ppermute | solution.py:352
  63.6 0.5 collective-permute-start.14
  64.1 0.7 shard_map.103.third_ref
  64.9 0.7 shard_map.102.second_ref
  65.6 5.1 %collective-permute-done.14.delta_ref = bf16[128,1024]{1,0:T(8,128)(2,1)S(1)} collective-permute-done((bf16[128,1024]{1,0:T(8,128)(2,1)S(1)}, bf16[128,1024]{1,0:T(8,128)(2,1)S(1)}, u32[]{:S(2)}, u32[]{:S(2)}) %collective-permute-start.14) | collective-permute-done | bytes 262176 | tf_op jit(solution)/shard_map/ppermute | solution.py:352
  70.6 0.8 shard_map.104
  71.4 0.1 collective-permute-start.15
  71.5 0.1 pad_maximum_fusion
  71.6 1.4 %collective-permute-done.15 = bf16[128,896]{1,0:T(8,128)(2,1)S(1)} collective-permute-done((bf16[128,896]{1,0:T(8,128)(2,1)S(1)}, bf16[128,896]{1,0:T(8,128)(2,1)S(1)}, u32[]{:S(2)}, u32[]{:S(2)}) %collective-permute-start.15) | collective-permute-done | bytes 229408 | tf_op jit(solution)/shard_map/ppermute | solution.py:352
  73.0 0.1 add_convert_fusion.1
  73.0 0.6 collective-permute-start.17
  73.7 3.0 %convolution_multiply_fusion = f32[896,1024]{1,0:T(8,128)} fusion(bf16[512,896]{1,0:T(8,128)(2,1)S(1)} %get-tuple-element.68.normed_ref, bf16[512,1024]{1,0:T(8,128)(2,1)S(1)} %pad_maximum_fusion), kind=kOutput, calls=%fused_computation | convolution fusion | flops 940441600 | bytes 5636096 | tf_op jit(solution)/shard_map/dot_general | solution.py:22
  76.6 4.1 %collective-permute-done.17.crossed_ref = bf16[128,896]{1,0:T(8,128)(2,1)S(1)} collective-permute-done((bf16[128,896]{1,0:T(8,128)(2,1)S(1)}, bf16[128,896]{1,0:T(8,128)(2,1)S(1)}, u32[]{:S(2)}, u32[]{:S(2)}) %collective-permute-start.17) | collective-permute-done | bytes 229408 | tf_op jit(solution)/shard_map/ppermute | solution.py:352
  80.7 0.3 shard_map.105
  81.1 1.8 %collective-permute-start.18 = (bf16[48,896]{1,0:T(8,128)(2,1)S(1)}, bf16[48,896]{1,0:T(8,128)(2,1)S(1)}, u32[]{:S(2)}, u32[]{:S(2)}) collective-permute-start(bf16[48,896]{1,0:T(8,128)(2,1)S(1)} %get-tuple-element.80), channel_id=1, source_target_pairs={{0,4},{4,0},{8,12},{12,8},{1,5},{5,1},{9,13},{13,9},{2,6},{6,2},{1... | collective-permute-start | bytes 258056 | tf_op jit(solution)/shard_map/ppermute | solution.py:352
  82.9 3.4 %collective-permute-start.19 = (bf16[48,896]{1,0:T(8,128)(2,1)S(1)}, bf16[48,896]{1,0:T(8,128)(2,1)S(1)}, u32[]{:S(2)}, u32[]{:S(2)}) collective-permute-start(bf16[48,896]{1,0:T(8,128)(2,1)S(1)} %get-tuple-element.82), channel_id=1, source_target_pairs={{0,8},{4,12},{8,0},{12,4},{1,9},{5,13},{9,1},{13,5},{2,10},{6,14},... | collective-permute-start | bytes 258056 | tf_op jit(solution)/shard_map/ppermute | solution.py:352
  86.3 0.6 collective-permute-start.22
  86.9 1.5 %collective-permute-start.23 = (bf16[48,896]{1,0:T(8,128)(2,1)S(1)}, bf16[48,896]{1,0:T(8,128)(2,1)S(1)}, u32[]{:S(2)}, u32[]{:S(2)}) collective-permute-start(bf16[48,896]{1,0:T(8,128)(2,1)S(1)} %collective-permute-done.18.refs_1_), channel_id=1, source_target_pairs={{0,2},{2,0},{1,3},{3,1},{4,6},{6,4},{5,7},{7,5},{8,10},{10,8},{9,1... | collective-permute-start | bytes 258056 | tf_op jit(solution)/shard_map/ppermute | solution.py:352
  88.3 3.3 %collective-permute-done.19.refs_2_ = bf16[48,896]{1,0:T(8,128)(2,1)S(1)} collective-permute-done((bf16[48,896]{1,0:T(8,128)(2,1)S(1)}, bf16[48,896]{1,0:T(8,128)(2,1)S(1)}, u32[]{:S(2)}, u32[]{:S(2)}) %collective-permute-start.19) | collective-permute-done | bytes 86048 | tf_op jit(solution)/shard_map/ppermute | solution.py:352
  91.6 0.6 collective-permute-start.24
  92.1 0.5 collective-permute-done.20.refs_3_
  92.7 0.9 collective-permute-start.25
  93.6 0.4 shard_map.106.refs_0_
  94.0 0.1 collective-permute-start.21
  94.1 2.0 %collective-permute-done.24.refs_2_ = bf16[48,896]{1,0:T(8,128)(2,1)S(1)} collective-permute-done((bf16[48,896]{1,0:T(8,128)(2,1)S(1)}, bf16[48,896]{1,0:T(8,128)(2,1)S(1)}, u32[]{:S(2)}, u32[]{:S(2)}) %collective-permute-start.24) | collective-permute-done | bytes 86048 | tf_op jit(solution)/shard_map/ppermute | solution.py:352
  96.1 1.1 %collective-permute-done.25.refs_3_ = bf16[48,896]{1,0:T(8,128)(2,1)S(1)} collective-permute-done((bf16[48,896]{1,0:T(8,128)(2,1)S(1)}, bf16[48,896]{1,0:T(8,128)(2,1)S(1)}, u32[]{:S(2)}, u32[]{:S(2)}) %collective-permute-start.25) | collective-permute-done | bytes 86048 | tf_op jit(solution)/shard_map/ppermute | solution.py:352
  97.2 0.4 shard_map.107.refs_2_
  97.5 0.1 collective-permute-start.26
  97.6 1.0 shard_map.108.t
  98.6 0.6 collective-permute-done.26.refs_0_
  99.2 0.7 shard_map.109
  (19 shorter events, 0.1 us)
Async XLA Ops:
  0.6 25.1 %copy-start = (bf16[896,1024]{1,0:T(8,128)(2,1)S(1)}, bf16[896,1024]{1,0:T(8,128)(2,1)}, u32[]{:S(2)}) copy-start(bf16[896,1024]{1,0:T(8,128)(2,1)} %proj_ref.9) | copy-start | bytes 5505028
  2.8 12.8 %collective-permute-start = (bf16[48,1024]{1,0:T(8,128)(2,1)S(1)}, bf16[48,1024]{1,0:T(8,128)(2,1)S(1)}, u32[]{:S(2)}, u32[]{:S(2)}) collective-permute-start(bf16[48,1024]{1,0:T(8,128)(2,1)S(1)} %get-tuple-element.45), channel_id=1, source_target_pairs={{0,12},{4,8},{8,4},{12,0},{1,13},{5,9},{9,5},{13,1},{2,14},{6,10},... | collective-permute-start | bytes 294920 | tf_op jit(solution)/shard_map/ppermute | solution.py:352
  7.9 8.3 %collective-permute-start.2 = (bf16[48,1024]{1,0:T(8,128)(2,1)S(1)}, bf16[48,1024]{1,0:T(8,128)(2,1)S(1)}, u32[]{:S(2)}, u32[]{:S(2)}) collective-permute-start(bf16[48,1024]{1,0:T(8,128)(2,1)S(1)} %get-tuple-element.49), channel_id=1, source_target_pairs={{0,8},{4,12},{8,0},{12,4},{1,9},{5,13},{9,1},{13,5},{2,10},{6,14},... | collective-permute-start | bytes 294920 | tf_op jit(solution)/shard_map/ppermute | solution.py:352
  7.9 8.3 %collective-permute-start.3 = (bf16[48,1024]{1,0:T(8,128)(2,1)S(1)}, bf16[48,1024]{1,0:T(8,128)(2,1)S(1)}, u32[]{:S(2)}, u32[]{:S(2)}) collective-permute-start(bf16[48,1024]{1,0:T(8,128)(2,1)S(1)} %get-tuple-element.51), channel_id=1, source_target_pairs={{0,4},{4,0},{8,12},{12,8},{1,5},{5,1},{9,13},{13,9},{2,6},{6,2},{1... | collective-permute-start | bytes 294920 | tf_op jit(solution)/shard_map/ppermute | solution.py:352
  9.4 6.3 %collective-permute-start.1 = (bf16[256,128]{1,0:T(8,128)(2,1)S(1)}, bf16[256,128]{1,0:T(8,128)(2,1)S(1)}, u32[]{:S(2)}, u32[]{:S(2)}) collective-permute-start(bf16[256,128]{1,0:T(8,128)(2,1)S(1)} %pad_maximum_fusion.1.refs_0_), channel_id=1, source_target_pairs={{0,4},{4,8},{8,12},{1,5},{5,9},{9,13},{2,6},{6,10},{10,14},{3,7},{... | collective-permute-start | bytes 196616 | tf_op jit(solution)/shard_map/ppermute | solution.py:356
  16.6 6.7 %collective-permute-start.4 = (bf16[128,896]{1,0:T(8,128)(2,1)S(1)}, bf16[128,896]{1,0:T(8,128)(2,1)S(1)}, u32[]{:S(2)}, u32[]{:S(2)}) collective-permute-start(bf16[128,896]{1,0:T(8,128)(2,1)S(1)} %get-tuple-element.62.refs_3_), channel_id=1, source_target_pairs={{0,2},{2,0},{1,3},{3,1},{4,6},{6,4},{5,7},{7,5},{8,10},{10,8},{9,1... | collective-permute-start | bytes 688136 | tf_op jit(solution)/shard_map/ppermute | solution.py:352
  18.2 5.7 %collective-permute-start.5 = (bf16[256,128]{1,0:T(8,128)(2,1)S(1)}, bf16[256,128]{1,0:T(8,128)(2,1)S(1)}, u32[]{:S(2)}, u32[]{:S(2)}) collective-permute-start(bf16[256,128]{1,0:T(8,128)(2,1)S(1)} %collective-permute-done.1.refs_1_), channel_id=1, source_target_pairs={{0,4},{4,8},{8,12},{1,5},{5,9},{9,13},{2,6},{6,10},{10,14},{3,7},{... | collective-permute-start | bytes 196616 | tf_op jit(solution)/shard_map/ppermute | solution.py:356
  23.9 1.5 %collective-permute-start.6 = (bf16[128,896]{1,0:T(8,128)(2,1)S(1)}, bf16[128,896]{1,0:T(8,128)(2,1)S(1)}, u32[]{:S(2)}, u32[]{:S(2)}) collective-permute-start(bf16[128,896]{1,0:T(8,128)(2,1)S(1)} %collective-permute-done.4.refs_1_), channel_id=1, source_target_pairs={{0,1},{1,0},{2,3},{3,2},{4,5},{5,4},{6,7},{7,6},{8,9},{9,8},{10,11... | collective-permute-start | bytes 688136 | tf_op jit(solution)/shard_map/ppermute | solution.py:352
  23.9 1.8 %collective-permute-start.7 = (bf16[128,896]{1,0:T(8,128)(2,1)S(1)}, bf16[128,896]{1,0:T(8,128)(2,1)S(1)}, u32[]{:S(2)}, u32[]{:S(2)}) collective-permute-start(bf16[128,896]{1,0:T(8,128)(2,1)S(1)} %get-tuple-element.62.refs_3_), channel_id=1, source_target_pairs={{0,1},{1,0},{2,3},{3,2},{4,5},{5,4},{6,7},{7,6},{8,9},{9,8},{10,11... | collective-permute-start | bytes 688136 | tf_op jit(solution)/shard_map/ppermute | solution.py:352
  26.2 9.7 %collective-permute-start.8 = (bf16[128,1024]{1,0:T(8,128)(2,1)S(1)}, bf16[128,1024]{1,0:T(8,128)(2,1)S(1)}, u32[]{:S(2)}, u32[]{:S(2)}) collective-permute-start(bf16[128,1024]{1,0:T(8,128)(2,1)S(1)} %shard_map.97), channel_id=1, source_target_pairs={{0,4},{4,0},{8,12},{12,8},{1,5},{5,1},{9,13},{13,9},{2,6},{6,2},{1... | collective-permute-start | bytes 786440 | tf_op jit(solution)/shard_map/ppermute | solution.py:352
  28.6 7.3 %collective-permute-start.9 = (bf16[256,128]{1,0:T(8,128)(2,1)S(1)}, bf16[256,128]{1,0:T(8,128)(2,1)S(1)}, u32[]{:S(2)}, u32[]{:S(2)}) collective-permute-start(bf16[256,128]{1,0:T(8,128)(2,1)S(1)} %collective-permute-done.5.refs_2_), channel_id=1, source_target_pairs={{0,4},{4,8},{8,12},{1,5},{5,9},{9,13},{2,6},{6,10},{10,14},{3,7},{... | collective-permute-start | bytes 196616 | tf_op jit(solution)/shard_map/ppermute | solution.py:356
  31.4 9.9 %copy-start.1 = (bf16[128,1024]{1,0:T(8,128)(2,1)S(1)}, bf16[128,1024]{1,0:T(8,128)(2,1)}, u32[]{:S(2)}) copy-start(bf16[128,1024]{1,0:T(8,128)(2,1)} %queries_ref) | copy-start | bytes 786436
  36.0 14.3 %collective-permute-start.10 = (bf16[128,1024]{1,0:T(8,128)(2,1)S(1)}, bf16[128,1024]{1,0:T(8,128)(2,1)S(1)}, u32[]{:S(2)}, u32[]{:S(2)}) collective-permute-start(bf16[128,1024]{1,0:T(8,128)(2,1)S(1)} %add_convert_fusion), channel_id=1, source_target_pairs={{0,8},{4,12},{8,0},{12,4},{1,9},{5,13},{9,1},{13,5},{2,10},{6,14},... | collective-permute-start | bytes 786440 | tf_op jit(solution)/shard_map/ppermute | solution.py:352
  38.8 11.7 %collective-permute-start.11 = (bf16[128,1024]{1,0:T(8,128)(2,1)S(1)}, bf16[128,1024]{1,0:T(8,128)(2,1)S(1)}, u32[]{:S(2)}, u32[]{:S(2)}) collective-permute-start(bf16[128,1024]{1,0:T(8,128)(2,1)S(1)} %shard_map.99), channel_id=1, source_target_pairs={{0,4},{4,0},{8,12},{12,8},{1,5},{5,1},{9,13},{13,9},{2,6},{6,2},{1... | collective-permute-start | bytes 786440 | tf_op jit(solution)/shard_map/ppermute | solution.py:352
  50.6 13.0 %collective-permute-start.13 = (bf16[128,1024]{1,0:T(8,128)(2,1)S(1)}, bf16[128,1024]{1,0:T(8,128)(2,1)S(1)}, u32[]{:S(2)}, u32[]{:S(2)}) collective-permute-start(bf16[128,1024]{1,0:T(8,128)(2,1)S(1)} %subtract_convert_fusion.delta_ref), channel_id=1, source_target_pairs={{0,8},{4,12},{8,0},{12,4},{1,9},{5,13},{9,1},{13,5},{2,10},{6,14},... | collective-permute-start | bytes 786440 | tf_op jit(solution)/shard_map/ppermute | solution.py:352
  53.5 11.3 %collective-permute-start.12 = (bf16[128,1024]{1,0:T(8,128)(2,1)S(1)}, bf16[128,1024]{1,0:T(8,128)(2,1)S(1)}, u32[]{:S(2)}, u32[]{:S(2)}) collective-permute-start(bf16[128,1024]{1,0:T(8,128)(2,1)S(1)} %subtract_convert_fusion.delta_ref), channel_id=1, source_target_pairs={{0,4},{4,0},{8,12},{12,8},{1,5},{5,1},{9,13},{13,9},{2,6},{6,2},{1... | collective-permute-start | bytes 786440 | tf_op jit(solution)/shard_map/ppermute | solution.py:352
  63.6 7.0 %collective-permute-start.14 = (bf16[128,1024]{1,0:T(8,128)(2,1)S(1)}, bf16[128,1024]{1,0:T(8,128)(2,1)S(1)}, u32[]{:S(2)}, u32[]{:S(2)}) collective-permute-start(bf16[128,1024]{1,0:T(8,128)(2,1)S(1)} %collective-permute-done.13.delta_ref), channel_id=1, source_target_pairs={{0,4},{4,0},{8,12},{12,8},{1,5},{5,1},{9,13},{13,9},{2,6},{6,2},{1... | collective-permute-start | bytes 786440 | tf_op jit(solution)/shard_map/ppermute | solution.py:352
  71.4 1.6 %collective-permute-start.15 = (bf16[128,896]{1,0:T(8,128)(2,1)S(1)}, bf16[128,896]{1,0:T(8,128)(2,1)S(1)}, u32[]{:S(2)}, u32[]{:S(2)}) collective-permute-start(bf16[128,896]{1,0:T(8,128)(2,1)S(1)} %get-tuple-element.74), channel_id=1, source_target_pairs={{0,1},{1,0},{2,3},{3,2},{4,5},{5,4},{6,7},{7,6},{8,9},{9,8},{10,11... | collective-permute-start | bytes 688136 | tf_op jit(solution)/shard_map/ppermute | solution.py:352
  73.0 7.7 %collective-permute-start.17 = (bf16[128,896]{1,0:T(8,128)(2,1)S(1)}, bf16[128,896]{1,0:T(8,128)(2,1)S(1)}, u32[]{:S(2)}, u32[]{:S(2)}) collective-permute-start(bf16[128,896]{1,0:T(8,128)(2,1)S(1)} %add_convert_fusion.1), channel_id=1, source_target_pairs={{0,2},{2,0},{1,3},{3,1},{4,6},{6,4},{5,7},{7,5},{8,10},{10,8},{9,1... | collective-permute-start | bytes 688136 | tf_op jit(solution)/shard_map/ppermute | solution.py:352
  73.6 7.1 %collective-permute-start.16 = (bf16[128,896]{1,0:T(8,128)(2,1)S(1)}, bf16[128,896]{1,0:T(8,128)(2,1)S(1)}, u32[]{:S(2)}, u32[]{:S(2)}) collective-permute-start(bf16[128,896]{1,0:T(8,128)(2,1)S(1)} %get-tuple-element.75), channel_id=1, source_target_pairs={{0,1},{1,0},{2,3},{3,2},{4,5},{5,4},{6,7},{7,6},{8,9},{9,8},{10,11... | collective-permute-start | bytes 688136 | tf_op jit(solution)/shard_map/ppermute | solution.py:352
  81.1 5.8 %collective-permute-start.18 = (bf16[48,896]{1,0:T(8,128)(2,1)S(1)}, bf16[48,896]{1,0:T(8,128)(2,1)S(1)}, u32[]{:S(2)}, u32[]{:S(2)}) collective-permute-start(bf16[48,896]{1,0:T(8,128)(2,1)S(1)} %get-tuple-element.80), channel_id=1, source_target_pairs={{0,4},{4,0},{8,12},{12,8},{1,5},{5,1},{9,13},{13,9},{2,6},{6,2},{1... | collective-permute-start | bytes 258056 | tf_op jit(solution)/shard_map/ppermute | solution.py:352
  82.9 8.7 %collective-permute-start.19 = (bf16[48,896]{1,0:T(8,128)(2,1)S(1)}, bf16[48,896]{1,0:T(8,128)(2,1)S(1)}, u32[]{:S(2)}, u32[]{:S(2)}) collective-permute-start(bf16[48,896]{1,0:T(8,128)(2,1)S(1)} %get-tuple-element.82), channel_id=1, source_target_pairs={{0,8},{4,12},{8,0},{12,4},{1,9},{5,13},{9,1},{13,5},{2,10},{6,14},... | collective-permute-start | bytes 258056 | tf_op jit(solution)/shard_map/ppermute | solution.py:352
  86.3 6.4 %collective-permute-start.20 = (bf16[48,896]{1,0:T(8,128)(2,1)S(1)}, bf16[48,896]{1,0:T(8,128)(2,1)S(1)}, u32[]{:S(2)}, u32[]{:S(2)}) collective-permute-start(bf16[48,896]{1,0:T(8,128)(2,1)S(1)} %get-tuple-element.84), channel_id=1, source_target_pairs={{0,12},{4,8},{8,4},{12,0},{1,13},{5,9},{9,5},{13,1},{2,14},{6,10},... | collective-permute-start | bytes 258056 | tf_op jit(solution)/shard_map/ppermute | solution.py:352
  86.3 7.8 %collective-permute-start.22 = (bf16[48,896]{1,0:T(8,128)(2,1)S(1)}, bf16[48,896]{1,0:T(8,128)(2,1)S(1)}, u32[]{:S(2)}, u32[]{:S(2)}) collective-permute-start(bf16[48,896]{1,0:T(8,128)(2,1)S(1)} %get-tuple-element.79.refs_0_), channel_id=1, source_target_pairs={{0,2},{2,0},{1,3},{3,1},{4,6},{6,4},{5,7},{7,5},{8,10},{10,8},{9,1... | collective-permute-start | bytes 258056 | tf_op jit(solution)/shard_map/ppermute | solution.py:352
  86.9 7.2 %collective-permute-start.23 = (bf16[48,896]{1,0:T(8,128)(2,1)S(1)}, bf16[48,896]{1,0:T(8,128)(2,1)S(1)}, u32[]{:S(2)}, u32[]{:S(2)}) collective-permute-start(bf16[48,896]{1,0:T(8,128)(2,1)S(1)} %collective-permute-done.18.refs_1_), channel_id=1, source_target_pairs={{0,2},{2,0},{1,3},{3,1},{4,6},{6,4},{5,7},{7,5},{8,10},{10,8},{9,1... | collective-permute-start | bytes 258056 | tf_op jit(solution)/shard_map/ppermute | solution.py:352
  91.6 4.5 %collective-permute-start.24 = (bf16[48,896]{1,0:T(8,128)(2,1)S(1)}, bf16[48,896]{1,0:T(8,128)(2,1)S(1)}, u32[]{:S(2)}, u32[]{:S(2)}) collective-permute-start(bf16[48,896]{1,0:T(8,128)(2,1)S(1)} %collective-permute-done.19.refs_2_), channel_id=1, source_target_pairs={{0,2},{2,0},{1,3},{3,1},{4,6},{6,4},{5,7},{7,5},{8,10},{10,8},{9,1... | collective-permute-start | bytes 258056 | tf_op jit(solution)/shard_map/ppermute | solution.py:352
  92.7 4.5 %collective-permute-start.25 = (bf16[48,896]{1,0:T(8,128)(2,1)S(1)}, bf16[48,896]{1,0:T(8,128)(2,1)S(1)}, u32[]{:S(2)}, u32[]{:S(2)}) collective-permute-start(bf16[48,896]{1,0:T(8,128)(2,1)S(1)} %collective-permute-done.20.refs_3_), channel_id=1, source_target_pairs={{0,2},{2,0},{1,3},{3,1},{4,6},{6,4},{5,7},{7,5},{8,10},{10,8},{9,1... | collective-permute-start | bytes 258056 | tf_op jit(solution)/shard_map/ppermute | solution.py:352
  94.0 3.6 %collective-permute-start.21 = (bf16[48,3584]{1,0:T(8,128)(2,1)S(1)}, bf16[48,3584]{1,0:T(8,128)(2,1)S(1)}, u32[]{:S(2)}, u32[]{:S(2)}) collective-permute-start(bf16[48,3584]{1,0:T(8,128)(2,1)S(1)} %shard_map.106.refs_0_), channel_id=1, source_target_pairs={{0,1},{1,0},{2,3},{3,2},{4,5},{5,4},{6,7},{7,6},{8,9},{9,8},{10,11... | collective-permute-start | bytes 1032200 | tf_op jit(solution)/shard_map/ppermute | solution.py:352
  97.5 1.7 %collective-permute-start.26 = (bf16[48,3584]{1,0:T(8,128)(2,1)S(1)}, bf16[48,3584]{1,0:T(8,128)(2,1)S(1)}, u32[]{:S(2)}, u32[]{:S(2)}) collective-permute-start(bf16[48,3584]{1,0:T(8,128)(2,1)S(1)} %shard_map.107.refs_2_), channel_id=1, source_target_pairs={{0,1},{1,0},{2,3},{3,2},{4,5},{5,4},{6,7},{7,6},{8,9},{9,8},{10,11... | collective-permute-start | bytes 1032200 | tf_op jit(solution)/shard_map/ppermute | solution.py:352
